TPU v7x, 128 devices: a whole 4x4x4 slice. The times are simulated.
128 devices in a mesh: grp: 8 (over y, z_hi), lm: 16 (over x, z_lo, core).
Axes of the slice: x: 4, y: 4, z: 4 (z_hi: 2, z_lo: 2; z = z_hi * 2 + z_lo), core: 2. Of those that a mesh axis runs over, the one named last changes fastest.
Arguments:
- embeddings: bfloat16 [32768, 512], P(('grp', 'lm')), may hold values from -14 to 14
- landmarks: bfloat16 [32768, 512], P('lm'), may hold values from -14 to 14
- start_vectors: float32 [32768, 128], P(('grp', 'lm')), may hold values from -10 to 10
- row_weight: float32 [32768], P(('grp', 'lm')), may hold values from 0.1 to 9
- spread: float32 [1], replicated, may hold values from 11.313708 to 33.941124
Outputs:
- subspace: float32 [32768, 128], P(('grp', 'lm'))
All inputs are finite; a program needn't handle non-finite values.
Results may differ from a plain program's by a relative error of at most 0.019.
Values may be sent and summed in bfloat16 or wider, within the bound.
No kernel may reach another device: no remote copies, remote signals or barrier semaphores. Data moves between devices by JAX's collectives and lax.ppermute only.
A program may use at most 128 MiB of HBM per device.

v0:
```python
import jax
import jax.numpy as jnp
from jax import lax
from jax.sharding import PartitionSpec as P

ITERS = 2


def unit_rows(values):
    values = values.astype(jnp.float32)
    scale = lax.rsqrt(jnp.sum(values * values, axis=1, keepdims=True) + 1e-06)
    return (values * scale).astype(jnp.bfloat16)


def kernel_values(rows_unit, marks_unit, gamma):
    cosine = jnp.einsum("rd,ld->rl", rows_unit, marks_unit, preferred_element_type=jnp.float32)
    return jnp.exp(gamma * cosine)


def local(embeddings, landmarks, start_vectors, row_weight, spread):
    own_rows = embeddings.shape[0]
    marks = landmarks.shape[0]
    groups = lax.axis_size("grp")
    members = lax.axis_size("lm")
    total_rows = own_rows * groups * members
    group_rows = own_rows * members
    gamma = spread[0]
    rows_unit = unit_rows(embeddings)
    marks_unit = unit_rows(landmarks)
    sums = jnp.zeros((marks,), jnp.float32)
    weights = jnp.zeros((group_rows,), jnp.float32)
    part_rows = lax.all_gather(rows_unit, "lm", axis=0, tiled=True)
    part_weight = lax.all_gather(row_weight.astype(jnp.bfloat16), "lm", axis=0, tiled=True).astype(
        jnp.float32
    )
    values = kernel_values(part_rows, marks_unit, gamma)
    build_tile = values.astype(jnp.bfloat16)
    weights = lax.dynamic_update_slice_in_dim(weights, part_weight, jnp.int32(0), 0)
    sums = sums + jnp.sum(part_weight[:, None] * values, axis=0)
    mean_sum, weight_sum = lax.psum((sums, jnp.sum(weights)), "grp")
    means = mean_sum / weight_sum
    vectors = start_vectors
    weighted_full = row_weight[:, None] * vectors
    totals = lax.psum(jnp.sum(weighted_full, axis=0), ("grp", "lm"))
    group_weighted = lax.all_gather(weighted_full.astype(jnp.bfloat16), "lm", axis=0, tiled=True)
    for step in range(ITERS):
        side = (
            lax.psum(
                jnp.einsum(
                    "rl,rv->lv", build_tile, group_weighted, preferred_element_type=jnp.float32
                ),
                "grp",
            )
            - means[:, None] * totals[None, :]
        )
        side_b = side.astype(jnp.bfloat16)
        shift = jnp.dot(means, side_b.astype(jnp.float32), precision=lax.Precision.HIGHEST)
        image = lax.psum_scatter(
            weights[:, None]
            * (jnp.dot(build_tile, side_b, preferred_element_type=jnp.float32) - shift[None, :]),
            "lm",
            scatter_dimension=0,
            tiled=True,
        )
        square, column = lax.psum(
            (jnp.sum(image * image, axis=0), jnp.sum(row_weight[:, None] * image, axis=0)),
            ("grp", "lm"),
        )
        scale = jnp.sqrt(square / total_rows + 1e-06)
        vectors = image / scale[None, :]
        totals = column / scale
        if step + 1 < ITERS:
            group_weighted = lax.all_gather(
                (row_weight[:, None] * vectors).astype(jnp.bfloat16), "lm", axis=0, tiled=True
            )
    return vectors


def solution(mesh):
    in_specs = (
        P(("grp", "lm"), None),
        P("lm", None),
        P(("grp", "lm"), None),
        P(("grp", "lm")),
        P(),
    )
    out_specs = P(("grp", "lm"), None)
    return jax.shard_map(local, mesh=mesh, in_specs=in_specs, out_specs=out_specs, check_vma=False)
```

profile of v0, /device:TPU:1, one launch (start us, length us, event | category | flops | bytes accessed | tf_op | source)
XLA Modules:
  0.0 612.0 jit_solution(1574066524591326856)
XLA Ops:
  6.5 0.0 all-gather.5.cloned.1.call-start
  6.5 1.1 fusion.8
  7.6 1.8 fusion.9
  9.4 0.0 all-gather.5.cloned.1.call-update
  9.4 0.0 all-gather.7.cloned.1.call-start
  9.5 1.6 multiply_reduce_fusion.4
  11.1 0.0 all-gather.7.cloned.1.call-update
  11.1 0.0 all-reduce.5.cloned.1.call-start
  11.2 2.1 fusion.3
  13.3 0.7 convert_element_type.35
  14.0 21.3 %all-gather = bf16[16,1,256]{2,1,0:T(2,128)(2,1)S(1)} all-gather(bf16[1,1,256]{2,1,0:T(2,128)(2,1)S(1)} %reshape.21), channel_id=1, replica_groups=mesh['grp'=8,'lm'=16] {'lm'}, dimensions={0}, use_global_device_ids=true | all-gather | bytes 8704 | tf_op jit(solution)/shard_map/all_gather | solution.py:33
  36.0 14.6 %all-gather.5.cloned.1.call-done = bf16[4096,512]{1,0:T(8,128)(2,1)} async-done(((bf16[256,512]{1,0:T(8,128)(2,1)}), bf16[4096,512]{1,0:T(8,128)(2,1)}) %all-gather.5.cloned.1.call-update) | async-done | bytes 4194320 | tf_op jit(solution)/shard_map/all_gather | solution.py:32
  50.6 16.2 %multiply_reduce_fusion = (f32[2048]{0:T(1024)S(1)}, bf16[4096,2048]{1,0:T(8,128)(2,1)}) fusion(f32[4096]{0:T(1024)S(1)} %bitcast.20, f32[]{:T(128)} %bitcast.17, bf16[4096,512]{1,0:T(8,128)(2,1)} %all-gather.5.cloned.1.call-done, bf16[2048,512]{1,0:T(8,128)(2,1)} %param.6, f32[2048]{0:T(1024)S(1)} %add_rsqrt_fusion), kind=kOutput, calls=%fused_computation | convolution fusion | flops 8626632704 | bytes 23101444 | tf_op jit(solution)/shard_map/rd,ld->rl/dot_general | solution.py:16
  66.7 18.1 %all-gather.7.cloned.1.call-done = bf16[4096,128]{1,0:T(8,128)(2,1)} async-done(((bf16[256,128]{1,0:T(8,128)(2,1)}), bf16[4096,128]{1,0:T(8,128)(2,1)}) %all-gather.7.cloned.1.call-update) | async-done | bytes 1048592 | tf_op jit(solution)/shard_map/all_gather | solution.py:45
  84.8 11.6 %fusion.11 = f32[2048,128]{1,0:T(8,128)} fusion(bf16[4096,2048]{1,0:T(8,128)(2,1)} %get-tuple-element.12, bf16[4096,128]{1,0:T(8,128)(2,1)} %all-gather.7.cloned.1.call-done), kind=kOutput, calls=%fused_computation.35 | convolution fusion | flops 2147483648 | bytes 18874368 | tf_op jit(solution)/shard_map/rl,rv->lv/dot_general | solution.py:49
  96.4 0.0 all-reduce.5.cloned.1.call-update
  96.5 0.0 reduce-scatter.3.cloned.1.call-start
  96.5 69.1 %psum.59 = f32[128]{0:T(128)S(1)} all-reduce(f32[128]{0:T(128)S(1)} %get-tuple-element.13), channel_id=1, replica_groups=mesh['grp'=8,'lm'=16] {'grp','lm'}, use_global_device_ids=true, to_apply=%region_8.0 | all-reduce | flops 128 | bytes 1024 | tf_op jit(solution)/shard_map/psum | solution.py:44
  165.7 0.6 convert_reduce_fusion
  166.3 19.9 %all-reduce.1 = (f32[2048]{0:T(1024)S(1)}, f32[]{:T(128)}) all-reduce(f32[2048]{0:T(1024)S(1)} %get-tuple-element.11, f32[]{:T(128)} %convert_reduce_fusion), channel_id=1, replica_groups=mesh['grp'=8,'lm'=16] {'grp'}, use_global_device_ids=true, to_apply=%region_4.0 | all-reduce | flops 2049 | bytes 16392 | tf_op jit(solution)/shard_map/psum | solution.py:40
  186.2 0.6 broadcast_divide_fusion.1
  186.8 0.0 all-reduce.5.cloned.1.call-done
  186.9 1.8 convolution_bitcast_fusion.1
  188.7 0.0 copy-start
  188.7 12.0 %fusion.2 = f32[4096,128]{1,0:T(8,128)} fusion(bf16[4096,2048]{1,0:T(8,128)(2,1)} %get-tuple-element.12, f32[128]{0:T(128)S(1)} %convolution_bitcast_fusion.1, f32[4096]{0:T(1024)S(1)} %bitcast.21, f32[2048,128]{1,0:T(8,128)} %all-reduce.5.cloned.1.call-done, f32[128]{0:T(128)S(1)} %psum.59, f32[2048]{0:T(1024)S(1)} %broadcast_divide_fusion.1), kind=kOutput, calls=%fused_computation.8 | convolution fusion | flops 2149318656 | bytes 19948544 | tf_op jit(solution)/shard_map/dot_general | solution.py:60
  200.7 0.0 reduce-scatter.3.cloned.1.call-update
  200.7 0.0 all-gather.9.cloned.1.call-start
  200.7 61.7 %reduce-scatter.3.cloned.1.call-done = f32[256,128]{1,0:T(8,128)} async-done(((f32[4096,128]{1,0:T(8,128)}), f32[256,128]{1,0:T(8,128)}) %reduce-scatter.3.cloned.1.call-update) | async-done | bytes 131088 | tf_op jit(solution)/shard_map/reduce_scatter | solution.py:58
  262.4 0.0 copy-done
  262.4 1.0 multiply_reduce_fusion.2
  263.5 67.6 %all-reduce = (f32[128]{0:T(128)S(1)}, f32[128]{0:T(128)S(1)}) all-reduce(f32[128]{0:T(128)S(1)} %get-tuple-element.6, f32[128]{0:T(128)S(1)} %get-tuple-element.5), channel_id=1, replica_groups=mesh['grp'=8,'lm'=16] {'grp','lm'}, use_global_device_ids=true, to_apply=%region_11.0 | all-reduce | flops 256 | bytes 2048 | tf_op jit(solution)/shard_map/psum | solution.py:65
  331.1 1.6 multiply_convert_fusion
  332.8 0.0 all-gather.9.cloned.1.call-update
  332.8 0.3 all-reduce.7.cloned.1.call-start
  333.1 29.2 %all-gather.9.cloned.1.call-done = bf16[4096,128]{1,0:T(8,128)(2,1)} async-done(((bf16[256,128]{1,0:T(8,128)(2,1)}), bf16[4096,128]{1,0:T(8,128)(2,1)}) %all-gather.9.cloned.1.call-update) | async-done | bytes 1048592 | tf_op jit(solution)/shard_map/all_gather | solution.py:73
  362.2 11.6 %fusion.12 = f32[2048,128]{1,0:T(8,128)} fusion(bf16[4096,2048]{1,0:T(8,128)(2,1)} %get-tuple-element.12, bf16[4096,128]{1,0:T(8,128)(2,1)} %all-gather.9.cloned.1.call-done), kind=kOutput, calls=%fused_computation.36 | convolution fusion | flops 2147483648 | bytes 18874368 | tf_op jit(solution)/shard_map/rl,rv->lv/dot_general | solution.py:49
  373.9 0.0 all-reduce.7.cloned.1.call-update
  373.9 0.0 reduce-scatter.5.cloned.1.call-start
  373.9 83.7 %all-reduce.7.cloned.1.call-done = f32[2048,128]{1,0:T(8,128)} async-done(((f32[2048,128]{1,0:T(8,128)}), f32[2048,128]{1,0:T(8,128)}) %all-reduce.7.cloned.1.call-update) | async-done | bytes 1048592 | tf_op jit(solution)/shard_map/psum | solution.py:48
  457.6 1.8 convolution_bitcast_fusion
  459.4 12.0 %fusion.1 = f32[4096,128]{1,0:T(8,128)} fusion(bf16[4096,2048]{1,0:T(8,128)(2,1)} %get-tuple-element.12, f32[128]{0:T(128)S(1)} %convolution_bitcast_fusion, f32[4096]{0:T(1024)S(1)} %bitcast.22, f32[2048,128]{1,0:T(8,128)} %all-reduce.7.cloned.1.call-done, f32[128]{0:T(128)S(1)} %get-tuple-element.15, f32[2048]{0:T(1024)S(1)} %broadcast_divide_fusion.1), kind=kOutput, calls=%fused_computation.6 | convolution fusion | flops 2149318656 | bytes 19948544 | tf_op jit(solution)/shard_map/dot_general | solution.py:60
  471.4 0.0 reduce-scatter.5.cloned.1.call-update
  471.4 63.1 %reduce-scatter.5.cloned.1.call-done = f32[256,128]{1,0:T(8,128)} async-done(((f32[4096,128]{1,0:T(8,128)}), f32[256,128]{1,0:T(8,128)}) %reduce-scatter.5.cloned.1.call-update) | async-done | bytes 131088 | tf_op jit(solution)/shard_map/reduce_scatter | solution.py:58
  534.5 1.0 multiply_reduce_fusion.1
  535.4 68.2 %psum.63 = f32[128]{0:T(128)S(1)} all-reduce(f32[128]{0:T(128)S(1)} %multiply_reduce_fusion.1), channel_id=1, replica_groups=mesh['grp'=8,'lm'=16] {'grp','lm'}, use_global_device_ids=true, to_apply=%region_17.0 | all-reduce | flops 128 | bytes 1024 | tf_op jit(solution)/shard_map/psum | solution.py:65
  603.6 1.6 broadcast_divide_fusion
  (6 shorter events, 0.1 us)
Async XLA Ops:
  6.5 44.0 %all-gather.5.cloned.1.call-start = ((), (), s32[]{:S(2)}) async-start(), calls=%async_computation.2 | async-start | bytes 4456448 | tf_op jit(solution)/shard_map/all_gather | solution.py:32
  9.4 75.4 %all-gather.7.cloned.1.call-start = ((), (), s32[]{:S(2)}) async-start(), calls=%async_computation.3 | async-start | bytes 1114112 | tf_op jit(solution)/shard_map/all_gather | solution.py:45
  11.1 175.7 %all-reduce.5.cloned.1.call-start = ((), (), s32[]{:S(2)}) async-start(), calls=%async_computation.4 | async-start | bytes 2097152 | tf_op jit(solution)/shard_map/psum | solution.py:48
  96.5 166.0 %reduce-scatter.3.cloned.1.call-start = ((), (), s32[]{:S(2)}) async-start(), calls=%async_computation.5 | async-start | bytes 2228224 | tf_op jit(solution)/shard_map/reduce_scatter | solution.py:58
  188.7 73.8 %copy-start = (f32[256]{0:T(256)S(1)}, f32[256]{0:T(256)}, u32[]{:S(2)}) copy-start(f32[256]{0:T(256)} %param.8) | copy-start | bytes 3076
  200.7 161.5 %all-gather.9.cloned.1.call-start = ((), (), s32[]{:S(2)}) async-start(), calls=%async_computation.6 | async-start | bytes 1114112 | tf_op jit(solution)/shard_map/all_gather | solution.py:73
  332.8 124.8 %all-reduce.7.cloned.1.call-start = ((), (), s32[]{:S(2)}) async-start(), calls=%async_computation.7 | async-start | bytes 2097152 | tf_op jit(solution)/shard_map/psum | solution.py:48
  373.9 160.6 %reduce-scatter.5.cloned.1.call-start = ((), (), s32[]{:S(2)}) async-start(), calls=%async_computation.8 | async-start | bytes 2228224 | tf_op jit(solution)/shard_map/reduce_scatter | solution.py:58
Sparse Core Ops, SparseCore 0:
  9.5 40.9 all-gather.4
  52.3 32.5 all-gather.6
  96.6 84.5 all-reduce.4
  200.8 61.5 reduce-scatter.2
  332.9 29.2 all-gather.8
  374.0 83.5 all-reduce.6
  471.5 62.8 reduce-scatter.4
where the time goes:
time: 613 us; the launch traced here: 612 us
  waiting for transfers between devices  270 us (44%)
  blocking collectives  246 us (40%)
  matrix products  67 us (11%)
  between operations  14.2 us (2%)
  other arithmetic  13.8 us (2%)
    psum x2, blocking collectives, local(): lax.psum((jnp.sum(image * image, axis=0), jnp.sum(row_weight[:, None] * i...  136 us
    reduce_scatter x2, waiting for transfers between devices, local(): lax.psum_scatter(weights[:, None] * (jnp.dot(build_tile, side_b, preferre...  125 us
    psum x2, waiting for transfers between devices, local(): lax.psum(jnp.einsum('rl,rv->lv', build_tile, group_weighted, preferred_el...  83.7 us
    psum x1, blocking collectives, local(): totals = lax.psum(jnp.sum(weighted_full, axis=0), ('grp', 'lm'))  69.1 us
    all_gather x1, waiting for transfers between devices, local(): lax.all_gather((row_weight[:, None] * vectors).astype(jnp.bfloat16), 'lm'...  29.2 us
    dot_general x2, matrix products, local(): jnp.dot(build_tile, side_b, preferred_element_type=jnp.float32)  24 us
    dot_general x2, matrix products, local(): jnp.einsum('rl,rv->lv', build_tile, group_weighted, preferred_element_typ...  23.2 us
    all_gather x1, blocking collectives, local(): lax.all_gather(row_weight.astype(jnp.bfloat16), 'lm', axis=0, tiled=True)  21.3 us
  transfers between devices with their start and end apart: 7, of which 6 were waited for; matrix products, arithmetic and copies ran while one was open for 4% of the time, Pallas kernels for 0%

commit v1 on v0

v1 whole, which is shorter than its diff:
```python
import jax
import jax.numpy as jnp
from jax import lax
from jax.sharding import Mesh
from jax.sharding import PartitionSpec as P

ITERS = 2
AXES = ("y", "zh", "x", "zl", "core")
ROW_AXES = ("x", "zl")
MARK_AXES = ("y", "zh")
F32, B16 = jnp.float32, jnp.bfloat16
DOWN = 2.0**-20
UP = 2.0**20


def unit_rows(values):
    values = values.astype(F32)
    scale = lax.rsqrt(jnp.sum(values * values, axis=1, keepdims=True) + 1e-06)
    return (values * scale).astype(B16)


def split3(values):
    high = lax.reduce_precision(values, 8, 7)
    rest = values - high
    mid = lax.reduce_precision(rest, 8, 7)
    low = rest - mid
    return [high.astype(B16), mid.astype(B16), low.astype(B16)]


def join3(parts):
    parts = parts.astype(F32)
    return (parts[..., 2, :] + parts[..., 1, :]) + parts[..., 0, :]


def spread_to(payload, axes):
    count = lax.axis_size(axes)
    return lax.all_to_all(jnp.broadcast_to(payload[None], (count,) + payload.shape), axes, 0, 0)


def swap_core(values):
    return lax.ppermute(values, "core", [(0, 1), (1, 0)])


def with_tail(body, stats):
    width = body.shape[1]
    parts = [jnp.pad(part, (0, width - part.shape[0])) for stat in stats for part in split3(stat)]
    tail = jnp.pad(jnp.stack(parts), ((0, 16 - len(parts)), (0, 0)))
    return jnp.concatenate([body, tail], axis=0)


def local(embeddings, landmarks, start_vectors, row_weight, spread):
    own = embeddings.shape[0]
    marks = landmarks.shape[0]
    width = start_vectors.shape[1]
    members = lax.axis_size(ROW_AXES)
    groups = lax.axis_size(MARK_AXES)
    piece = marks // groups
    total_rows = own * lax.axis_size(AXES)
    gamma = spread[0]

    rows_unit = unit_rows(embeddings)
    gathered = spread_to(with_tail(rows_unit, [row_weight]), ROW_AXES)
    part_rows = gathered[:, :own].reshape(members * own, -1)
    part_weight = join3(gathered[:, own : own + 3, :own]).reshape(-1)

    marks_unit = unit_rows(landmarks)
    marks_unit = jnp.concatenate([marks_unit, swap_core(marks_unit)], axis=0)

    product = row_weight[:, None] * start_vectors
    packed = spread_to(with_tail(product.astype(B16), [jnp.sum(product, axis=0)]), ROW_AXES)

    cosine = jnp.einsum("rd,ld->rl", part_rows, marks_unit, preferred_element_type=F32)
    values = jnp.exp(gamma * cosine)
    tile = values.astype(B16)
    sums = jnp.sum(part_weight[:, None] * values, axis=0)
    sums = sums.reshape(2, groups, piece // width, width)
    weight_sum = jnp.full((width,), jnp.sum(part_weight), F32)

    means = None
    scale = None
    for step in range(ITERS):
        weighted = packed[:, :own].reshape(members * own, width)
        totals = jnp.sum(join3(packed[:, own : own + 3]), axis=0)
        if step == 0:
            squares = jnp.zeros_like(totals)
        else:
            squares = jnp.sum(join3(packed[:, own + 3 : own + 6]), axis=0)
        raw = jnp.einsum("rl,rv->lv", tile, weighted, preferred_element_type=F32)
        raw = raw.reshape(2, groups, piece, width)
        stats = jnp.stack([totals, squares, weight_sum] + [jnp.zeros_like(totals)] * 3)
        stats = jnp.broadcast_to(stats, (2, groups) + stats.shape)
        payload = jnp.concatenate([raw, sums, stats], axis=2)
        both = payload[0] + swap_core(payload[1])
        summed = jnp.sum(lax.all_to_all(both, MARK_AXES, 0, 0), axis=0)
        side = summed[:piece]
        totals, squares, all_weight = summed[piece + 2], summed[piece + 3], summed[piece + 4]
        if step == 0:
            means = summed[piece : piece + 2].reshape(piece) / all_weight[0]
            side = side - means[:, None] * totals[None, :]
        else:
            scale = jnp.sqrt(squares / total_rows + 1e-06)
            side = (side * UP - means[:, None] * totals[None, :]) / scale[None, :]
        side_b = lax.reduce_precision(side, 8, 7)
        shift = jnp.sum(means[:, None] * side_b, axis=0)
        sides = spread_to(with_tail(side_b.astype(B16), [shift]), MARK_AXES)
        sides = jnp.stack([sides, swap_core(sides)])
        shift = jnp.sum(join3(sides[:, :, piece : piece + 3]), axis=(0, 1))
        side_all = sides[:, :, :piece].reshape(2 * marks, width)
        part = jnp.dot(tile, side_all, preferred_element_type=F32) - shift[None, :]
        part = part.astype(B16).reshape(members, own, width)
        image = jnp.sum(lax.all_to_all(part, ROW_AXES, 0, 0).astype(F32), axis=0)
        image = row_weight[:, None] * image
        squares = jnp.sum(image * image, axis=0)
        if step + 1 < ITERS:
            product = row_weight[:, None] * image
            packed = spread_to(
                with_tail((product * DOWN).astype(B16), [jnp.sum(product, axis=0), squares]),
                ROW_AXES,
            )
    every = spread_to(jnp.broadcast_to(squares[None], (8, width)), AXES)
    scale = jnp.sqrt(jnp.sum(every[:, 0], axis=0) / total_rows + 1e-06)
    return image / scale[None, :]


def solution(mesh):
    fine = Mesh(mesh.devices.reshape(4, 2, 4, 2, 2), AXES)
    rows = P(AXES, None)
    in_specs = (rows, P(("x", "zl", "core"), None), rows, P(AXES), P())
    return jax.shard_map(local, mesh=fine, in_specs=in_specs, out_specs=rows, check_vma=False)
```

time: 613 us -> 274 us (0.45)
  waiting for transfers between devices: 270 us -> 41.3 us
  blocking collectives: 246 us -> 122 us
  local copies, waits for them, and re-layouts: 0.01 us -> 28.4 us
  starting transfers between devices: 0.47 us -> 21.9 us
  matrix products: 67 us -> 48 us
  between operations: 14.2 us -> 1.05 us
    psum x4 -> x0, blocking collectives: 225 us -> none  [the longest x2 136 us: local(): lax.psum((jnp.sum(image * image, axis=0), jnp.sum(row_weight[:, None] * i...]
    reduce_scatter x2 -> x0, waiting for transfers between devices: 125 us -> none  [local(): lax.psum_scatter(weights[:, None] * (jnp.dot(build_tile, side_b, preferre...]
    all_to_all x0 -> x8, blocking collectives: none -> 122 us  [the longest x4 55.4 us: spread_to(): lax.all_to_all(jnp.broadcast_to(payload[None], (count,) + payload.shape),...]
    psum x2 -> x0, waiting for transfers between devices: 83.7 us -> none  [local(): lax.psum(jnp.einsum('rl,rv->lv', build_tile, group_weighted, preferred_el...]
    all_gather x3 -> x0, waiting for transfers between devices: 61.9 us -> none  [the longest x1 29.2 us: local(): lax.all_gather((row_weight[:, None] * vectors).astype(jnp.bfloat16), 'lm'...]
    all_to_all x0 -> x2, waiting for transfers between devices: none -> 33.5 us  [spread_to(): lax.all_to_all(jnp.broadcast_to(payload[None], (count,) + payload.shape),...]
    dot_general x0 -> x1, local copies, waits for them, and re-layouts: none -> 22.6 us  [local(): raw = jnp.einsum('rl,rv->lv', tile, weighted, preferred_element_type=F32)]
    all_gather x1 -> x0, blocking collectives: 21.3 us -> none  [local(): lax.all_gather(row_weight.astype(jnp.bfloat16), 'lm', axis=0, tiled=True)]
  transfers between devices with their start and end apart: 7 -> 7, of which waited for: 6 -> 6; matrix products, arithmetic and copies ran while one was open for 4% -> 3% of each run, Pallas kernels for 0% -> 0%
where the time goes in v1:
time: 274 us; the launch traced here: 273 us
  blocking collectives  122 us (45%)
  matrix products  48 us (18%)
  waiting for transfers between devices  41.3 us (15%)
  local copies, waits for them, and re-layouts  28.4 us (10%)
  starting transfers between devices  21.9 us (8%)
  other arithmetic  9.85 us (4%)
    all_to_all x4, blocking collectives, spread_to(): lax.all_to_all(jnp.broadcast_to(payload[None], (count,) + payload.shape),...  55.4 us
    all_to_all x2, blocking collectives, local(): summed = jnp.sum(lax.all_to_all(both, MARK_AXES, 0, 0), axis=0)  43.5 us
    all_to_all x2, waiting for transfers between devices, spread_to(): lax.all_to_all(jnp.broadcast_to(payload[None], (count,) + payload.shape),...  33.5 us
    all_to_all x2, blocking collectives, local(): image = jnp.sum(lax.all_to_all(part, ROW_AXES, 0, 0).astype(F32), axis=0)  23.5 us
    dot_general x1, local copies, waits for them, and re-layouts, local(): raw = jnp.einsum('rl,rv->lv', tile, weighted, preferred_element_type=F32)  22.6 us
    dot_general x2, matrix products, local(): part = jnp.dot(tile, side_all, preferred_element_type=F32) - shift[None, :]  16.4 us
    dot_general x2, matrix products, local(): raw = jnp.einsum('rl,rv->lv', tile, weighted, preferred_element_type=F32)  16.4 us
    dot_general x1, matrix products, local(): jnp.einsum('rd,ld->rl', part_rows, marks_unit, preferred_element_type=F32)  15.2 us
  transfers between devices with their start and end apart: 7, of which 6 were waited for; matrix products, arithmetic and copies ran while one was open for 3% of the time, Pallas kernels for 0%

profile of v1, /device:TPU:1, one launch (start us, length us, event | category | flops | bytes accessed | tf_op | source)
XLA Modules:
  0.0 272.9 jit_solution(4428998835618933109)
XLA Ops:
  0.0 1.2 multiply_convert_fusion.1
  1.2 0.9 broadcast_in_dim.15
  2.1 6.2 %all-to-all-start.1 = ((bf16[8,272,128]{2,1,0:T(8,128)(2,1)}), bf16[8,272,128]{2,1,0:T(8,128)(2,1)S(1)}, u32[]{:S(2)}, u32[]{:S(2)}) async-start(bf16[8,272,128]{2,1,0:T(8,128)(2,1)} %broadcast_in_dim.15), calls=%async_computation.1 | async-start | bytes 1114112 | tf_op jit(solution)/shard_map/all_to_all | solution.py:37
  8.3 0.7 reduce-precision_convert_fusion.1
  9.0 0.1 fusion.15
  9.4 0.5 fusion.1
  9.9 7.6 %all-to-all-done.1 = bf16[8,272,128]{2,1,0:T(8,128)(2,1)S(1)} async-done(((bf16[8,272,128]{2,1,0:T(8,128)(2,1)}), bf16[8,272,128]{2,1,0:T(8,128)(2,1)S(1)}, u32[]{:S(2)}, u32[]{:S(2)}) %all-to-all-start.1) | async-done | bytes 557088 | tf_op jit(solution)/shard_map/all_to_all | solution.py:37
  17.5 1.6 broadcast_in_dim.14
  19.1 3.6 %all-to-all-start = ((bf16[8,272,512]{2,1,0:T(8,128)(2,1)}), bf16[8,272,512]{2,1,0:T(8,128)(2,1)S(1)}, u32[]{:S(2)}, u32[]{:S(2)}) async-start(bf16[8,272,512]{2,1,0:T(8,128)(2,1)} %broadcast_in_dim.14), calls=%async_computation | async-start | bytes 4456448 | tf_op jit(solution)/shard_map/all_to_all | solution.py:37
  22.7 3.4 %fusion.2 = bf16[2048,512]{1,0:T(8,128)(2,1)} fusion(bf16[2048,512]{1,0:T(8,128)(2,1)} %param.6, f32[2048]{0:T(1024)S(1)} %add_rsqrt_fusion), kind=kLoop, calls=%fused_computation.6 | loop fusion | flops 3145728 | bytes 4202496 | tf_op jit(solution)/shard_map/convert_element_type | solution.py:19
  26.1 1.6 collective-permute-start
  28.4 25.8 %all-to-all-done = bf16[8,272,512]{2,1,0:T(8,128)(2,1)S(1)} async-done(((bf16[8,272,512]{2,1,0:T(8,128)(2,1)}), bf16[8,272,512]{2,1,0:T(8,128)(2,1)S(1)}, u32[]{:S(2)}, u32[]{:S(2)}) %all-to-all-start) | async-done | bytes 2228256 | tf_op jit(solution)/shard_map/all_to_all | solution.py:37
  54.2 0.6 fusion.63
  54.8 0.6 stack_broadcast_in_dim.4
  55.5 1.5 slice.167
  57.1 15.2 %multiply_reduce_fusion = (f32[4096]{0:T(1024)S(1)}, bf16[2048,4096]{1,0:T(8,128)(2,1)}) fusion(f32[2048]{0:T(1024)S(1)} %bitcast.119, f32[]{:T(128)} %bitcast.95, bf16[2048,512]{1,0:T(8,128)(2,1)} %bitcast.108, bf16[2048,512]{1,0:T(8,128)(2,1)} %collective-permute-done, bf16[2048,512]{1,0:T(8,128)(2,1)} %fusion.2), kind=kOutput, calls=%fused_computation | convolution fusion | flops 8631873536 | bytes 23093252 | tf_op jit(solution)/shard_map/rd,ld->rl/dot_general | solution.py:72
  72.3 22.6 %copy.23 = bf16[4096,2048]{1,0:T(8,128)(2,1)} copy(bf16[4096,2048]{0,1:T(8,128)(2,1)} %bitcast.96) | data formatting | bytes 33554432 | tf_op jit(solution)/shard_map/rl,rv->lv/dot_general | solution.py:88
  94.9 8.2 %fusion.64 = f32[2,8,256,128]{3,2,1,0:T(8,128)S(1)} fusion(bf16[2,8,256,2048]{3,2,1,0:T(8,128)(2,1)} %bitcast.97, bf16[2048,128,1,1]{1,0,3,2:T(8,128)(2,1)S(1)} %bitcast.107), kind=kOutput, calls=%fused_computation.149 | convolution fusion | flops 2147483648 | bytes 19398656 | tf_op jit(solution)/shard_map/rl,rv->lv/dot_general | solution.py:88
  103.2 0.2 fusion.9
  103.4 2.0 collective-permute-start.1
  105.4 2.3 collective-permute-done.1
  107.7 0.1 fusion.12
  107.8 24.0 %all_to_all.50 = f32[8,264,128]{2,1,0:T(8,128)S(1)} all-to-all(f32[8,264,128]{2,1,0:T(8,128)S(1)} %fusion.12), channel_id=1, replica_groups=mesh['y'=4,'zh'=2,'x'=4,'zl'=2,'core'=2] {'y','zh'}, dimensions={0} | all-to-all | bytes 2162688 | tf_op jit(solution)/shard_map/all_to_all | solution.py:94
  131.9 0.5 slice.181
  132.5 0.6 fusion.52
  133.1 0.1 fusion.22
  133.4 12.7 %all_to_all.51 = bf16[8,272,128]{2,1,0:T(8,128)(2,1)S(1)} all-to-all(bf16[8,272,128]{2,1,0:T(8,128)(2,1)S(1)} %broadcast_in_dim.17), channel_id=1, replica_groups=mesh['y'=4,'zh'=2,'x'=4,'zl'=2,'core'=2] {'y','zh'}, dimensions={0} | all-to-all | bytes 1114112 | tf_op jit(solution)/shard_map/all_to_all | solution.py:37
  146.0 2.9 %collective-permute-start.2 = (bf16[8,272,128]{2,1,0:T(8,128)(2,1)S(1)}, bf16[8,272,128]{2,1,0:T(8,128)(2,1)S(1)}, u32[]{:S(2)}, u32[]{:S(2)}) collective-permute-start(bf16[8,272,128]{2,1,0:T(8,128)(2,1)S(1)} %all_to_all.51), channel_id=1, source_target_pairs={{0,1},{1,0},{2,3},{3,2},{4,5},{5,4},{6,7},{7,6},{8,9},{9,8},{10,11... | collective-permute-start | bytes 1671176 | tf_op jit(solution)/shard_map/ppermute | solution.py:41
  148.9 1.6 collective-permute-done.2
  150.6 8.2 %fusion.8 = bf16[2048,128]{1,0:T(8,128)(2,1)S(1)} fusion(bf16[2048,4096]{1,0:T(8,128)(2,1)} %get-tuple-element.10, bf16[4096,128]{1,0:T(8,128)(2,1)S(1)} %bitcast.110, f32[128]{0:T(128)S(1)} %reduce_sum.200), kind=kOutput, calls=%fused_computation.16 | convolution fusion | flops 2148007936 | bytes 18350592 | tf_op jit(solution)/shard_map/dot_general | solution.py:109
  158.8 11.7 %all_to_all.52 = bf16[8,256,128]{2,1,0:T(8,128)(2,1)S(1)} all-to-all(bf16[8,256,128]{2,1,0:T(8,128)(2,1)S(1)} %bitcast.112), channel_id=1, replica_groups=mesh['y'=4,'zh'=2,'x'=4,'zl'=2,'core'=2] {'x','zl'}, dimensions={0} | all-to-all | bytes 1048576 | tf_op jit(solution)/shard_map/all_to_all | solution.py:111
  170.7 0.1 multiply_reduce_fusion.3
  170.9 11.3 %all_to_all.53 = bf16[8,272,128]{2,1,0:T(8,128)(2,1)S(1)} all-to-all(bf16[8,272,128]{2,1,0:T(8,128)(2,1)S(1)} %broadcast_in_dim.18), channel_id=1, replica_groups=mesh['y'=4,'zh'=2,'x'=4,'zl'=2,'core'=2] {'x','zl'}, dimensions={0} | all-to-all | bytes 1114112 | tf_op jit(solution)/shard_map/all_to_all | solution.py:37
  182.3 8.2 %fusion.65 = f32[2,8,256,128]{3,2,1,0:T(8,128)S(1)} fusion(bf16[2,8,256,2048]{3,2,1,0:T(8,128)(2,1)} %bitcast.98, bf16[2048,128,1,1]{1,0,3,2:T(8,128)(2,1)S(1)} %bitcast.113), kind=kOutput, calls=%fused_computation.150 | convolution fusion | flops 2147483648 | bytes 19398656 | tf_op jit(solution)/shard_map/rl,rv->lv/dot_general | solution.py:88
  190.6 0.2 fusion.10
  190.8 3.0 %collective-permute-start.3 = (f32[8,264,128]{2,1,0:T(8,128)S(1)}, f32[8,264,128]{2,1,0:T(8,128)S(1)}, u32[]{:S(2)}, u32[]{:S(2)}) collective-permute-start(f32[8,264,128]{2,1,0:T(8,128)S(1)} %slice_bitcast_fusion), channel_id=1, source_target_pairs={{0,1},{1,0},{2,3},{3,2},{4,5},{5,4},{6,7},{7,6},{8,9},{9,8},{10,11... | collective-permute-start | bytes 3244040 | tf_op jit(solution)/shard_map/ppermute | solution.py:41
  193.8 2.3 collective-permute-done.3
  196.1 0.1 fusion.11
  196.2 19.4 %all_to_all.54 = f32[8,264,128]{2,1,0:T(8,128)S(1)} all-to-all(f32[8,264,128]{2,1,0:T(8,128)S(1)} %fusion.11), channel_id=1, replica_groups=mesh['y'=4,'zh'=2,'x'=4,'zl'=2,'core'=2] {'y','zh'}, dimensions={0} | all-to-all | bytes 2162688 | tf_op jit(solution)/shard_map/all_to_all | solution.py:94
  215.7 0.1 fusion.62
  216.0 12.8 %all_to_all.55 = bf16[8,272,128]{2,1,0:T(8,128)(2,1)S(1)} all-to-all(bf16[8,272,128]{2,1,0:T(8,128)(2,1)S(1)} %broadcast_in_dim.20), channel_id=1, replica_groups=mesh['y'=4,'zh'=2,'x'=4,'zl'=2,'core'=2] {'y','zh'}, dimensions={0} | all-to-all | bytes 1114112 | tf_op jit(solution)/shard_map/all_to_all | solution.py:37
  228.8 2.7 %collective-permute-start.4 = (bf16[8,272,128]{2,1,0:T(8,128)(2,1)S(1)}, bf16[8,272,128]{2,1,0:T(8,128)(2,1)S(1)}, u32[]{:S(2)}, u32[]{:S(2)}) collective-permute-start(bf16[8,272,128]{2,1,0:T(8,128)(2,1)S(1)} %all_to_all.55), channel_id=1, source_target_pairs={{0,1},{1,0},{2,3},{3,2},{4,5},{5,4},{6,7},{7,6},{8,9},{9,8},{10,11... | collective-permute-start | bytes 1671176 | tf_op jit(solution)/shard_map/ppermute | solution.py:41
  231.6 1.6 collective-permute-done.4
  233.3 8.2 %fusion.7 = bf16[2048,128]{1,0:T(8,128)(2,1)S(1)} fusion(bf16[2048,4096]{1,0:T(8,128)(2,1)} %get-tuple-element.10, bf16[4096,128]{1,0:T(8,128)(2,1)S(1)} %bitcast.109, f32[128]{0:T(128)S(1)} %reduce_sum.211), kind=kOutput, calls=%fused_computation.14 | convolution fusion | flops 2148007936 | bytes 18350592 | tf_op jit(solution)/shard_map/dot_general | solution.py:109
  241.5 11.7 %all_to_all.56 = bf16[8,256,128]{2,1,0:T(8,128)(2,1)S(1)} all-to-all(bf16[8,256,128]{2,1,0:T(8,128)(2,1)S(1)} %bitcast.111), channel_id=1, replica_groups=mesh['y'=4,'zh'=2,'x'=4,'zl'=2,'core'=2] {'x','zl'}, dimensions={0} | all-to-all | bytes 1048576 | tf_op jit(solution)/shard_map/all_to_all | solution.py:111
  253.3 0.1 multiply_reduce_fusion.1
  253.5 18.5 %all_to_all.57 = f32[128,8,128]{2,1,0:T(8,128)S(1)} all-to-all(f32[128,8,128]{2,1,0:T(8,128)S(1)} %broadcast_in_dim_broadcast_in_dim_broadcast_in_dim.2), channel_id=1, replica_groups=mesh['y'=4,'zh'=2,'x'=4,'zl'=2,'core'=2] {'y','zh','x','zl','core'}, dimensions={0} | all-to-all | bytes 1048576 | tf_op jit(solution)/shard_map/all_to_all | solution.py:37
  272.1 0.8 multiply_divide_fusion
  (68 shorter events, 1.6 us)
Async XLA Ops:
  0.0 9.0 %copy-start.2 = (bf16[256,512]{1,0:T(8,128)(2,1)S(1)}, bf16[256,512]{1,0:T(8,128)(2,1)}, u32[]{:S(2)}) copy-start(bf16[256,512]{1,0:T(8,128)(2,1)} %param.5) | copy-start | bytes 786436
  0.0 9.4 %copy-start = (bf16[2048,512]{1,0:T(8,128)(2,1)S(1)}, bf16[2048,512]{1,0:T(8,128)(2,1)}, u32[]{:S(2)}) copy-start(bf16[2048,512]{1,0:T(8,128)(2,1)} %param.6) | copy-start | bytes 6291460
  2.1 15.4 %all-to-all-start.1 = ((bf16[8,272,128]{2,1,0:T(8,128)(2,1)}), bf16[8,272,128]{2,1,0:T(8,128)(2,1)S(1)}, u32[]{:S(2)}, u32[]{:S(2)}) async-start(bf16[8,272,128]{2,1,0:T(8,128)(2,1)} %broadcast_in_dim.15), calls=%async_computation.1 | async-start | bytes 1114112 | tf_op jit(solution)/shard_map/all_to_all | solution.py:37
  17.5 10.8 %copy-start.1 = (bf16[8,272,128]{2,1,0:T(8,128)(2,1)}, bf16[8,272,128]{2,1,0:T(8,128)(2,1)S(1)}, u32[]{:S(2)}) copy-start(bf16[8,272,128]{2,1,0:T(8,128)(2,1)S(1)} %all-to-all-done.1) | copy-start | bytes 1671172
  19.1 35.1 %all-to-all-start = ((bf16[8,272,512]{2,1,0:T(8,128)(2,1)}), bf16[8,272,512]{2,1,0:T(8,128)(2,1)S(1)}, u32[]{:S(2)}, u32[]{:S(2)}) async-start(bf16[8,272,512]{2,1,0:T(8,128)(2,1)} %broadcast_in_dim.14), calls=%async_computation | async-start | bytes 4456448 | tf_op jit(solution)/shard_map/all_to_all | solution.py:37
  26.1 30.9 %collective-permute-start = (bf16[2048,512]{1,0:T(8,128)(2,1)}, bf16[2048,512]{1,0:T(8,128)(2,1)}, u32[]{:S(2)}, u32[]{:S(2)}) collective-permute-start(bf16[2048,512]{1,0:T(8,128)(2,1)} %fusion.2), channel_id=1, source_target_pairs={{0,1},{1,0},{2,3},{3,2},{4,5},{5,4},{6,7},{7,6},{8,9},{9,8},{10,11... | collective-permute-start | bytes 6291464 | tf_op jit(solution)/shard_map/ppermute | solution.py:41
  72.3 22.6 %slice-start = ((bf16[8,272,128]{2,1,0:T(8,128)(2,1)}), bf16[8,256,128]{2,1,0:T(8,128)(2,1)S(1)}, s32[]{:S(2)}) async-start(bf16[8,272,128]{2,1,0:T(8,128)(2,1)} %copy-done.1), calls=%async_computation.10 | async-start | bytes 1048576 | tf_op jit(solution)/shard_map/slice | solution.py:82
  103.4 4.3 %collective-permute-start.1 = (f32[8,264,128]{2,1,0:T(8,128)S(1)}, f32[8,264,128]{2,1,0:T(8,128)S(1)}, u32[]{:S(2)}, u32[]{:S(2)}) collective-permute-start(f32[8,264,128]{2,1,0:T(8,128)S(1)} %slice_bitcast_fusion.2), channel_id=1, source_target_pairs={{0,1},{1,0},{2,3},{3,2},{4,5},{5,4},{6,7},{7,6},{8,9},{9,8},{10,11... | collective-permute-start | bytes 3244040 | tf_op jit(solution)/shard_map/ppermute | solution.py:41
  146.0 4.4 %collective-permute-start.2 = (bf16[8,272,128]{2,1,0:T(8,128)(2,1)S(1)}, bf16[8,272,128]{2,1,0:T(8,128)(2,1)S(1)}, u32[]{:S(2)}, u32[]{:S(2)}) collective-permute-start(bf16[8,272,128]{2,1,0:T(8,128)(2,1)S(1)} %all_to_all.51), channel_id=1, source_target_pairs={{0,1},{1,0},{2,3},{3,2},{4,5},{5,4},{6,7},{7,6},{8,9},{9,8},{10,11... | collective-permute-start | bytes 1671176 | tf_op jit(solution)/shard_map/ppermute | solution.py:41
  150.6 20.0 %copy-start.3 = (f32[256]{0:T(256)S(1)}, f32[256]{0:T(256)}, u32[]{:S(2)}) copy-start(f32[256]{0:T(256)} %param.8) | copy-start | bytes 3076
  190.8 5.3 %collective-permute-start.3 = (f32[8,264,128]{2,1,0:T(8,128)S(1)}, f32[8,264,128]{2,1,0:T(8,128)S(1)}, u32[]{:S(2)}, u32[]{:S(2)}) collective-permute-start(f32[8,264,128]{2,1,0:T(8,128)S(1)} %slice_bitcast_fusion), channel_id=1, source_target_pairs={{0,1},{1,0},{2,3},{3,2},{4,5},{5,4},{6,7},{7,6},{8,9},{9,8},{10,11... | collective-permute-start | bytes 3244040 | tf_op jit(solution)/shard_map/ppermute | solution.py:41
  228.8 4.3 %collective-permute-start.4 = (bf16[8,272,128]{2,1,0:T(8,128)(2,1)S(1)}, bf16[8,272,128]{2,1,0:T(8,128)(2,1)S(1)}, u32[]{:S(2)}, u32[]{:S(2)}) collective-permute-start(bf16[8,272,128]{2,1,0:T(8,128)(2,1)S(1)} %all_to_all.55), channel_id=1, source_target_pairs={{0,1},{1,0},{2,3},{3,2},{4,5},{5,4},{6,7},{7,6},{8,9},{9,8},{10,11... | collective-permute-start | bytes 1671176 | tf_op jit(solution)/shard_map/ppermute | solution.py:41

commit v2 on v1

v2 whole, which is shorter than its diff:
```python
import jax
import jax.numpy as jnp
from jax import lax
from jax.experimental import pallas as pl
from jax.experimental.pallas import tpu as pltpu
from jax.sharding import Mesh
from jax.sharding import PartitionSpec as P

ITERS = 2
AXES = ("y", "zh", "x", "zl", "core")
ROW_AXES = ("x", "zl")
MARK_AXES = ("y", "zh")
F32, B16 = jnp.float32, jnp.bfloat16
DOWN = 2.0**-20
UP = 2.0**20
LOG2E = 1.4426950408889634
VMEM = pl.BlockSpec(memory_space=pltpu.VMEM)
SMEM = pl.BlockSpec(memory_space=pltpu.SMEM)
OWN = 256
PIECE = 256
WIDTH = 128
MARKS = 2048
EIGHT = 8
ROWS = EIGHT * OWN
PACK = OWN + WIDTH // 2 + 16


def params(mib):
    return pltpu.CompilerParams(vmem_limit_bytes=mib * 2**20)


def dot(left, right, left_dim, right_dim):
    dims = (((left_dim,), (right_dim,)), ((), ()))
    return lax.dot_general(left, right, dims, preferred_element_type=F32)


def unit_rows(values):
    values = values.astype(F32)
    scale = lax.rsqrt(jnp.sum(values * values, axis=1, keepdims=True) + 1e-06)
    return (values * scale).astype(B16)


def split3(values):
    high = lax.reduce_precision(values, 8, 7)
    rest = values - high
    mid = lax.reduce_precision(rest, 8, 7)
    low = rest - mid
    return [high.astype(B16), mid.astype(B16), low.astype(B16)]


def parts_in_kernel(values):
    high = values.astype(B16)
    rest = values - high.astype(F32)
    mid = rest.astype(B16)
    low = (rest - mid.astype(F32)).astype(B16)
    return high.astype(F32), mid.astype(F32), low.astype(F32)


def tail_in_kernel(row):
    at = lax.broadcasted_iota(jnp.int32, (16, row.shape[1]), 0)
    high, mid, low = parts_in_kernel(row)
    zero = jnp.zeros((16, row.shape[1]), F32)
    block = jnp.where(at == 0, high, jnp.where(at == 1, mid, jnp.where(at == 2, low, zero)))
    return block.astype(B16)


def join_tail(block):
    block = block.astype(F32)
    return (block[2:3] + block[1:2]) + block[0:1]


def stat_rows(first, second, third):
    at = lax.broadcasted_iota(jnp.int32, (8, PIECE), 0)
    zero = jnp.zeros((8, PIECE), F32)
    return jnp.where(at == 0, first, jnp.where(at == 1, second, jnp.where(at == 2, third, zero)))


def first_kernel(spread_ref, packed_ref, near_ref, far_ref, tile_ref, own_ref, other_ref, wt_ref, wide_ref):
    gamma = spread_ref[0] * LOG2E
    totals = jnp.zeros((1, WIDTH), F32)
    weight_sum = jnp.zeros((1, 1), F32)
    for source in range(EIGHT):
        half = WIDTH // 2
        wt_ref[source, :half] = packed_ref[source, OWN : OWN + half, :OWN]
        wt_ref[source, half:] = packed_ref[source, OWN : OWN + half, OWN:]
        tail = join_tail(packed_ref[source, OWN + half :, :])
        weight = tail[:, :OWN]
        totals = totals + tail[:, OWN : OWN + WIDTH]
        weight_sum = weight_sum + jnp.sum(weight, axis=1, keepdims=True)
        column = jnp.transpose(jnp.broadcast_to(weight, (WIDTH, OWN)))
        wide_ref[source * OWN : (source + 1) * OWN, :] = column
    second = jnp.concatenate([totals, jnp.zeros((1, PIECE - WIDTH), F32)], axis=1)
    third = jnp.broadcast_to(weight_sum, (1, PIECE))
    block = 2 * PIECE
    chunk = 2 * OWN

    def half_of(marks_ref, out_ref, base):
        def body(index, _):
            start = pl.multiple_of(index * block, block)
            marks = marks_ref[pl.ds(start, block), :]
            lanes = pl.ds(pl.multiple_of(base + start, block), block)
            sums = [jnp.zeros((8, WIDTH), F32) for _ in range(block // WIDTH)]
            product = None
            for part in range(ROWS // chunk):
                rows = packed_ref[2 * part : 2 * part + 2, :OWN, :].reshape(chunk, -1)
                values = jnp.exp2(dot(rows, marks, 1, 1) * gamma)
                kernel = values.astype(B16)
                tile_ref[part * chunk : (part + 1) * chunk, lanes] = kernel
                wide = wide_ref[part * chunk : (part + 1) * chunk, :]
                for at in range(block // WIDTH):
                    term = values[:, at * WIDTH : (at + 1) * WIDTH] * wide
                    sums[at] = sums[at] + jnp.sum(term.reshape(chunk // 8, 8, WIDTH), axis=0)
                for at in range(2):
                    term = dot(wt_ref[2 * part + at], kernel[at * OWN : (at + 1) * OWN], 1, 0)
                    product = term if product is None else product + term
            sums = jnp.sum(jnp.concatenate(sums, axis=1), axis=0, keepdims=True)
            for at in range(2):
                lane = slice(at * PIECE, (at + 1) * PIECE)
                out_ref[2 * index + at, :WIDTH, :] = product[:, lane]
                out_ref[2 * index + at, WIDTH:, :] = stat_rows(sums[:, lane], second, third)
            return 0

        lax.fori_loop(0, MARKS // block, body, 0)

    half_of(near_ref, own_ref, 0)
    half_of(far_ref, other_ref, MARKS)


def build(spread, packed, near, far):
    side = jax.ShapeDtypeStruct((EIGHT, WIDTH + 8, PIECE), F32)
    return pl.pallas_call(
        first_kernel,
        out_shape=[pltpu.VMEM((ROWS, 2 * MARKS), B16), side, side],
        in_specs=[SMEM, VMEM, VMEM, VMEM],
        out_specs=[VMEM, VMEM, VMEM],
        scratch_shapes=[pltpu.VMEM((EIGHT, WIDTH, OWN), B16), pltpu.VMEM((ROWS, WIDTH), F32)],
        compiler_params=params(24),
        name="build",
    )(spread, packed, near, far)


def side_kernel(tile_ref, packed_ref, own_ref, other_ref):
    totals = jnp.zeros((1, PIECE), F32)
    for source in range(EIGHT):
        totals = totals + join_tail(packed_ref[source, WIDTH:, :])
    stats = stat_rows(jnp.zeros((1, PIECE), F32), totals, jnp.zeros((1, PIECE), F32))
    block = 4 * PIECE

    def half_of(out_ref, base):
        def body(index, _):
            lanes = pl.ds(pl.multiple_of(base + index * block, block), block)
            product = None
            for source in range(EIGHT):
                kernel = tile_ref[source * OWN : (source + 1) * OWN, lanes]
                term = dot(packed_ref[source, :WIDTH, :], kernel, 1, 0)
                product = term if product is None else product + term
            for at in range(4):
                out_ref[4 * index + at, :WIDTH, :] = product[:, at * PIECE : (at + 1) * PIECE]
                out_ref[4 * index + at, WIDTH:, :] = stats
            return 0

        lax.fori_loop(0, MARKS // block, body, 0)

    half_of(own_ref, 0)
    half_of(other_ref, MARKS)


def side_terms(tile, packed):
    side = jax.ShapeDtypeStruct((EIGHT, WIDTH + 8, PIECE), F32)
    return pl.pallas_call(
        side_kernel,
        out_shape=[side, side],
        in_specs=[VMEM, VMEM],
        out_specs=[VMEM, VMEM],
        compiler_params=params(24),
        name="side_terms",
    )(tile, packed)


def centre_kernel(first, total_rows, *refs):
    if first:
        terms_ref, out_ref, means_ref = refs
    else:
        terms_ref, before_ref, out_ref = refs
    summed = terms_ref[0]
    for group in range(1, EIGHT):
        summed = summed + terms_ref[group]
    stats = summed[WIDTH:]
    if first:
        means = stats[0:1] / stats[2:3]
        means_ref[...] = jnp.broadcast_to(means, (8, PIECE))
    else:
        means = before_ref[0:1]
    columns = jnp.transpose(jnp.broadcast_to(stats[1:2], (WIDTH, PIECE)))
    totals = columns[:WIDTH, 0:1]
    side = summed[:WIDTH]
    if first:
        side = side - totals * means
    else:
        squares = columns[WIDTH:, 0:1]
        side = (side * UP - totals * means) / jnp.sqrt(squares / total_rows + 1e-06)
    side = side.astype(B16)
    tail = tail_in_kernel(means)
    for group in range(EIGHT):
        out_ref[group, :WIDTH, :] = side
        out_ref[group, WIDTH:, :] = tail


def centre(first, total_rows, *args):
    shapes = [jax.ShapeDtypeStruct((EIGHT, WIDTH + 16, PIECE), B16)]
    if first:
        shapes.append(jax.ShapeDtypeStruct((8, PIECE), F32))
    return pl.pallas_call(
        lambda *refs: centre_kernel(first, total_rows, *refs),
        out_shape=shapes,
        in_specs=[VMEM] * len(args),
        out_specs=[VMEM] * len(shapes),
        compiler_params=params(16),
        name="centre",
    )(*args)


def image_kernel(tile_ref, own_ref, other_ref, out_ref, side_ref, shift_ref):
    shift = jnp.zeros((16, WIDTH), F32)
    for half, ref in enumerate((own_ref, other_ref)):
        for piece in range(EIGHT):
            side = ref[piece, :WIDTH, :]
            lane = half * MARKS + piece * PIECE
            side_ref[:, lane : lane + PIECE] = side
            shift = shift + dot(ref[piece, WIDTH:, :], side, 1, 1)
    shift_ref[...] = (shift[2:3] + shift[1:2]) + shift[0:1]

    def body(index, _):
        rows = pl.ds(pl.multiple_of(index * 2 * OWN, 2 * OWN), 2 * OWN)
        term = dot(tile_ref[rows, :], side_ref[...], 1, 1) - shift_ref[...]
        out_ref[pl.ds(2 * index, 2)] = term.astype(B16).reshape(2, OWN, WIDTH)
        return 0

    lax.fori_loop(0, EIGHT // 2, body, 0)


def image_terms(tile, own, other):
    return pl.pallas_call(
        image_kernel,
        out_shape=jax.ShapeDtypeStruct((EIGHT, OWN, WIDTH), B16),
        in_specs=[VMEM] * 3,
        out_specs=VMEM,
        scratch_shapes=[pltpu.VMEM((WIDTH, 2 * MARKS), B16), pltpu.VMEM((1, WIDTH), F32)],
        compiler_params=params(24),
        name="image_terms",
    )(tile, own, other)


def owner_kernel(last, terms_ref, weight_ref, out_ref, *more):
    image = terms_ref[0].astype(F32)
    for member in range(1, EIGHT):
        image = image + terms_ref[member].astype(F32)
    weight = weight_ref[...]
    image = weight * image
    squares = jnp.sum(image * image, axis=0, keepdims=True)
    if last:
        out_ref[...] = image
        more[0][...] = jnp.broadcast_to(squares, (8, WIDTH))
    else:
        product = weight * image
        totals = jnp.sum(product, axis=0, keepdims=True)
        body = jnp.transpose(product * DOWN).astype(B16)
        tail = tail_in_kernel(jnp.concatenate([totals, squares], axis=1))
        for member in range(EIGHT):
            out_ref[member, :WIDTH, :] = body
            out_ref[member, WIDTH:, :] = tail


def owner(last, terms, weight):
    if last:
        shapes = [jax.ShapeDtypeStruct((OWN, WIDTH), F32), jax.ShapeDtypeStruct((8, WIDTH), F32)]
    else:
        shapes = [jax.ShapeDtypeStruct((EIGHT, WIDTH + 16, OWN), B16)]
    return pl.pallas_call(
        lambda *refs: owner_kernel(last, *refs),
        out_shape=shapes,
        in_specs=[VMEM, VMEM],
        out_specs=[VMEM] * len(shapes),
        compiler_params=params(16),
        name="owner",
    )(terms, weight)


def spread_to(payload, axes):
    count = lax.axis_size(axes)
    return lax.all_to_all(jnp.broadcast_to(payload[None], (count,) + payload.shape), axes, 0, 0)


def exchange(payload, axes):
    return lax.all_to_all(payload, axes, 0, 0)


def swap_core(values):
    return lax.ppermute(values, "core", [(0, 1), (1, 0)])


def pack(rows_unit, product, row_weight):
    transposed = product.T.astype(B16)
    half = WIDTH // 2
    vectors = jnp.concatenate([transposed[:half], transposed[half:]], axis=1)
    totals = jnp.pad(jnp.sum(product, axis=0), (0, OWN - WIDTH))
    tail = jnp.stack(split3(jnp.concatenate([row_weight, totals])))
    tail = jnp.pad(tail, ((0, 13), (0, 0)))
    return jnp.concatenate([rows_unit, vectors, tail], axis=0)


def local(embeddings, landmarks, start_vectors, row_weight, spread):
    total_rows = embeddings.shape[0] * lax.axis_size(AXES)
    weight = jnp.broadcast_to(row_weight[:, None], (OWN, WIDTH))
    product = row_weight[:, None] * start_vectors
    packed = spread_to(pack(unit_rows(embeddings), product, row_weight), ROW_AXES)
    near = unit_rows(landmarks)
    far = swap_core(near)
    tile, own, other = build(spread, packed, near, far)
    means = None
    for step in range(ITERS):
        if step > 0:
            own, other = side_terms(tile, packed)
        terms = exchange(own + swap_core(other), MARK_AXES)
        if step == 0:
            sides, means = centre(True, total_rows, terms)
        else:
            (sides,) = centre(False, total_rows, terms, means)
        sides = exchange(sides, MARK_AXES)
        parts = exchange(image_terms(tile, sides, swap_core(sides)), ROW_AXES)
        if step + 1 < ITERS:
            (packed,) = owner(False, parts, weight)
            packed = exchange(packed, ROW_AXES)
    image, squares = owner(True, parts, weight)
    every = spread_to(squares, AXES)
    scale = jnp.sqrt(jnp.sum(every[:, 0], axis=0) / total_rows + 1e-06)
    return image / scale[None, :]


def solution(mesh):
    fine = Mesh(mesh.devices.reshape(4, 2, 4, 2, 2), AXES)
    rows = P(AXES, None)
    in_specs = (rows, P(("x", "zl", "core"), None), rows, P(AXES), P())
    return jax.shard_map(local, mesh=fine, in_specs=in_specs, out_specs=rows, check_vma=False)
```

time: 274 us -> 244 us (0.89)
  matrix products: 48 us -> 0 us
  Pallas kernels: 0 us -> 33.7 us
  local copies, waits for them, and re-layouts: 28.4 us -> 19.5 us
  starting transfers between devices: 21.9 us -> 17.7 us
    dot_general x5 -> x0, matrix products: 48 us -> none  [the longest x2 16.4 us: local(): part = jnp.dot(tile, side_all, preferred_element_type=F32) - shift[None, :]]
    all_to_all x4 -> x7, blocking collectives: 67 us -> 104 us  [exchange(): return lax.all_to_all(payload, axes, 0, 0)]
    all_to_all x4 -> x1, blocking collectives: 55.4 us -> 19.5 us  [spread_to(): lax.all_to_all(jnp.broadcast_to(payload[None], (count,) + payload.shape),...]
    pallas_call x0 -> x8, Pallas kernels: none -> 33.7 us  [the longest x1 19.3 us: build(): pl.pallas_call(first_kernel, out_shape=[pltpu.VMEM((ROWS, 2 * MARKS), B16...]
    dot_general x1 -> x0, local copies, waits for them, and re-layouts: 22.6 us -> none  [local(): raw = jnp.einsum('rl,rv->lv', tile, weighted, preferred_element_type=F32)]
    unnamed x8 -> x16, local copies, waits for them, and re-layouts: 0.01 us -> 17.4 us
    all_to_all x2 -> x1, starting transfers between devices: 9.81 us -> 6.2 us  [spread_to(): lax.all_to_all(jnp.broadcast_to(payload[None], (count,) + payload.shape),...]
    all_to_all x2 -> x1, waiting for transfers between devices: 33.5 us -> 30.6 us  [spread_to(): lax.all_to_all(jnp.broadcast_to(payload[None], (count,) + payload.shape),...]
  transfers between devices with their start and end apart: 7 -> 6, of which waited for: 6 -> 6; matrix products, arithmetic and copies ran while one was open for 3% -> 1% of each run, Pallas kernels for 0% -> 0%
where the time goes in v2:
time: 244 us; the launch traced here: 243 us
  blocking collectives  124 us (51%)
  waiting for transfers between devices  40.5 us (17%)
  Pallas kernels  33.7 us (14%)
  local copies, waits for them, and re-layouts  19.5 us (8%)
  starting transfers between devices  17.7 us (7%)
  other arithmetic  7.61 us (3%)
    all_to_all x7, blocking collectives, exchange(): return lax.all_to_all(payload, axes, 0, 0)  104 us
    all_to_all x1, waiting for transfers between devices, spread_to(): lax.all_to_all(jnp.broadcast_to(payload[None], (count,) + payload.shape),...  30.6 us
    all_to_all x1, blocking collectives, spread_to(): lax.all_to_all(jnp.broadcast_to(payload[None], (count,) + payload.shape),...  19.5 us
    pallas_call x1, Pallas kernels, build(): pl.pallas_call(first_kernel, out_shape=[pltpu.VMEM((ROWS, 2 * MARKS), B16...  19.3 us
    unnamed x16, local copies, waits for them, and re-layouts  17.4 us
    ppermute x5, starting transfers between devices, swap_core(): return lax.ppermute(values, 'core', [(0, 1), (1, 0)])  11.5 us
    pallas_call x2, Pallas kernels, image_terms(): pl.pallas_call(image_kernel, out_shape=jax.ShapeDtypeStruct((EIGHT, OWN,...  10.9 us
    ppermute x5, waiting for transfers between devices, swap_core(): return lax.ppermute(values, 'core', [(0, 1), (1, 0)])  9.83 us
  transfers between devices with their start and end apart: 6, of which 6 were waited for; matrix products, arithmetic and copies ran while one was open for 1% of the time, Pallas kernels for 0%

profile of v2, /device:TPU:1, one launch (start us, length us, event | category | flops | bytes accessed | tf_op | source)
XLA Modules:
  0.0 243.4 jit_solution(7103908732783552790)
XLA Ops:
  0.0 1.0 fusion.4
  1.0 0.1 fusion.11
  1.2 0.1 copy.8
  1.3 1.1 fusion.2
  2.3 1.1 fusion.3
  3.4 0.7 reduce-precision_convert_fusion.1
  4.2 1.8 broadcast_in_dim.4
  5.9 6.2 %all-to-all-start = ((bf16[8,336,512]{2,1,0:T(8,128)(2,1)}), bf16[8,336,512]{2,1,0:T(8,128)(2,1)S(1)}, u32[]{:S(2)}, u32[]{:S(2)}) async-start(bf16[8,336,512]{2,1,0:T(8,128)(2,1)} %broadcast_in_dim.4), calls=%async_computation | async-start | bytes 5505024 | tf_op jit(solution)/shard_map/all_to_all | solution.py:291
  12.2 2.2 fusion
  14.4 0.0 copy-done.6
  14.4 0.5 fusion.1.near_ref
  14.9 1.0 collective-permute-start
  15.9 1.3 copy-done.2
  17.9 1.8 collective-permute-done.far_ref
  19.7 1.4 copy-done.4
  21.0 30.6 %all-to-all-done.packed_ref = bf16[8,336,512]{2,1,0:T(8,128)(2,1)S(1)} async-done(((bf16[8,336,512]{2,1,0:T(8,128)(2,1)}), bf16[8,336,512]{2,1,0:T(8,128)(2,1)S(1)}, u32[]{:S(2)}, u32[]{:S(2)}) %all-to-all-start) | async-done | bytes 2752544 | tf_op jit(solution)/shard_map/all_to_all | solution.py:291
  51.7 1.6 copy-done.3
  53.3 1.6 copy-done.5
  54.9 19.3 %build.1 = (bf16[2048,4096]{1,0:T(8,128)(2,1)S(1)}, f32[8,136,256]{2,1,0:T(8,128)S(1)}, f32[8,136,256]{2,1,0:T(8,128)S(1)}) custom-call(f32[1]{0:T(128)S(6)} %copy.10.spread_ref, bf16[8,336,512]{2,1,0:T(8,128)(2,1)S(1)} %all-to-all-done.packed_ref, bf16[2048,512]{1,0:T(8,128)(2,1)S(1)} %copy-done.3, bf16[2048,512]{1,0:T(8,128)(2,1)S(1)} %copy-done.5), custom_call_target="tpu_custom_call" | custom-call | tf_op jit(solution)/shard_map/build/pallas_call | solution.py:131
  74.2 5.7 %copy-done = bf16[2048,4096]{1,0:T(8,128)(2,1)} copy-done((bf16[2048,4096]{1,0:T(8,128)(2,1)}, bf16[2048,4096]{1,0:T(8,128)(2,1)S(1)}, u32[]{:S(2)}) %copy-start) | copy-done | bytes 16777240
  80.0 1.6 collective-permute-start.1
  81.6 2.4 collective-permute-done.1
  84.0 0.1 add.46
  84.1 24.1 %all_to_all.45.refs_0_ = f32[8,136,256]{2,1,0:T(8,128)S(1)} all-to-all(f32[8,136,256]{2,1,0:T(8,128)S(1)} %add.46), channel_id=1, replica_groups=mesh['y'=4,'zh'=2,'x'=4,'zl'=2,'core'=2] {'y','zh'}, dimensions={0} | all-to-all | bytes 2228224 | tf_op jit(solution)/shard_map/all_to_all | solution.py:295
  108.2 0.2 centre.2
  108.4 13.1 %all_to_all.46.own_ref = bf16[8,144,256]{2,1,0:T(8,128)(2,1)S(1)} all-to-all(bf16[8,144,256]{2,1,0:T(8,128)(2,1)S(1)} %get-tuple-element.17), channel_id=1, replica_groups=mesh['y'=4,'zh'=2,'x'=4,'zl'=2,'core'=2] {'y','zh'}, dimensions={0} | all-to-all | bytes 1179648 | tf_op jit(solution)/shard_map/all_to_all | solution.py:295
  121.4 2.9 %collective-permute-start.2 = (bf16[8,144,256]{2,1,0:T(8,128)(2,1)S(1)}, bf16[8,144,256]{2,1,0:T(8,128)(2,1)S(1)}, u32[]{:S(2)}, u32[]{:S(2)}) collective-permute-start(bf16[8,144,256]{2,1,0:T(8,128)(2,1)S(1)} %all_to_all.46.own_ref), channel_id=1, source_target_pairs={{0,1},{1,0},{2,3},{3,2},{4,5},{5,4},{6,7},{7,6},{8,9},{9,8},{10,11... | collective-permute-start | bytes 1769480 | tf_op jit(solution)/shard_map/ppermute | solution.py:299
  124.3 1.6 collective-permute-done.2.other_ref
  126.0 5.8 %copy-done.1 = bf16[2048,4096]{1,0:T(8,128)(2,1)S(1)} copy-done((bf16[2048,4096]{1,0:T(8,128)(2,1)S(1)}, bf16[2048,4096]{1,0:T(8,128)(2,1)}, u32[]{:S(2)}) %copy-start.1) | copy-done | bytes 16777240
  131.7 5.4 %image_terms.2 = bf16[8,256,128]{2,1,0:T(8,128)(2,1)S(1)} custom-call(bf16[2048,4096]{1,0:T(8,128)(2,1)S(1)} %copy-done.1, bf16[8,144,256]{2,1,0:T(8,128)(2,1)S(1)} %all_to_all.46.own_ref, bf16[8,144,256]{2,1,0:T(8,128)(2,1)S(1)} %collective-permute-done.2.other_ref), custom_call_target="tpu_custom_call" | custom-call | tf_op jit(solution)/shard_map/image_terms/pallas_call | solution.py:243
  137.2 11.7 %all_to_all.47.refs_0_ = bf16[8,256,128]{2,1,0:T(8,128)(2,1)S(1)} all-to-all(bf16[8,256,128]{2,1,0:T(8,128)(2,1)S(1)} %image_terms.2), channel_id=1, replica_groups=mesh['y'=4,'zh'=2,'x'=4,'zl'=2,'core'=2] {'x','zl'}, dimensions={0} | all-to-all | bytes 1048576 | tf_op jit(solution)/shard_map/all_to_all | solution.py:295
  148.9 0.1 mul.33.refs_1_
  149.0 0.2 owner.2
  149.2 11.5 %all_to_all.48.packed_ref = bf16[8,144,256]{2,1,0:T(8,128)(2,1)S(1)} all-to-all(bf16[8,144,256]{2,1,0:T(8,128)(2,1)S(1)} %owner.2), channel_id=1, replica_groups=mesh['y'=4,'zh'=2,'x'=4,'zl'=2,'core'=2] {'x','zl'}, dimensions={0} | all-to-all | bytes 1179648 | tf_op jit(solution)/shard_map/all_to_all | solution.py:295
  160.7 2.9 %side_terms.1 = (f32[8,136,256]{2,1,0:T(8,128)S(1)}, f32[8,136,256]{2,1,0:T(8,128)S(1)}) custom-call(bf16[2048,4096]{1,0:T(8,128)(2,1)S(1)} %copy-done.1, bf16[8,144,256]{2,1,0:T(8,128)(2,1)S(1)} %all_to_all.48.packed_ref), custom_call_target="tpu_custom_call" | custom-call | tf_op jit(solution)/shard_map/side_terms/pallas_call | solution.py:170
  163.6 3.1 %collective-permute-start.3 = (f32[8,136,256]{2,1,0:T(8,128)S(1)}, f32[8,136,256]{2,1,0:T(8,128)S(1)}, u32[]{:S(2)}, u32[]{:S(2)}) collective-permute-start(f32[8,136,256]{2,1,0:T(8,128)S(1)} %get-tuple-element.19), channel_id=1, source_target_pairs={{0,1},{1,0},{2,3},{3,2},{4,5},{5,4},{6,7},{7,6},{8,9},{9,8},{10,11... | collective-permute-start | bytes 3342344 | tf_op jit(solution)/shard_map/ppermute | solution.py:299
  166.6 2.4 collective-permute-done.3
  169.0 0.1 add.47
  169.1 19.4 %all_to_all.49.refs_0_ = f32[8,136,256]{2,1,0:T(8,128)S(1)} all-to-all(f32[8,136,256]{2,1,0:T(8,128)S(1)} %add.47), channel_id=1, replica_groups=mesh['y'=4,'zh'=2,'x'=4,'zl'=2,'core'=2] {'y','zh'}, dimensions={0} | all-to-all | bytes 2228224 | tf_op jit(solution)/shard_map/all_to_all | solution.py:295
  188.5 0.2 centre.3
  188.7 13.1 %all_to_all.50.own_ref = bf16[8,144,256]{2,1,0:T(8,128)(2,1)S(1)} all-to-all(bf16[8,144,256]{2,1,0:T(8,128)(2,1)S(1)} %centre.3), channel_id=1, replica_groups=mesh['y'=4,'zh'=2,'x'=4,'zl'=2,'core'=2] {'y','zh'}, dimensions={0} | all-to-all | bytes 1179648 | tf_op jit(solution)/shard_map/all_to_all | solution.py:295
  201.9 2.9 %collective-permute-start.4 = (bf16[8,144,256]{2,1,0:T(8,128)(2,1)S(1)}, bf16[8,144,256]{2,1,0:T(8,128)(2,1)S(1)}, u32[]{:S(2)}, u32[]{:S(2)}) collective-permute-start(bf16[8,144,256]{2,1,0:T(8,128)(2,1)S(1)} %all_to_all.50.own_ref), channel_id=1, source_target_pairs={{0,1},{1,0},{2,3},{3,2},{4,5},{5,4},{6,7},{7,6},{8,9},{9,8},{10,11... | collective-permute-start | bytes 1769480 | tf_op jit(solution)/shard_map/ppermute | solution.py:299
  204.8 1.6 collective-permute-done.4.other_ref
  206.4 5.4 %image_terms.3 = bf16[8,256,128]{2,1,0:T(8,128)(2,1)S(1)} custom-call(bf16[2048,4096]{1,0:T(8,128)(2,1)S(1)} %copy-done.1, bf16[8,144,256]{2,1,0:T(8,128)(2,1)S(1)} %all_to_all.50.own_ref, bf16[8,144,256]{2,1,0:T(8,128)(2,1)S(1)} %collective-permute-done.4.other_ref), custom_call_target="tpu_custom_call" | custom-call | tf_op jit(solution)/shard_map/image_terms/pallas_call | solution.py:243
  211.9 11.1 %all_to_all.51.refs_0_ = bf16[8,256,128]{2,1,0:T(8,128)(2,1)S(1)} all-to-all(bf16[8,256,128]{2,1,0:T(8,128)(2,1)S(1)} %image_terms.3), channel_id=1, replica_groups=mesh['y'=4,'zh'=2,'x'=4,'zl'=2,'core'=2] {'x','zl'}, dimensions={0} | all-to-all | bytes 1048576 | tf_op jit(solution)/shard_map/all_to_all | solution.py:295
  223.0 0.1 owner.3
  223.1 19.5 %all_to_all.52 = f32[128,8,128]{2,1,0:T(8,128)S(1)} all-to-all(f32[128,8,128]{2,1,0:T(8,128)S(1)} %broadcast_in_dim.5), channel_id=1, replica_groups=mesh['y'=4,'zh'=2,'x'=4,'zl'=2,'core'=2] {'y','zh','x','zl','core'}, dimensions={0} | all-to-all | bytes 1048576 | tf_op jit(solution)/shard_map/all_to_all | solution.py:291
  242.7 0.7 broadcast_divide_fusion
  (19 shorter events, 0.2 us)
Async XLA Ops:
  5.9 45.7 %all-to-all-start = ((bf16[8,336,512]{2,1,0:T(8,128)(2,1)}), bf16[8,336,512]{2,1,0:T(8,128)(2,1)S(1)}, u32[]{:S(2)}, u32[]{:S(2)}) async-start(bf16[8,336,512]{2,1,0:T(8,128)(2,1)} %broadcast_in_dim.4), calls=%async_computation | async-start | bytes 5505024 | tf_op jit(solution)/shard_map/all_to_all | solution.py:291
  12.2 2.2 copy-start.6
  14.9 4.8 %collective-permute-start = (bf16[2048,512]{1,0:T(8,128)(2,1)S(1)}, bf16[2048,512]{1,0:T(8,128)(2,1)S(1)}, u32[]{:S(2)}, u32[]{:S(2)}) collective-permute-start(bf16[2048,512]{1,0:T(8,128)(2,1)S(1)} %fusion.1.near_ref), channel_id=1, source_target_pairs={{0,1},{1,0},{2,3},{3,2},{4,5},{5,4},{6,7},{7,6},{8,9},{9,8},{10,11... | collective-permute-start | bytes 6291464 | tf_op jit(solution)/shard_map/ppermute | solution.py:299
  15.9 1.3 copy-start.2
  19.7 1.4 copy-start.4
  51.7 1.6 copy-start.3
  53.3 1.6 copy-start.5
  74.2 5.7 %copy-start = (bf16[2048,4096]{1,0:T(8,128)(2,1)}, bf16[2048,4096]{1,0:T(8,128)(2,1)S(1)}, u32[]{:S(2)}) copy-start(bf16[2048,4096]{1,0:T(8,128)(2,1)S(1)} %get-tuple-element.14.tile_ref) | copy-start | bytes 50331652
  80.0 4.0 %collective-permute-start.1 = (f32[8,136,256]{2,1,0:T(8,128)S(1)}, f32[8,136,256]{2,1,0:T(8,128)S(1)}, u32[]{:S(2)}, u32[]{:S(2)}) collective-permute-start(f32[8,136,256]{2,1,0:T(8,128)S(1)} %get-tuple-element.16), channel_id=1, source_target_pairs={{0,1},{1,0},{2,3},{3,2},{4,5},{5,4},{6,7},{7,6},{8,9},{9,8},{10,11... | collective-permute-start | bytes 3342344 | tf_op jit(solution)/shard_map/ppermute | solution.py:299
  121.4 4.5 %collective-permute-start.2 = (bf16[8,144,256]{2,1,0:T(8,128)(2,1)S(1)}, bf16[8,144,256]{2,1,0:T(8,128)(2,1)S(1)}, u32[]{:S(2)}, u32[]{:S(2)}) collective-permute-start(bf16[8,144,256]{2,1,0:T(8,128)(2,1)S(1)} %all_to_all.46.own_ref), channel_id=1, source_target_pairs={{0,1},{1,0},{2,3},{3,2},{4,5},{5,4},{6,7},{7,6},{8,9},{9,8},{10,11... | collective-permute-start | bytes 1769480 | tf_op jit(solution)/shard_map/ppermute | solution.py:299
  126.0 5.8 %copy-start.1 = (bf16[2048,4096]{1,0:T(8,128)(2,1)S(1)}, bf16[2048,4096]{1,0:T(8,128)(2,1)}, u32[]{:S(2)}) copy-start(bf16[2048,4096]{1,0:T(8,128)(2,1)} %copy-done) | copy-start | bytes 50331652
  131.7 17.2 %copy-start.7 = (f32[256]{0:T(256)S(1)}, f32[256]{0:T(256)}, u32[]{:S(2)}) copy-start(f32[256]{0:T(256)} %param.8) | copy-start | bytes 3076
  163.6 5.4 %collective-permute-start.3 = (f32[8,136,256]{2,1,0:T(8,128)S(1)}, f32[8,136,256]{2,1,0:T(8,128)S(1)}, u32[]{:S(2)}, u32[]{:S(2)}) collective-permute-start(f32[8,136,256]{2,1,0:T(8,128)S(1)} %get-tuple-element.19), channel_id=1, source_target_pairs={{0,1},{1,0},{2,3},{3,2},{4,5},{5,4},{6,7},{7,6},{8,9},{9,8},{10,11... | collective-permute-start | bytes 3342344 | tf_op jit(solution)/shard_map/ppermute | solution.py:299
  201.9 4.5 %collective-permute-start.4 = (bf16[8,144,256]{2,1,0:T(8,128)(2,1)S(1)}, bf16[8,144,256]{2,1,0:T(8,128)(2,1)S(1)}, u32[]{:S(2)}, u32[]{:S(2)}) collective-permute-start(bf16[8,144,256]{2,1,0:T(8,128)(2,1)S(1)} %all_to_all.50.own_ref), channel_id=1, source_target_pairs={{0,1},{1,0},{2,3},{3,2},{4,5},{5,4},{6,7},{7,6},{8,9},{9,8},{10,11... | collective-permute-start | bytes 1769480 | tf_op jit(solution)/shard_map/ppermute | solution.py:299

commit v3 on v2

v3 whole, which is shorter than its diff:
```python
import jax
import jax.numpy as jnp
from jax import lax
from jax.experimental import pallas as pl
from jax.experimental.pallas import tpu as pltpu
from jax.sharding import Mesh
from jax.sharding import PartitionSpec as P

ITERS = 2
AXES = ("y", "zh", "x", "zl", "core")
ROW_AXES = ("x", "zl")
MARK_AXES = ("y", "zh")
F32, B16 = jnp.float32, jnp.bfloat16
DOWN = 2.0**-20
UP = 2.0**20
LOG2E = 1.4426950408889634
VMEM = pl.BlockSpec(memory_space=pltpu.VMEM)
SMEM = pl.BlockSpec(memory_space=pltpu.SMEM)
OWN = 256
PIECE = 256
WIDTH = 128
MARKS = 2048
EIGHT = 8
ROWS = EIGHT * OWN
PACK = OWN + WIDTH // 2 + 16
BLOCK = 4 * PIECE


def params(mib):
    return pltpu.CompilerParams(vmem_limit_bytes=mib * 2**20)


def dot(left, right, left_dim, right_dim):
    dims = (((left_dim,), (right_dim,)), ((), ()))
    return lax.dot_general(left, right, dims, preferred_element_type=F32)


def unit_rows(values):
    values = values.astype(F32)
    scale = lax.rsqrt(jnp.sum(values * values, axis=1, keepdims=True) + 1e-06)
    return (values * scale).astype(B16)


def split3(values):
    high = lax.reduce_precision(values, 8, 7)
    rest = values - high
    mid = lax.reduce_precision(rest, 8, 7)
    low = rest - mid
    return [high.astype(B16), mid.astype(B16), low.astype(B16)]


def parts_in_kernel(values):
    high = values.astype(B16)
    rest = values - high.astype(F32)
    mid = rest.astype(B16)
    low = (rest - mid.astype(F32)).astype(B16)
    return high.astype(F32), mid.astype(F32), low.astype(F32)


def tail_in_kernel(row):
    at = lax.broadcasted_iota(jnp.int32, (16, row.shape[1]), 0)
    high, mid, low = parts_in_kernel(row)
    zero = jnp.zeros((16, row.shape[1]), F32)
    block = jnp.where(at == 0, high, jnp.where(at == 1, mid, jnp.where(at == 2, low, zero)))
    return block.astype(B16)


def join_tail(block):
    block = block.astype(F32)
    return (block[2:3] + block[1:2]) + block[0:1]


def stat_rows(first, second, third):
    at = lax.broadcasted_iota(jnp.int32, (8, PIECE), 0)
    zero = jnp.zeros((8, PIECE), F32)
    return jnp.where(at == 0, first, jnp.where(at == 1, second, jnp.where(at == 2, third, zero)))


def tails_in_kernel(rows):
    at = lax.broadcasted_iota(jnp.int32, (16, rows[0].shape[1]), 0)
    block = jnp.zeros(at.shape, F32)
    for index, row in enumerate(rows):
        for part, value in enumerate(parts_in_kernel(row)):
            block = jnp.where(at == 3 * index + part, value, block)
    return block.astype(B16)


def join_at(block, index):
    block = block[3 * index : 3 * index + 3].astype(F32)
    return (block[2:3] + block[1:2]) + block[0:1]


def columns_of(rows):
    at = lax.broadcasted_iota(jnp.int32, (WIDTH, WIDTH), 0)
    block = jnp.zeros((WIDTH, WIDTH), F32)
    for index, row in enumerate(rows):
        block = jnp.where(at == index, row, block)
    return jnp.transpose(block)


def call(kernel, shapes, specs, args, name, scratch=(), flops=0, mib=24):
    cost = pl.CostEstimate(flops=flops, bytes_accessed=0, transcendentals=0)
    return pl.pallas_call(
        kernel,
        out_shape=shapes,
        in_specs=specs,
        out_specs=[VMEM] * len(shapes),
        scratch_shapes=list(scratch),
        compiler_params=params(mib),
        cost_estimate=cost,
        name=name,
    )(*args)


def build_kernel(groups, block, *refs):
    count = sum(groups)
    spread_ref, packed, (near_ref, far_ref) = refs[0], refs[1 : 1 + count], refs[1 + count : 3 + count]
    tile_ref, sums_ref, wide_ref = refs[3 + count :]
    gamma = spread_ref[0] * LOG2E
    for source in range(count):
        weight = join_tail(packed[source][PACK - 16 :, :])[:, :OWN]
        column = jnp.transpose(jnp.broadcast_to(weight, (WIDTH, OWN)))
        wide_ref[source * OWN : (source + 1) * OWN, :] = column

    def half_of(marks_ref, base):
        def body(index, _):
            start = pl.multiple_of(index * block, block)
            marks = marks_ref[pl.ds(start, block), :]
            lanes = pl.ds(pl.multiple_of(base + start, block), block)
            sums = [jnp.zeros((8, WIDTH), F32) for _ in range(block // WIDTH)]
            first = 0
            for size in groups:
                rows = jnp.concatenate([ref[:OWN, :] for ref in packed[first : first + size]], axis=0)
                values = jnp.exp2(dot(rows, marks, 1, 1) * gamma)
                at = slice(first * OWN, (first + size) * OWN)
                tile_ref[at, lanes] = values.astype(B16)
                wide = wide_ref[at, :]
                for lane in range(block // WIDTH):
                    term = values[:, lane * WIDTH : (lane + 1) * WIDTH] * wide
                    sums[lane] = sums[lane] + jnp.sum(term.reshape(-1, 8, WIDTH), axis=0)
                first += size
            sums_ref[:, lanes] = jnp.concatenate(sums, axis=1)
            return 0

        lax.fori_loop(0, MARKS // block, body, 0)

    half_of(near_ref, 0)
    half_of(far_ref, MARKS)


def build(groups, block, spread, packed, near, far):
    rows = sum(groups) * OWN
    return call(
        lambda *refs: build_kernel(groups, block, *refs),
        [pltpu.VMEM((rows, 2 * MARKS), B16), jax.ShapeDtypeStruct((8, 2 * MARKS), F32)],
        [SMEM] + [VMEM] * (len(packed) + 2),
        [spread, *packed, near, far],
        "build",
        scratch=[pltpu.VMEM((rows, WIDTH), F32)],
        flops=4 * rows * 2 * MARKS * 512,
    )


def tile_rows(tiles, slot, lanes):
    for tile in tiles:
        if slot * OWN < tile.shape[0]:
            return tile[slot * OWN : (slot + 1) * OWN, lanes]
        slot -= tile.shape[0] // OWN


def side_kernel(first, *refs):
    slots_ref, tiles, refs = refs[0], refs[1:4], refs[4:]
    zero = jnp.zeros((1, PIECE - WIDTH), F32)
    ones = jnp.ones((16, OWN), B16)
    totals = jnp.zeros((1, WIDTH), F32)
    third = jnp.zeros((1, WIDTH), F32)
    rounded = jnp.zeros((16, WIDTH), F32)
    half = WIDTH // 2
    if first:
        packed, sums, (own_ref, other_ref, wt_ref) = refs[:8], refs[8:11], refs[11:]
    else:
        packed_ref, own_ref, other_ref, wt_ref = refs
    for slot in range(EIGHT):
        if first:
            wt_ref[slot, :half] = packed[slot][OWN : OWN + half, :OWN]
            wt_ref[slot, half:] = packed[slot][OWN : OWN + half, OWN:]
            tail = join_tail(packed[slot][OWN + half :, :])
            totals = totals + tail[:, OWN : OWN + WIDTH]
            third = third + jnp.sum(tail[:, :OWN], axis=1, keepdims=True)
        else:
            wt_ref[slot] = packed_ref[slots_ref[slot], :WIDTH, :]
            tail = join_tail(packed_ref[slot, WIDTH:, :])
            totals = totals + tail[:, :WIDTH]
            third = third + tail[:, WIDTH:]
        rounded = rounded + dot(ones, wt_ref[slot], 1, 1)
    second = jnp.concatenate([totals, rounded[:1]], axis=1)
    third = jnp.concatenate([third, zero], axis=1)

    def half_of(out_ref, base):
        def body(index, _):
            lanes = pl.ds(pl.multiple_of(base + index * BLOCK, BLOCK), BLOCK)
            product = None
            for slot in range(EIGHT):
                term = dot(wt_ref[slot], tile_rows(tiles, slot, lanes), 1, 0)
                product = term if product is None else product + term
            if first:
                column = (sums[0][:, lanes] + sums[1][:, lanes]) + sums[2][:, lanes]
                column = jnp.sum(column, axis=0, keepdims=True)
            else:
                column = jnp.zeros((1, BLOCK), F32)
            for at in range(BLOCK // PIECE):
                lane = slice(at * PIECE, (at + 1) * PIECE)
                out_ref[BLOCK // PIECE * index + at, :WIDTH, :] = product[:, lane]
                out_ref[BLOCK // PIECE * index + at, WIDTH:, :] = stat_rows(column[:, lane], second, third)
            return 0

        lax.fori_loop(0, MARKS // BLOCK, body, 0)

    half_of(own_ref, 0)
    half_of(other_ref, MARKS)


def side_terms(first, slots, tiles, more):
    side = jax.ShapeDtypeStruct((EIGHT, WIDTH + 8, PIECE), F32)
    return call(
        lambda *refs: side_kernel(first, *refs),
        [side, side],
        [SMEM] + [VMEM] * (3 + len(more)),
        [slots, *tiles, *more],
        "side_terms",
        scratch=[pltpu.VMEM((EIGHT, WIDTH, OWN), B16)],
        flops=2 * ROWS * 2 * MARKS * WIDTH,
    )


def pair_kernel(first, *refs):
    refs = refs[3:]
    if first:
        own_ref, other_ref, out_ref, pair_ref = refs
    else:
        own_ref, other_ref, before_ref, out_ref = refs
    stats = own_ref[0, WIDTH:, :] + other_ref[0, WIDTH:, :]
    second, third = stats[1:2], stats[2:3]
    rounded = columns_of([second[:, WIDTH:]])[:, 0:1]
    for piece in range(EIGHT):
        if first:
            column = own_ref[piece, WIDTH : WIDTH + 8, :] + other_ref[piece, WIDTH : WIDTH + 8, :]
            means = column[0:1] / third[:, 0:1]
            pair_ref[piece : piece + 1, :] = means
        else:
            means = before_ref[piece : piece + 1, :]
        side = own_ref[piece, :WIDTH, :] + other_ref[piece, :WIDTH, :]
        out_ref[piece, :WIDTH, :] = (side - rounded * means).astype(B16)
        out_ref[piece, WIDTH:, :] = tails_in_kernel([means, second, third])


def pair(first, tiles, *args):
    shapes = [jax.ShapeDtypeStruct((EIGHT, WIDTH + 16, PIECE), B16)]
    if first:
        shapes.append(jax.ShapeDtypeStruct((EIGHT, PIECE), F32))
    return call(
        lambda *refs: pair_kernel(first, *refs),
        shapes,
        [VMEM] * (3 + len(args)),
        [*tiles, *args],
        "pair",
        flops=10**9,
    )


def centre_kernel(first, total_rows, *refs):
    refs = refs[3:]
    if first:
        terms_ref, out_ref, means_ref = refs
    else:
        terms_ref, before_ref, out_ref = refs
    tails = [terms_ref[group, WIDTH:, :] for group in range(EIGHT)]
    pairs = [join_at(tail, 0) for tail in tails]
    second = [join_at(tail, 1) for tail in tails]
    third = [join_at(tail, 2) for tail in tails]
    total, every = second[0], third[0]
    for group in range(1, EIGHT):
        total, every = total + second[group], every + third[group]
    columns = columns_of([row[:, WIDTH:] for row in second] + [total[:, :WIDTH], every[:, :WIDTH]])
    if first:
        means = third[0][:, 0:1] * pairs[0]
        for group in range(1, EIGHT):
            means = means + third[group][:, 0:1] * pairs[group]
        means = means / every[:, 0:1]
        means_ref[...] = jnp.broadcast_to(means, (8, PIECE))
    else:
        means = before_ref[0:1]
    side = terms_ref[0, :WIDTH, :].astype(F32) + columns[:, 0:1] * pairs[0]
    for group in range(1, EIGHT):
        side = side + (terms_ref[group, :WIDTH, :].astype(F32) + columns[:, group : group + 1] * pairs[group])
    totals = columns[:, EIGHT : EIGHT + 1]
    if first:
        side = side - totals * means
    else:
        squares = columns[:, EIGHT + 1 : EIGHT + 2]
        side = (side * UP - totals * means) / jnp.sqrt(squares / total_rows + 1e-06)
    side = side.astype(B16)
    tail = tail_in_kernel(means)
    for group in range(EIGHT):
        out_ref[group, :WIDTH, :] = side
        out_ref[group, WIDTH:, :] = tail


def centre(first, total_rows, tiles, *args):
    shapes = [jax.ShapeDtypeStruct((EIGHT, WIDTH + 16, PIECE), B16)]
    if first:
        shapes.append(jax.ShapeDtypeStruct((8, PIECE), F32))
    return call(
        lambda *refs: centre_kernel(first, total_rows, *refs),
        shapes,
        [VMEM] * (3 + len(args)),
        [*tiles, *args],
        "centre",
        flops=10**9,
    )


def image_kernel(slots_ref, *refs):
    tiles, (own_ref, other_ref, out_ref, side_ref) = refs[:3], refs[3:]
    shift = jnp.zeros((16, WIDTH), F32)
    for half, ref in enumerate((own_ref, other_ref)):
        for piece in range(EIGHT):
            side = ref[piece, :WIDTH, :]
            lane = half * MARKS + piece * PIECE
            side_ref[:, lane : lane + PIECE] = side
            shift = shift + dot(ref[piece, WIDTH:, :], side, 1, 1)
    shift = (shift[2:3] + shift[1:2]) + shift[0:1]
    slot = 0
    for tile in tiles:
        term = dot(tile[...], side_ref[...], 1, 1) - shift
        for at in range(tile.shape[0] // OWN):
            out_ref[slots_ref[slot]] = term[at * OWN : (at + 1) * OWN].astype(B16)
            slot += 1


def image_terms(slots, tiles, own, other):
    return call(
        image_kernel,
        [jax.ShapeDtypeStruct((EIGHT, OWN, WIDTH), B16)],
        [SMEM] + [VMEM] * 5,
        [slots, *tiles, own, other],
        "image_terms",
        scratch=[pltpu.VMEM((WIDTH, 2 * MARKS), B16)],
        flops=2 * ROWS * 2 * MARKS * WIDTH,
    )[0]


def owner_kernel(last, *refs):
    if not last:
        refs = refs[3:]
    terms_ref, weight_ref, out_ref, *more = refs
    image = terms_ref[0].astype(F32)
    for member in range(1, EIGHT):
        image = image + terms_ref[member].astype(F32)
    weight = weight_ref[...]
    image = weight * image
    squares = jnp.sum(image * image, axis=0, keepdims=True)
    if last:
        out_ref[...] = image
        more[0][...] = jnp.broadcast_to(squares, (8, WIDTH))
    else:
        product = weight * image
        totals = jnp.sum(product, axis=0, keepdims=True)
        body = jnp.transpose(product * DOWN).astype(B16)
        tail = tail_in_kernel(jnp.concatenate([totals, squares], axis=1))
        for member in range(EIGHT):
            out_ref[member, :WIDTH, :] = body
            out_ref[member, WIDTH:, :] = tail


def owner(last, tiles, terms, weight):
    if last:
        shapes = [jax.ShapeDtypeStruct((OWN, WIDTH), F32), jax.ShapeDtypeStruct((8, WIDTH), F32)]
        tiles = []
    else:
        shapes = [jax.ShapeDtypeStruct((EIGHT, WIDTH + 16, OWN), B16)]
    return call(
        lambda *refs: owner_kernel(last, *refs),
        shapes,
        [VMEM] * (len(tiles) + 2),
        [*tiles, terms, weight],
        "owner",
        flops=10**9,
    )


def exchange(payload, axes):
    return lax.all_to_all(payload, axes, 0, 0)


def swap_core(values):
    return lax.ppermute(values, "core", [(0, 1), (1, 0)])


def swap_z(values):
    return lax.ppermute(values, "zl", [(0, 1), (1, 0)])


def from_below(values):
    return lax.ppermute(values, "x", [(at, (at + 1) % 4) for at in range(4)])


def from_above(values):
    return lax.ppermute(values, "x", [(at, (at + 3) % 4) for at in range(4)])


def pack(rows_unit, product, row_weight):
    transposed = product.T.astype(B16)
    half = WIDTH // 2
    vectors = jnp.concatenate([transposed[:half], transposed[half:]], axis=1)
    totals = jnp.pad(jnp.sum(product, axis=0), (0, OWN - WIDTH))
    tail = jnp.stack(split3(jnp.concatenate([row_weight, totals])))
    tail = jnp.pad(tail, ((0, 13), (0, 0)))
    return jnp.concatenate([rows_unit, vectors, tail], axis=0)


def slot_owners():
    x, z = lax.axis_index("x"), lax.axis_index("zl")
    moves = [(0, 0), (3, 0), (1, 0), (0, 1), (2, 0), (1, 1), (3, 1), (2, 1)]
    return jnp.stack([(x + dx) % 4 * 2 + (z + dz) % 2 for dx, dz in moves]).astype(jnp.int32)


def local(embeddings, landmarks, start_vectors, row_weight, spread):
    total_rows = embeddings.shape[0] * lax.axis_size(AXES)
    slots = slot_owners()
    weight = jnp.broadcast_to(row_weight[:, None], (OWN, WIDTH))
    packed = pack(unit_rows(embeddings), row_weight[:, None] * start_vectors, row_weight)
    near = unit_rows(landmarks)
    far = swap_core(near)
    below, above, across = from_below(packed), from_above(packed), swap_z(packed)
    opposite, across_above, across_below = from_below(below), from_above(across), swap_z(below)
    last = swap_z(opposite)
    packs = [packed, below, above, across, opposite, across_above, across_below, last]
    one, sums_one = build((2, 2), 1024, spread, packs[:4], near, far)
    two, sums_two = build((3,), 512, spread, packs[4:7], near, far)
    three, sums_three = build((1,), 1024, spread, packs[7:], near, far)
    tiles = (one, two, three)
    own, other = side_terms(True, slots, tiles, [*packs, sums_one, sums_two, sums_three])
    for step in range(ITERS):
        if step == 0:
            payload, pair_means = pair(True, tiles, own, swap_core(other))
            sides, means = centre(True, total_rows, tiles, exchange(payload, MARK_AXES))
        else:
            own, other = side_terms(False, slots, tiles, [vectors])
            (payload,) = pair(False, tiles, own, swap_core(other), pair_means)
            (sides,) = centre(False, total_rows, tiles, exchange(payload, MARK_AXES), means)
        sides = exchange(sides, MARK_AXES)
        parts = exchange(image_terms(slots, tiles, sides, swap_core(sides)), ROW_AXES)
        if step + 1 < ITERS:
            (vectors,) = owner(False, tiles, parts, weight)
            vectors = exchange(vectors, ROW_AXES)
    image, squares = owner(True, tiles, parts, weight)
    count = lax.axis_size(AXES)
    every = exchange(jnp.broadcast_to(squares[:1][None], (count, 1, WIDTH)), AXES)
    scale = jnp.sqrt(jnp.sum(every[:, 0], axis=0) / total_rows + 1e-06)
    return image / scale[None, :]


def solution(mesh):
    fine = Mesh(mesh.devices.reshape(4, 2, 4, 2, 2), AXES)
    rows = P(AXES, None)
    in_specs = (rows, P(("x", "zl", "core"), None), rows, P(AXES), P())
    return jax.shard_map(local, mesh=fine, in_specs=in_specs, out_specs=rows, check_vma=False)
```

time: 244 us -> 196 us (0.80)
  local copies, waits for them, and re-layouts: 19.5 us -> 0.43 us
  waiting for transfers between devices: 40.5 us -> 21.5 us
  blocking collectives: 124 us -> 110 us
  Pallas kernels: 33.7 us -> 37.9 us
  other arithmetic: 7.61 us -> 3.85 us
  starting transfers between devices: 17.7 us -> 21.1 us
    all_to_all x1 -> x0, waiting for transfers between devices: 30.6 us -> none  [spread_to(): lax.all_to_all(jnp.broadcast_to(payload[None], (count,) + payload.shape),...]
    all_to_all x1 -> x0, blocking collectives: 19.5 us -> none  [spread_to(): lax.all_to_all(jnp.broadcast_to(payload[None], (count,) + payload.shape),...]
    unnamed x16 -> x8, local copies, waits for them, and re-layouts: 17.4 us -> 0.02 us
    ppermute x0 -> x7, waiting for transfers between devices: none -> 13.5 us  [the longest x2 12 us: from_below(): return lax.ppermute(values, 'x', [(at, (at + 1) % 4) for at in range(4)])]
    ppermute x0 -> x7, starting transfers between devices: none -> 9.19 us  [the longest x3 5.1 us: swap_z(): return lax.ppermute(values, 'zl', [(0, 1), (1, 0)])]
    all_to_all x1 -> x0, starting transfers between devices: 6.2 us -> none  [spread_to(): lax.all_to_all(jnp.broadcast_to(payload[None], (count,) + payload.shape),...]
    all_to_all x7 -> x8, blocking collectives: 104 us -> 110 us  [exchange(): return lax.all_to_all(payload, axes, 0, 0)]
    pallas_call x8 -> x13, Pallas kernels: 33.7 us -> 37.9 us  [call(): pl.pallas_call(kernel, out_shape=shapes, in_specs=specs, out_specs=[VMEM]...]
  transfers between devices with their start and end apart: 6 -> 12, of which waited for: 6 -> 7; matrix products, arithmetic and copies ran while one was open for 1% -> 0% of each run, Pallas kernels for 0% -> 6%
where the time goes in v3:
time: 196 us
  blocking collectives  110 us (56%)
  Pallas kernels  37.9 us (19%)
  waiting for transfers between devices  21.5 us (11%)
  starting transfers between devices  21.1 us (11%)
  other arithmetic  3.85 us (2%)
    all_to_all x8, blocking collectives, exchange(): return lax.all_to_all(payload, axes, 0, 0)  110 us
    pallas_call x13, Pallas kernels, call(): pl.pallas_call(kernel, out_shape=shapes, in_specs=specs, out_specs=[VMEM]...  37.9 us
    ppermute x2, waiting for transfers between devices, from_below(): return lax.ppermute(values, 'x', [(at, (at + 1) % 4) for at in range(4)])  12 us
    ppermute x5, starting transfers between devices, swap_core(): return lax.ppermute(values, 'core', [(0, 1), (1, 0)])  11.9 us
    ppermute x5, waiting for transfers between devices, swap_core(): return lax.ppermute(values, 'core', [(0, 1), (1, 0)])  8.02 us
    ppermute x3, starting transfers between devices, swap_z(): return lax.ppermute(values, 'zl', [(0, 1), (1, 0)])  5.1 us
  transfers between devices with their start and end apart: 12, of which 7 were waited for; matrix products, arithmetic and copies ran while one was open for 0% of the time, Pallas kernels for 6%

profile of v3, /device:TPU:1, one launch (start us, length us, event | category | flops | bytes accessed | tf_op | source)
XLA Modules:
  0.0 195.7 jit_solution(7766484832458778525)
XLA Ops:
  0.0 2.2 %fusion = f32[2048]{0:T(1024)S(1)} fusion(bf16[2048,512]{1,0:T(8,128)(2,1)} %param.6), kind=kLoop, calls=%fused_computation.2 | loop fusion | flops 3143680 | bytes 2105344 | tf_op jit(solution)/shard_map/reduce_sum | solution.py:40
  2.3 0.5 fusion.1.refs_5_.refs_4_.refs_2_
  2.7 1.5 collective-permute-start.3
  4.3 0.1 fusion.4
  4.4 0.1 fusion.11
  4.5 0.1 copy.8
  4.7 0.1 fusion.2
  4.8 0.1 fusion.3
  5.0 1.4 collective-permute-start
  6.3 1.6 collective-permute-start.2
  8.0 7.6 %collective-permute-done.refs_2_.refs_5_ = bf16[336,512]{1,0:T(8,128)(2,1)S(1)} collective-permute-done((bf16[336,512]{1,0:T(8,128)(2,1)S(1)}, bf16[336,512]{1,0:T(8,128)(2,1)S(1)}, u32[]{:S(2)}, u32[]{:S(2)}) %collective-permute-start) | collective-permute-done | bytes 344096 | tf_op jit(solution)/shard_map/ppermute | solution.py:405
  15.7 2.6 %collective-permute-start.1 = (bf16[336,512]{1,0:T(8,128)(2,1)S(1)}, bf16[336,512]{1,0:T(8,128)(2,1)}, u32[]{:S(2)}, u32[]{:S(2)}) collective-permute-start(bf16[336,512]{1,0:T(8,128)(2,1)S(1)} %pad_maximum_fusion.refs_1_.refs_4_), channel_id=1, source_target_pairs={{0,12},{4,0},{8,4},{12,8},{1,13},{5,1},{9,5},{13,9},{2,14},{6,2},{... | collective-permute-start | bytes 1032200 | tf_op jit(solution)/shard_map/ppermute | solution.py:409
  18.9 0.1 stack.41.refs_0_.slots_ref
  19.0 1.7 collective-permute-start.6
  20.8 4.4 %collective-permute-done.4.refs_1_.refs_8_ = bf16[336,512]{1,0:T(8,128)(2,1)S(1)} collective-permute-done((bf16[336,512]{1,0:T(8,128)(2,1)S(1)}, bf16[336,512]{1,0:T(8,128)(2,1)S(1)}, u32[]{:S(2)}, u32[]{:S(2)}) %collective-permute-start.4) | collective-permute-done | bytes 344096 | tf_op jit(solution)/shard_map/ppermute | solution.py:405
  25.2 1.7 collective-permute-start.7
  26.9 7.2 %build.3 = (bf16[1024,4096]{1,0:T(8,128)(2,1)S(1)}, f32[8,4096]{1,0:T(8,128)S(1)}) custom-call(f32[1]{0:T(128)S(6)} %copy.10.refs_0_, bf16[336,512]{1,0:T(8,128)(2,1)S(1)} %pad_maximum_fusion.refs_1_.refs_4_, bf16[336,512]{1,0:T(8,128)(2,1)S(1)} %collective-permute-done.refs_2_.refs_5_, bf16[336,512]{1,0:T(8,128)(2,1)} %collective-permute-done.1.refs_3_.refs_6_, ...), custom_call_target="tpu_custom_call" | custom-call | flops 8589934592 | tf_op jit(solution)/shard_map/build/pallas_call | solution.py:103
  34.1 1.5 collective-permute-done.7.refs_1_.refs_11_
  35.6 3.6 %build.5 = (bf16[256,4096]{1,0:T(8,128)(2,1)S(1)}, f32[8,4096]{1,0:T(8,128)S(1)}) custom-call(f32[1]{0:T(128)S(6)} %copy.10.refs_0_, bf16[336,512]{1,0:T(8,128)(2,1)S(1)} %collective-permute-done.7.refs_1_.refs_11_, bf16[2048,512]{1,0:T(8,128)(2,1)S(1)} %fusion.1.refs_5_.refs_4_.refs_2_, bf16[2048,512]{1,0:T(8,128)(2,1)} %collective-permute-done.3.refs_6_.refs_5_.refs_3_), custom_call_target="tpu_custom_call" | custom-call | flops 2147483648 | tf_op jit(solution)/shard_map/build/pallas_call | solution.py:103
  39.3 6.9 %build.4 = (bf16[768,4096]{1,0:T(8,128)(2,1)S(1)}, f32[8,4096]{1,0:T(8,128)S(1)}) custom-call(f32[1]{0:T(128)S(6)} %copy.10.refs_0_, bf16[336,512]{1,0:T(8,128)(2,1)S(1)} %collective-permute-done.4.refs_1_.refs_8_, bf16[336,512]{1,0:T(8,128)(2,1)S(1)} %collective-permute-done.5.refs_2_.refs_9_, bf16[336,512]{1,0:T(8,128)(2,1)S(1)} %collective-permute-done.6.refs_3_.refs_10_, ...), custom_call_target="tpu_custom_call" | custom-call | flops 6442450944 | tf_op jit(solution)/shard_map/build/pallas_call | solution.py:103
  46.2 4.2 %side_terms.2 = (f32[8,136,256]{2,1,0:T(8,128)S(1)}, f32[8,136,256]{2,1,0:T(8,128)S(1)}) custom-call(s32[8]{0:T(128)S(1)} %stack.41.refs_0_.slots_ref, bf16[1024,4096]{1,0:T(8,128)(2,1)S(1)} %get-tuple-element.21.refs_1_.refs_0_, bf16[768,4096]{1,0:T(8,128)(2,1)S(1)} %get-tuple-element.22.refs_2_.refs_1_, ...), custom_call_target="tpu_custom_call" | custom-call | flops 2147483648 | tf_op jit(solution)/shard_map/side_terms/pallas_call | solution.py:103
  50.4 1.6 collective-permute-start.8
  52.0 2.4 %collective-permute-done.8.refs_4_ = f32[8,136,256]{2,1,0:T(8,128)S(1)} collective-permute-done((f32[8,136,256]{2,1,0:T(8,128)S(1)}, f32[8,136,256]{2,1,0:T(8,128)S(1)}, u32[]{:S(2)}, u32[]{:S(2)}) %collective-permute-start.8) | collective-permute-done | bytes 1114144 | tf_op jit(solution)/shard_map/ppermute | solution.py:397
  54.4 0.3 pair.2
  54.7 18.6 %all_to_all.40.refs_3_ = bf16[8,144,256]{2,1,0:T(8,128)(2,1)S(1)} all-to-all(bf16[8,144,256]{2,1,0:T(8,128)(2,1)S(1)} %get-tuple-element.29), channel_id=1, replica_groups=mesh['y'=4,'zh'=2,'x'=4,'zl'=2,'core'=2] {'y','zh'}, dimensions={0} | all-to-all | bytes 1179648 | tf_op jit(solution)/shard_map/all_to_all | solution.py:393
  73.2 0.4 centre.2
  73.6 13.1 %all_to_all.41.refs_3_ = bf16[8,144,256]{2,1,0:T(8,128)(2,1)S(1)} all-to-all(bf16[8,144,256]{2,1,0:T(8,128)(2,1)S(1)} %get-tuple-element.30), channel_id=1, replica_groups=mesh['y'=4,'zh'=2,'x'=4,'zl'=2,'core'=2] {'y','zh'}, dimensions={0} | all-to-all | bytes 1179648 | tf_op jit(solution)/shard_map/all_to_all | solution.py:393
  86.7 2.9 %collective-permute-start.9 = (bf16[8,144,256]{2,1,0:T(8,128)(2,1)S(1)}, bf16[8,144,256]{2,1,0:T(8,128)(2,1)S(1)}, u32[]{:S(2)}, u32[]{:S(2)}) collective-permute-start(bf16[8,144,256]{2,1,0:T(8,128)(2,1)S(1)} %all_to_all.41.refs_3_), channel_id=1, source_target_pairs={{0,1},{1,0},{2,3},{3,2},{4,5},{5,4},{6,7},{7,6},{8,9},{9,8},{10,11... | collective-permute-start | bytes 1769480 | tf_op jit(solution)/shard_map/ppermute | solution.py:397
  89.6 1.6 collective-permute-done.9.refs_4_
  91.2 5.3 %image_terms.2 = bf16[8,256,128]{2,1,0:T(8,128)(2,1)S(1)} custom-call(s32[8]{0:T(128)S(1)} %stack.41.refs_0_.slots_ref, bf16[1024,4096]{1,0:T(8,128)(2,1)S(1)} %get-tuple-element.21.refs_1_.refs_0_, bf16[768,4096]{1,0:T(8,128)(2,1)S(1)} %get-tuple-element.22.refs_2_.refs_1_, bf16[256,4096]{1,0:T(8,128)(2,1)S(1)} %get-tuple-element.23.refs_3_.refs_2_, ...), custom_call_target="tpu_custom_call" | custom-call | flops 2147483648 | tf_op jit(solution)/shard_map/image_terms/pallas_call | solution.py:103
  96.5 12.5 %all_to_all.42.refs_3_ = bf16[8,256,128]{2,1,0:T(8,128)(2,1)S(1)} all-to-all(bf16[8,256,128]{2,1,0:T(8,128)(2,1)S(1)} %image_terms.2), channel_id=1, replica_groups=mesh['y'=4,'zh'=2,'x'=4,'zl'=2,'core'=2] {'x','zl'}, dimensions={0} | all-to-all | bytes 1048576 | tf_op jit(solution)/shard_map/all_to_all | solution.py:393
  109.0 0.1 mul.53.refs_4_.refs_1_
  109.1 0.2 owner.2
  109.3 12.3 %all_to_all.43.refs_4_ = bf16[8,144,256]{2,1,0:T(8,128)(2,1)S(1)} all-to-all(bf16[8,144,256]{2,1,0:T(8,128)(2,1)S(1)} %owner.2), channel_id=1, replica_groups=mesh['y'=4,'zh'=2,'x'=4,'zl'=2,'core'=2] {'x','zl'}, dimensions={0} | all-to-all | bytes 1179648 | tf_op jit(solution)/shard_map/all_to_all | solution.py:393
  121.6 3.8 %side_terms.3 = (f32[8,136,256]{2,1,0:T(8,128)S(1)}, f32[8,136,256]{2,1,0:T(8,128)S(1)}) custom-call(s32[8]{0:T(128)S(1)} %stack.41.refs_0_.slots_ref, bf16[1024,4096]{1,0:T(8,128)(2,1)S(1)} %get-tuple-element.21.refs_1_.refs_0_, bf16[768,4096]{1,0:T(8,128)(2,1)S(1)} %get-tuple-element.22.refs_2_.refs_1_, ...), custom_call_target="tpu_custom_call" | custom-call | flops 2147483648 | tf_op jit(solution)/shard_map/side_terms/pallas_call | solution.py:103
  125.4 3.0 %collective-permute-start.10 = (f32[8,136,256]{2,1,0:T(8,128)S(1)}, f32[8,136,256]{2,1,0:T(8,128)S(1)}, u32[]{:S(2)}, u32[]{:S(2)}) collective-permute-start(f32[8,136,256]{2,1,0:T(8,128)S(1)} %get-tuple-element.32), channel_id=1, source_target_pairs={{0,1},{1,0},{2,3},{3,2},{4,5},{5,4},{6,7},{7,6},{8,9},{9,8},{10,11... | collective-permute-start | bytes 3342344 | tf_op jit(solution)/shard_map/ppermute | solution.py:397
  128.4 2.4 %collective-permute-done.10.refs_4_ = f32[8,136,256]{2,1,0:T(8,128)S(1)} collective-permute-done((f32[8,136,256]{2,1,0:T(8,128)S(1)}, f32[8,136,256]{2,1,0:T(8,128)S(1)}, u32[]{:S(2)}, u32[]{:S(2)}) %collective-permute-start.10) | collective-permute-done | bytes 1114144 | tf_op jit(solution)/shard_map/ppermute | solution.py:397
  130.8 0.3 pair.3
  131.1 14.3 %all_to_all.44.refs_3_ = bf16[8,144,256]{2,1,0:T(8,128)(2,1)S(1)} all-to-all(bf16[8,144,256]{2,1,0:T(8,128)(2,1)S(1)} %pair.3), channel_id=1, replica_groups=mesh['y'=4,'zh'=2,'x'=4,'zl'=2,'core'=2] {'y','zh'}, dimensions={0} | all-to-all | bytes 1179648 | tf_op jit(solution)/shard_map/all_to_all | solution.py:393
  145.4 0.4 centre.3
  145.8 13.1 %all_to_all.45.refs_3_ = bf16[8,144,256]{2,1,0:T(8,128)(2,1)S(1)} all-to-all(bf16[8,144,256]{2,1,0:T(8,128)(2,1)S(1)} %centre.3), channel_id=1, replica_groups=mesh['y'=4,'zh'=2,'x'=4,'zl'=2,'core'=2] {'y','zh'}, dimensions={0} | all-to-all | bytes 1179648 | tf_op jit(solution)/shard_map/all_to_all | solution.py:393
  158.8 2.9 %collective-permute-start.11 = (bf16[8,144,256]{2,1,0:T(8,128)(2,1)S(1)}, bf16[8,144,256]{2,1,0:T(8,128)(2,1)S(1)}, u32[]{:S(2)}, u32[]{:S(2)}) collective-permute-start(bf16[8,144,256]{2,1,0:T(8,128)(2,1)S(1)} %all_to_all.45.refs_3_), channel_id=1, source_target_pairs={{0,1},{1,0},{2,3},{3,2},{4,5},{5,4},{6,7},{7,6},{8,9},{9,8},{10,11... | collective-permute-start | bytes 1769480 | tf_op jit(solution)/shard_map/ppermute | solution.py:397
  161.7 1.6 collective-permute-done.11.refs_4_
  163.4 5.3 %image_terms.3 = bf16[8,256,128]{2,1,0:T(8,128)(2,1)S(1)} custom-call(s32[8]{0:T(128)S(1)} %stack.41.refs_0_.slots_ref, bf16[1024,4096]{1,0:T(8,128)(2,1)S(1)} %get-tuple-element.21.refs_1_.refs_0_, bf16[768,4096]{1,0:T(8,128)(2,1)S(1)} %get-tuple-element.22.refs_2_.refs_1_, bf16[256,4096]{1,0:T(8,128)(2,1)S(1)} %get-tuple-element.23.refs_3_.refs_2_, ...), custom_call_target="tpu_custom_call" | custom-call | flops 2147483648 | tf_op jit(solution)/shard_map/image_terms/pallas_call | solution.py:103
  168.7 11.7 %all_to_all.46.refs_0_ = bf16[8,256,128]{2,1,0:T(8,128)(2,1)S(1)} all-to-all(bf16[8,256,128]{2,1,0:T(8,128)(2,1)S(1)} %image_terms.3), channel_id=1, replica_groups=mesh['y'=4,'zh'=2,'x'=4,'zl'=2,'core'=2] {'x','zl'}, dimensions={0} | all-to-all | bytes 1048576 | tf_op jit(solution)/shard_map/all_to_all | solution.py:393
  180.4 0.1 owner.3
  180.6 14.4 %all_to_all.47 = f32[128,1,128]{2,1,0:T(1,128)S(1)} all-to-all(f32[128,1,128]{2,1,0:T(1,128)S(1)} %broadcast_in_dim.5), channel_id=1, replica_groups=mesh['y'=4,'zh'=2,'x'=4,'zl'=2,'core'=2] {'y','zh','x','zl','core'}, dimensions={0} | all-to-all | bytes 131072 | tf_op jit(solution)/shard_map/all_to_all | solution.py:393
  195.1 0.7 broadcast_divide_fusion
  (26 shorter events, 0.4 us)
Async XLA Ops:
  0.0 2.2 %copy-start = (bf16[2048,512]{1,0:T(8,128)(2,1)S(1)}, bf16[2048,512]{1,0:T(8,128)(2,1)}, u32[]{:S(2)}) copy-start(bf16[2048,512]{1,0:T(8,128)(2,1)} %param.6) | copy-start | bytes 6291460
  2.2 2.0 %copy-start.2 = (f32[256,128]{1,0:T(8,128)S(1)}, f32[256,128]{1,0:T(8,128)}, u32[]{:S(2)}) copy-start(f32[256,128]{1,0:T(8,128)} %param.7) | copy-start | bytes 393220
  2.3 2.0 %copy-start.3 = (f32[256]{0:T(256)S(1)}, f32[256]{0:T(256)}, u32[]{:S(2)}) copy-start(f32[256]{0:T(256)} %param.8) | copy-start | bytes 3076
  2.3 2.4 %copy-start.1 = (bf16[256,512]{1,0:T(8,128)(2,1)S(1)}, bf16[256,512]{1,0:T(8,128)(2,1)}, u32[]{:S(2)}) copy-start(bf16[256,512]{1,0:T(8,128)(2,1)} %param.5) | copy-start | bytes 786436
  2.7 24.2 %collective-permute-start.3 = (bf16[2048,512]{1,0:T(8,128)(2,1)S(1)}, bf16[2048,512]{1,0:T(8,128)(2,1)}, u32[]{:S(2)}, u32[]{:S(2)}) collective-permute-start(bf16[2048,512]{1,0:T(8,128)(2,1)S(1)} %fusion.1.refs_5_.refs_4_.refs_2_), channel_id=1, source_target_pairs={{0,1},{1,0},{2,3},{3,2},{4,5},{5,4},{6,7},{7,6},{8,9},{9,8},{10,11... | collective-permute-start | bytes 6291464 | tf_op jit(solution)/shard_map/ppermute | solution.py:397
  5.0 10.6 %collective-permute-start = (bf16[336,512]{1,0:T(8,128)(2,1)S(1)}, bf16[336,512]{1,0:T(8,128)(2,1)S(1)}, u32[]{:S(2)}, u32[]{:S(2)}) collective-permute-start(bf16[336,512]{1,0:T(8,128)(2,1)S(1)} %pad_maximum_fusion.refs_1_.refs_4_), channel_id=1, source_target_pairs={{0,4},{4,8},{8,12},{12,0},{1,5},{5,9},{9,13},{13,1},{2,6},{6,10},{... | collective-permute-start | bytes 1032200 | tf_op jit(solution)/shard_map/ppermute | solution.py:405
  6.3 14.4 %collective-permute-start.2 = (bf16[336,512]{1,0:T(8,128)(2,1)S(1)}, bf16[336,512]{1,0:T(8,128)(2,1)S(1)}, u32[]{:S(2)}, u32[]{:S(2)}) collective-permute-start(bf16[336,512]{1,0:T(8,128)(2,1)S(1)} %pad_maximum_fusion.refs_1_.refs_4_), channel_id=1, source_target_pairs={{0,2},{2,0},{1,3},{3,1},{4,6},{6,4},{5,7},{7,5},{8,10},{10,8},{9,1... | collective-permute-start | bytes 1032200 | tf_op jit(solution)/shard_map/ppermute | solution.py:401
  15.6 9.6 %collective-permute-start.4 = (bf16[336,512]{1,0:T(8,128)(2,1)S(1)}, bf16[336,512]{1,0:T(8,128)(2,1)S(1)}, u32[]{:S(2)}, u32[]{:S(2)}) collective-permute-start(bf16[336,512]{1,0:T(8,128)(2,1)S(1)} %collective-permute-done.refs_2_.refs_5_), channel_id=1, source_target_pairs={{0,4},{4,8},{8,12},{12,0},{1,5},{5,9},{9,13},{13,1},{2,6},{6,10},{... | collective-permute-start | bytes 1032200 | tf_op jit(solution)/shard_map/ppermute | solution.py:405
  15.7 11.3 %collective-permute-start.1 = (bf16[336,512]{1,0:T(8,128)(2,1)S(1)}, bf16[336,512]{1,0:T(8,128)(2,1)}, u32[]{:S(2)}, u32[]{:S(2)}) collective-permute-start(bf16[336,512]{1,0:T(8,128)(2,1)S(1)} %pad_maximum_fusion.refs_1_.refs_4_), channel_id=1, source_target_pairs={{0,12},{4,0},{8,4},{12,8},{1,13},{5,1},{9,5},{13,9},{2,14},{6,2},{... | collective-permute-start | bytes 1032200 | tf_op jit(solution)/shard_map/ppermute | solution.py:409
  19.0 20.3 %collective-permute-start.6 = (bf16[336,512]{1,0:T(8,128)(2,1)S(1)}, bf16[336,512]{1,0:T(8,128)(2,1)S(1)}, u32[]{:S(2)}, u32[]{:S(2)}) collective-permute-start(bf16[336,512]{1,0:T(8,128)(2,1)S(1)} %collective-permute-done.refs_2_.refs_5_), channel_id=1, source_target_pairs={{0,2},{2,0},{1,3},{3,1},{4,6},{6,4},{5,7},{7,5},{8,10},{10,8},{9,1... | collective-permute-start | bytes 1032200 | tf_op jit(solution)/shard_map/ppermute | solution.py:401
  20.7 18.5 %collective-permute-start.5 = (bf16[336,512]{1,0:T(8,128)(2,1)S(1)}, bf16[336,512]{1,0:T(8,128)(2,1)S(1)}, u32[]{:S(2)}, u32[]{:S(2)}) collective-permute-start(bf16[336,512]{1,0:T(8,128)(2,1)S(1)} %collective-permute-done.2.refs_4_.refs_7_), channel_id=1, source_target_pairs={{0,12},{4,0},{8,4},{12,8},{1,13},{5,1},{9,5},{13,9},{2,14},{6,2},{... | collective-permute-start | bytes 1032200 | tf_op jit(solution)/shard_map/ppermute | solution.py:409
  25.2 10.4 %collective-permute-start.7 = (bf16[336,512]{1,0:T(8,128)(2,1)S(1)}, bf16[336,512]{1,0:T(8,128)(2,1)S(1)}, u32[]{:S(2)}, u32[]{:S(2)}) collective-permute-start(bf16[336,512]{1,0:T(8,128)(2,1)S(1)} %collective-permute-done.4.refs_1_.refs_8_), channel_id=1, source_target_pairs={{0,2},{2,0},{1,3},{3,1},{4,6},{6,4},{5,7},{7,5},{8,10},{10,8},{9,1... | collective-permute-start | bytes 1032200 | tf_op jit(solution)/shard_map/ppermute | solution.py:401
  50.4 4.0 %collective-permute-start.8 = (f32[8,136,256]{2,1,0:T(8,128)S(1)}, f32[8,136,256]{2,1,0:T(8,128)S(1)}, u32[]{:S(2)}, u32[]{:S(2)}) collective-permute-start(f32[8,136,256]{2,1,0:T(8,128)S(1)} %get-tuple-element.28), channel_id=1, source_target_pairs={{0,1},{1,0},{2,3},{3,2},{4,5},{5,4},{6,7},{7,6},{8,9},{9,8},{10,11... | collective-permute-start | bytes 3342344 | tf_op jit(solution)/shard_map/ppermute | solution.py:397
  86.7 4.5 %collective-permute-start.9 = (bf16[8,144,256]{2,1,0:T(8,128)(2,1)S(1)}, bf16[8,144,256]{2,1,0:T(8,128)(2,1)S(1)}, u32[]{:S(2)}, u32[]{:S(2)}) collective-permute-start(bf16[8,144,256]{2,1,0:T(8,128)(2,1)S(1)} %all_to_all.41.refs_3_), channel_id=1, source_target_pairs={{0,1},{1,0},{2,3},{3,2},{4,5},{5,4},{6,7},{7,6},{8,9},{9,8},{10,11... | collective-permute-start | bytes 1769480 | tf_op jit(solution)/shard_map/ppermute | solution.py:397
  125.4 5.4 %collective-permute-start.10 = (f32[8,136,256]{2,1,0:T(8,128)S(1)}, f32[8,136,256]{2,1,0:T(8,128)S(1)}, u32[]{:S(2)}, u32[]{:S(2)}) collective-permute-start(f32[8,136,256]{2,1,0:T(8,128)S(1)} %get-tuple-element.32), channel_id=1, source_target_pairs={{0,1},{1,0},{2,3},{3,2},{4,5},{5,4},{6,7},{7,6},{8,9},{9,8},{10,11... | collective-permute-start | bytes 3342344 | tf_op jit(solution)/shard_map/ppermute | solution.py:397
  158.8 4.5 %collective-permute-start.11 = (bf16[8,144,256]{2,1,0:T(8,128)(2,1)S(1)}, bf16[8,144,256]{2,1,0:T(8,128)(2,1)S(1)}, u32[]{:S(2)}, u32[]{:S(2)}) collective-permute-start(bf16[8,144,256]{2,1,0:T(8,128)(2,1)S(1)} %all_to_all.45.refs_3_), channel_id=1, source_target_pairs={{0,1},{1,0},{2,3},{3,2},{4,5},{5,4},{6,7},{7,6},{8,9},{9,8},{10,11... | collective-permute-start | bytes 1769480 | tf_op jit(solution)/shard_map/ppermute | solution.py:397

commit v4 on v3

--- a/solution.py
+++ b/solution.py
@@ -39,14 +39,6 @@
     values = values.astype(F32)
     scale = lax.rsqrt(jnp.sum(values * values, axis=1, keepdims=True) + 1e-06)
     return (values * scale).astype(B16)
-
-
-def split3(values):
-    high = lax.reduce_precision(values, 8, 7)
-    rest = values - high
-    mid = lax.reduce_precision(rest, 8, 7)
-    low = rest - mid
-    return [high.astype(B16), mid.astype(B16), low.astype(B16)]
 
 
 def parts_in_kernel(values):
@@ -168,7 +160,7 @@
         slot -= tile.shape[0] // OWN
 
 
-def side_kernel(first, *refs):
+def side_kernel(first, base, *refs):
     slots_ref, tiles, refs = refs[0], refs[1:4], refs[4:]
     zero = jnp.zeros((1, PIECE - WIDTH), F32)
     ones = jnp.ones((16, OWN), B16)
@@ -177,9 +169,9 @@
     rounded = jnp.zeros((16, WIDTH), F32)
     half = WIDTH // 2
     if first:
-        packed, sums, (own_ref, other_ref, wt_ref) = refs[:8], refs[8:11], refs[11:]
-    else:
-        packed_ref, own_ref, other_ref, wt_ref = refs
+        packed, sums, (out_ref, wt_ref) = refs[:8], refs[8:11], refs[11:]
+    else:
+        packed_ref, out_ref, wt_ref = refs
     for slot in range(EIGHT):
         if first:
             wt_ref[slot, :half] = packed[slot][OWN : OWN + half, :OWN]
@@ -196,41 +188,36 @@
     second = jnp.concatenate([totals, rounded[:1]], axis=1)
     third = jnp.concatenate([third, zero], axis=1)
 
-    def half_of(out_ref, base):
-        def body(index, _):
-            lanes = pl.ds(pl.multiple_of(base + index * BLOCK, BLOCK), BLOCK)
-            product = None
-            for slot in range(EIGHT):
-                term = dot(wt_ref[slot], tile_rows(tiles, slot, lanes), 1, 0)
-                product = term if product is None else product + term
-            if first:
-                column = (sums[0][:, lanes] + sums[1][:, lanes]) + sums[2][:, lanes]
-                column = jnp.sum(column, axis=0, keepdims=True)
-            else:
-                column = jnp.zeros((1, BLOCK), F32)
-            for at in range(BLOCK // PIECE):
-                lane = slice(at * PIECE, (at + 1) * PIECE)
-                out_ref[BLOCK // PIECE * index + at, :WIDTH, :] = product[:, lane]
-                out_ref[BLOCK // PIECE * index + at, WIDTH:, :] = stat_rows(column[:, lane], second, third)
-            return 0
-
-        lax.fori_loop(0, MARKS // BLOCK, body, 0)
-
-    half_of(own_ref, 0)
-    half_of(other_ref, MARKS)
-
-
-def side_terms(first, slots, tiles, more):
-    side = jax.ShapeDtypeStruct((EIGHT, WIDTH + 8, PIECE), F32)
-    return call(
-        lambda *refs: side_kernel(first, *refs),
-        [side, side],
+    def body(index, _):
+        lanes = pl.ds(pl.multiple_of(base + index * BLOCK, BLOCK), BLOCK)
+        product = None
+        for slot in range(EIGHT):
+            term = dot(wt_ref[slot], tile_rows(tiles, slot, lanes), 1, 0)
+            product = term if product is None else product + term
+        if first:
+            column = (sums[0][:, lanes] + sums[1][:, lanes]) + sums[2][:, lanes]
+            column = jnp.sum(column, axis=0, keepdims=True)
+        else:
+            column = jnp.zeros((1, BLOCK), F32)
+        for at in range(BLOCK // PIECE):
+            lane = slice(at * PIECE, (at + 1) * PIECE)
+            out_ref[BLOCK // PIECE * index + at, :WIDTH, :] = product[:, lane]
+            out_ref[BLOCK // PIECE * index + at, WIDTH:, :] = stat_rows(column[:, lane], second, third)
+        return 0
+
+    lax.fori_loop(0, MARKS // BLOCK, body, 0)
+
+
+def side_terms(first, base, slots, tiles, more):
+    return call(
+        lambda *refs: side_kernel(first, base, *refs),
+        [jax.ShapeDtypeStruct((EIGHT, WIDTH + 8, PIECE), F32)],
         [SMEM] + [VMEM] * (3 + len(more)),
         [slots, *tiles, *more],
         "side_terms",
         scratch=[pltpu.VMEM((EIGHT, WIDTH, OWN), B16)],
-        flops=2 * ROWS * 2 * MARKS * WIDTH,
-    )
+        flops=2 * ROWS * MARKS * WIDTH,
+    )[0]
 
 
 def pair_kernel(first, *refs):
@@ -320,33 +307,44 @@
     )
 
 
-def image_kernel(slots_ref, *refs):
-    tiles, (own_ref, other_ref, out_ref, side_ref) = refs[:3], refs[3:]
+def image_kernel(base, slots_ref, *refs):
+    tiles, half_ref, refs = refs[:3], refs[3], refs[4:]
+    if base:
+        before_ref, out_ref, side_ref = refs
+    else:
+        out_ref, side_ref = refs
     shift = jnp.zeros((16, WIDTH), F32)
-    for half, ref in enumerate((own_ref, other_ref)):
-        for piece in range(EIGHT):
-            side = ref[piece, :WIDTH, :]
-            lane = half * MARKS + piece * PIECE
-            side_ref[:, lane : lane + PIECE] = side
-            shift = shift + dot(ref[piece, WIDTH:, :], side, 1, 1)
+    for piece in range(EIGHT):
+        side = half_ref[piece, :WIDTH, :]
+        side_ref[:, piece * PIECE : (piece + 1) * PIECE] = side
+        shift = shift + dot(half_ref[piece, WIDTH:, :], side, 1, 1)
     shift = (shift[2:3] + shift[1:2]) + shift[0:1]
     slot = 0
     for tile in tiles:
-        term = dot(tile[...], side_ref[...], 1, 1) - shift
-        for at in range(tile.shape[0] // OWN):
-            out_ref[slots_ref[slot]] = term[at * OWN : (at + 1) * OWN].astype(B16)
-            slot += 1
-
-
-def image_terms(slots, tiles, own, other):
-    return call(
-        image_kernel,
-        [jax.ShapeDtypeStruct((EIGHT, OWN, WIDTH), B16)],
-        [SMEM] + [VMEM] * 5,
-        [slots, *tiles, own, other],
+        count = tile.shape[0] // OWN
+        term = dot(tile[:, base : base + MARKS], side_ref[...], 1, 1) - shift
+        if base:
+            term = term + before_ref[slot * OWN : (slot + count) * OWN, :]
+            for at in range(count):
+                out_ref[slots_ref[slot + at]] = term[at * OWN : (at + 1) * OWN].astype(B16)
+        else:
+            out_ref[slot * OWN : (slot + count) * OWN, :] = term
+        slot += count
+
+
+def image_terms(slots, tiles, half, before=None):
+    if before is None:
+        base, more, shape = 0, [], jax.ShapeDtypeStruct((ROWS, WIDTH), F32)
+    else:
+        base, more, shape = MARKS, [before], jax.ShapeDtypeStruct((EIGHT, OWN, WIDTH), B16)
+    return call(
+        lambda *refs: image_kernel(base, *refs),
+        [shape],
+        [SMEM] + [VMEM] * (4 + len(more)),
+        [slots, *tiles, half, *more],
         "image_terms",
-        scratch=[pltpu.VMEM((WIDTH, 2 * MARKS), B16)],
-        flops=2 * ROWS * 2 * MARKS * WIDTH,
+        scratch=[pltpu.VMEM((WIDTH, MARKS), B16)],
+        flops=2 * ROWS * MARKS * WIDTH,
     )[0]
 
 
@@ -409,14 +407,26 @@
     return lax.ppermute(values, "x", [(at, (at + 3) % 4) for at in range(4)])
 
 
-def pack(rows_unit, product, row_weight):
-    transposed = product.T.astype(B16)
+def pack_kernel(rows_ref, start_ref, weight_ref, out_ref, wide_ref):
+    values = rows_ref[...].astype(F32)
+    scale = lax.rsqrt(jnp.sum(values * values, axis=1, keepdims=True) + 1e-06)
+    out_ref[:OWN, :] = (values * scale).astype(B16)
+    weight = weight_ref[...]
+    wide = jnp.transpose(jnp.broadcast_to(weight, (WIDTH, OWN)))
+    wide_ref[...] = wide
+    product = wide * start_ref[...]
+    totals = jnp.sum(product, axis=0, keepdims=True)
+    vectors = jnp.transpose(product).astype(B16)
     half = WIDTH // 2
-    vectors = jnp.concatenate([transposed[:half], transposed[half:]], axis=1)
-    totals = jnp.pad(jnp.sum(product, axis=0), (0, OWN - WIDTH))
-    tail = jnp.stack(split3(jnp.concatenate([row_weight, totals])))
-    tail = jnp.pad(tail, ((0, 13), (0, 0)))
-    return jnp.concatenate([rows_unit, vectors, tail], axis=0)
+    out_ref[OWN : OWN + half, :OWN] = vectors[:half]
+    out_ref[OWN : OWN + half, OWN:] = vectors[half:]
+    rest = jnp.zeros((1, OWN - WIDTH), F32)
+    out_ref[OWN + half :, :] = tail_in_kernel(jnp.concatenate([weight, totals, rest], axis=1))
+
+
+def pack(rows, start, weight):
+    shapes = [jax.ShapeDtypeStruct((PACK, rows.shape[1]), B16), jax.ShapeDtypeStruct((OWN, WIDTH), F32)]
+    return call(pack_kernel, shapes, [VMEM] * 3, [rows, start, weight], "pack")
 
 
 def slot_owners():
@@ -428,29 +438,37 @@
 def local(embeddings, landmarks, start_vectors, row_weight, spread):
     total_rows = embeddings.shape[0] * lax.axis_size(AXES)
     slots = slot_owners()
-    weight = jnp.broadcast_to(row_weight[:, None], (OWN, WIDTH))
-    packed = pack(unit_rows(embeddings), row_weight[:, None] * start_vectors, row_weight)
+    packed, weight = pack(embeddings, start_vectors, row_weight[None, :])
+    below, above, across = from_below(packed), from_above(packed), swap_z(packed)
+    far = unit_rows(swap_core(landmarks))
     near = unit_rows(landmarks)
-    far = swap_core(near)
-    below, above, across = from_below(packed), from_above(packed), swap_z(packed)
     opposite, across_above, across_below = from_below(below), from_above(across), swap_z(below)
+    packs = [packed, below, above, across, opposite, across_above, across_below]
+    one, sums_one = build((2, 2), 1024, spread, packs[:4], near, far)
+    opposite, sums_one = lax.optimization_barrier((opposite, sums_one))
     last = swap_z(opposite)
-    packs = [packed, below, above, across, opposite, across_above, across_below, last]
-    one, sums_one = build((2, 2), 1024, spread, packs[:4], near, far)
+    packs[4] = opposite
+    packs.append(last)
     two, sums_two = build((3,), 512, spread, packs[4:7], near, far)
+    last, sums_two = lax.optimization_barrier((last, sums_two))
+    packs[7] = last
     three, sums_three = build((1,), 1024, spread, packs[7:], near, far)
     tiles = (one, two, three)
-    own, other = side_terms(True, slots, tiles, [*packs, sums_one, sums_two, sums_three])
+    first = [*packs, sums_one, sums_two, sums_three]
     for step in range(ITERS):
+        more = first if step == 0 else [vectors]
+        other = swap_core(side_terms(step == 0, MARKS, slots, tiles, more))
+        own = side_terms(step == 0, 0, slots, tiles, more)
         if step == 0:
-            payload, pair_means = pair(True, tiles, own, swap_core(other))
+            payload, pair_means = pair(True, tiles, own, other)
             sides, means = centre(True, total_rows, tiles, exchange(payload, MARK_AXES))
         else:
-            own, other = side_terms(False, slots, tiles, [vectors])
-            (payload,) = pair(False, tiles, own, swap_core(other), pair_means)
+            (payload,) = pair(False, tiles, own, other, pair_means)
             (sides,) = centre(False, total_rows, tiles, exchange(payload, MARK_AXES), means)
         sides = exchange(sides, MARK_AXES)
-        parts = exchange(image_terms(slots, tiles, sides, swap_core(sides)), ROW_AXES)
+        across_core = swap_core(sides)
+        parts = image_terms(slots, tiles, across_core, image_terms(slots, tiles, sides))
+        parts = exchange(parts, ROW_AXES)
         if step + 1 < ITERS:
             (vectors,) = owner(False, tiles, parts, weight)
             vectors = exchange(vectors, ROW_AXES)

time: 196 us -> 186 us (0.949)
  waiting for transfers between devices: 21.5 us -> 8.25 us
  other arithmetic: 3.85 us -> 7.53 us
  Pallas kernels: 37.9 us -> 35.6 us
  local copies, waits for them, and re-layouts: 0.43 us -> 2.66 us
    ppermute x5, waiting for transfers between devices: 8.02 us -> 0.26 us  [swap_core(): return lax.ppermute(values, 'core', [(0, 1), (1, 0)])]
    ppermute x2, waiting for transfers between devices: 12 us -> 6.81 us  [from_below(): return lax.ppermute(values, 'x', [(at, (at + 1) % 4) for at in range(4)])]
    unnamed x8, local copies, waits for them, and re-layouts: 0.02 us -> 2.54 us
    ppermute x2, starting transfers between devices: 2.65 us -> 5.15 us  [from_above(): return lax.ppermute(values, 'x', [(at, (at + 3) % 4) for at in range(4)])]
    pallas_call x13 -> x18, Pallas kernels: 37.9 us -> 35.6 us  [call(): pl.pallas_call(kernel, out_shape=shapes, in_specs=specs, out_specs=[VMEM]...]
  transfers between devices with their start and end apart: 12 -> 12, of which waited for: 7 -> 4; matrix products, arithmetic and copies ran while one was open for 0% -> 4% of each run, Pallas kernels for 6% -> 12%
where the time goes in v4:
time: 186 us; the launch traced here: 185 us
  blocking collectives  109 us (59%)
  Pallas kernels  35.6 us (19%)
  starting transfers between devices  21.4 us (12%)
  waiting for transfers between devices  8.25 us (4%)
  other arithmetic  7.53 us (4%)
  local copies, waits for them, and re-layouts  2.66 us (1%)
    all_to_all x8, blocking collectives, exchange(): return lax.all_to_all(payload, axes, 0, 0)  109 us
    pallas_call x18, Pallas kernels, call(): pl.pallas_call(kernel, out_shape=shapes, in_specs=specs, out_specs=[VMEM]...  35.6 us
    ppermute x5, starting transfers between devices, swap_core(): return lax.ppermute(values, 'core', [(0, 1), (1, 0)])  12.9 us
    ppermute x2, waiting for transfers between devices, from_below(): return lax.ppermute(values, 'x', [(at, (at + 1) % 4) for at in range(4)])  6.81 us
    ppermute x2, starting transfers between devices, from_above(): return lax.ppermute(values, 'x', [(at, (at + 3) % 4) for at in range(4)])  5.15 us
    reduce_sum x2, other arithmetic, unit_rows(): scale = lax.rsqrt(jnp.sum(values * values, axis=1, keepdims=True) + 1e-06)  4.3 us
  transfers between devices with their start and end apart: 12, of which 4 were waited for; matrix products, arithmetic and copies ran while one was open for 4% of the time, Pallas kernels for 12%

profile of v4, /device:TPU:1, one launch (start us, length us, event | category | flops | bytes accessed | tf_op | source)
XLA Modules:
  0.0 185.0 jit_solution(14690563573351768208)
XLA Ops:
  0.0 1.4 collective-permute-start.3
  1.4 0.9 copy-done
  2.4 0.9 copy-done.1
  3.3 0.7 copy-done.2
  4.0 0.2 pack.1
  4.2 1.8 collective-permute-start.2
  6.0 2.5 %collective-permute-start.1 = (bf16[336,512]{1,0:T(8,128)(2,1)S(1)}, bf16[336,512]{1,0:T(8,128)(2,1)S(1)}, u32[]{:S(2)}, u32[]{:S(2)}) collective-permute-start(bf16[336,512]{1,0:T(8,128)(2,1)S(1)} %get-tuple-element.23.refs_1_.refs_4_), channel_id=1, source_target_pairs={{0,12},{4,0},{8,4},{12,8},{1,13},{5,1},{9,5},{13,9},{2,14},{6,2},{... | collective-permute-start | bytes 1032200 | tf_op jit(solution)/shard_map/ppermute | solution.py:407
  9.2 2.2 %fusion = f32[2048]{0:T(1024)S(1)} fusion(bf16[2048,512]{1,0:T(8,128)(2,1)} %param.6), kind=kLoop, calls=%fused_computation.4 | loop fusion | flops 3143680 | bytes 2105344 | tf_op jit(solution)/shard_map/reduce_sum | solution.py:40
  11.5 0.5 fusion.1.refs_5_.refs_4_.refs_2_
  11.9 6.8 %collective-permute-done.refs_2_.refs_5_ = bf16[336,512]{1,0:T(8,128)(2,1)S(1)} collective-permute-done((bf16[336,512]{1,0:T(8,128)(2,1)S(1)}, bf16[336,512]{1,0:T(8,128)(2,1)S(1)}, u32[]{:S(2)}, u32[]{:S(2)}) %collective-permute-start) | collective-permute-done | bytes 344096 | tf_op jit(solution)/shard_map/ppermute | solution.py:403
  18.8 0.4 collective-permute-start.6
  19.1 2.7 %collective-permute-start.5 = (bf16[336,512]{1,0:T(8,128)(2,1)S(1)}, bf16[336,512]{1,0:T(8,128)(2,1)S(1)}, u32[]{:S(2)}, u32[]{:S(2)}) collective-permute-start(bf16[336,512]{1,0:T(8,128)(2,1)S(1)} %collective-permute-done.2.refs_4_.refs_7_), channel_id=1, source_target_pairs={{0,12},{4,0},{8,4},{12,8},{1,13},{5,1},{9,5},{13,9},{2,14},{6,2},{... | collective-permute-start | bytes 1032200 | tf_op jit(solution)/shard_map/ppermute | solution.py:407
  21.8 2.1 %fusion.2 = f32[2048]{0:T(1024)S(1)} fusion(bf16[2048,512]{1,0:T(8,128)(2,1)} %collective-permute-done.3), kind=kLoop, calls=%fused_computation.6 | loop fusion | flops 3143680 | bytes 2105344 | tf_op jit(solution)/shard_map/reduce_sum | solution.py:40
  23.9 2.0 %fusion.3.refs_6_.refs_5_.refs_3_ = bf16[2048,512]{1,0:T(8,128)(2,1)S(1)} fusion(bf16[2048,512]{1,0:T(8,128)(2,1)} %collective-permute-done.3, f32[2048]{0:T(1024)S(1)} %add_rsqrt_fusion), kind=kLoop, calls=%fused_computation.7 | loop fusion | flops 3145728 | bytes 4202496 | tf_op jit(solution)/shard_map/convert_element_type | solution.py:41
  26.0 5.5 %build.3 = (bf16[1024,4096]{1,0:T(8,128)(2,1)S(1)}, f32[8,4096]{1,0:T(8,128)S(1)}) custom-call(f32[1]{0:T(128)S(6)} %copy.7.refs_0_, bf16[336,512]{1,0:T(8,128)(2,1)S(1)} %get-tuple-element.23.refs_1_.refs_4_, bf16[336,512]{1,0:T(8,128)(2,1)S(1)} %collective-permute-done.refs_2_.refs_5_, bf16[336,512]{1,0:T(8,128)(2,1)S(1)} %collective-permute-done.1.refs_3_.refs_6_, ...), custom_call_target="tpu_custom_call" | custom-call | flops 8589934592 | tf_op jit(solution)/shard_map/build/pallas_call | solution.py:95
  31.4 1.2 collective-permute-start.7
  32.6 5.3 %build.4 = (bf16[768,4096]{1,0:T(8,128)(2,1)S(1)}, f32[8,4096]{1,0:T(8,128)S(1)}) custom-call(f32[1]{0:T(128)S(6)} %copy.7.refs_0_, bf16[336,512]{1,0:T(8,128)(2,1)S(1)} %collective-permute-done.4.refs_1_.refs_8_, bf16[336,512]{1,0:T(8,128)(2,1)S(1)} %collective-permute-done.5.refs_2_.refs_9_, bf16[336,512]{1,0:T(8,128)(2,1)S(1)} %collective-permute-done.6.refs_3_.refs_10_, ...), custom_call_target="tpu_custom_call" | custom-call | flops 6442450944 | tf_op jit(solution)/shard_map/build/pallas_call | solution.py:95
  37.9 1.2 collective-permute-done.7.refs_1_.refs_11_
  39.1 2.1 %build.5 = (bf16[256,4096]{1,0:T(8,128)(2,1)S(1)}, f32[8,4096]{1,0:T(8,128)S(1)}) custom-call(f32[1]{0:T(128)S(6)} %copy.7.refs_0_, bf16[336,512]{1,0:T(8,128)(2,1)S(1)} %collective-permute-done.7.refs_1_.refs_11_, bf16[2048,512]{1,0:T(8,128)(2,1)S(1)} %fusion.1.refs_5_.refs_4_.refs_2_, bf16[2048,512]{1,0:T(8,128)(2,1)S(1)} %fusion.3.refs_6_.refs_5_.refs_3_), custom_call_target="tpu_custom_call" | custom-call | flops 2147483648 | tf_op jit(solution)/shard_map/build/pallas_call | solution.py:95
  41.2 2.3 %side_terms.5 = f32[8,136,256]{2,1,0:T(8,128)S(1)} custom-call(s32[8]{0:T(128)S(1)} %stack.35.refs_0_, bf16[1024,4096]{1,0:T(8,128)(2,1)S(1)} %get-tuple-element.24.refs_1_.refs_0_, bf16[768,4096]{1,0:T(8,128)(2,1)S(1)} %get-tuple-element.27.refs_2_.refs_1_, bf16[256,4096]{1,0:T(8,128)(2,1)S(1)} %get-tuple-element.30.refs_3_.refs_2_, ...), custom_call_target="tpu_custom_call" | custom-call | flops 1073741824 | tf_op jit(solution)/shard_map/side_terms/pallas_call | solution.py:95
  43.4 3.0 %collective-permute-start.8 = (f32[8,136,256]{2,1,0:T(8,128)S(1)}, f32[8,136,256]{2,1,0:T(8,128)S(1)}, u32[]{:S(2)}, u32[]{:S(2)}) collective-permute-start(f32[8,136,256]{2,1,0:T(8,128)S(1)} %side_terms.5), channel_id=1, source_target_pairs={{0,1},{1,0},{2,3},{3,2},{4,5},{5,4},{6,7},{7,6},{8,9},{9,8},{10,11... | collective-permute-start | bytes 3342344 | tf_op jit(solution)/shard_map/ppermute | solution.py:395
  46.4 2.3 %side_terms.4.refs_3_ = f32[8,136,256]{2,1,0:T(8,128)S(1)} custom-call(s32[8]{0:T(128)S(1)} %stack.35.refs_0_, bf16[1024,4096]{1,0:T(8,128)(2,1)S(1)} %get-tuple-element.24.refs_1_.refs_0_, bf16[768,4096]{1,0:T(8,128)(2,1)S(1)} %get-tuple-element.27.refs_2_.refs_1_, bf16[256,4096]{1,0:T(8,128)(2,1)S(1)} %get-tuple-element.30.refs_3_.refs_2_, ...), custom_call_target="tpu_custom_call" | custom-call | flops 1073741824 | tf_op jit(solution)/shard_map/side_terms/pallas_call | solution.py:95
  48.7 0.1 collective-permute-done.8.refs_4_
  48.8 0.3 pair.2
  49.1 18.2 %all_to_all.40.refs_3_ = bf16[8,144,256]{2,1,0:T(8,128)(2,1)S(1)} all-to-all(bf16[8,144,256]{2,1,0:T(8,128)(2,1)S(1)} %get-tuple-element.34), channel_id=1, replica_groups=mesh['y'=4,'zh'=2,'x'=4,'zl'=2,'core'=2] {'y','zh'}, dimensions={0} | all-to-all | bytes 1179648 | tf_op jit(solution)/shard_map/all_to_all | solution.py:391
  67.3 0.4 centre.2
  67.7 13.1 %all_to_all.41.refs_4_ = bf16[8,144,256]{2,1,0:T(8,128)(2,1)S(1)} all-to-all(bf16[8,144,256]{2,1,0:T(8,128)(2,1)S(1)} %get-tuple-element.35), channel_id=1, replica_groups=mesh['y'=4,'zh'=2,'x'=4,'zl'=2,'core'=2] {'y','zh'}, dimensions={0} | all-to-all | bytes 1179648 | tf_op jit(solution)/shard_map/all_to_all | solution.py:391
  80.8 2.9 %collective-permute-start.9 = (bf16[8,144,256]{2,1,0:T(8,128)(2,1)S(1)}, bf16[8,144,256]{2,1,0:T(8,128)(2,1)S(1)}, u32[]{:S(2)}, u32[]{:S(2)}) collective-permute-start(bf16[8,144,256]{2,1,0:T(8,128)(2,1)S(1)} %all_to_all.41.refs_4_), channel_id=1, source_target_pairs={{0,1},{1,0},{2,3},{3,2},{4,5},{5,4},{6,7},{7,6},{8,9},{9,8},{10,11... | collective-permute-start | bytes 1769480 | tf_op jit(solution)/shard_map/ppermute | solution.py:395
  83.7 3.0 %image_terms.4.refs_5_ = f32[2048,128]{1,0:T(8,128)S(1)} custom-call(s32[8]{0:T(128)S(1)} %stack.35.refs_0_, bf16[1024,4096]{1,0:T(8,128)(2,1)S(1)} %get-tuple-element.24.refs_1_.refs_0_, bf16[768,4096]{1,0:T(8,128)(2,1)S(1)} %get-tuple-element.27.refs_2_.refs_1_, bf16[256,4096]{1,0:T(8,128)(2,1)S(1)} %get-tuple-element.30.refs_3_.refs_2_, ...), custom_call_target="tpu_custom_call" | custom-call | flops 1073741824 | tf_op jit(solution)/shard_map/image_terms/pallas_call | solution.py:95
  86.7 3.0 %image_terms.5 = bf16[8,256,128]{2,1,0:T(8,128)(2,1)S(1)} custom-call(s32[8]{0:T(128)S(1)} %stack.35.refs_0_, bf16[1024,4096]{1,0:T(8,128)(2,1)S(1)} %get-tuple-element.24.refs_1_.refs_0_, bf16[768,4096]{1,0:T(8,128)(2,1)S(1)} %get-tuple-element.27.refs_2_.refs_1_, bf16[256,4096]{1,0:T(8,128)(2,1)S(1)} %get-tuple-element.30.refs_3_.refs_2_, ...), custom_call_target="tpu_custom_call" | custom-call | flops 1073741824 | tf_op jit(solution)/shard_map/image_terms/pallas_call | solution.py:95
  89.7 12.1 %all_to_all.42.refs_3_ = bf16[8,256,128]{2,1,0:T(8,128)(2,1)S(1)} all-to-all(bf16[8,256,128]{2,1,0:T(8,128)(2,1)S(1)} %image_terms.5), channel_id=1, replica_groups=mesh['y'=4,'zh'=2,'x'=4,'zl'=2,'core'=2] {'x','zl'}, dimensions={0} | all-to-all | bytes 1048576 | tf_op jit(solution)/shard_map/all_to_all | solution.py:391
  101.7 0.2 owner.2
  101.9 12.1 %all_to_all.43.refs_4_ = bf16[8,144,256]{2,1,0:T(8,128)(2,1)S(1)} all-to-all(bf16[8,144,256]{2,1,0:T(8,128)(2,1)S(1)} %owner.2), channel_id=1, replica_groups=mesh['y'=4,'zh'=2,'x'=4,'zl'=2,'core'=2] {'x','zl'}, dimensions={0} | all-to-all | bytes 1179648 | tf_op jit(solution)/shard_map/all_to_all | solution.py:391
  114.0 2.2 %side_terms.7 = f32[8,136,256]{2,1,0:T(8,128)S(1)} custom-call(s32[8]{0:T(128)S(1)} %stack.35.refs_0_, bf16[1024,4096]{1,0:T(8,128)(2,1)S(1)} %get-tuple-element.24.refs_1_.refs_0_, bf16[768,4096]{1,0:T(8,128)(2,1)S(1)} %get-tuple-element.27.refs_2_.refs_1_, bf16[256,4096]{1,0:T(8,128)(2,1)S(1)} %get-tuple-element.30.refs_3_.refs_2_, ...), custom_call_target="tpu_custom_call" | custom-call | flops 1073741824 | tf_op jit(solution)/shard_map/side_terms/pallas_call | solution.py:95
  116.3 2.6 %collective-permute-start.10 = (f32[8,136,256]{2,1,0:T(8,128)S(1)}, f32[8,136,256]{2,1,0:T(8,128)S(1)}, u32[]{:S(2)}, u32[]{:S(2)}) collective-permute-start(f32[8,136,256]{2,1,0:T(8,128)S(1)} %side_terms.7), channel_id=1, source_target_pairs={{0,1},{1,0},{2,3},{3,2},{4,5},{5,4},{6,7},{7,6},{8,9},{9,8},{10,11... | collective-permute-start | bytes 3342344 | tf_op jit(solution)/shard_map/ppermute | solution.py:395
  118.8 2.2 %side_terms.6.refs_3_ = f32[8,136,256]{2,1,0:T(8,128)S(1)} custom-call(s32[8]{0:T(128)S(1)} %stack.35.refs_0_, bf16[1024,4096]{1,0:T(8,128)(2,1)S(1)} %get-tuple-element.24.refs_1_.refs_0_, bf16[768,4096]{1,0:T(8,128)(2,1)S(1)} %get-tuple-element.27.refs_2_.refs_1_, bf16[256,4096]{1,0:T(8,128)(2,1)S(1)} %get-tuple-element.30.refs_3_.refs_2_, ...), custom_call_target="tpu_custom_call" | custom-call | flops 1073741824 | tf_op jit(solution)/shard_map/side_terms/pallas_call | solution.py:95
  121.1 0.1 collective-permute-done.10.refs_4_
  121.2 0.3 pair.3
  121.5 14.1 %all_to_all.44.refs_3_ = bf16[8,144,256]{2,1,0:T(8,128)(2,1)S(1)} all-to-all(bf16[8,144,256]{2,1,0:T(8,128)(2,1)S(1)} %pair.3), channel_id=1, replica_groups=mesh['y'=4,'zh'=2,'x'=4,'zl'=2,'core'=2] {'y','zh'}, dimensions={0} | all-to-all | bytes 1179648 | tf_op jit(solution)/shard_map/all_to_all | solution.py:391
  135.6 0.4 centre.3
  136.0 12.8 %all_to_all.45.refs_4_ = bf16[8,144,256]{2,1,0:T(8,128)(2,1)S(1)} all-to-all(bf16[8,144,256]{2,1,0:T(8,128)(2,1)S(1)} %centre.3), channel_id=1, replica_groups=mesh['y'=4,'zh'=2,'x'=4,'zl'=2,'core'=2] {'y','zh'}, dimensions={0} | all-to-all | bytes 1179648 | tf_op jit(solution)/shard_map/all_to_all | solution.py:391
  148.8 3.0 %collective-permute-start.11 = (bf16[8,144,256]{2,1,0:T(8,128)(2,1)S(1)}, bf16[8,144,256]{2,1,0:T(8,128)(2,1)S(1)}, u32[]{:S(2)}, u32[]{:S(2)}) collective-permute-start(bf16[8,144,256]{2,1,0:T(8,128)(2,1)S(1)} %all_to_all.45.refs_4_), channel_id=1, source_target_pairs={{0,1},{1,0},{2,3},{3,2},{4,5},{5,4},{6,7},{7,6},{8,9},{9,8},{10,11... | collective-permute-start | bytes 1769480 | tf_op jit(solution)/shard_map/ppermute | solution.py:395
  151.8 3.0 %image_terms.6.refs_5_ = f32[2048,128]{1,0:T(8,128)S(1)} custom-call(s32[8]{0:T(128)S(1)} %stack.35.refs_0_, bf16[1024,4096]{1,0:T(8,128)(2,1)S(1)} %get-tuple-element.24.refs_1_.refs_0_, bf16[768,4096]{1,0:T(8,128)(2,1)S(1)} %get-tuple-element.27.refs_2_.refs_1_, bf16[256,4096]{1,0:T(8,128)(2,1)S(1)} %get-tuple-element.30.refs_3_.refs_2_, ...), custom_call_target="tpu_custom_call" | custom-call | flops 1073741824 | tf_op jit(solution)/shard_map/image_terms/pallas_call | solution.py:95
  154.8 3.0 %image_terms.7 = bf16[8,256,128]{2,1,0:T(8,128)(2,1)S(1)} custom-call(s32[8]{0:T(128)S(1)} %stack.35.refs_0_, bf16[1024,4096]{1,0:T(8,128)(2,1)S(1)} %get-tuple-element.24.refs_1_.refs_0_, bf16[768,4096]{1,0:T(8,128)(2,1)S(1)} %get-tuple-element.27.refs_2_.refs_1_, bf16[256,4096]{1,0:T(8,128)(2,1)S(1)} %get-tuple-element.30.refs_3_.refs_2_, ...), custom_call_target="tpu_custom_call" | custom-call | flops 1073741824 | tf_op jit(solution)/shard_map/image_terms/pallas_call | solution.py:95
  157.8 12.0 %all_to_all.46.refs_0_ = bf16[8,256,128]{2,1,0:T(8,128)(2,1)S(1)} all-to-all(bf16[8,256,128]{2,1,0:T(8,128)(2,1)S(1)} %image_terms.7), channel_id=1, replica_groups=mesh['y'=4,'zh'=2,'x'=4,'zl'=2,'core'=2] {'x','zl'}, dimensions={0} | all-to-all | bytes 1048576 | tf_op jit(solution)/shard_map/all_to_all | solution.py:391
  169.9 0.1 owner.3
  170.0 14.3 %all_to_all.47 = f32[128,1,128]{2,1,0:T(1,128)S(1)} all-to-all(f32[128,1,128]{2,1,0:T(1,128)S(1)} %broadcast_in_dim.16), channel_id=1, replica_groups=mesh['y'=4,'zh'=2,'x'=4,'zl'=2,'core'=2] {'y','zh','x','zl','core'}, dimensions={0} | all-to-all | bytes 131072 | tf_op jit(solution)/shard_map/all_to_all | solution.py:391
  184.4 0.7 broadcast_divide_fusion
  (22 shorter events, 0.2 us)
Async XLA Ops:
  0.0 21.8 %collective-permute-start.3 = (bf16[2048,512]{1,0:T(8,128)(2,1)}, bf16[2048,512]{1,0:T(8,128)(2,1)}, u32[]{:S(2)}, u32[]{:S(2)}) collective-permute-start(bf16[2048,512]{1,0:T(8,128)(2,1)} %param.6), channel_id=1, source_target_pairs={{0,1},{1,0},{2,3},{3,2},{4,5},{5,4},{6,7},{7,6},{8,9},{9,8},{10,11... | collective-permute-start | bytes 6291464 | tf_op jit(solution)/shard_map/ppermute | solution.py:395
  1.4 0.9 copy-start
  2.4 0.9 copy-start.1
  3.3 0.7 copy-start.2
  4.2 14.9 %collective-permute-start.2 = (bf16[336,512]{1,0:T(8,128)(2,1)S(1)}, bf16[336,512]{1,0:T(8,128)(2,1)S(1)}, u32[]{:S(2)}, u32[]{:S(2)}) collective-permute-start(bf16[336,512]{1,0:T(8,128)(2,1)S(1)} %get-tuple-element.23.refs_1_.refs_4_), channel_id=1, source_target_pairs={{0,2},{2,0},{1,3},{3,1},{4,6},{6,4},{5,7},{7,5},{8,10},{10,8},{9,1... | collective-permute-start | bytes 1032200 | tf_op jit(solution)/shard_map/ppermute | solution.py:399
  6.0 19.9 %collective-permute-start.1 = (bf16[336,512]{1,0:T(8,128)(2,1)S(1)}, bf16[336,512]{1,0:T(8,128)(2,1)S(1)}, u32[]{:S(2)}, u32[]{:S(2)}) collective-permute-start(bf16[336,512]{1,0:T(8,128)(2,1)S(1)} %get-tuple-element.23.refs_1_.refs_4_), channel_id=1, source_target_pairs={{0,12},{4,0},{8,4},{12,8},{1,13},{5,1},{9,5},{13,9},{2,14},{6,2},{... | collective-permute-start | bytes 1032200 | tf_op jit(solution)/shard_map/ppermute | solution.py:407
  8.5 10.3 %collective-permute-start = (bf16[336,512]{1,0:T(8,128)(2,1)S(1)}, bf16[336,512]{1,0:T(8,128)(2,1)S(1)}, u32[]{:S(2)}, u32[]{:S(2)}) collective-permute-start(bf16[336,512]{1,0:T(8,128)(2,1)S(1)} %get-tuple-element.23.refs_1_.refs_4_), channel_id=1, source_target_pairs={{0,4},{4,8},{8,12},{12,0},{1,5},{5,9},{9,13},{13,1},{2,6},{6,10},{... | collective-permute-start | bytes 1032200 | tf_op jit(solution)/shard_map/ppermute | solution.py:403
  9.2 2.2 %copy-start.3 = (bf16[2048,512]{1,0:T(8,128)(2,1)S(1)}, bf16[2048,512]{1,0:T(8,128)(2,1)}, u32[]{:S(2)}) copy-start(bf16[2048,512]{1,0:T(8,128)(2,1)} %param.6) | copy-start | bytes 6291460
  18.8 13.9 %collective-permute-start.6 = (bf16[336,512]{1,0:T(8,128)(2,1)S(1)}, bf16[336,512]{1,0:T(8,128)(2,1)S(1)}, u32[]{:S(2)}, u32[]{:S(2)}) collective-permute-start(bf16[336,512]{1,0:T(8,128)(2,1)S(1)} %collective-permute-done.refs_2_.refs_5_), channel_id=1, source_target_pairs={{0,2},{2,0},{1,3},{3,1},{4,6},{6,4},{5,7},{7,5},{8,10},{10,8},{9,1... | collective-permute-start | bytes 1032200 | tf_op jit(solution)/shard_map/ppermute | solution.py:399
  19.1 12.3 %collective-permute-start.4 = (bf16[336,512]{1,0:T(8,128)(2,1)S(1)}, bf16[336,512]{1,0:T(8,128)(2,1)S(1)}, u32[]{:S(2)}, u32[]{:S(2)}) collective-permute-start(bf16[336,512]{1,0:T(8,128)(2,1)S(1)} %collective-permute-done.refs_2_.refs_5_), channel_id=1, source_target_pairs={{0,4},{4,8},{8,12},{12,0},{1,5},{5,9},{9,13},{13,1},{2,6},{6,10},{... | collective-permute-start | bytes 1032200 | tf_op jit(solution)/shard_map/ppermute | solution.py:403
  19.1 13.5 %collective-permute-start.5 = (bf16[336,512]{1,0:T(8,128)(2,1)S(1)}, bf16[336,512]{1,0:T(8,128)(2,1)S(1)}, u32[]{:S(2)}, u32[]{:S(2)}) collective-permute-start(bf16[336,512]{1,0:T(8,128)(2,1)S(1)} %collective-permute-done.2.refs_4_.refs_7_), channel_id=1, source_target_pairs={{0,12},{4,0},{8,4},{12,8},{1,13},{5,1},{9,5},{13,9},{2,14},{6,2},{... | collective-permute-start | bytes 1032200 | tf_op jit(solution)/shard_map/ppermute | solution.py:407
  31.4 7.7 %collective-permute-start.7 = (bf16[336,512]{1,0:T(8,128)(2,1)S(1)}, bf16[336,512]{1,0:T(8,128)(2,1)S(1)}, u32[]{:S(2)}, u32[]{:S(2)}) collective-permute-start(bf16[336,512]{1,0:T(8,128)(2,1)S(1)} %collective-permute-done.4.refs_1_.refs_8_), channel_id=1, source_target_pairs={{0,2},{2,0},{1,3},{3,1},{4,6},{6,4},{5,7},{7,5},{8,10},{10,8},{9,1... | collective-permute-start | bytes 1032200 | tf_op jit(solution)/shard_map/ppermute | solution.py:399
  43.4 5.4 %collective-permute-start.8 = (f32[8,136,256]{2,1,0:T(8,128)S(1)}, f32[8,136,256]{2,1,0:T(8,128)S(1)}, u32[]{:S(2)}, u32[]{:S(2)}) collective-permute-start(f32[8,136,256]{2,1,0:T(8,128)S(1)} %side_terms.5), channel_id=1, source_target_pairs={{0,1},{1,0},{2,3},{3,2},{4,5},{5,4},{6,7},{7,6},{8,9},{9,8},{10,11... | collective-permute-start | bytes 3342344 | tf_op jit(solution)/shard_map/ppermute | solution.py:395
  80.8 5.9 %collective-permute-start.9 = (bf16[8,144,256]{2,1,0:T(8,128)(2,1)S(1)}, bf16[8,144,256]{2,1,0:T(8,128)(2,1)S(1)}, u32[]{:S(2)}, u32[]{:S(2)}) collective-permute-start(bf16[8,144,256]{2,1,0:T(8,128)(2,1)S(1)} %all_to_all.41.refs_4_), channel_id=1, source_target_pairs={{0,1},{1,0},{2,3},{3,2},{4,5},{5,4},{6,7},{7,6},{8,9},{9,8},{10,11... | collective-permute-start | bytes 1769480 | tf_op jit(solution)/shard_map/ppermute | solution.py:395
  116.3 5.0 %collective-permute-start.10 = (f32[8,136,256]{2,1,0:T(8,128)S(1)}, f32[8,136,256]{2,1,0:T(8,128)S(1)}, u32[]{:S(2)}, u32[]{:S(2)}) collective-permute-start(f32[8,136,256]{2,1,0:T(8,128)S(1)} %side_terms.7), channel_id=1, source_target_pairs={{0,1},{1,0},{2,3},{3,2},{4,5},{5,4},{6,7},{7,6},{8,9},{9,8},{10,11... | collective-permute-start | bytes 3342344 | tf_op jit(solution)/shard_map/ppermute | solution.py:395
  148.8 6.0 %collective-permute-start.11 = (bf16[8,144,256]{2,1,0:T(8,128)(2,1)S(1)}, bf16[8,144,256]{2,1,0:T(8,128)(2,1)S(1)}, u32[]{:S(2)}, u32[]{:S(2)}) collective-permute-start(bf16[8,144,256]{2,1,0:T(8,128)(2,1)S(1)} %all_to_all.45.refs_4_), channel_id=1, source_target_pairs={{0,1},{1,0},{2,3},{3,2},{4,5},{5,4},{6,7},{7,6},{8,9},{9,8},{10,11... | collective-permute-start | bytes 1769480 | tf_op jit(solution)/shard_map/ppermute | solution.py:395

commit v5 on v4

--- a/solution.py
+++ b/solution.py
@@ -24,6 +24,8 @@
 ROWS = EIGHT * OWN
 PACK = OWN + WIDTH // 2 + 16
 BLOCK = 4 * PIECE
+THIRD = PACK // 3
+TILES = 4
 
 
 def params(mib):
@@ -33,12 +35,6 @@
 def dot(left, right, left_dim, right_dim):
     dims = (((left_dim,), (right_dim,)), ((), ()))
     return lax.dot_general(left, right, dims, preferred_element_type=F32)
-
-
-def unit_rows(values):
-    values = values.astype(F32)
-    scale = lax.rsqrt(jnp.sum(values * values, axis=1, keepdims=True) + 1e-06)
-    return (values * scale).astype(B16)
 
 
 def parts_in_kernel(values):
@@ -104,13 +100,50 @@
     )(*args)
 
 
-def build_kernel(groups, block, *refs):
-    count = sum(groups)
-    spread_ref, packed, (near_ref, far_ref) = refs[0], refs[1 : 1 + count], refs[1 + count : 3 + count]
-    tile_ref, sums_ref, wide_ref = refs[3 + count :]
+def rows_of(refs):
+    if len(refs) == 1:
+        return refs[0][:OWN, :]
+    return jnp.concatenate([refs[0][...], refs[1][...], refs[2][: OWN - 2 * THIRD, :]], axis=0)
+
+
+def rest_of(refs, start, stop, lanes=slice(None)):
+    skip = 0 if len(refs) == 1 else 2 * THIRD
+    return refs[-1][start - skip : stop - skip, lanes]
+
+
+def take(refs, counts):
+    taken = []
+    for count in counts:
+        taken.append(refs[:count])
+        refs = refs[count:]
+    return taken, refs
+
+
+def unit_kernel(in_ref, out_ref):
+    block = 2 * OWN
+
+    def body(index, _):
+        rows = pl.ds(pl.multiple_of(index * block, block), block)
+        values = in_ref[rows, :].astype(F32)
+        scale = lax.rsqrt(jnp.sum(values * values, axis=1, keepdims=True) + 1e-06)
+        out_ref[rows, :] = (values * scale).astype(B16)
+        return 0
+
+    lax.fori_loop(0, MARKS // block, body, 0)
+
+
+def unit(values):
+    shape = jax.ShapeDtypeStruct(values.shape, B16)
+    return call(unit_kernel, [shape], [VMEM], [values], "unit", flops=2 * 10**9)[0]
+
+
+def build_kernel(counts, groups, block, *refs):
+    spread_ref = refs[0]
+    packed, refs = take(refs[1:], counts)
+    near_ref, far_ref, tile_ref, sums_ref, wide_ref = refs
     gamma = spread_ref[0] * LOG2E
-    for source in range(count):
-        weight = join_tail(packed[source][PACK - 16 :, :])[:, :OWN]
+    for source, parts in enumerate(packed):
+        weight = join_tail(rest_of(parts, PACK - 16, PACK))[:, :OWN]
         column = jnp.transpose(jnp.broadcast_to(weight, (WIDTH, OWN)))
         wide_ref[source * OWN : (source + 1) * OWN, :] = column
 
@@ -122,7 +155,7 @@
             sums = [jnp.zeros((8, WIDTH), F32) for _ in range(block // WIDTH)]
             first = 0
             for size in groups:
-                rows = jnp.concatenate([ref[:OWN, :] for ref in packed[first : first + size]], axis=0)
+                rows = jnp.concatenate([rows_of(parts) for parts in packed[first : first + size]], axis=0)
                 values = jnp.exp2(dot(rows, marks, 1, 1) * gamma)
                 at = slice(first * OWN, (first + size) * OWN)
                 tile_ref[at, lanes] = values.astype(B16)
@@ -142,11 +175,13 @@
 
 def build(groups, block, spread, packed, near, far):
     rows = sum(groups) * OWN
+    counts = [len(parts) for parts in packed]
+    flat = [part for parts in packed for part in parts]
     return call(
-        lambda *refs: build_kernel(groups, block, *refs),
+        lambda *refs: build_kernel(counts, groups, block, *refs),
         [pltpu.VMEM((rows, 2 * MARKS), B16), jax.ShapeDtypeStruct((8, 2 * MARKS), F32)],
-        [SMEM] + [VMEM] * (len(packed) + 2),
-        [spread, *packed, near, far],
+        [SMEM] + [VMEM] * (len(flat) + 2),
+        [spread, *flat, near, far],
         "build",
         scratch=[pltpu.VMEM((rows, WIDTH), F32)],
         flops=4 * rows * 2 * MARKS * 512,
@@ -161,7 +196,7 @@
 
 
 def side_kernel(first, base, *refs):
-    slots_ref, tiles, refs = refs[0], refs[1:4], refs[4:]
+    slots_ref, tiles, refs = refs[0], refs[1 : 1 + TILES], refs[1 + TILES :]
     zero = jnp.zeros((1, PIECE - WIDTH), F32)
     ones = jnp.ones((16, OWN), B16)
     totals = jnp.zeros((1, WIDTH), F32)
@@ -169,14 +204,15 @@
     rounded = jnp.zeros((16, WIDTH), F32)
     half = WIDTH // 2
     if first:
-        packed, sums, (out_ref, wt_ref) = refs[:8], refs[8:11], refs[11:]
+        packed, refs = take(refs, [1] * 7 + [3])
+        sums, (out_ref, wt_ref) = refs[:TILES], refs[TILES:]
     else:
         packed_ref, out_ref, wt_ref = refs
     for slot in range(EIGHT):
         if first:
-            wt_ref[slot, :half] = packed[slot][OWN : OWN + half, :OWN]
-            wt_ref[slot, half:] = packed[slot][OWN : OWN + half, OWN:]
-            tail = join_tail(packed[slot][OWN + half :, :])
+            wt_ref[slot, :half] = rest_of(packed[slot], OWN, OWN + half, slice(0, OWN))
+            wt_ref[slot, half:] = rest_of(packed[slot], OWN, OWN + half, slice(OWN, 2 * OWN))
+            tail = join_tail(rest_of(packed[slot], OWN + half, PACK))
             totals = totals + tail[:, OWN : OWN + WIDTH]
             third = third + jnp.sum(tail[:, :OWN], axis=1, keepdims=True)
         else:
@@ -195,7 +231,9 @@
             term = dot(wt_ref[slot], tile_rows(tiles, slot, lanes), 1, 0)
             product = term if product is None else product + term
         if first:
-            column = (sums[0][:, lanes] + sums[1][:, lanes]) + sums[2][:, lanes]
+            column = sums[0][:, lanes]
+            for more in sums[1:]:
+                column = column + more[:, lanes]
             column = jnp.sum(column, axis=0, keepdims=True)
         else:
             column = jnp.zeros((1, BLOCK), F32)
@@ -212,7 +250,7 @@
     return call(
         lambda *refs: side_kernel(first, base, *refs),
         [jax.ShapeDtypeStruct((EIGHT, WIDTH + 8, PIECE), F32)],
-        [SMEM] + [VMEM] * (3 + len(more)),
+        [SMEM] + [VMEM] * (TILES + len(more)),
         [slots, *tiles, *more],
         "side_terms",
         scratch=[pltpu.VMEM((EIGHT, WIDTH, OWN), B16)],
@@ -221,7 +259,7 @@
 
 
 def pair_kernel(first, *refs):
-    refs = refs[3:]
+    refs = refs[TILES:]
     if first:
         own_ref, other_ref, out_ref, pair_ref = refs
     else:
@@ -248,7 +286,7 @@
     return call(
         lambda *refs: pair_kernel(first, *refs),
         shapes,
-        [VMEM] * (3 + len(args)),
+        [VMEM] * (TILES + len(args)),
         [*tiles, *args],
         "pair",
         flops=10**9,
@@ -256,7 +294,7 @@
 
 
 def centre_kernel(first, total_rows, *refs):
-    refs = refs[3:]
+    refs = refs[TILES:]
     if first:
         terms_ref, out_ref, means_ref = refs
     else:
@@ -287,20 +325,20 @@
         squares = columns[:, EIGHT + 1 : EIGHT + 2]
         side = (side * UP - totals * means) / jnp.sqrt(squares / total_rows + 1e-06)
     side = side.astype(B16)
-    tail = tail_in_kernel(means)
     for group in range(EIGHT):
         out_ref[group, :WIDTH, :] = side
-        out_ref[group, WIDTH:, :] = tail
+        if first:
+            out_ref[group, WIDTH:, :] = tail_in_kernel(means)
 
 
 def centre(first, total_rows, tiles, *args):
-    shapes = [jax.ShapeDtypeStruct((EIGHT, WIDTH + 16, PIECE), B16)]
+    shapes = [jax.ShapeDtypeStruct((EIGHT, WIDTH + 16 * first, PIECE), B16)]
     if first:
         shapes.append(jax.ShapeDtypeStruct((8, PIECE), F32))
     return call(
         lambda *refs: centre_kernel(first, total_rows, *refs),
         shapes,
-        [VMEM] * (3 + len(args)),
+        [VMEM] * (TILES + len(args)),
         [*tiles, *args],
         "centre",
         flops=10**9,
@@ -308,7 +346,7 @@
 
 
 def image_kernel(base, slots_ref, *refs):
-    tiles, half_ref, refs = refs[:3], refs[3], refs[4:]
+    tiles, (half_ref, means_ref), refs = refs[:TILES], refs[TILES : TILES + 2], refs[TILES + 2 :]
     if base:
         before_ref, out_ref, side_ref = refs
     else:
@@ -317,7 +355,7 @@
     for piece in range(EIGHT):
         side = half_ref[piece, :WIDTH, :]
         side_ref[:, piece * PIECE : (piece + 1) * PIECE] = side
-        shift = shift + dot(half_ref[piece, WIDTH:, :], side, 1, 1)
+        shift = shift + dot(means_ref[piece, WIDTH:, :], side, 1, 1)
     shift = (shift[2:3] + shift[1:2]) + shift[0:1]
     slot = 0
     for tile in tiles:
@@ -332,7 +370,7 @@
         slot += count
 
 
-def image_terms(slots, tiles, half, before=None):
+def image_terms(slots, tiles, half, means, before=None):
     if before is None:
         base, more, shape = 0, [], jax.ShapeDtypeStruct((ROWS, WIDTH), F32)
     else:
@@ -340,8 +378,8 @@
     return call(
         lambda *refs: image_kernel(base, *refs),
         [shape],
-        [SMEM] + [VMEM] * (4 + len(more)),
-        [slots, *tiles, half, *more],
+        [SMEM] + [VMEM] * (TILES + 2 + len(more)),
+        [slots, *tiles, half, means, *more],
         "image_terms",
         scratch=[pltpu.VMEM((WIDTH, MARKS), B16)],
         flops=2 * ROWS * MARKS * WIDTH,
@@ -350,7 +388,7 @@
 
 def owner_kernel(last, *refs):
     if not last:
-        refs = refs[3:]
+        refs = refs[TILES:]
     terms_ref, weight_ref, out_ref, *more = refs
     image = terms_ref[0].astype(F32)
     for member in range(1, EIGHT):
@@ -440,21 +478,26 @@
     slots = slot_owners()
     packed, weight = pack(embeddings, start_vectors, row_weight[None, :])
     below, above, across = from_below(packed), from_above(packed), swap_z(packed)
-    far = unit_rows(swap_core(landmarks))
-    near = unit_rows(landmarks)
+    near = unit(landmarks)
+    far = unit(swap_core(landmarks))
+    zero, sums_zero = build((1,), 1024, spread, [[packed]], near, far)
+    below, above, across, sums_zero = lax.optimization_barrier((below, above, across, sums_zero))
     opposite, across_above, across_below = from_below(below), from_above(across), swap_z(below)
-    packs = [packed, below, above, across, opposite, across_above, across_below]
-    one, sums_one = build((2, 2), 1024, spread, packs[:4], near, far)
-    opposite, sums_one = lax.optimization_barrier((opposite, sums_one))
-    last = swap_z(opposite)
-    packs[4] = opposite
-    packs.append(last)
-    two, sums_two = build((3,), 512, spread, packs[4:7], near, far)
-    last, sums_two = lax.optimization_barrier((last, sums_two))
-    packs[7] = last
-    three, sums_three = build((1,), 1024, spread, packs[7:], near, far)
-    tiles = (one, two, three)
-    first = [*packs, sums_one, sums_two, sums_three]
+    one, sums_one = build((3,), 512, spread, [[below], [above], [across]], near, far)
+    opposite, across_above, across_below, sums_one = lax.optimization_barrier(
+        (opposite, across_above, across_below, sums_one)
+    )
+    last = [
+        swap_z(opposite[:THIRD]),
+        from_above(across_above[THIRD : 2 * THIRD]),
+        from_below(across_below[2 * THIRD :]),
+    ]
+    two, sums_two = build((3,), 512, spread, [[opposite], [across_above], [across_below]], near, far)
+    *last, sums_two = lax.optimization_barrier((*last, sums_two))
+    three, sums_three = build((1,), 1024, spread, [last], near, far)
+    packs = [packed, below, above, across, opposite, across_above, across_below, *last]
+    tiles = (zero, one, two, three)
+    first = [*packs, sums_zero, sums_one, sums_two, sums_three]
     for step in range(ITERS):
         more = first if step == 0 else [vectors]
         other = swap_core(side_terms(step == 0, MARKS, slots, tiles, more))
@@ -467,7 +510,10 @@
             (sides,) = centre(False, total_rows, tiles, exchange(payload, MARK_AXES), means)
         sides = exchange(sides, MARK_AXES)
         across_core = swap_core(sides)
-        parts = image_terms(slots, tiles, across_core, image_terms(slots, tiles, sides))
+        if step == 0:
+            tails = (sides, across_core)
+        parts = image_terms(slots, tiles, sides, tails[0])
+        parts = image_terms(slots, tiles, across_core, tails[1], parts)
         parts = exchange(parts, ROW_AXES)
         if step + 1 < ITERS:
             (vectors,) = owner(False, tiles, parts, weight)

time: 186 us -> 183 us (0.984)
  waiting for transfers between devices: 8.25 us -> 1.13 us
  other arithmetic: 7.53 us -> 0.72 us
  Pallas kernels: 35.6 us -> 40.8 us
  starting transfers between devices: 21.4 us -> 25.8 us
    ppermute x2 -> x3, waiting for transfers between devices: 6.81 us -> 0.49 us  [from_below(): return lax.ppermute(values, 'x', [(at, (at + 1) % 4) for at in range(4)])]
    pallas_call x18 -> x21, Pallas kernels: 35.6 us -> 40.8 us  [call(): pl.pallas_call(kernel, out_shape=shapes, in_specs=specs, out_specs=[VMEM]...]
    reduce_sum x2 -> x0, other arithmetic: 4.3 us -> none  [unit_rows(): scale = lax.rsqrt(jnp.sum(values * values, axis=1, keepdims=True) + 1e-06)]
    convert_element_type x2 -> x0, other arithmetic: 2.5 us -> none  [unit_rows(): return (values * scale).astype(B16)]
    ppermute x2 -> x3, starting transfers between devices: 5.15 us -> 6.75 us  [from_above(): return lax.ppermute(values, 'x', [(at, (at + 3) % 4) for at in range(4)])]
  transfers between devices with their start and end apart: 12 -> 14, of which waited for: 4 -> 4; matrix products, arithmetic and copies ran while one was open for 4% -> 0% of each run, Pallas kernels for 12% -> 14%
where the time goes in v5:
time: 183 us
  blocking collectives  109 us (60%)
  Pallas kernels  40.8 us (22%)
  starting transfers between devices  25.8 us (14%)
  local copies, waits for them, and re-layouts  4.28 us (2%)
    all_to_all x8, blocking collectives, exchange(): return lax.all_to_all(payload, axes, 0, 0)  109 us
    pallas_call x21, Pallas kernels, call(): pl.pallas_call(kernel, out_shape=shapes, in_specs=specs, out_specs=[VMEM]...  40.8 us
    ppermute x5, starting transfers between devices, swap_core(): return lax.ppermute(values, 'core', [(0, 1), (1, 0)])  13.7 us
    ppermute x3, starting transfers between devices, from_above(): return lax.ppermute(values, 'x', [(at, (at + 3) % 4) for at in range(4)])  6.75 us
    unnamed x8, local copies, waits for them, and re-layouts  4.13 us
    ppermute x3, starting transfers between devices, swap_z(): return lax.ppermute(values, 'zl', [(0, 1), (1, 0)])  3.92 us
  transfers between devices with their start and end apart: 14, of which 4 were waited for; matrix products, arithmetic and copies ran while one was open for 0% of the time, Pallas kernels for 14%

profile of v5, /device:TPU:1, one launch (start us, length us, event | category | flops | bytes accessed | tf_op | source)
XLA Modules:
  0.0 182.8 jit_solution(10409487976572442098)
XLA Ops:
  0.0 1.4 collective-permute-start
  1.4 0.9 copy-done
  2.4 0.9 copy-done.1
  3.3 0.7 copy-done.2
  4.0 0.2 pack.1
  4.2 1.4 collective-permute-start.1
  5.6 1.4 collective-permute-start.2
  7.0 1.7 collective-permute-start.3
  9.4 1.6 copy-done.3
  11.0 0.7 unit.2.refs_2_.refs_4_
  11.7 2.3 %unit.3.refs_3_.refs_5_ = bf16[2048,512]{1,0:T(8,128)(2,1)S(1)} custom-call(bf16[2048,512]{1,0:T(8,128)(2,1)} %collective-permute-done.in_ref), custom_call_target="tpu_custom_call" | custom-call | flops 2000000000 | tf_op jit(solution)/shard_map/unit/pallas_call | solution.py:91
  14.1 2.1 %build.4 = (bf16[256,4096]{1,0:T(8,128)(2,1)S(1)}, f32[8,4096]{1,0:T(8,128)S(1)}) custom-call(f32[1]{0:T(128)S(6)} %copy.7.refs_0_, bf16[336,512]{1,0:T(8,128)(2,1)S(1)} %get-tuple-element.33.refs_1_.refs_5_, bf16[2048,512]{1,0:T(8,128)(2,1)S(1)} %unit.2.refs_2_.refs_4_, bf16[2048,512]{1,0:T(8,128)(2,1)S(1)} %unit.3.refs_3_.refs_5_), custom_call_target="tpu_custom_call" | custom-call | flops 2147483648 | tf_op jit(solution)/shard_map/build/pallas_call | solution.py:91
  16.2 0.4 collective-permute-done.3.refs_3_.refs_8_
  16.6 1.2 collective-permute-start.6
  17.8 2.6 %collective-permute-start.5 = (bf16[336,512]{1,0:T(8,128)(2,1)S(1)}, bf16[336,512]{1,0:T(8,128)(2,1)S(1)}, u32[]{:S(2)}, u32[]{:S(2)}) collective-permute-start(bf16[336,512]{1,0:T(8,128)(2,1)S(1)} %collective-permute-done.3.refs_3_.refs_8_), channel_id=1, source_target_pairs={{0,12},{4,0},{8,4},{12,8},{1,13},{5,1},{9,5},{13,9},{2,14},{6,2},{... | collective-permute-start | bytes 1032200 | tf_op jit(solution)/shard_map/ppermute | solution.py:445
  20.4 5.3 %build.5 = (bf16[768,4096]{1,0:T(8,128)(2,1)S(1)}, f32[8,4096]{1,0:T(8,128)S(1)}) custom-call(f32[1]{0:T(128)S(6)} %copy.7.refs_0_, bf16[336,512]{1,0:T(8,128)(2,1)S(1)} %collective-permute-done.1.refs_1_.refs_6_, bf16[336,512]{1,0:T(8,128)(2,1)S(1)} %collective-permute-done.2.refs_2_.refs_7_, bf16[336,512]{1,0:T(8,128)(2,1)S(1)} %collective-permute-done.3.refs_3_.refs_8_, ...), custom_call_target="tpu_custom_call" | custom-call | flops 6442450944 | tf_op jit(solution)/shard_map/build/pallas_call | solution.py:91
  25.7 0.5 collective-permute-done.4.refs_1_.refs_9_
  26.2 1.0 collective-permute-start.7
  27.2 2.8 %collective-permute-start.8 = (bf16[112,512]{1,0:T(8,128)(2,1)S(1)}, bf16[112,512]{1,0:T(8,128)(2,1)S(1)}, u32[]{:S(2)}, u32[]{:S(2)}) collective-permute-start(bf16[112,512]{1,0:T(8,128)(2,1)S(1)} %slice.13), channel_id=1, source_target_pairs={{0,12},{4,0},{8,4},{12,8},{1,13},{5,1},{9,5},{13,9},{2,14},{6,2},{... | collective-permute-start | bytes 344072 | tf_op jit(solution)/shard_map/ppermute | solution.py:445
  30.0 5.3 %build.6 = (bf16[768,4096]{1,0:T(8,128)(2,1)S(1)}, f32[8,4096]{1,0:T(8,128)S(1)}) custom-call(f32[1]{0:T(128)S(6)} %copy.7.refs_0_, bf16[336,512]{1,0:T(8,128)(2,1)S(1)} %collective-permute-done.4.refs_1_.refs_9_, bf16[336,512]{1,0:T(8,128)(2,1)S(1)} %collective-permute-done.5.refs_2_.refs_10_, bf16[336,512]{1,0:T(8,128)(2,1)S(1)} %collective-permute-done.6.refs_3_.refs_11_, ...), custom_call_target="tpu_custom_call" | custom-call | flops 6442450944 | tf_op jit(solution)/shard_map/build/pallas_call | solution.py:91
  35.4 2.1 %build.7 = (bf16[256,4096]{1,0:T(8,128)(2,1)S(1)}, f32[8,4096]{1,0:T(8,128)S(1)}) custom-call(f32[1]{0:T(128)S(6)} %copy.7.refs_0_, bf16[112,512]{1,0:T(8,128)(2,1)S(1)} %collective-permute-done.7.refs_1_.refs_12_, bf16[112,512]{1,0:T(8,128)(2,1)S(1)} %collective-permute-done.8.refs_2_.refs_13_, ...), custom_call_target="tpu_custom_call" | custom-call | flops 2147483648 | tf_op jit(solution)/shard_map/build/pallas_call | solution.py:91
  37.4 2.3 %side_terms.5 = f32[8,136,256]{2,1,0:T(8,128)S(1)} custom-call(s32[8]{0:T(128)S(1)} %stack.35.refs_0_, bf16[256,4096]{1,0:T(8,128)(2,1)S(1)} %get-tuple-element.34.refs_1_.refs_0_, bf16[768,4096]{1,0:T(8,128)(2,1)S(1)} %get-tuple-element.39.refs_2_.refs_1_, bf16[768,4096]{1,0:T(8,128)(2,1)S(1)} %get-tuple-element.44.refs_3_.refs_2_, ...), custom_call_target="tpu_custom_call" | custom-call | flops 1073741824 | tf_op jit(solution)/shard_map/side_terms/pallas_call | solution.py:91
  39.7 3.9 %collective-permute-start.10 = (f32[8,136,256]{2,1,0:T(8,128)S(1)}, f32[8,136,256]{2,1,0:T(8,128)S(1)}, u32[]{:S(2)}, u32[]{:S(2)}) collective-permute-start(f32[8,136,256]{2,1,0:T(8,128)S(1)} %side_terms.5), channel_id=1, source_target_pairs={{0,1},{1,0},{2,3},{3,2},{4,5},{5,4},{6,7},{7,6},{8,9},{9,8},{10,11... | collective-permute-start | bytes 3342344 | tf_op jit(solution)/shard_map/ppermute | solution.py:433
  43.6 2.3 %side_terms.4.refs_4_ = f32[8,136,256]{2,1,0:T(8,128)S(1)} custom-call(s32[8]{0:T(128)S(1)} %stack.35.refs_0_, bf16[256,4096]{1,0:T(8,128)(2,1)S(1)} %get-tuple-element.34.refs_1_.refs_0_, bf16[768,4096]{1,0:T(8,128)(2,1)S(1)} %get-tuple-element.39.refs_2_.refs_1_, bf16[768,4096]{1,0:T(8,128)(2,1)S(1)} %get-tuple-element.44.refs_3_.refs_2_, ...), custom_call_target="tpu_custom_call" | custom-call | flops 1073741824 | tf_op jit(solution)/shard_map/side_terms/pallas_call | solution.py:91
  45.9 0.1 collective-permute-done.10.refs_5_
  46.0 0.3 pair.2
  46.3 18.3 %all_to_all.40.refs_4_ = bf16[8,144,256]{2,1,0:T(8,128)(2,1)S(1)} all-to-all(bf16[8,144,256]{2,1,0:T(8,128)(2,1)S(1)} %get-tuple-element.54), channel_id=1, replica_groups=mesh['y'=4,'zh'=2,'x'=4,'zl'=2,'core'=2] {'y','zh'}, dimensions={0} | all-to-all | bytes 1179648 | tf_op jit(solution)/shard_map/all_to_all | solution.py:429
  64.6 0.4 centre.2
  65.0 13.1 %all_to_all.41.refs_5_.refs_6_ = bf16[8,144,256]{2,1,0:T(8,128)(2,1)S(1)} all-to-all(bf16[8,144,256]{2,1,0:T(8,128)(2,1)S(1)} %get-tuple-element.55), channel_id=1, replica_groups=mesh['y'=4,'zh'=2,'x'=4,'zl'=2,'core'=2] {'y','zh'}, dimensions={0} | all-to-all | bytes 1179648 | tf_op jit(solution)/shard_map/all_to_all | solution.py:429
  78.1 2.9 %collective-permute-start.11 = (bf16[8,144,256]{2,1,0:T(8,128)(2,1)S(1)}, bf16[8,144,256]{2,1,0:T(8,128)(2,1)S(1)}, u32[]{:S(2)}, u32[]{:S(2)}) collective-permute-start(bf16[8,144,256]{2,1,0:T(8,128)(2,1)S(1)} %all_to_all.41.refs_5_.refs_6_), channel_id=1, source_target_pairs={{0,1},{1,0},{2,3},{3,2},{4,5},{5,4},{6,7},{7,6},{8,9},{9,8},{10,11... | collective-permute-start | bytes 1769480 | tf_op jit(solution)/shard_map/ppermute | solution.py:433
  81.0 3.0 %image_terms.4.refs_7_ = f32[2048,128]{1,0:T(8,128)S(1)} custom-call(s32[8]{0:T(128)S(1)} %stack.35.refs_0_, bf16[256,4096]{1,0:T(8,128)(2,1)S(1)} %get-tuple-element.34.refs_1_.refs_0_, bf16[768,4096]{1,0:T(8,128)(2,1)S(1)} %get-tuple-element.39.refs_2_.refs_1_, bf16[768,4096]{1,0:T(8,128)(2,1)S(1)} %get-tuple-element.44.refs_3_.refs_2_, ...), custom_call_target="tpu_custom_call" | custom-call | flops 1073741824 | tf_op jit(solution)/shard_map/image_terms/pallas_call | solution.py:91
  84.0 3.0 %image_terms.5 = bf16[8,256,128]{2,1,0:T(8,128)(2,1)S(1)} custom-call(s32[8]{0:T(128)S(1)} %stack.35.refs_0_, bf16[256,4096]{1,0:T(8,128)(2,1)S(1)} %get-tuple-element.34.refs_1_.refs_0_, bf16[768,4096]{1,0:T(8,128)(2,1)S(1)} %get-tuple-element.39.refs_2_.refs_1_, bf16[768,4096]{1,0:T(8,128)(2,1)S(1)} %get-tuple-element.44.refs_3_.refs_2_, ...), custom_call_target="tpu_custom_call" | custom-call | flops 1073741824 | tf_op jit(solution)/shard_map/image_terms/pallas_call | solution.py:91
  87.0 13.3 %all_to_all.42.refs_4_ = bf16[8,256,128]{2,1,0:T(8,128)(2,1)S(1)} all-to-all(bf16[8,256,128]{2,1,0:T(8,128)(2,1)S(1)} %image_terms.5), channel_id=1, replica_groups=mesh['y'=4,'zh'=2,'x'=4,'zl'=2,'core'=2] {'x','zl'}, dimensions={0} | all-to-all | bytes 1048576 | tf_op jit(solution)/shard_map/all_to_all | solution.py:429
  100.4 0.2 owner.2
  100.5 11.6 %all_to_all.43.refs_5_ = bf16[8,144,256]{2,1,0:T(8,128)(2,1)S(1)} all-to-all(bf16[8,144,256]{2,1,0:T(8,128)(2,1)S(1)} %owner.2), channel_id=1, replica_groups=mesh['y'=4,'zh'=2,'x'=4,'zl'=2,'core'=2] {'x','zl'}, dimensions={0} | all-to-all | bytes 1179648 | tf_op jit(solution)/shard_map/all_to_all | solution.py:429
  112.2 2.3 %side_terms.7 = f32[8,136,256]{2,1,0:T(8,128)S(1)} custom-call(s32[8]{0:T(128)S(1)} %stack.35.refs_0_, bf16[256,4096]{1,0:T(8,128)(2,1)S(1)} %get-tuple-element.34.refs_1_.refs_0_, bf16[768,4096]{1,0:T(8,128)(2,1)S(1)} %get-tuple-element.39.refs_2_.refs_1_, bf16[768,4096]{1,0:T(8,128)(2,1)S(1)} %get-tuple-element.44.refs_3_.refs_2_, ...), custom_call_target="tpu_custom_call" | custom-call | flops 1073741824 | tf_op jit(solution)/shard_map/side_terms/pallas_call | solution.py:91
  114.4 2.9 %collective-permute-start.12 = (f32[8,136,256]{2,1,0:T(8,128)S(1)}, f32[8,136,256]{2,1,0:T(8,128)S(1)}, u32[]{:S(2)}, u32[]{:S(2)}) collective-permute-start(f32[8,136,256]{2,1,0:T(8,128)S(1)} %side_terms.7), channel_id=1, source_target_pairs={{0,1},{1,0},{2,3},{3,2},{4,5},{5,4},{6,7},{7,6},{8,9},{9,8},{10,11... | collective-permute-start | bytes 3342344 | tf_op jit(solution)/shard_map/ppermute | solution.py:433
  117.3 2.3 %side_terms.6.refs_4_ = f32[8,136,256]{2,1,0:T(8,128)S(1)} custom-call(s32[8]{0:T(128)S(1)} %stack.35.refs_0_, bf16[256,4096]{1,0:T(8,128)(2,1)S(1)} %get-tuple-element.34.refs_1_.refs_0_, bf16[768,4096]{1,0:T(8,128)(2,1)S(1)} %get-tuple-element.39.refs_2_.refs_1_, bf16[768,4096]{1,0:T(8,128)(2,1)S(1)} %get-tuple-element.44.refs_3_.refs_2_, ...), custom_call_target="tpu_custom_call" | custom-call | flops 1073741824 | tf_op jit(solution)/shard_map/side_terms/pallas_call | solution.py:91
  119.7 0.3 pair.3
  120.0 14.3 %all_to_all.44.refs_4_ = bf16[8,144,256]{2,1,0:T(8,128)(2,1)S(1)} all-to-all(bf16[8,144,256]{2,1,0:T(8,128)(2,1)S(1)} %pair.3), channel_id=1, replica_groups=mesh['y'=4,'zh'=2,'x'=4,'zl'=2,'core'=2] {'y','zh'}, dimensions={0} | all-to-all | bytes 1179648 | tf_op jit(solution)/shard_map/all_to_all | solution.py:429
  134.3 0.4 centre.3
  134.7 12.3 %all_to_all.45.refs_5_ = bf16[8,128,256]{2,1,0:T(8,128)(2,1)S(1)} all-to-all(bf16[8,128,256]{2,1,0:T(8,128)(2,1)S(1)} %centre.3), channel_id=1, replica_groups=mesh['y'=4,'zh'=2,'x'=4,'zl'=2,'core'=2] {'y','zh'}, dimensions={0} | all-to-all | bytes 1048576 | tf_op jit(solution)/shard_map/all_to_all | solution.py:429
  147.0 2.6 %collective-permute-start.13 = (bf16[8,128,256]{2,1,0:T(8,128)(2,1)S(1)}, bf16[8,128,256]{2,1,0:T(8,128)(2,1)S(1)}, u32[]{:S(2)}, u32[]{:S(2)}) collective-permute-start(bf16[8,128,256]{2,1,0:T(8,128)(2,1)S(1)} %all_to_all.45.refs_5_), channel_id=1, source_target_pairs={{0,1},{1,0},{2,3},{3,2},{4,5},{5,4},{6,7},{7,6},{8,9},{9,8},{10,11... | collective-permute-start | bytes 1572872 | tf_op jit(solution)/shard_map/ppermute | solution.py:433
  149.6 3.0 %image_terms.6.refs_7_ = f32[2048,128]{1,0:T(8,128)S(1)} custom-call(s32[8]{0:T(128)S(1)} %stack.35.refs_0_, bf16[256,4096]{1,0:T(8,128)(2,1)S(1)} %get-tuple-element.34.refs_1_.refs_0_, bf16[768,4096]{1,0:T(8,128)(2,1)S(1)} %get-tuple-element.39.refs_2_.refs_1_, bf16[768,4096]{1,0:T(8,128)(2,1)S(1)} %get-tuple-element.44.refs_3_.refs_2_, ...), custom_call_target="tpu_custom_call" | custom-call | flops 1073741824 | tf_op jit(solution)/shard_map/image_terms/pallas_call | solution.py:91
  152.6 3.0 %image_terms.7 = bf16[8,256,128]{2,1,0:T(8,128)(2,1)S(1)} custom-call(s32[8]{0:T(128)S(1)} %stack.35.refs_0_, bf16[256,4096]{1,0:T(8,128)(2,1)S(1)} %get-tuple-element.34.refs_1_.refs_0_, bf16[768,4096]{1,0:T(8,128)(2,1)S(1)} %get-tuple-element.39.refs_2_.refs_1_, bf16[768,4096]{1,0:T(8,128)(2,1)S(1)} %get-tuple-element.44.refs_3_.refs_2_, ...), custom_call_target="tpu_custom_call" | custom-call | flops 1073741824 | tf_op jit(solution)/shard_map/image_terms/pallas_call | solution.py:91
  155.7 12.0 %all_to_all.46.refs_0_ = bf16[8,256,128]{2,1,0:T(8,128)(2,1)S(1)} all-to-all(bf16[8,256,128]{2,1,0:T(8,128)(2,1)S(1)} %image_terms.7), channel_id=1, replica_groups=mesh['y'=4,'zh'=2,'x'=4,'zl'=2,'core'=2] {'x','zl'}, dimensions={0} | all-to-all | bytes 1048576 | tf_op jit(solution)/shard_map/all_to_all | solution.py:429
  167.8 14.3 %all_to_all.47 = f32[128,1,128]{2,1,0:T(1,128)S(1)} all-to-all(f32[128,1,128]{2,1,0:T(1,128)S(1)} %broadcast_in_dim.14), channel_id=1, replica_groups=mesh['y'=4,'zh'=2,'x'=4,'zl'=2,'core'=2] {'y','zh','x','zl','core'}, dimensions={0} | all-to-all | bytes 131072 | tf_op jit(solution)/shard_map/all_to_all | solution.py:429
  182.2 0.7 broadcast_divide_fusion
  (26 shorter events, 0.5 us)
Async XLA Ops:
  0.0 11.7 %collective-permute-start = (bf16[2048,512]{1,0:T(8,128)(2,1)}, bf16[2048,512]{1,0:T(8,128)(2,1)}, u32[]{:S(2)}, u32[]{:S(2)}) collective-permute-start(bf16[2048,512]{1,0:T(8,128)(2,1)} %in_ref.1), channel_id=1, source_target_pairs={{0,1},{1,0},{2,3},{3,2},{4,5},{5,4},{6,7},{7,6},{8,9},{9,8},{10,11... | collective-permute-start | bytes 6291464 | tf_op jit(solution)/shard_map/ppermute | solution.py:433
  1.4 0.9 copy-start
  2.4 0.9 copy-start.1
  3.3 0.7 copy-start.2
  4.2 11.9 %collective-permute-start.1 = (bf16[336,512]{1,0:T(8,128)(2,1)S(1)}, bf16[336,512]{1,0:T(8,128)(2,1)S(1)}, u32[]{:S(2)}, u32[]{:S(2)}) collective-permute-start(bf16[336,512]{1,0:T(8,128)(2,1)S(1)} %get-tuple-element.33.refs_1_.refs_5_), channel_id=1, source_target_pairs={{0,4},{4,8},{8,12},{12,0},{1,5},{5,9},{9,13},{13,1},{2,6},{6,10},{... | collective-permute-start | bytes 1032200 | tf_op jit(solution)/shard_map/ppermute | solution.py:441
  5.6 10.6 %collective-permute-start.2 = (bf16[336,512]{1,0:T(8,128)(2,1)S(1)}, bf16[336,512]{1,0:T(8,128)(2,1)S(1)}, u32[]{:S(2)}, u32[]{:S(2)}) collective-permute-start(bf16[336,512]{1,0:T(8,128)(2,1)S(1)} %get-tuple-element.33.refs_1_.refs_5_), channel_id=1, source_target_pairs={{0,12},{4,0},{8,4},{12,8},{1,13},{5,1},{9,5},{13,9},{2,14},{6,2},{... | collective-permute-start | bytes 1032200 | tf_op jit(solution)/shard_map/ppermute | solution.py:445
  7.0 9.6 %collective-permute-start.3 = (bf16[336,512]{1,0:T(8,128)(2,1)S(1)}, bf16[336,512]{1,0:T(8,128)(2,1)S(1)}, u32[]{:S(2)}, u32[]{:S(2)}) collective-permute-start(bf16[336,512]{1,0:T(8,128)(2,1)S(1)} %get-tuple-element.33.refs_1_.refs_5_), channel_id=1, source_target_pairs={{0,2},{2,0},{1,3},{3,1},{4,6},{6,4},{5,7},{7,5},{8,10},{10,8},{9,1... | collective-permute-start | bytes 1032200 | tf_op jit(solution)/shard_map/ppermute | solution.py:437
  9.4 1.6 copy-start.3
  16.6 9.6 %collective-permute-start.4 = (bf16[336,512]{1,0:T(8,128)(2,1)S(1)}, bf16[336,512]{1,0:T(8,128)(2,1)S(1)}, u32[]{:S(2)}, u32[]{:S(2)}) collective-permute-start(bf16[336,512]{1,0:T(8,128)(2,1)S(1)} %collective-permute-done.1.refs_1_.refs_6_), channel_id=1, source_target_pairs={{0,4},{4,8},{8,12},{12,0},{1,5},{5,9},{9,13},{13,1},{2,6},{6,10},{... | collective-permute-start | bytes 1032200 | tf_op jit(solution)/shard_map/ppermute | solution.py:441
  16.6 9.6 %collective-permute-start.6 = (bf16[336,512]{1,0:T(8,128)(2,1)S(1)}, bf16[336,512]{1,0:T(8,128)(2,1)S(1)}, u32[]{:S(2)}, u32[]{:S(2)}) collective-permute-start(bf16[336,512]{1,0:T(8,128)(2,1)S(1)} %collective-permute-done.1.refs_1_.refs_6_), channel_id=1, source_target_pairs={{0,2},{2,0},{1,3},{3,1},{4,6},{6,4},{5,7},{7,5},{8,10},{10,8},{9,1... | collective-permute-start | bytes 1032200 | tf_op jit(solution)/shard_map/ppermute | solution.py:437
  17.8 8.4 %collective-permute-start.5 = (bf16[336,512]{1,0:T(8,128)(2,1)S(1)}, bf16[336,512]{1,0:T(8,128)(2,1)S(1)}, u32[]{:S(2)}, u32[]{:S(2)}) collective-permute-start(bf16[336,512]{1,0:T(8,128)(2,1)S(1)} %collective-permute-done.3.refs_3_.refs_8_), channel_id=1, source_target_pairs={{0,12},{4,0},{8,4},{12,8},{1,13},{5,1},{9,5},{13,9},{2,14},{6,2},{... | collective-permute-start | bytes 1032200 | tf_op jit(solution)/shard_map/ppermute | solution.py:445
  26.2 9.1 %collective-permute-start.7 = (bf16[112,512]{1,0:T(8,128)(2,1)S(1)}, bf16[112,512]{1,0:T(8,128)(2,1)S(1)}, u32[]{:S(2)}, u32[]{:S(2)}) collective-permute-start(bf16[112,512]{1,0:T(8,128)(2,1)S(1)} %slice.12), channel_id=1, source_target_pairs={{0,2},{2,0},{1,3},{3,1},{4,6},{6,4},{5,7},{7,5},{8,10},{10,8},{9,1... | collective-permute-start | bytes 344072 | tf_op jit(solution)/shard_map/ppermute | solution.py:437
  27.2 8.2 %collective-permute-start.8 = (bf16[112,512]{1,0:T(8,128)(2,1)S(1)}, bf16[112,512]{1,0:T(8,128)(2,1)S(1)}, u32[]{:S(2)}, u32[]{:S(2)}) collective-permute-start(bf16[112,512]{1,0:T(8,128)(2,1)S(1)} %slice.13), channel_id=1, source_target_pairs={{0,12},{4,0},{8,4},{12,8},{1,13},{5,1},{9,5},{13,9},{2,14},{6,2},{... | collective-permute-start | bytes 344072 | tf_op jit(solution)/shard_map/ppermute | solution.py:445
  30.0 5.4 %collective-permute-start.9 = (bf16[112,512]{1,0:T(8,128)(2,1)S(1)}, bf16[112,512]{1,0:T(8,128)(2,1)S(1)}, u32[]{:S(2)}, u32[]{:S(2)}) collective-permute-start(bf16[112,512]{1,0:T(8,128)(2,1)S(1)} %slice.14), channel_id=1, source_target_pairs={{0,4},{4,8},{8,12},{12,0},{1,5},{5,9},{9,13},{13,1},{2,6},{6,10},{... | collective-permute-start | bytes 344072 | tf_op jit(solution)/shard_map/ppermute | solution.py:441
  39.7 6.3 %collective-permute-start.10 = (f32[8,136,256]{2,1,0:T(8,128)S(1)}, f32[8,136,256]{2,1,0:T(8,128)S(1)}, u32[]{:S(2)}, u32[]{:S(2)}) collective-permute-start(f32[8,136,256]{2,1,0:T(8,128)S(1)} %side_terms.5), channel_id=1, source_target_pairs={{0,1},{1,0},{2,3},{3,2},{4,5},{5,4},{6,7},{7,6},{8,9},{9,8},{10,11... | collective-permute-start | bytes 3342344 | tf_op jit(solution)/shard_map/ppermute | solution.py:433
  78.1 5.9 %collective-permute-start.11 = (bf16[8,144,256]{2,1,0:T(8,128)(2,1)S(1)}, bf16[8,144,256]{2,1,0:T(8,128)(2,1)S(1)}, u32[]{:S(2)}, u32[]{:S(2)}) collective-permute-start(bf16[8,144,256]{2,1,0:T(8,128)(2,1)S(1)} %all_to_all.41.refs_5_.refs_6_), channel_id=1, source_target_pairs={{0,1},{1,0},{2,3},{3,2},{4,5},{5,4},{6,7},{7,6},{8,9},{9,8},{10,11... | collective-permute-start | bytes 1769480 | tf_op jit(solution)/shard_map/ppermute | solution.py:433
  114.4 5.2 %collective-permute-start.12 = (f32[8,136,256]{2,1,0:T(8,128)S(1)}, f32[8,136,256]{2,1,0:T(8,128)S(1)}, u32[]{:S(2)}, u32[]{:S(2)}) collective-permute-start(f32[8,136,256]{2,1,0:T(8,128)S(1)} %side_terms.7), channel_id=1, source_target_pairs={{0,1},{1,0},{2,3},{3,2},{4,5},{5,4},{6,7},{7,6},{8,9},{9,8},{10,11... | collective-permute-start | bytes 3342344 | tf_op jit(solution)/shard_map/ppermute | solution.py:433
  147.0 5.6 %collective-permute-start.13 = (bf16[8,128,256]{2,1,0:T(8,128)(2,1)S(1)}, bf16[8,128,256]{2,1,0:T(8,128)(2,1)S(1)}, u32[]{:S(2)}, u32[]{:S(2)}) collective-permute-start(bf16[8,128,256]{2,1,0:T(8,128)(2,1)S(1)} %all_to_all.45.refs_5_), channel_id=1, source_target_pairs={{0,1},{1,0},{2,3},{3,2},{4,5},{5,4},{6,7},{7,6},{8,9},{9,8},{10,11... | collective-permute-start | bytes 1572872 | tf_op jit(solution)/shard_map/ppermute | solution.py:433

commit v6 on v5

--- a/solution.py
+++ b/solution.py
@@ -23,7 +23,7 @@
 EIGHT = 8
 ROWS = EIGHT * OWN
 PACK = OWN + WIDTH // 2 + 16
-BLOCK = 4 * PIECE
+BLOCK = 8 * PIECE
 THIRD = PACK // 3
 TILES = 4
 
@@ -188,48 +188,41 @@
     )
 
 
-def tile_rows(tiles, slot, lanes):
-    for tile in tiles:
-        if slot * OWN < tile.shape[0]:
-            return tile[slot * OWN : (slot + 1) * OWN, lanes]
-        slot -= tile.shape[0] // OWN
-
-
 def side_kernel(first, base, *refs):
     slots_ref, tiles, refs = refs[0], refs[1 : 1 + TILES], refs[1 + TILES :]
-    zero = jnp.zeros((1, PIECE - WIDTH), F32)
-    ones = jnp.ones((16, OWN), B16)
-    totals = jnp.zeros((1, WIDTH), F32)
-    third = jnp.zeros((1, WIDTH), F32)
-    rounded = jnp.zeros((16, WIDTH), F32)
     half = WIDTH // 2
     if first:
         packed, refs = take(refs, [1] * 7 + [3])
         sums, (out_ref, wt_ref) = refs[:TILES], refs[TILES:]
+        tails = [rest_of(parts, OWN + half, PACK) for parts in packed]
+        for slot, parts in enumerate(packed):
+            lanes = slice(slot * OWN, (slot + 1) * OWN)
+            wt_ref[:half, lanes] = rest_of(parts, OWN, OWN + half, slice(0, OWN))
+            wt_ref[half:, lanes] = rest_of(parts, OWN, OWN + half, slice(OWN, 2 * OWN))
     else:
         packed_ref, out_ref, wt_ref = refs
-    for slot in range(EIGHT):
-        if first:
-            wt_ref[slot, :half] = rest_of(packed[slot], OWN, OWN + half, slice(0, OWN))
-            wt_ref[slot, half:] = rest_of(packed[slot], OWN, OWN + half, slice(OWN, 2 * OWN))
-            tail = join_tail(rest_of(packed[slot], OWN + half, PACK))
-            totals = totals + tail[:, OWN : OWN + WIDTH]
-            third = third + jnp.sum(tail[:, :OWN], axis=1, keepdims=True)
-        else:
-            wt_ref[slot] = packed_ref[slots_ref[slot], :WIDTH, :]
-            tail = join_tail(packed_ref[slot, WIDTH:, :])
-            totals = totals + tail[:, :WIDTH]
-            third = third + tail[:, WIDTH:]
-        rounded = rounded + dot(ones, wt_ref[slot], 1, 1)
-    second = jnp.concatenate([totals, rounded[:1]], axis=1)
-    third = jnp.concatenate([third, zero], axis=1)
+        for slot in range(EIGHT):
+            wt_ref[:, slot * OWN : (slot + 1) * OWN] = packed_ref[slots_ref[slot], :WIDTH, :]
+        tails = [packed_ref[source, WIDTH:, :] for source in range(EIGHT)]
+    tail = tails[0].astype(F32)
+    for more in tails[1:]:
+        tail = tail + more.astype(F32)
+    if first:
+        tail = join_at(tail, 0)
+        second = tail[:, OWN:]
+        third = jnp.broadcast_to(jnp.sum(tail[:, :OWN], axis=1, keepdims=True), (1, PIECE))
+    else:
+        one, two = join_at(tail, 0), join_at(tail, 1)
+        second = jnp.concatenate([one[:, :WIDTH], two[:, :WIDTH]], axis=1)
+        third = jnp.concatenate([one[:, WIDTH:], two[:, WIDTH:]], axis=1)
 
     def body(index, _):
         lanes = pl.ds(pl.multiple_of(base + index * BLOCK, BLOCK), BLOCK)
-        product = None
-        for slot in range(EIGHT):
-            term = dot(wt_ref[slot], tile_rows(tiles, slot, lanes), 1, 0)
-            product = term if product is None else product + term
+        product, start = None, 0
+        for tile in tiles:
+            stop = start + tile.shape[0]
+            term = dot(wt_ref[:, start:stop], tile[:, lanes], 1, 0)
+            product, start = (term if product is None else product + term), stop
         if first:
             column = sums[0][:, lanes]
             for more in sums[1:]:
@@ -253,7 +246,7 @@
         [SMEM] + [VMEM] * (TILES + len(more)),
         [slots, *tiles, *more],
         "side_terms",
-        scratch=[pltpu.VMEM((EIGHT, WIDTH, OWN), B16)],
+        scratch=[pltpu.VMEM((WIDTH, ROWS), B16)],
         flops=2 * ROWS * MARKS * WIDTH,
     )[0]
 
@@ -348,14 +341,14 @@
 def image_kernel(base, slots_ref, *refs):
     tiles, (half_ref, means_ref), refs = refs[:TILES], refs[TILES : TILES + 2], refs[TILES + 2 :]
     if base:
-        before_ref, out_ref, side_ref = refs
-    else:
-        out_ref, side_ref = refs
-    shift = jnp.zeros((16, WIDTH), F32)
+        before_ref, out_ref, side_ref, tail_ref = refs
+    else:
+        out_ref, side_ref, tail_ref = refs
     for piece in range(EIGHT):
-        side = half_ref[piece, :WIDTH, :]
-        side_ref[:, piece * PIECE : (piece + 1) * PIECE] = side
-        shift = shift + dot(means_ref[piece, WIDTH:, :], side, 1, 1)
+        lanes = slice(piece * PIECE, (piece + 1) * PIECE)
+        side_ref[:, lanes] = half_ref[piece, :WIDTH, :]
+        tail_ref[:, lanes] = means_ref[piece, WIDTH:, :]
+    shift = dot(tail_ref[...], side_ref[...], 1, 1)
     shift = (shift[2:3] + shift[1:2]) + shift[0:1]
     slot = 0
     for tile in tiles:
@@ -381,7 +374,7 @@
         [SMEM] + [VMEM] * (TILES + 2 + len(more)),
         [slots, *tiles, half, means, *more],
         "image_terms",
-        scratch=[pltpu.VMEM((WIDTH, MARKS), B16)],
+        scratch=[pltpu.VMEM((WIDTH, MARKS), B16), pltpu.VMEM((16, MARKS), B16)],
         flops=2 * ROWS * MARKS * WIDTH,
     )[0]
 
@@ -402,8 +395,12 @@
     else:
         product = weight * image
         totals = jnp.sum(product, axis=0, keepdims=True)
-        body = jnp.transpose(product * DOWN).astype(B16)
-        tail = tail_in_kernel(jnp.concatenate([totals, squares], axis=1))
+        body = (product * DOWN).astype(B16).astype(F32)
+        rounded = jnp.sum(body, axis=0, keepdims=True)
+        body = jnp.transpose(body).astype(B16)
+        first = jnp.concatenate([totals, squares], axis=1)
+        second = jnp.concatenate([rounded, jnp.zeros((1, OWN - WIDTH), F32)], axis=1)
+        tail = tails_in_kernel([first, second])
         for member in range(EIGHT):
             out_ref[member, :WIDTH, :] = body
             out_ref[member, WIDTH:, :] = tail
@@ -458,8 +455,8 @@
     half = WIDTH // 2
     out_ref[OWN : OWN + half, :OWN] = vectors[:half]
     out_ref[OWN : OWN + half, OWN:] = vectors[half:]
-    rest = jnp.zeros((1, OWN - WIDTH), F32)
-    out_ref[OWN + half :, :] = tail_in_kernel(jnp.concatenate([weight, totals, rest], axis=1))
+    rounded = jnp.sum(product.astype(B16).astype(F32), axis=0, keepdims=True)
+    out_ref[OWN + half :, :] = tail_in_kernel(jnp.concatenate([weight, totals, rounded], axis=1))
 
 
 def pack(rows, start, weight):
@@ -480,10 +477,10 @@
     below, above, across = from_below(packed), from_above(packed), swap_z(packed)
     near = unit(landmarks)
     far = unit(swap_core(landmarks))
-    zero, sums_zero = build((1,), 1024, spread, [[packed]], near, far)
+    zero, sums_zero = build((1,), 2048, spread, [[packed]], near, far)
     below, above, across, sums_zero = lax.optimization_barrier((below, above, across, sums_zero))
     opposite, across_above, across_below = from_below(below), from_above(across), swap_z(below)
-    one, sums_one = build((3,), 512, spread, [[below], [above], [across]], near, far)
+    one, sums_one = build((3,), 2048, spread, [[below], [above], [across]], near, far)
     opposite, across_above, across_below, sums_one = lax.optimization_barrier(
         (opposite, across_above, across_below, sums_one)
     )
@@ -492,9 +489,9 @@
         from_above(across_above[THIRD : 2 * THIRD]),
         from_below(across_below[2 * THIRD :]),
     ]
-    two, sums_two = build((3,), 512, spread, [[opposite], [across_above], [across_below]], near, far)
+    two, sums_two = build((3,), 2048, spread, [[opposite], [across_above], [across_below]], near, far)
     *last, sums_two = lax.optimization_barrier((*last, sums_two))
-    three, sums_three = build((1,), 1024, spread, [last], near, far)
+    three, sums_three = build((1,), 2048, spread, [last], near, far)
     packs = [packed, below, above, across, opposite, across_above, across_below, *last]
     tiles = (zero, one, two, three)
     first = [*packs, sums_zero, sums_one, sums_two, sums_three]

time: 183 us -> 181 us (0.989)
  Pallas kernels: 40.8 us -> 34.1 us
  waiting for transfers between devices: 1.13 us -> 5.77 us
    pallas_call x21, Pallas kernels: 40.8 us -> 34.1 us  [call(): pl.pallas_call(kernel, out_shape=shapes, in_specs=specs, out_specs=[VMEM]...]
    ppermute x3, waiting for transfers between devices: 0.49 us -> 3.56 us  [from_below(): return lax.ppermute(values, 'x', [(at, (at + 1) % 4) for at in range(4)])]
  transfers between devices with their start and end apart: 14 -> 14, of which waited for: 4 -> 5; matrix products, arithmetic and copies ran while one was open for 0% -> 0% of each run, Pallas kernels for 14% -> 12%
where the time goes in v6:
time: 181 us; the launch traced here: 180 us
  blocking collectives  108 us (60%)
  Pallas kernels  34.1 us (19%)
  starting transfers between devices  26.2 us (14%)
  waiting for transfers between devices  5.77 us (3%)
  local copies, waits for them, and re-layouts  4.28 us (2%)
    all_to_all x8, blocking collectives, exchange(): return lax.all_to_all(payload, axes, 0, 0)  108 us
    pallas_call x21, Pallas kernels, call(): pl.pallas_call(kernel, out_shape=shapes, in_specs=specs, out_specs=[VMEM]...  34.1 us
    ppermute x5, starting transfers between devices, swap_core(): return lax.ppermute(values, 'core', [(0, 1), (1, 0)])  13.9 us
    ppermute x3, starting transfers between devices, from_above(): return lax.ppermute(values, 'x', [(at, (at + 3) % 4) for at in range(4)])  6.75 us
    unnamed x8, local copies, waits for them, and re-layouts  4.13 us
    ppermute x3, starting transfers between devices, swap_z(): return lax.ppermute(values, 'zl', [(0, 1), (1, 0)])  3.92 us
  transfers between devices with their start and end apart: 14, of which 5 were waited for; matrix products, arithmetic and copies ran while one was open for 0% of the time, Pallas kernels for 12%

profile of v6, /device:TPU:1, one launch (start us, length us, event | category | flops | bytes accessed | tf_op | source)
XLA Modules:
  0.0 180.4 jit_solution(13714250576111896926)
XLA Ops:
  0.0 1.4 collective-permute-start
  1.4 0.9 copy-done
  2.4 0.9 copy-done.1
  3.3 0.7 copy-done.2
  4.2 1.4 collective-permute-start.1
  5.6 1.4 collective-permute-start.2
  7.0 1.7 collective-permute-start.3
  9.4 1.6 copy-done.3
  11.0 0.7 unit.2.refs_2_.refs_4_
  11.8 2.3 %unit.3.refs_3_.refs_5_ = bf16[2048,512]{1,0:T(8,128)(2,1)S(1)} custom-call(bf16[2048,512]{1,0:T(8,128)(2,1)} %collective-permute-done.in_ref), custom_call_target="tpu_custom_call" | custom-call | flops 2000000000 | tf_op jit(solution)/shard_map/unit/pallas_call | solution.py:91
  14.1 1.3 build.4
  15.4 1.1 collective-permute-done.3.refs_3_.refs_8_
  16.6 1.2 collective-permute-start.6
  17.8 2.6 %collective-permute-start.5 = (bf16[336,512]{1,0:T(8,128)(2,1)S(1)}, bf16[336,512]{1,0:T(8,128)(2,1)S(1)}, u32[]{:S(2)}, u32[]{:S(2)}) collective-permute-start(bf16[336,512]{1,0:T(8,128)(2,1)S(1)} %collective-permute-done.3.refs_3_.refs_8_), channel_id=1, source_target_pairs={{0,12},{4,0},{8,4},{12,8},{1,13},{5,1},{9,5},{13,9},{2,14},{6,2},{... | collective-permute-start | bytes 1032200 | tf_op jit(solution)/shard_map/ppermute | solution.py:442
  20.4 3.5 %build.5 = (bf16[768,4096]{1,0:T(8,128)(2,1)S(1)}, f32[8,4096]{1,0:T(8,128)S(1)}) custom-call(f32[1]{0:T(128)S(6)} %copy.7.refs_0_, bf16[336,512]{1,0:T(8,128)(2,1)S(1)} %collective-permute-done.1.refs_1_.refs_6_, bf16[336,512]{1,0:T(8,128)(2,1)S(1)} %collective-permute-done.2.refs_2_.refs_7_, bf16[336,512]{1,0:T(8,128)(2,1)S(1)} %collective-permute-done.3.refs_3_.refs_8_, ...), custom_call_target="tpu_custom_call" | custom-call | flops 6442450944 | tf_op jit(solution)/shard_map/build/pallas_call | solution.py:91
  23.9 2.3 %collective-permute-done.4.refs_1_.refs_9_ = bf16[336,512]{1,0:T(8,128)(2,1)S(1)} collective-permute-done((bf16[336,512]{1,0:T(8,128)(2,1)S(1)}, bf16[336,512]{1,0:T(8,128)(2,1)S(1)}, u32[]{:S(2)}, u32[]{:S(2)}) %collective-permute-start.4) | collective-permute-done | bytes 344096 | tf_op jit(solution)/shard_map/ppermute | solution.py:438
  26.2 1.0 collective-permute-start.7
  27.2 2.8 %collective-permute-start.8 = (bf16[112,512]{1,0:T(8,128)(2,1)S(1)}, bf16[112,512]{1,0:T(8,128)(2,1)S(1)}, u32[]{:S(2)}, u32[]{:S(2)}) collective-permute-start(bf16[112,512]{1,0:T(8,128)(2,1)S(1)} %slice.13), channel_id=1, source_target_pairs={{0,12},{4,0},{8,4},{12,8},{1,13},{5,1},{9,5},{13,9},{2,14},{6,2},{... | collective-permute-start | bytes 344072 | tf_op jit(solution)/shard_map/ppermute | solution.py:442
  30.2 3.5 %build.6 = (bf16[768,4096]{1,0:T(8,128)(2,1)S(1)}, f32[8,4096]{1,0:T(8,128)S(1)}) custom-call(f32[1]{0:T(128)S(6)} %copy.7.refs_0_, bf16[336,512]{1,0:T(8,128)(2,1)S(1)} %collective-permute-done.4.refs_1_.refs_9_, bf16[336,512]{1,0:T(8,128)(2,1)S(1)} %collective-permute-done.5.refs_2_.refs_10_, bf16[336,512]{1,0:T(8,128)(2,1)S(1)} %collective-permute-done.6.refs_3_.refs_11_, ...), custom_call_target="tpu_custom_call" | custom-call | flops 6442450944 | tf_op jit(solution)/shard_map/build/pallas_call | solution.py:91
  33.8 1.3 collective-permute-done.9.refs_3_.refs_14_
  35.1 1.3 build.7
  36.4 1.9 %side_terms.5 = f32[8,136,256]{2,1,0:T(8,128)S(1)} custom-call(s32[8]{0:T(128)S(1)} %stack.35.refs_0_, bf16[256,4096]{1,0:T(8,128)(2,1)S(1)} %get-tuple-element.34.refs_1_.refs_0_, bf16[768,4096]{1,0:T(8,128)(2,1)S(1)} %get-tuple-element.39.refs_2_.refs_1_, bf16[768,4096]{1,0:T(8,128)(2,1)S(1)} %get-tuple-element.44.refs_3_.refs_2_, ...), custom_call_target="tpu_custom_call" | custom-call | flops 1073741824 | tf_op jit(solution)/shard_map/side_terms/pallas_call | solution.py:91
  38.3 4.4 %collective-permute-start.10 = (f32[8,136,256]{2,1,0:T(8,128)S(1)}, f32[8,136,256]{2,1,0:T(8,128)S(1)}, u32[]{:S(2)}, u32[]{:S(2)}) collective-permute-start(f32[8,136,256]{2,1,0:T(8,128)S(1)} %side_terms.5), channel_id=1, source_target_pairs={{0,1},{1,0},{2,3},{3,2},{4,5},{5,4},{6,7},{7,6},{8,9},{9,8},{10,11... | collective-permute-start | bytes 3342344 | tf_op jit(solution)/shard_map/ppermute | solution.py:430
  42.7 1.9 %side_terms.4.refs_4_ = f32[8,136,256]{2,1,0:T(8,128)S(1)} custom-call(s32[8]{0:T(128)S(1)} %stack.35.refs_0_, bf16[256,4096]{1,0:T(8,128)(2,1)S(1)} %get-tuple-element.34.refs_1_.refs_0_, bf16[768,4096]{1,0:T(8,128)(2,1)S(1)} %get-tuple-element.39.refs_2_.refs_1_, bf16[768,4096]{1,0:T(8,128)(2,1)S(1)} %get-tuple-element.44.refs_3_.refs_2_, ...), custom_call_target="tpu_custom_call" | custom-call | flops 1073741824 | tf_op jit(solution)/shard_map/side_terms/pallas_call | solution.py:91
  44.6 0.5 collective-permute-done.10.refs_5_
  45.1 0.3 pair.2
  45.4 18.3 %all_to_all.40.refs_4_ = bf16[8,144,256]{2,1,0:T(8,128)(2,1)S(1)} all-to-all(bf16[8,144,256]{2,1,0:T(8,128)(2,1)S(1)} %get-tuple-element.54), channel_id=1, replica_groups=mesh['y'=4,'zh'=2,'x'=4,'zl'=2,'core'=2] {'y','zh'}, dimensions={0} | all-to-all | bytes 1179648 | tf_op jit(solution)/shard_map/all_to_all | solution.py:426
  63.7 0.4 centre.2
  64.1 13.1 %all_to_all.41.refs_5_.refs_6_ = bf16[8,144,256]{2,1,0:T(8,128)(2,1)S(1)} all-to-all(bf16[8,144,256]{2,1,0:T(8,128)(2,1)S(1)} %get-tuple-element.55), channel_id=1, replica_groups=mesh['y'=4,'zh'=2,'x'=4,'zl'=2,'core'=2] {'y','zh'}, dimensions={0} | all-to-all | bytes 1179648 | tf_op jit(solution)/shard_map/all_to_all | solution.py:426
  77.1 2.9 %collective-permute-start.11 = (bf16[8,144,256]{2,1,0:T(8,128)(2,1)S(1)}, bf16[8,144,256]{2,1,0:T(8,128)(2,1)S(1)}, u32[]{:S(2)}, u32[]{:S(2)}) collective-permute-start(bf16[8,144,256]{2,1,0:T(8,128)(2,1)S(1)} %all_to_all.41.refs_5_.refs_6_), channel_id=1, source_target_pairs={{0,1},{1,0},{2,3},{3,2},{4,5},{5,4},{6,7},{7,6},{8,9},{9,8},{10,11... | collective-permute-start | bytes 1769480 | tf_op jit(solution)/shard_map/ppermute | solution.py:430
  80.0 3.0 %image_terms.4.refs_7_ = f32[2048,128]{1,0:T(8,128)S(1)} custom-call(s32[8]{0:T(128)S(1)} %stack.35.refs_0_, bf16[256,4096]{1,0:T(8,128)(2,1)S(1)} %get-tuple-element.34.refs_1_.refs_0_, bf16[768,4096]{1,0:T(8,128)(2,1)S(1)} %get-tuple-element.39.refs_2_.refs_1_, bf16[768,4096]{1,0:T(8,128)(2,1)S(1)} %get-tuple-element.44.refs_3_.refs_2_, ...), custom_call_target="tpu_custom_call" | custom-call | flops 1073741824 | tf_op jit(solution)/shard_map/image_terms/pallas_call | solution.py:91
  83.1 3.0 %image_terms.5 = bf16[8,256,128]{2,1,0:T(8,128)(2,1)S(1)} custom-call(s32[8]{0:T(128)S(1)} %stack.35.refs_0_, bf16[256,4096]{1,0:T(8,128)(2,1)S(1)} %get-tuple-element.34.refs_1_.refs_0_, bf16[768,4096]{1,0:T(8,128)(2,1)S(1)} %get-tuple-element.39.refs_2_.refs_1_, bf16[768,4096]{1,0:T(8,128)(2,1)S(1)} %get-tuple-element.44.refs_3_.refs_2_, ...), custom_call_target="tpu_custom_call" | custom-call | flops 1073741824 | tf_op jit(solution)/shard_map/image_terms/pallas_call | solution.py:91
  86.1 12.1 %all_to_all.42.refs_4_ = bf16[8,256,128]{2,1,0:T(8,128)(2,1)S(1)} all-to-all(bf16[8,256,128]{2,1,0:T(8,128)(2,1)S(1)} %image_terms.5), channel_id=1, replica_groups=mesh['y'=4,'zh'=2,'x'=4,'zl'=2,'core'=2] {'x','zl'}, dimensions={0} | all-to-all | bytes 1048576 | tf_op jit(solution)/shard_map/all_to_all | solution.py:426
  98.3 12.1 %all_to_all.43.refs_5_ = bf16[8,144,256]{2,1,0:T(8,128)(2,1)S(1)} all-to-all(bf16[8,144,256]{2,1,0:T(8,128)(2,1)S(1)} %owner.2), channel_id=1, replica_groups=mesh['y'=4,'zh'=2,'x'=4,'zl'=2,'core'=2] {'x','zl'}, dimensions={0} | all-to-all | bytes 1179648 | tf_op jit(solution)/shard_map/all_to_all | solution.py:426
  110.4 1.8 side_terms.7
  112.2 2.6 %collective-permute-start.12 = (f32[8,136,256]{2,1,0:T(8,128)S(1)}, f32[8,136,256]{2,1,0:T(8,128)S(1)}, u32[]{:S(2)}, u32[]{:S(2)}) collective-permute-start(f32[8,136,256]{2,1,0:T(8,128)S(1)} %side_terms.7), channel_id=1, source_target_pairs={{0,1},{1,0},{2,3},{3,2},{4,5},{5,4},{6,7},{7,6},{8,9},{9,8},{10,11... | collective-permute-start | bytes 3342344 | tf_op jit(solution)/shard_map/ppermute | solution.py:430
  114.8 1.8 side_terms.6.refs_4_
  116.6 0.6 collective-permute-done.12.refs_5_
  117.2 0.3 pair.3
  117.5 14.1 %all_to_all.44.refs_4_ = bf16[8,144,256]{2,1,0:T(8,128)(2,1)S(1)} all-to-all(bf16[8,144,256]{2,1,0:T(8,128)(2,1)S(1)} %pair.3), channel_id=1, replica_groups=mesh['y'=4,'zh'=2,'x'=4,'zl'=2,'core'=2] {'y','zh'}, dimensions={0} | all-to-all | bytes 1179648 | tf_op jit(solution)/shard_map/all_to_all | solution.py:426
  131.6 0.4 centre.3
  132.1 12.1 %all_to_all.45.refs_5_ = bf16[8,128,256]{2,1,0:T(8,128)(2,1)S(1)} all-to-all(bf16[8,128,256]{2,1,0:T(8,128)(2,1)S(1)} %centre.3), channel_id=1, replica_groups=mesh['y'=4,'zh'=2,'x'=4,'zl'=2,'core'=2] {'y','zh'}, dimensions={0} | all-to-all | bytes 1048576 | tf_op jit(solution)/shard_map/all_to_all | solution.py:426
  144.2 2.6 %collective-permute-start.13 = (bf16[8,128,256]{2,1,0:T(8,128)(2,1)S(1)}, bf16[8,128,256]{2,1,0:T(8,128)(2,1)S(1)}, u32[]{:S(2)}, u32[]{:S(2)}) collective-permute-start(bf16[8,128,256]{2,1,0:T(8,128)(2,1)S(1)} %all_to_all.45.refs_5_), channel_id=1, source_target_pairs={{0,1},{1,0},{2,3},{3,2},{4,5},{5,4},{6,7},{7,6},{8,9},{9,8},{10,11... | collective-permute-start | bytes 1572872 | tf_op jit(solution)/shard_map/ppermute | solution.py:430
  146.8 3.0 %image_terms.6.refs_7_ = f32[2048,128]{1,0:T(8,128)S(1)} custom-call(s32[8]{0:T(128)S(1)} %stack.35.refs_0_, bf16[256,4096]{1,0:T(8,128)(2,1)S(1)} %get-tuple-element.34.refs_1_.refs_0_, bf16[768,4096]{1,0:T(8,128)(2,1)S(1)} %get-tuple-element.39.refs_2_.refs_1_, bf16[768,4096]{1,0:T(8,128)(2,1)S(1)} %get-tuple-element.44.refs_3_.refs_2_, ...), custom_call_target="tpu_custom_call" | custom-call | flops 1073741824 | tf_op jit(solution)/shard_map/image_terms/pallas_call | solution.py:91
  149.8 3.0 %image_terms.7 = bf16[8,256,128]{2,1,0:T(8,128)(2,1)S(1)} custom-call(s32[8]{0:T(128)S(1)} %stack.35.refs_0_, bf16[256,4096]{1,0:T(8,128)(2,1)S(1)} %get-tuple-element.34.refs_1_.refs_0_, bf16[768,4096]{1,0:T(8,128)(2,1)S(1)} %get-tuple-element.39.refs_2_.refs_1_, bf16[768,4096]{1,0:T(8,128)(2,1)S(1)} %get-tuple-element.44.refs_3_.refs_2_, ...), custom_call_target="tpu_custom_call" | custom-call | flops 1073741824 | tf_op jit(solution)/shard_map/image_terms/pallas_call | solution.py:91
  152.8 12.0 %all_to_all.46.refs_0_ = bf16[8,256,128]{2,1,0:T(8,128)(2,1)S(1)} all-to-all(bf16[8,256,128]{2,1,0:T(8,128)(2,1)S(1)} %image_terms.7), channel_id=1, replica_groups=mesh['y'=4,'zh'=2,'x'=4,'zl'=2,'core'=2] {'x','zl'}, dimensions={0} | all-to-all | bytes 1048576 | tf_op jit(solution)/shard_map/all_to_all | solution.py:426
  165.0 14.7 %all_to_all.47 = f32[128,1,128]{2,1,0:T(1,128)S(1)} all-to-all(f32[128,1,128]{2,1,0:T(1,128)S(1)} %broadcast_in_dim.14), channel_id=1, replica_groups=mesh['y'=4,'zh'=2,'x'=4,'zl'=2,'core'=2] {'y','zh','x','zl','core'}, dimensions={0} | all-to-all | bytes 131072 | tf_op jit(solution)/shard_map/all_to_all | solution.py:426
  179.8 0.7 broadcast_divide_fusion
  (26 shorter events, 1.0 us)
Async XLA Ops:
  0.0 11.7 %collective-permute-start = (bf16[2048,512]{1,0:T(8,128)(2,1)}, bf16[2048,512]{1,0:T(8,128)(2,1)}, u32[]{:S(2)}, u32[]{:S(2)}) collective-permute-start(bf16[2048,512]{1,0:T(8,128)(2,1)} %in_ref.1), channel_id=1, source_target_pairs={{0,1},{1,0},{2,3},{3,2},{4,5},{5,4},{6,7},{7,6},{8,9},{9,8},{10,11... | collective-permute-start | bytes 6291464 | tf_op jit(solution)/shard_map/ppermute | solution.py:430
  1.4 0.9 copy-start
  2.4 0.9 copy-start.1
  3.3 0.7 copy-start.2
  4.2 11.2 %collective-permute-start.1 = (bf16[336,512]{1,0:T(8,128)(2,1)S(1)}, bf16[336,512]{1,0:T(8,128)(2,1)S(1)}, u32[]{:S(2)}, u32[]{:S(2)}) collective-permute-start(bf16[336,512]{1,0:T(8,128)(2,1)S(1)} %get-tuple-element.33.refs_1_.refs_5_), channel_id=1, source_target_pairs={{0,4},{4,8},{8,12},{12,0},{1,5},{5,9},{9,13},{13,1},{2,6},{6,10},{... | collective-permute-start | bytes 1032200 | tf_op jit(solution)/shard_map/ppermute | solution.py:438
  5.6 9.8 %collective-permute-start.2 = (bf16[336,512]{1,0:T(8,128)(2,1)S(1)}, bf16[336,512]{1,0:T(8,128)(2,1)S(1)}, u32[]{:S(2)}, u32[]{:S(2)}) collective-permute-start(bf16[336,512]{1,0:T(8,128)(2,1)S(1)} %get-tuple-element.33.refs_1_.refs_5_), channel_id=1, source_target_pairs={{0,12},{4,0},{8,4},{12,8},{1,13},{5,1},{9,5},{13,9},{2,14},{6,2},{... | collective-permute-start | bytes 1032200 | tf_op jit(solution)/shard_map/ppermute | solution.py:442
  7.0 9.6 %collective-permute-start.3 = (bf16[336,512]{1,0:T(8,128)(2,1)S(1)}, bf16[336,512]{1,0:T(8,128)(2,1)S(1)}, u32[]{:S(2)}, u32[]{:S(2)}) collective-permute-start(bf16[336,512]{1,0:T(8,128)(2,1)S(1)} %get-tuple-element.33.refs_1_.refs_5_), channel_id=1, source_target_pairs={{0,2},{2,0},{1,3},{3,1},{4,6},{6,4},{5,7},{7,5},{8,10},{10,8},{9,1... | collective-permute-start | bytes 1032200 | tf_op jit(solution)/shard_map/ppermute | solution.py:434
  9.4 1.6 copy-start.3
  16.6 9.6 %collective-permute-start.4 = (bf16[336,512]{1,0:T(8,128)(2,1)S(1)}, bf16[336,512]{1,0:T(8,128)(2,1)S(1)}, u32[]{:S(2)}, u32[]{:S(2)}) collective-permute-start(bf16[336,512]{1,0:T(8,128)(2,1)S(1)} %collective-permute-done.1.refs_1_.refs_6_), channel_id=1, source_target_pairs={{0,4},{4,8},{8,12},{12,0},{1,5},{5,9},{9,13},{13,1},{2,6},{6,10},{... | collective-permute-start | bytes 1032200 | tf_op jit(solution)/shard_map/ppermute | solution.py:438
  16.6 9.6 %collective-permute-start.6 = (bf16[336,512]{1,0:T(8,128)(2,1)S(1)}, bf16[336,512]{1,0:T(8,128)(2,1)S(1)}, u32[]{:S(2)}, u32[]{:S(2)}) collective-permute-start(bf16[336,512]{1,0:T(8,128)(2,1)S(1)} %collective-permute-done.1.refs_1_.refs_6_), channel_id=1, source_target_pairs={{0,2},{2,0},{1,3},{3,1},{4,6},{6,4},{5,7},{7,5},{8,10},{10,8},{9,1... | collective-permute-start | bytes 1032200 | tf_op jit(solution)/shard_map/ppermute | solution.py:434
  17.8 8.4 %collective-permute-start.5 = (bf16[336,512]{1,0:T(8,128)(2,1)S(1)}, bf16[336,512]{1,0:T(8,128)(2,1)S(1)}, u32[]{:S(2)}, u32[]{:S(2)}) collective-permute-start(bf16[336,512]{1,0:T(8,128)(2,1)S(1)} %collective-permute-done.3.refs_3_.refs_8_), channel_id=1, source_target_pairs={{0,12},{4,0},{8,4},{12,8},{1,13},{5,1},{9,5},{13,9},{2,14},{6,2},{... | collective-permute-start | bytes 1032200 | tf_op jit(solution)/shard_map/ppermute | solution.py:442
  26.2 7.5 %collective-permute-start.7 = (bf16[112,512]{1,0:T(8,128)(2,1)S(1)}, bf16[112,512]{1,0:T(8,128)(2,1)S(1)}, u32[]{:S(2)}, u32[]{:S(2)}) collective-permute-start(bf16[112,512]{1,0:T(8,128)(2,1)S(1)} %slice.12), channel_id=1, source_target_pairs={{0,2},{2,0},{1,3},{3,1},{4,6},{6,4},{5,7},{7,5},{8,10},{10,8},{9,1... | collective-permute-start | bytes 344072 | tf_op jit(solution)/shard_map/ppermute | solution.py:434
  27.2 6.6 %collective-permute-start.8 = (bf16[112,512]{1,0:T(8,128)(2,1)S(1)}, bf16[112,512]{1,0:T(8,128)(2,1)S(1)}, u32[]{:S(2)}, u32[]{:S(2)}) collective-permute-start(bf16[112,512]{1,0:T(8,128)(2,1)S(1)} %slice.13), channel_id=1, source_target_pairs={{0,12},{4,0},{8,4},{12,8},{1,13},{5,1},{9,5},{13,9},{2,14},{6,2},{... | collective-permute-start | bytes 344072 | tf_op jit(solution)/shard_map/ppermute | solution.py:442
  30.0 5.1 %collective-permute-start.9 = (bf16[112,512]{1,0:T(8,128)(2,1)S(1)}, bf16[112,512]{1,0:T(8,128)(2,1)S(1)}, u32[]{:S(2)}, u32[]{:S(2)}) collective-permute-start(bf16[112,512]{1,0:T(8,128)(2,1)S(1)} %slice.14), channel_id=1, source_target_pairs={{0,4},{4,8},{8,12},{12,0},{1,5},{5,9},{9,13},{13,1},{2,6},{6,10},{... | collective-permute-start | bytes 344072 | tf_op jit(solution)/shard_map/ppermute | solution.py:438
  38.3 6.8 %collective-permute-start.10 = (f32[8,136,256]{2,1,0:T(8,128)S(1)}, f32[8,136,256]{2,1,0:T(8,128)S(1)}, u32[]{:S(2)}, u32[]{:S(2)}) collective-permute-start(f32[8,136,256]{2,1,0:T(8,128)S(1)} %side_terms.5), channel_id=1, source_target_pairs={{0,1},{1,0},{2,3},{3,2},{4,5},{5,4},{6,7},{7,6},{8,9},{9,8},{10,11... | collective-permute-start | bytes 3342344 | tf_op jit(solution)/shard_map/ppermute | solution.py:430
  77.1 5.9 %collective-permute-start.11 = (bf16[8,144,256]{2,1,0:T(8,128)(2,1)S(1)}, bf16[8,144,256]{2,1,0:T(8,128)(2,1)S(1)}, u32[]{:S(2)}, u32[]{:S(2)}) collective-permute-start(bf16[8,144,256]{2,1,0:T(8,128)(2,1)S(1)} %all_to_all.41.refs_5_.refs_6_), channel_id=1, source_target_pairs={{0,1},{1,0},{2,3},{3,2},{4,5},{5,4},{6,7},{7,6},{8,9},{9,8},{10,11... | collective-permute-start | bytes 1769480 | tf_op jit(solution)/shard_map/ppermute | solution.py:430
  112.2 4.9 %collective-permute-start.12 = (f32[8,136,256]{2,1,0:T(8,128)S(1)}, f32[8,136,256]{2,1,0:T(8,128)S(1)}, u32[]{:S(2)}, u32[]{:S(2)}) collective-permute-start(f32[8,136,256]{2,1,0:T(8,128)S(1)} %side_terms.7), channel_id=1, source_target_pairs={{0,1},{1,0},{2,3},{3,2},{4,5},{5,4},{6,7},{7,6},{8,9},{9,8},{10,11... | collective-permute-start | bytes 3342344 | tf_op jit(solution)/shard_map/ppermute | solution.py:430
  144.2 5.6 %collective-permute-start.13 = (bf16[8,128,256]{2,1,0:T(8,128)(2,1)S(1)}, bf16[8,128,256]{2,1,0:T(8,128)(2,1)S(1)}, u32[]{:S(2)}, u32[]{:S(2)}) collective-permute-start(bf16[8,128,256]{2,1,0:T(8,128)(2,1)S(1)} %all_to_all.45.refs_5_), channel_id=1, source_target_pairs={{0,1},{1,0},{2,3},{3,2},{4,5},{5,4},{6,7},{7,6},{8,9},{9,8},{10,11... | collective-permute-start | bytes 1572872 | tf_op jit(solution)/shard_map/ppermute | solution.py:430

commit v7 on v6

--- a/solution.py
+++ b/solution.py
@@ -24,7 +24,7 @@
 ROWS = EIGHT * OWN
 PACK = OWN + WIDTH // 2 + 16
 BLOCK = 8 * PIECE
-THIRD = PACK // 3
+SPLIT = 160
 TILES = 4
 
 
@@ -103,11 +103,11 @@
 def rows_of(refs):
     if len(refs) == 1:
         return refs[0][:OWN, :]
-    return jnp.concatenate([refs[0][...], refs[1][...], refs[2][: OWN - 2 * THIRD, :]], axis=0)
+    return jnp.concatenate([refs[0][...], refs[1][: OWN - SPLIT, :]], axis=0)
 
 
 def rest_of(refs, start, stop, lanes=slice(None)):
-    skip = 0 if len(refs) == 1 else 2 * THIRD
+    skip = 0 if len(refs) == 1 else SPLIT
     return refs[-1][start - skip : stop - skip, lanes]
 
 
@@ -192,7 +192,7 @@
     slots_ref, tiles, refs = refs[0], refs[1 : 1 + TILES], refs[1 + TILES :]
     half = WIDTH // 2
     if first:
-        packed, refs = take(refs, [1] * 7 + [3])
+        packed, refs = take(refs, [1] * 7 + [2])
         sums, (out_ref, wt_ref) = refs[:TILES], refs[TILES:]
         tails = [rest_of(parts, OWN + half, PACK) for parts in packed]
         for slot, parts in enumerate(packed):
@@ -442,7 +442,16 @@
     return lax.ppermute(values, "x", [(at, (at + 3) % 4) for at in range(4)])
 
 
-def pack_kernel(rows_ref, start_ref, weight_ref, out_ref, wide_ref):
+def pack_kernel(rows_hbm, start_hbm, weight_hbm, out_ref, wide_ref, rows_ref, start_ref, weight_ref, sems):
+    copies = [
+        pltpu.make_async_copy(rows_hbm, rows_ref, sems.at[0]),
+        pltpu.make_async_copy(start_hbm, start_ref, sems.at[1]),
+        pltpu.make_async_copy(weight_hbm, weight_ref, sems.at[2]),
+    ]
+    for copy in copies:
+        copy.start()
+    for copy in copies:
+        copy.wait()
     values = rows_ref[...].astype(F32)
     scale = lax.rsqrt(jnp.sum(values * values, axis=1, keepdims=True) + 1e-06)
     out_ref[:OWN, :] = (values * scale).astype(B16)
@@ -461,7 +470,14 @@
 
 def pack(rows, start, weight):
     shapes = [jax.ShapeDtypeStruct((PACK, rows.shape[1]), B16), jax.ShapeDtypeStruct((OWN, WIDTH), F32)]
-    return call(pack_kernel, shapes, [VMEM] * 3, [rows, start, weight], "pack")
+    scratch = [
+        pltpu.VMEM(rows.shape, B16),
+        pltpu.VMEM(start.shape, F32),
+        pltpu.VMEM(weight.shape, F32),
+        pltpu.SemaphoreType.DMA((3,)),
+    ]
+    specs = [pl.BlockSpec(memory_space=pl.ANY)] * 3
+    return call(pack_kernel, shapes, specs, [rows, start, weight], "pack", scratch=scratch, mib=56)
 
 
 def slot_owners():
@@ -484,11 +500,7 @@
     opposite, across_above, across_below, sums_one = lax.optimization_barrier(
         (opposite, across_above, across_below, sums_one)
     )
-    last = [
-        swap_z(opposite[:THIRD]),
-        from_above(across_above[THIRD : 2 * THIRD]),
-        from_below(across_below[2 * THIRD :]),
-    ]
+    last = [swap_z(opposite[:SPLIT]), from_above(across_above[SPLIT:])]
     two, sums_two = build((3,), 2048, spread, [[opposite], [across_above], [across_below]], near, far)
     *last, sums_two = lax.optimization_barrier((*last, sums_two))
     three, sums_three = build((1,), 2048, spread, [last], near, far)

time: 181 us -> 179 us (0.989)
  local copies, waits for them, and re-layouts: 4.28 us -> 1.97 us
    unnamed x8 -> x6, local copies, waits for them, and re-layouts: 4.13 us -> 1.82 us
    ppermute x3 -> x2, waiting for transfers between devices: 3.56 us -> 3.7 us  [from_below(): return lax.ppermute(values, 'x', [(at, (at + 1) % 4) for at in range(4)])]
  transfers between devices with their start and end apart: 14 -> 13, of which waited for: 5 -> 6; matrix products, arithmetic and copies ran while one was open for 0% -> 0% of each run, Pallas kernels for 12% -> 12%
where the time goes in v7:
time: 179 us
  blocking collectives  109 us (61%)
  Pallas kernels  34.3 us (19%)
  starting transfers between devices  25.9 us (14%)
  waiting for transfers between devices  6.33 us (4%)
  local copies, waits for them, and re-layouts  1.97 us (1%)
    all_to_all x8, blocking collectives, exchange(): return lax.all_to_all(payload, axes, 0, 0)  109 us
    pallas_call x21, Pallas kernels, call(): pl.pallas_call(kernel, out_shape=shapes, in_specs=specs, out_specs=[VMEM]...  34.3 us
    ppermute x5, starting transfers between devices, swap_core(): return lax.ppermute(values, 'core', [(0, 1), (1, 0)])  13.8 us
    ppermute x3, starting transfers between devices, from_above(): return lax.ppermute(values, 'x', [(at, (at + 3) % 4) for at in range(4)])  6.96 us
    ppermute x3, starting transfers between devices, swap_z(): return lax.ppermute(values, 'zl', [(0, 1), (1, 0)])  3.83 us
    ppermute x2, waiting for transfers between devices, from_below(): return lax.ppermute(values, 'x', [(at, (at + 1) % 4) for at in range(4)])  3.7 us
  transfers between devices with their start and end apart: 13, of which 6 were waited for; matrix products, arithmetic and copies ran while one was open for 0% of the time, Pallas kernels for 12%

profile of v7, /device:TPU:1, one launch (start us, length us, event | category | flops | bytes accessed | tf_op | source)
XLA Modules:
  0.0 178.7 jit_solution(3054554127858453814)
XLA Ops:
  0.0 1.4 collective-permute-start
  1.4 2.0 %pack.1 = (bf16[336,512]{1,0:T(8,128)(2,1)}, f32[256,128]{1,0:T(8,128)}) custom-call(bf16[256,512]{1,0:T(8,128)(2,1)} %rows_hbm.1, f32[256,128]{1,0:T(8,128)} %start_hbm.1, f32[1,256]{1,0:T(1,128)} %bitcast.13), custom_call_target="tpu_custom_call" | custom-call | tf_op jit(solution)/shard_map/pack/pallas_call | solution.py:91
  3.4 1.4 collective-permute-start.1
  4.8 1.4 collective-permute-start.2
  6.2 1.7 collective-permute-start.3
  8.6 1.6 copy-done.2
  10.2 0.7 unit.2.refs_2_.refs_4_.refs_3_
  11.0 0.7 unit.3.refs_3_.refs_5_.refs_4_
  11.7 0.2 copy-done
  11.9 1.3 build.4
  13.3 1.3 collective-permute-done.1.refs_1_.refs_6_
  14.6 1.4 collective-permute-done.3.refs_3_.refs_8_
  16.0 1.2 collective-permute-start.6
  17.2 2.6 %collective-permute-start.5 = (bf16[336,512]{1,0:T(8,128)(2,1)S(1)}, bf16[336,512]{1,0:T(8,128)(2,1)S(1)}, u32[]{:S(2)}, u32[]{:S(2)}) collective-permute-start(bf16[336,512]{1,0:T(8,128)(2,1)S(1)} %collective-permute-done.3.refs_3_.refs_8_), channel_id=1, source_target_pairs={{0,12},{4,0},{8,4},{12,8},{1,13},{5,1},{9,5},{13,9},{2,14},{6,2},{... | collective-permute-start | bytes 1032200 | tf_op jit(solution)/shard_map/ppermute | solution.py:442
  19.8 3.5 %build.5 = (bf16[768,4096]{1,0:T(8,128)(2,1)S(1)}, f32[8,4096]{1,0:T(8,128)S(1)}) custom-call(f32[1]{0:T(128)S(6)} %copy.7.refs_0_, bf16[336,512]{1,0:T(8,128)(2,1)S(1)} %collective-permute-done.1.refs_1_.refs_6_, bf16[336,512]{1,0:T(8,128)(2,1)S(1)} %collective-permute-done.2.refs_2_.refs_7_, bf16[336,512]{1,0:T(8,128)(2,1)S(1)} %collective-permute-done.3.refs_3_.refs_8_, ...), custom_call_target="tpu_custom_call" | custom-call | flops 6442450944 | tf_op jit(solution)/shard_map/build/pallas_call | solution.py:91
  23.3 2.4 %collective-permute-done.4.refs_1_.refs_9_ = bf16[336,512]{1,0:T(8,128)(2,1)S(1)} collective-permute-done((bf16[336,512]{1,0:T(8,128)(2,1)S(1)}, bf16[336,512]{1,0:T(8,128)(2,1)S(1)}, u32[]{:S(2)}, u32[]{:S(2)}) %collective-permute-start.4) | collective-permute-done | bytes 344096 | tf_op jit(solution)/shard_map/ppermute | solution.py:438
  25.7 3.0 %collective-permute-start.8 = (bf16[176,512]{1,0:T(8,128)(2,1)S(1)}, bf16[176,512]{1,0:T(8,128)(2,1)S(1)}, u32[]{:S(2)}, u32[]{:S(2)}) collective-permute-start(bf16[176,512]{1,0:T(8,128)(2,1)S(1)} %slice.10), channel_id=1, source_target_pairs={{0,12},{4,0},{8,4},{12,8},{1,13},{5,1},{9,5},{13,9},{2,14},{6,2},{... | collective-permute-start | bytes 540680 | tf_op jit(solution)/shard_map/ppermute | solution.py:442
  28.7 0.9 collective-permute-start.7
  29.7 3.5 %build.6 = (bf16[768,4096]{1,0:T(8,128)(2,1)S(1)}, f32[8,4096]{1,0:T(8,128)S(1)}) custom-call(f32[1]{0:T(128)S(6)} %copy.7.refs_0_, bf16[336,512]{1,0:T(8,128)(2,1)S(1)} %collective-permute-done.4.refs_1_.refs_9_, bf16[336,512]{1,0:T(8,128)(2,1)S(1)} %collective-permute-done.5.refs_2_.refs_10_, bf16[336,512]{1,0:T(8,128)(2,1)S(1)} %collective-permute-done.6.refs_3_.refs_11_, ...), custom_call_target="tpu_custom_call" | custom-call | flops 6442450944 | tf_op jit(solution)/shard_map/build/pallas_call | solution.py:91
  33.3 1.3 build.7
  34.6 1.9 %side_terms.5 = f32[8,136,256]{2,1,0:T(8,128)S(1)} custom-call(s32[8]{0:T(128)S(1)} %stack.35.refs_0_, bf16[256,4096]{1,0:T(8,128)(2,1)S(1)} %get-tuple-element.33.refs_1_.refs_0_, bf16[768,4096]{1,0:T(8,128)(2,1)S(1)} %get-tuple-element.38.refs_2_.refs_1_, bf16[768,4096]{1,0:T(8,128)(2,1)S(1)} %get-tuple-element.43.refs_3_.refs_2_, ...), custom_call_target="tpu_custom_call" | custom-call | flops 1073741824 | tf_op jit(solution)/shard_map/side_terms/pallas_call | solution.py:91
  36.5 4.3 %collective-permute-start.9 = (f32[8,136,256]{2,1,0:T(8,128)S(1)}, f32[8,136,256]{2,1,0:T(8,128)S(1)}, u32[]{:S(2)}, u32[]{:S(2)}) collective-permute-start(f32[8,136,256]{2,1,0:T(8,128)S(1)} %side_terms.5), channel_id=1, source_target_pairs={{0,1},{1,0},{2,3},{3,2},{4,5},{5,4},{6,7},{7,6},{8,9},{9,8},{10,11... | collective-permute-start | bytes 3342344 | tf_op jit(solution)/shard_map/ppermute | solution.py:430
  40.8 1.9 %side_terms.4.refs_4_ = f32[8,136,256]{2,1,0:T(8,128)S(1)} custom-call(s32[8]{0:T(128)S(1)} %stack.35.refs_0_, bf16[256,4096]{1,0:T(8,128)(2,1)S(1)} %get-tuple-element.33.refs_1_.refs_0_, bf16[768,4096]{1,0:T(8,128)(2,1)S(1)} %get-tuple-element.38.refs_2_.refs_1_, bf16[768,4096]{1,0:T(8,128)(2,1)S(1)} %get-tuple-element.43.refs_3_.refs_2_, ...), custom_call_target="tpu_custom_call" | custom-call | flops 1073741824 | tf_op jit(solution)/shard_map/side_terms/pallas_call | solution.py:91
  42.7 0.5 collective-permute-done.9.refs_5_
  43.2 0.3 pair.2
  43.5 18.5 %all_to_all.40.refs_4_ = bf16[8,144,256]{2,1,0:T(8,128)(2,1)S(1)} all-to-all(bf16[8,144,256]{2,1,0:T(8,128)(2,1)S(1)} %get-tuple-element.52), channel_id=1, replica_groups=mesh['y'=4,'zh'=2,'x'=4,'zl'=2,'core'=2] {'y','zh'}, dimensions={0} | all-to-all | bytes 1179648 | tf_op jit(solution)/shard_map/all_to_all | solution.py:426
  62.0 0.4 centre.2
  62.4 13.1 %all_to_all.41.refs_5_.refs_6_ = bf16[8,144,256]{2,1,0:T(8,128)(2,1)S(1)} all-to-all(bf16[8,144,256]{2,1,0:T(8,128)(2,1)S(1)} %get-tuple-element.53), channel_id=1, replica_groups=mesh['y'=4,'zh'=2,'x'=4,'zl'=2,'core'=2] {'y','zh'}, dimensions={0} | all-to-all | bytes 1179648 | tf_op jit(solution)/shard_map/all_to_all | solution.py:426
  75.4 2.9 %collective-permute-start.10 = (bf16[8,144,256]{2,1,0:T(8,128)(2,1)S(1)}, bf16[8,144,256]{2,1,0:T(8,128)(2,1)S(1)}, u32[]{:S(2)}, u32[]{:S(2)}) collective-permute-start(bf16[8,144,256]{2,1,0:T(8,128)(2,1)S(1)} %all_to_all.41.refs_5_.refs_6_), channel_id=1, source_target_pairs={{0,1},{1,0},{2,3},{3,2},{4,5},{5,4},{6,7},{7,6},{8,9},{9,8},{10,11... | collective-permute-start | bytes 1769480 | tf_op jit(solution)/shard_map/ppermute | solution.py:430
  78.3 3.0 %image_terms.4.refs_7_ = f32[2048,128]{1,0:T(8,128)S(1)} custom-call(s32[8]{0:T(128)S(1)} %stack.35.refs_0_, bf16[256,4096]{1,0:T(8,128)(2,1)S(1)} %get-tuple-element.33.refs_1_.refs_0_, bf16[768,4096]{1,0:T(8,128)(2,1)S(1)} %get-tuple-element.38.refs_2_.refs_1_, bf16[768,4096]{1,0:T(8,128)(2,1)S(1)} %get-tuple-element.43.refs_3_.refs_2_, ...), custom_call_target="tpu_custom_call" | custom-call | flops 1073741824 | tf_op jit(solution)/shard_map/image_terms/pallas_call | solution.py:91
  81.3 3.0 %image_terms.5 = bf16[8,256,128]{2,1,0:T(8,128)(2,1)S(1)} custom-call(s32[8]{0:T(128)S(1)} %stack.35.refs_0_, bf16[256,4096]{1,0:T(8,128)(2,1)S(1)} %get-tuple-element.33.refs_1_.refs_0_, bf16[768,4096]{1,0:T(8,128)(2,1)S(1)} %get-tuple-element.38.refs_2_.refs_1_, bf16[768,4096]{1,0:T(8,128)(2,1)S(1)} %get-tuple-element.43.refs_3_.refs_2_, ...), custom_call_target="tpu_custom_call" | custom-call | flops 1073741824 | tf_op jit(solution)/shard_map/image_terms/pallas_call | solution.py:91
  84.4 12.1 %all_to_all.42.refs_4_ = bf16[8,256,128]{2,1,0:T(8,128)(2,1)S(1)} all-to-all(bf16[8,256,128]{2,1,0:T(8,128)(2,1)S(1)} %image_terms.5), channel_id=1, replica_groups=mesh['y'=4,'zh'=2,'x'=4,'zl'=2,'core'=2] {'x','zl'}, dimensions={0} | all-to-all | bytes 1048576 | tf_op jit(solution)/shard_map/all_to_all | solution.py:426
  96.4 0.2 owner.2
  96.6 12.1 %all_to_all.43.refs_5_ = bf16[8,144,256]{2,1,0:T(8,128)(2,1)S(1)} all-to-all(bf16[8,144,256]{2,1,0:T(8,128)(2,1)S(1)} %owner.2), channel_id=1, replica_groups=mesh['y'=4,'zh'=2,'x'=4,'zl'=2,'core'=2] {'x','zl'}, dimensions={0} | all-to-all | bytes 1179648 | tf_op jit(solution)/shard_map/all_to_all | solution.py:426
  108.7 1.8 %side_terms.7 = f32[8,136,256]{2,1,0:T(8,128)S(1)} custom-call(s32[8]{0:T(128)S(1)} %stack.35.refs_0_, bf16[256,4096]{1,0:T(8,128)(2,1)S(1)} %get-tuple-element.33.refs_1_.refs_0_, bf16[768,4096]{1,0:T(8,128)(2,1)S(1)} %get-tuple-element.38.refs_2_.refs_1_, bf16[768,4096]{1,0:T(8,128)(2,1)S(1)} %get-tuple-element.43.refs_3_.refs_2_, ...), custom_call_target="tpu_custom_call" | custom-call | flops 1073741824 | tf_op jit(solution)/shard_map/side_terms/pallas_call | solution.py:91
  110.5 2.6 %collective-permute-start.11 = (f32[8,136,256]{2,1,0:T(8,128)S(1)}, f32[8,136,256]{2,1,0:T(8,128)S(1)}, u32[]{:S(2)}, u32[]{:S(2)}) collective-permute-start(f32[8,136,256]{2,1,0:T(8,128)S(1)} %side_terms.7), channel_id=1, source_target_pairs={{0,1},{1,0},{2,3},{3,2},{4,5},{5,4},{6,7},{7,6},{8,9},{9,8},{10,11... | collective-permute-start | bytes 3342344 | tf_op jit(solution)/shard_map/ppermute | solution.py:430
  113.1 1.8 %side_terms.6.refs_4_ = f32[8,136,256]{2,1,0:T(8,128)S(1)} custom-call(s32[8]{0:T(128)S(1)} %stack.35.refs_0_, bf16[256,4096]{1,0:T(8,128)(2,1)S(1)} %get-tuple-element.33.refs_1_.refs_0_, bf16[768,4096]{1,0:T(8,128)(2,1)S(1)} %get-tuple-element.38.refs_2_.refs_1_, bf16[768,4096]{1,0:T(8,128)(2,1)S(1)} %get-tuple-element.43.refs_3_.refs_2_, ...), custom_call_target="tpu_custom_call" | custom-call | flops 1073741824 | tf_op jit(solution)/shard_map/side_terms/pallas_call | solution.py:91
  114.9 0.6 collective-permute-done.11.refs_5_
  115.5 0.3 pair.3
  115.8 13.8 %all_to_all.44.refs_4_ = bf16[8,144,256]{2,1,0:T(8,128)(2,1)S(1)} all-to-all(bf16[8,144,256]{2,1,0:T(8,128)(2,1)S(1)} %pair.3), channel_id=1, replica_groups=mesh['y'=4,'zh'=2,'x'=4,'zl'=2,'core'=2] {'y','zh'}, dimensions={0} | all-to-all | bytes 1179648 | tf_op jit(solution)/shard_map/all_to_all | solution.py:426
  129.6 0.4 centre.3
  130.0 12.3 %all_to_all.45.refs_5_ = bf16[8,128,256]{2,1,0:T(8,128)(2,1)S(1)} all-to-all(bf16[8,128,256]{2,1,0:T(8,128)(2,1)S(1)} %centre.3), channel_id=1, replica_groups=mesh['y'=4,'zh'=2,'x'=4,'zl'=2,'core'=2] {'y','zh'}, dimensions={0} | all-to-all | bytes 1048576 | tf_op jit(solution)/shard_map/all_to_all | solution.py:426
  142.3 2.6 %collective-permute-start.12 = (bf16[8,128,256]{2,1,0:T(8,128)(2,1)S(1)}, bf16[8,128,256]{2,1,0:T(8,128)(2,1)S(1)}, u32[]{:S(2)}, u32[]{:S(2)}) collective-permute-start(bf16[8,128,256]{2,1,0:T(8,128)(2,1)S(1)} %all_to_all.45.refs_5_), channel_id=1, source_target_pairs={{0,1},{1,0},{2,3},{3,2},{4,5},{5,4},{6,7},{7,6},{8,9},{9,8},{10,11... | collective-permute-start | bytes 1572872 | tf_op jit(solution)/shard_map/ppermute | solution.py:430
  145.0 3.0 %image_terms.6.refs_7_ = f32[2048,128]{1,0:T(8,128)S(1)} custom-call(s32[8]{0:T(128)S(1)} %stack.35.refs_0_, bf16[256,4096]{1,0:T(8,128)(2,1)S(1)} %get-tuple-element.33.refs_1_.refs_0_, bf16[768,4096]{1,0:T(8,128)(2,1)S(1)} %get-tuple-element.38.refs_2_.refs_1_, bf16[768,4096]{1,0:T(8,128)(2,1)S(1)} %get-tuple-element.43.refs_3_.refs_2_, ...), custom_call_target="tpu_custom_call" | custom-call | flops 1073741824 | tf_op jit(solution)/shard_map/image_terms/pallas_call | solution.py:91
  148.0 3.0 %image_terms.7 = bf16[8,256,128]{2,1,0:T(8,128)(2,1)S(1)} custom-call(s32[8]{0:T(128)S(1)} %stack.35.refs_0_, bf16[256,4096]{1,0:T(8,128)(2,1)S(1)} %get-tuple-element.33.refs_1_.refs_0_, bf16[768,4096]{1,0:T(8,128)(2,1)S(1)} %get-tuple-element.38.refs_2_.refs_1_, bf16[768,4096]{1,0:T(8,128)(2,1)S(1)} %get-tuple-element.43.refs_3_.refs_2_, ...), custom_call_target="tpu_custom_call" | custom-call | flops 1073741824 | tf_op jit(solution)/shard_map/image_terms/pallas_call | solution.py:91
  151.0 12.0 %all_to_all.46.refs_0_ = bf16[8,256,128]{2,1,0:T(8,128)(2,1)S(1)} all-to-all(bf16[8,256,128]{2,1,0:T(8,128)(2,1)S(1)} %image_terms.7), channel_id=1, replica_groups=mesh['y'=4,'zh'=2,'x'=4,'zl'=2,'core'=2] {'x','zl'}, dimensions={0} | all-to-all | bytes 1048576 | tf_op jit(solution)/shard_map/all_to_all | solution.py:426
  163.2 14.8 %all_to_all.47 = f32[128,1,128]{2,1,0:T(1,128)S(1)} all-to-all(f32[128,1,128]{2,1,0:T(1,128)S(1)} %broadcast_in_dim.14), channel_id=1, replica_groups=mesh['y'=4,'zh'=2,'x'=4,'zl'=2,'core'=2] {'y','zh','x','zl','core'}, dimensions={0} | all-to-all | bytes 131072 | tf_op jit(solution)/shard_map/all_to_all | solution.py:426
  178.0 0.7 broadcast_divide_fusion
  (21 shorter events, 0.4 us)
Async XLA Ops:
  0.0 11.0 %collective-permute-start = (bf16[2048,512]{1,0:T(8,128)(2,1)}, bf16[2048,512]{1,0:T(8,128)(2,1)S(1)}, u32[]{:S(2)}, u32[]{:S(2)}) collective-permute-start(bf16[2048,512]{1,0:T(8,128)(2,1)} %in_ref.1), channel_id=1, source_target_pairs={{0,1},{1,0},{2,3},{3,2},{4,5},{5,4},{6,7},{7,6},{8,9},{9,8},{10,11... | collective-permute-start | bytes 6291464 | tf_op jit(solution)/shard_map/ppermute | solution.py:430
  3.4 11.2 %collective-permute-start.1 = (bf16[336,512]{1,0:T(8,128)(2,1)}, bf16[336,512]{1,0:T(8,128)(2,1)S(1)}, u32[]{:S(2)}, u32[]{:S(2)}) collective-permute-start(bf16[336,512]{1,0:T(8,128)(2,1)} %get-tuple-element.32.refs_1_.refs_5_), channel_id=1, source_target_pairs={{0,4},{4,8},{8,12},{12,0},{1,5},{5,9},{9,13},{13,1},{2,6},{6,10},{... | collective-permute-start | bytes 1032200 | tf_op jit(solution)/shard_map/ppermute | solution.py:438
  4.8 9.8 %collective-permute-start.2 = (bf16[336,512]{1,0:T(8,128)(2,1)}, bf16[336,512]{1,0:T(8,128)(2,1)S(1)}, u32[]{:S(2)}, u32[]{:S(2)}) collective-permute-start(bf16[336,512]{1,0:T(8,128)(2,1)} %get-tuple-element.32.refs_1_.refs_5_), channel_id=1, source_target_pairs={{0,12},{4,0},{8,4},{12,8},{1,13},{5,1},{9,5},{13,9},{2,14},{6,2},{... | collective-permute-start | bytes 1032200 | tf_op jit(solution)/shard_map/ppermute | solution.py:442
  6.2 9.9 %collective-permute-start.3 = (bf16[336,512]{1,0:T(8,128)(2,1)}, bf16[336,512]{1,0:T(8,128)(2,1)S(1)}, u32[]{:S(2)}, u32[]{:S(2)}) collective-permute-start(bf16[336,512]{1,0:T(8,128)(2,1)} %get-tuple-element.32.refs_1_.refs_5_), channel_id=1, source_target_pairs={{0,2},{2,0},{1,3},{3,1},{4,6},{6,4},{5,7},{7,5},{8,10},{10,8},{9,1... | collective-permute-start | bytes 1032200 | tf_op jit(solution)/shard_map/ppermute | solution.py:434
  8.6 1.6 copy-start.2
  11.0 1.0 copy-start
  16.0 9.7 %collective-permute-start.4 = (bf16[336,512]{1,0:T(8,128)(2,1)S(1)}, bf16[336,512]{1,0:T(8,128)(2,1)S(1)}, u32[]{:S(2)}, u32[]{:S(2)}) collective-permute-start(bf16[336,512]{1,0:T(8,128)(2,1)S(1)} %collective-permute-done.1.refs_1_.refs_6_), channel_id=1, source_target_pairs={{0,4},{4,8},{8,12},{12,0},{1,5},{5,9},{9,13},{13,1},{2,6},{6,10},{... | collective-permute-start | bytes 1032200 | tf_op jit(solution)/shard_map/ppermute | solution.py:438
  16.0 9.7 %collective-permute-start.6 = (bf16[336,512]{1,0:T(8,128)(2,1)S(1)}, bf16[336,512]{1,0:T(8,128)(2,1)S(1)}, u32[]{:S(2)}, u32[]{:S(2)}) collective-permute-start(bf16[336,512]{1,0:T(8,128)(2,1)S(1)} %collective-permute-done.1.refs_1_.refs_6_), channel_id=1, source_target_pairs={{0,2},{2,0},{1,3},{3,1},{4,6},{6,4},{5,7},{7,5},{8,10},{10,8},{9,1... | collective-permute-start | bytes 1032200 | tf_op jit(solution)/shard_map/ppermute | solution.py:434
  17.2 8.5 %collective-permute-start.5 = (bf16[336,512]{1,0:T(8,128)(2,1)S(1)}, bf16[336,512]{1,0:T(8,128)(2,1)S(1)}, u32[]{:S(2)}, u32[]{:S(2)}) collective-permute-start(bf16[336,512]{1,0:T(8,128)(2,1)S(1)} %collective-permute-done.3.refs_3_.refs_8_), channel_id=1, source_target_pairs={{0,12},{4,0},{8,4},{12,8},{1,13},{5,1},{9,5},{13,9},{2,14},{6,2},{... | collective-permute-start | bytes 1032200 | tf_op jit(solution)/shard_map/ppermute | solution.py:442
  25.7 7.6 %collective-permute-start.8 = (bf16[176,512]{1,0:T(8,128)(2,1)S(1)}, bf16[176,512]{1,0:T(8,128)(2,1)S(1)}, u32[]{:S(2)}, u32[]{:S(2)}) collective-permute-start(bf16[176,512]{1,0:T(8,128)(2,1)S(1)} %slice.10), channel_id=1, source_target_pairs={{0,12},{4,0},{8,4},{12,8},{1,13},{5,1},{9,5},{13,9},{2,14},{6,2},{... | collective-permute-start | bytes 540680 | tf_op jit(solution)/shard_map/ppermute | solution.py:442
  28.7 4.6 %collective-permute-start.7 = (bf16[160,512]{1,0:T(8,128)(2,1)S(1)}, bf16[160,512]{1,0:T(8,128)(2,1)S(1)}, u32[]{:S(2)}, u32[]{:S(2)}) collective-permute-start(bf16[160,512]{1,0:T(8,128)(2,1)S(1)} %slice.9), channel_id=1, source_target_pairs={{0,2},{2,0},{1,3},{3,1},{4,6},{6,4},{5,7},{7,5},{8,10},{10,8},{9,1... | collective-permute-start | bytes 491528 | tf_op jit(solution)/shard_map/ppermute | solution.py:434
  36.5 6.6 %collective-permute-start.9 = (f32[8,136,256]{2,1,0:T(8,128)S(1)}, f32[8,136,256]{2,1,0:T(8,128)S(1)}, u32[]{:S(2)}, u32[]{:S(2)}) collective-permute-start(f32[8,136,256]{2,1,0:T(8,128)S(1)} %side_terms.5), channel_id=1, source_target_pairs={{0,1},{1,0},{2,3},{3,2},{4,5},{5,4},{6,7},{7,6},{8,9},{9,8},{10,11... | collective-permute-start | bytes 3342344 | tf_op jit(solution)/shard_map/ppermute | solution.py:430
  75.4 5.9 %collective-permute-start.10 = (bf16[8,144,256]{2,1,0:T(8,128)(2,1)S(1)}, bf16[8,144,256]{2,1,0:T(8,128)(2,1)S(1)}, u32[]{:S(2)}, u32[]{:S(2)}) collective-permute-start(bf16[8,144,256]{2,1,0:T(8,128)(2,1)S(1)} %all_to_all.41.refs_5_.refs_6_), channel_id=1, source_target_pairs={{0,1},{1,0},{2,3},{3,2},{4,5},{5,4},{6,7},{7,6},{8,9},{9,8},{10,11... | collective-permute-start | bytes 1769480 | tf_op jit(solution)/shard_map/ppermute | solution.py:430
  81.3 15.1 %copy-start.1 = (f32[256,128]{1,0:T(8,128)S(1)}, f32[256,128]{1,0:T(8,128)}, u32[]{:S(2)}) copy-start(f32[256,128]{1,0:T(8,128)} %get-tuple-element.54.refs_5_.refs_1_) | copy-start | bytes 393220
  110.5 4.9 %collective-permute-start.11 = (f32[8,136,256]{2,1,0:T(8,128)S(1)}, f32[8,136,256]{2,1,0:T(8,128)S(1)}, u32[]{:S(2)}, u32[]{:S(2)}) collective-permute-start(f32[8,136,256]{2,1,0:T(8,128)S(1)} %side_terms.7), channel_id=1, source_target_pairs={{0,1},{1,0},{2,3},{3,2},{4,5},{5,4},{6,7},{7,6},{8,9},{9,8},{10,11... | collective-permute-start | bytes 3342344 | tf_op jit(solution)/shard_map/ppermute | solution.py:430
  142.3 5.6 %collective-permute-start.12 = (bf16[8,128,256]{2,1,0:T(8,128)(2,1)S(1)}, bf16[8,128,256]{2,1,0:T(8,128)(2,1)S(1)}, u32[]{:S(2)}, u32[]{:S(2)}) collective-permute-start(bf16[8,128,256]{2,1,0:T(8,128)(2,1)S(1)} %all_to_all.45.refs_5_), channel_id=1, source_target_pairs={{0,1},{1,0},{2,3},{3,2},{4,5},{5,4},{6,7},{7,6},{8,9},{9,8},{10,11... | collective-permute-start | bytes 1572872 | tf_op jit(solution)/shard_map/ppermute | solution.py:430

commit v8 on v7

--- a/solution.py
+++ b/solution.py
@@ -134,7 +134,7 @@
 
 def unit(values):
     shape = jax.ShapeDtypeStruct(values.shape, B16)
-    return call(unit_kernel, [shape], [VMEM], [values], "unit", flops=2 * 10**9)[0]
+    return call(unit_kernel, [shape], [VMEM], [values], "unit", flops=2 * 10**9, mib=12)[0]
 
 
 def build_kernel(counts, groups, block, *refs):
@@ -173,16 +173,17 @@
     half_of(far_ref, MARKS)
 
 
-def build(groups, block, spread, packed, near, far):
+def build(groups, block, spread, packed, near, far, after=()):
     rows = sum(groups) * OWN
     counts = [len(parts) for parts in packed]
     flat = [part for parts in packed for part in parts]
     return call(
-        lambda *refs: build_kernel(counts, groups, block, *refs),
+        lambda *refs: build_kernel(counts, groups, block, *refs[len(after) :]),
         [pltpu.VMEM((rows, 2 * MARKS), B16), jax.ShapeDtypeStruct((8, 2 * MARKS), F32)],
-        [SMEM] + [VMEM] * (len(flat) + 2),
-        [spread, *flat, near, far],
+        [VMEM] * len(after) + [SMEM] + [VMEM] * (len(flat) + 2),
+        [*after, spread, *flat, near, far],
         "build",
+        mib=18,
         scratch=[pltpu.VMEM((rows, WIDTH), F32)],
         flops=4 * rows * 2 * MARKS * 512,
     )
@@ -248,11 +249,11 @@
         "side_terms",
         scratch=[pltpu.VMEM((WIDTH, ROWS), B16)],
         flops=2 * ROWS * MARKS * WIDTH,
+        mib=12,
     )[0]
 
 
 def pair_kernel(first, *refs):
-    refs = refs[TILES:]
     if first:
         own_ref, other_ref, out_ref, pair_ref = refs
     else:
@@ -272,22 +273,22 @@
         out_ref[piece, WIDTH:, :] = tails_in_kernel([means, second, third])
 
 
-def pair(first, tiles, *args):
+def pair(first, keep, *args):
     shapes = [jax.ShapeDtypeStruct((EIGHT, WIDTH + 16, PIECE), B16)]
     if first:
         shapes.append(jax.ShapeDtypeStruct((EIGHT, PIECE), F32))
     return call(
-        lambda *refs: pair_kernel(first, *refs),
+        lambda *refs: pair_kernel(first, *refs[len(keep) :]),
         shapes,
-        [VMEM] * (TILES + len(args)),
-        [*tiles, *args],
+        [VMEM] * (len(keep) + len(args)),
+        [*keep, *args],
         "pair",
         flops=10**9,
+        mib=12,
     )
 
 
 def centre_kernel(first, total_rows, *refs):
-    refs = refs[TILES:]
     if first:
         terms_ref, out_ref, means_ref = refs
     else:
@@ -324,23 +325,46 @@
             out_ref[group, WIDTH:, :] = tail_in_kernel(means)
 
 
-def centre(first, total_rows, tiles, *args):
+def centre(first, total_rows, keep, *args):
     shapes = [jax.ShapeDtypeStruct((EIGHT, WIDTH + 16 * first, PIECE), B16)]
     if first:
         shapes.append(jax.ShapeDtypeStruct((8, PIECE), F32))
     return call(
-        lambda *refs: centre_kernel(first, total_rows, *refs),
+        lambda *refs: centre_kernel(first, total_rows, *refs[len(keep) :]),
         shapes,
-        [VMEM] * (TILES + len(args)),
-        [*tiles, *args],
+        [VMEM] * (len(keep) + len(args)),
+        [*keep, *args],
         "centre",
         flops=10**9,
-    )
-
-
-def image_kernel(base, slots_ref, *refs):
-    tiles, (half_ref, means_ref), refs = refs[:TILES], refs[TILES : TILES + 2], refs[TILES + 2 :]
-    if base:
+        mib=12,
+    )
+
+
+def turn_kernel(base, _, *refs):
+    *tiles, out_ref, done_ref = refs
+    start = 0
+    for tile in tiles:
+        for row in range(0, tile.shape[0], OWN):
+            out_ref[:, start : start + OWN] = jnp.transpose(tile[row : row + OWN, base : base + MARKS])
+            start += OWN
+    done_ref[...] = jnp.zeros(done_ref.shape, F32)
+
+
+def turn(base, slots, tiles):
+    rows = sum(tile.shape[0] for tile in tiles)
+    return call(
+        lambda *refs: turn_kernel(base, *refs),
+        [pltpu.VMEM((MARKS, rows), B16), jax.ShapeDtypeStruct((8, WIDTH), F32)],
+        [SMEM] + [VMEM] * len(tiles),
+        [slots, *tiles],
+        "turn",
+        flops=10**9,
+        mib=12,
+    )
+
+
+def image_kernel(last, slots_ref, early_ref, late_ref, half_ref, means_ref, *refs):
+    if last:
         before_ref, out_ref, side_ref, tail_ref = refs
     else:
         out_ref, side_ref, tail_ref = refs
@@ -348,56 +372,62 @@
         lanes = slice(piece * PIECE, (piece + 1) * PIECE)
         side_ref[:, lanes] = half_ref[piece, :WIDTH, :]
         tail_ref[:, lanes] = means_ref[piece, WIDTH:, :]
-    shift = dot(tail_ref[...], side_ref[...], 1, 1)
-    shift = (shift[2:3] + shift[1:2]) + shift[0:1]
-    slot = 0
-    for tile in tiles:
-        count = tile.shape[0] // OWN
-        term = dot(tile[:, base : base + MARKS], side_ref[...], 1, 1) - shift
-        if base:
-            term = term + before_ref[slot * OWN : (slot + count) * OWN, :]
-            for at in range(count):
-                out_ref[slots_ref[slot + at]] = term[at * OWN : (at + 1) * OWN].astype(B16)
+    shift = dot(side_ref[...], tail_ref[...], 1, 1)
+    shift = (shift[:, 2:3] + shift[:, 1:2]) + shift[:, 0:1]
+    for part, ref in enumerate((early_ref, late_ref)):
+        lanes = slice(part * ROWS // 2, (part + 1) * ROWS // 2)
+        term = dot(side_ref[...], ref[...], 1, 0) - shift
+        if last:
+            term = term + before_ref[:, lanes]
+            for at in range(EIGHT // 2):
+                slot = part * EIGHT // 2 + at
+                out_ref[slots_ref[slot]] = term[:, at * OWN : (at + 1) * OWN].astype(B16)
         else:
-            out_ref[slot * OWN : (slot + count) * OWN, :] = term
-        slot += count
-
-
-def image_terms(slots, tiles, half, means, before=None):
+            out_ref[:, lanes] = term
+
+
+def image_terms(slots, early, late, half, means, before=None):
     if before is None:
-        base, more, shape = 0, [], jax.ShapeDtypeStruct((ROWS, WIDTH), F32)
-    else:
-        base, more, shape = MARKS, [before], jax.ShapeDtypeStruct((EIGHT, OWN, WIDTH), B16)
-    return call(
-        lambda *refs: image_kernel(base, *refs),
+        more, shape = [], jax.ShapeDtypeStruct((WIDTH, ROWS), F32)
+    else:
+        more, shape = [before], jax.ShapeDtypeStruct((EIGHT, WIDTH, OWN), B16)
+    return call(
+        lambda *refs: image_kernel(before is not None, *refs),
         [shape],
-        [SMEM] + [VMEM] * (TILES + 2 + len(more)),
-        [slots, *tiles, half, means, *more],
+        [SMEM] + [VMEM] * (4 + len(more)),
+        [slots, early, late, half, means, *more],
         "image_terms",
         scratch=[pltpu.VMEM((WIDTH, MARKS), B16), pltpu.VMEM((16, MARKS), B16)],
         flops=2 * ROWS * MARKS * WIDTH,
+        mib=12,
     )[0]
 
 
-def owner_kernel(last, *refs):
-    if not last:
-        refs = refs[TILES:]
-    terms_ref, weight_ref, out_ref, *more = refs
+def rows_from(columns):
+    at = lax.broadcasted_iota(jnp.int32, (WIDTH, WIDTH), 1)
+    block = jnp.zeros((WIDTH, WIDTH), F32)
+    for index, column in enumerate(columns):
+        block = jnp.where(at == index, column, block)
+    block = jnp.transpose(block)
+    return [block[index : index + 1] for index in range(len(columns))]
+
+
+def owner_kernel(last, terms_ref, weight_ref, out_ref, *more):
     image = terms_ref[0].astype(F32)
     for member in range(1, EIGHT):
         image = image + terms_ref[member].astype(F32)
-    weight = weight_ref[...]
+    weight = weight_ref[0:1, :]
     image = weight * image
-    squares = jnp.sum(image * image, axis=0, keepdims=True)
+    squares = jnp.sum(image * image, axis=1, keepdims=True)
     if last:
-        out_ref[...] = image
-        more[0][...] = jnp.broadcast_to(squares, (8, WIDTH))
+        out_ref[...] = jnp.transpose(image)
+        more[0][...] = jnp.broadcast_to(rows_from([squares])[0], (8, WIDTH))
     else:
         product = weight * image
-        totals = jnp.sum(product, axis=0, keepdims=True)
-        body = (product * DOWN).astype(B16).astype(F32)
-        rounded = jnp.sum(body, axis=0, keepdims=True)
-        body = jnp.transpose(body).astype(B16)
+        totals = jnp.sum(product, axis=1, keepdims=True)
+        body = (product * DOWN).astype(B16)
+        rounded = jnp.sum(body.astype(F32), axis=1, keepdims=True)
+        totals, squares, rounded = rows_from([totals, squares, rounded])
         first = jnp.concatenate([totals, squares], axis=1)
         second = jnp.concatenate([rounded, jnp.zeros((1, OWN - WIDTH), F32)], axis=1)
         tail = tails_in_kernel([first, second])
@@ -406,19 +436,19 @@
             out_ref[member, WIDTH:, :] = tail
 
 
-def owner(last, tiles, terms, weight):
+def owner(last, keep, terms, weight):
     if last:
         shapes = [jax.ShapeDtypeStruct((OWN, WIDTH), F32), jax.ShapeDtypeStruct((8, WIDTH), F32)]
-        tiles = []
     else:
         shapes = [jax.ShapeDtypeStruct((EIGHT, WIDTH + 16, OWN), B16)]
     return call(
-        lambda *refs: owner_kernel(last, *refs),
+        lambda *refs: owner_kernel(last, *refs[len(keep) :]),
         shapes,
-        [VMEM] * (len(tiles) + 2),
-        [*tiles, terms, weight],
+        [VMEM] * (len(keep) + 2),
+        [*keep, terms, weight],
         "owner",
         flops=10**9,
+        mib=12,
     )
 
 
@@ -442,7 +472,7 @@
     return lax.ppermute(values, "x", [(at, (at + 3) % 4) for at in range(4)])
 
 
-def pack_kernel(rows_hbm, start_hbm, weight_hbm, out_ref, wide_ref, rows_ref, start_ref, weight_ref, sems):
+def pack_kernel(rows_hbm, start_hbm, weight_hbm, out_ref, line_ref, rows_ref, start_ref, weight_ref, sems):
     copies = [
         pltpu.make_async_copy(rows_hbm, rows_ref, sems.at[0]),
         pltpu.make_async_copy(start_hbm, start_ref, sems.at[1]),
@@ -457,7 +487,7 @@
     out_ref[:OWN, :] = (values * scale).astype(B16)
     weight = weight_ref[...]
     wide = jnp.transpose(jnp.broadcast_to(weight, (WIDTH, OWN)))
-    wide_ref[...] = wide
+    line_ref[...] = jnp.broadcast_to(weight, (8, OWN))
     product = wide * start_ref[...]
     totals = jnp.sum(product, axis=0, keepdims=True)
     vectors = jnp.transpose(product).astype(B16)
@@ -469,7 +499,7 @@
 
 
 def pack(rows, start, weight):
-    shapes = [jax.ShapeDtypeStruct((PACK, rows.shape[1]), B16), jax.ShapeDtypeStruct((OWN, WIDTH), F32)]
+    shapes = [jax.ShapeDtypeStruct((PACK, rows.shape[1]), B16), jax.ShapeDtypeStruct((8, OWN), F32)]
     scratch = [
         pltpu.VMEM(rows.shape, B16),
         pltpu.VMEM(start.shape, F32),
@@ -497,11 +527,15 @@
     below, above, across, sums_zero = lax.optimization_barrier((below, above, across, sums_zero))
     opposite, across_above, across_below = from_below(below), from_above(across), swap_z(below)
     one, sums_one = build((3,), 2048, spread, [[below], [above], [across]], near, far)
-    opposite, across_above, across_below, sums_one = lax.optimization_barrier(
-        (opposite, across_above, across_below, sums_one)
+    early_own, done_own = turn(0, slots, [zero, one])
+    early_other, done_other = turn(MARKS, slots, [zero, one])
+    opposite, across_above, across_below, sums_one, done_own, done_other = lax.optimization_barrier(
+        (opposite, across_above, across_below, sums_one, done_own, done_other)
     )
     last = [swap_z(opposite[:SPLIT]), from_above(across_above[SPLIT:])]
-    two, sums_two = build((3,), 2048, spread, [[opposite], [across_above], [across_below]], near, far)
+    two, sums_two = build(
+        (3,), 2048, spread, [[opposite], [across_above], [across_below]], near, far, [done_own, done_other]
+    )
     *last, sums_two = lax.optimization_barrier((*last, sums_two))
     three, sums_three = build((1,), 2048, spread, [last], near, far)
     packs = [packed, below, above, across, opposite, across_above, across_below, *last]
@@ -512,22 +546,30 @@
         other = swap_core(side_terms(step == 0, MARKS, slots, tiles, more))
         own = side_terms(step == 0, 0, slots, tiles, more)
         if step == 0:
-            payload, pair_means = pair(True, tiles, own, other)
-            sides, means = centre(True, total_rows, tiles, exchange(payload, MARK_AXES))
+            late_own, done = turn(0, slots, [two, three])
+            own, done = lax.optimization_barrier((own, done))
+            keep = [*tiles, early_own, late_own, early_other]
+            payload, pair_means = pair(True, keep, own, other)
+            sides, means = centre(True, total_rows, keep, exchange(payload, MARK_AXES))
         else:
-            (payload,) = pair(False, tiles, own, other, pair_means)
-            (sides,) = centre(False, total_rows, tiles, exchange(payload, MARK_AXES), means)
+            keep = []
+            (payload,) = pair(False, keep, own, other, pair_means)
+            (sides,) = centre(False, total_rows, keep, exchange(payload, MARK_AXES), means)
         sides = exchange(sides, MARK_AXES)
         across_core = swap_core(sides)
         if step == 0:
             tails = (sides, across_core)
-        parts = image_terms(slots, tiles, sides, tails[0])
-        parts = image_terms(slots, tiles, across_core, tails[1], parts)
+        parts = image_terms(slots, early_own, late_own, sides, tails[0])
+        if step == 0:
+            parts, after = lax.optimization_barrier((parts, slots))
+            late_other, _ = turn(MARKS, after, [two, three])
+            keep = [*keep, late_other]
+        parts = image_terms(slots, early_other, late_other, across_core, tails[1], parts)
         parts = exchange(parts, ROW_AXES)
         if step + 1 < ITERS:
-            (vectors,) = owner(False, tiles, parts, weight)
+            (vectors,) = owner(False, keep, parts, weight)
             vectors = exchange(vectors, ROW_AXES)
-    image, squares = owner(True, tiles, parts, weight)
+    image, squares = owner(True, [], parts, weight)
     count = lax.axis_size(AXES)
     every = exchange(jnp.broadcast_to(squares[:1][None], (count, 1, WIDTH)), AXES)
     scale = jnp.sqrt(jnp.sum(every[:, 0], axis=0) / total_rows + 1e-06)

time: 179 us -> 182 us (1.017)
  Pallas kernels: 34.3 us -> 39.7 us
  starting transfers between devices: 25.9 us -> 22 us
  local copies, waits for them, and re-layouts: 1.97 us -> 3.99 us
    pallas_call x21 -> x25, Pallas kernels: 34.3 us -> 39.7 us  [call(): pl.pallas_call(kernel, out_shape=shapes, in_specs=specs, out_specs=[VMEM]...]
    unnamed x6 -> x22, local copies, waits for them, and re-layouts: 1.82 us -> 3.84 us
  transfers between devices with their start and end apart: 13 -> 13, of which waited for: 6 -> 4; matrix products, arithmetic and copies ran while one was open for 0% -> 0% of each run, Pallas kernels for 12% -> 16%
where the time goes in v8:
time: 182 us
  blocking collectives  109 us (60%)
  Pallas kernels  39.7 us (22%)
  starting transfers between devices  22 us (12%)
  waiting for transfers between devices  5.36 us (3%)
  local copies, waits for them, and re-layouts  3.99 us (2%)
    all_to_all x8, blocking collectives, exchange(): return lax.all_to_all(payload, axes, 0, 0)  109 us
    pallas_call x25, Pallas kernels, call(): pl.pallas_call(kernel, out_shape=shapes, in_specs=specs, out_specs=[VMEM]...  39.7 us
    ppermute x5, starting transfers between devices, swap_core(): return lax.ppermute(values, 'core', [(0, 1), (1, 0)])  13.2 us
    ppermute x3, starting transfers between devices, from_above(): return lax.ppermute(values, 'x', [(at, (at + 3) % 4) for at in range(4)])  5.41 us
    unnamed x22, local copies, waits for them, and re-layouts  3.84 us
  transfers between devices with their start and end apart: 13, of which 4 were waited for; matrix products, arithmetic and copies ran while one was open for 0% of the time, Pallas kernels for 16%

profile of v8, /device:TPU:1, one launch (start us, length us, event | category | flops | bytes accessed | tf_op | source)
XLA Modules:
  0.0 181.8 jit_solution(4523330444448588906)
XLA Ops:
  0.0 1.4 collective-permute-start
  1.4 2.0 %pack.1 = (bf16[336,512]{1,0:T(8,128)(2,1)}, f32[8,256]{1,0:T(8,128)}) custom-call(bf16[256,512]{1,0:T(8,128)(2,1)} %rows_hbm.1, f32[256,128]{1,0:T(8,128)} %start_hbm.1, f32[1,256]{1,0:T(1,128)} %bitcast.13), custom_call_target="tpu_custom_call" | custom-call | tf_op jit(solution)/shard_map/pack/pallas_call | solution.py:91
  3.4 1.8 collective-permute-start.3
  5.2 2.5 %collective-permute-start.2 = (bf16[336,512]{1,0:T(8,128)(2,1)}, bf16[336,512]{1,0:T(8,128)(2,1)S(1)}, u32[]{:S(2)}, u32[]{:S(2)}) collective-permute-start(bf16[336,512]{1,0:T(8,128)(2,1)} %get-tuple-element.42.refs_1_.refs_5_), channel_id=1, source_target_pairs={{0,12},{4,0},{8,4},{12,8},{1,13},{5,1},{9,5},{13,9},{2,14},{6,2},{... | collective-permute-start | bytes 1032200 | tf_op jit(solution)/shard_map/ppermute | solution.py:472
  8.4 1.6 copy-done.10
  10.0 0.7 unit.2.refs_2_.refs_4_.refs_6_.refs_3_
  10.8 2.4 %unit.3.refs_3_.refs_5_.refs_7_.refs_4_ = bf16[2048,512]{1,0:T(8,128)(2,1)S(1)} custom-call(bf16[2048,512]{1,0:T(8,128)(2,1)} %collective-permute-done.in_ref), custom_call_target="tpu_custom_call" | custom-call | flops 2000000000 | tf_op jit(solution)/shard_map/unit/pallas_call | solution.py:91
  13.2 1.3 build.4
  14.5 0.7 collective-permute-done.2.refs_2_.refs_7_
  15.2 3.0 %collective-permute-done.1.refs_1_.refs_6_ = bf16[336,512]{1,0:T(8,128)(2,1)S(1)} collective-permute-done((bf16[336,512]{1,0:T(8,128)(2,1)}, bf16[336,512]{1,0:T(8,128)(2,1)S(1)}, u32[]{:S(2)}, u32[]{:S(2)}) %collective-permute-start.1) | collective-permute-done | bytes 344096 | tf_op jit(solution)/shard_map/ppermute | solution.py:468
  18.2 0.4 collective-permute-start.6
  18.5 2.7 %collective-permute-start.5 = (bf16[336,512]{1,0:T(8,128)(2,1)S(1)}, bf16[336,512]{1,0:T(8,128)(2,1)S(1)}, u32[]{:S(2)}, u32[]{:S(2)}) collective-permute-start(bf16[336,512]{1,0:T(8,128)(2,1)S(1)} %collective-permute-done.3.refs_3_.refs_8_), channel_id=1, source_target_pairs={{0,12},{4,0},{8,4},{12,8},{1,13},{5,1},{9,5},{13,9},{2,14},{6,2},{... | collective-permute-start | bytes 1032200 | tf_op jit(solution)/shard_map/ppermute | solution.py:472
  21.2 3.5 %build.5 = (bf16[768,4096]{1,0:T(8,128)(2,1)S(1)}, f32[8,4096]{1,0:T(8,128)S(1)}) custom-call(f32[1]{0:T(128)S(6)} %copy.7.refs_0_.refs_2_, bf16[336,512]{1,0:T(8,128)(2,1)S(1)} %collective-permute-done.1.refs_1_.refs_6_, bf16[336,512]{1,0:T(8,128)(2,1)S(1)} %collective-permute-done.2.refs_2_.refs_7_, ...), custom_call_target="tpu_custom_call" | custom-call | flops 6442450944 | tf_op jit(solution)/shard_map/build/pallas_call | solution.py:91
  24.7 1.8 turn.5
  26.5 1.8 turn.4
  28.3 2.0 %copy-done = bf16[2048,1024]{1,0:T(8,128)(2,1)} copy-done((bf16[2048,1024]{1,0:T(8,128)(2,1)}, bf16[2048,1024]{1,0:T(8,128)(2,1)S(1)}, u32[]{:S(2)}) %copy-start) | copy-done | bytes 4194328
  30.4 1.2 collective-permute-start.7
  31.8 3.5 %build.6 = (bf16[768,4096]{1,0:T(8,128)(2,1)S(1)}, f32[8,4096]{1,0:T(8,128)S(1)}) custom-call(f32[8,128]{1,0:T(8,128)S(1)} %get-tuple-element.54.refs_0_, f32[8,128]{1,0:T(8,128)S(1)} %get-tuple-element.55.refs_1_, f32[1]{0:T(128)S(6)} %copy.7.refs_0_.refs_2_, bf16[336,512]{1,0:T(8,128)(2,1)S(1)} %collective-permute-done.4.refs_3_.refs_9_, ...), custom_call_target="tpu_custom_call" | custom-call | flops 6442450944 | tf_op jit(solution)/shard_map/build/pallas_call | solution.py:91
  35.4 1.1 collective-permute-done.8.refs_2_.refs_13_
  36.5 1.4 build.7
  37.8 1.8 side_terms.5
  39.6 3.5 %collective-permute-start.9 = (f32[8,136,256]{2,1,0:T(8,128)S(1)}, f32[8,136,256]{2,1,0:T(8,128)S(1)}, u32[]{:S(2)}, u32[]{:S(2)}) collective-permute-start(f32[8,136,256]{2,1,0:T(8,128)S(1)} %side_terms.5), channel_id=1, source_target_pairs={{0,1},{1,0},{2,3},{3,2},{4,5},{5,4},{6,7},{7,6},{8,9},{9,8},{10,11... | collective-permute-start | bytes 3342344 | tf_op jit(solution)/shard_map/ppermute | solution.py:460
  43.1 1.8 side_terms.4.refs_7_
  44.9 2.3 %turn.6 = (bf16[2048,1024]{1,0:T(8,128)(2,1)S(1)}, f32[8,128]{1,0:T(8,128)}) custom-call(s32[8]{0:T(128)S(1)} %stack.35.refs_0_, bf16[768,4096]{1,0:T(8,128)(2,1)S(1)} %get-tuple-element.59.refs_1_.refs_3_.refs_2_, bf16[256,4096]{1,0:T(8,128)(2,1)S(1)} %get-tuple-element.63.refs_2_.refs_4_.refs_3_), custom_call_target="tpu_custom_call" | custom-call | flops 1000000000 | tf_op jit(solution)/shard_map/turn/pallas_call | solution.py:91
  47.2 0.3 pair.2
  47.6 18.8 %all_to_all.40.refs_7_ = bf16[8,144,256]{2,1,0:T(8,128)(2,1)S(1)} all-to-all(bf16[8,144,256]{2,1,0:T(8,128)(2,1)S(1)} %get-tuple-element.69), channel_id=1, replica_groups=mesh['y'=4,'zh'=2,'x'=4,'zl'=2,'core'=2] {'y','zh'}, dimensions={0} | all-to-all | bytes 1179648 | tf_op jit(solution)/shard_map/all_to_all | solution.py:456
  66.4 0.4 centre.2
  66.8 13.0 %all_to_all.41.refs_3_.refs_4_ = bf16[8,144,256]{2,1,0:T(8,128)(2,1)S(1)} all-to-all(bf16[8,144,256]{2,1,0:T(8,128)(2,1)S(1)} %get-tuple-element.70), channel_id=1, replica_groups=mesh['y'=4,'zh'=2,'x'=4,'zl'=2,'core'=2] {'y','zh'}, dimensions={0} | all-to-all | bytes 1179648 | tf_op jit(solution)/shard_map/all_to_all | solution.py:456
  79.8 2.8 %collective-permute-start.10 = (bf16[8,144,256]{2,1,0:T(8,128)(2,1)S(1)}, bf16[8,144,256]{2,1,0:T(8,128)(2,1)S(1)}, u32[]{:S(2)}, u32[]{:S(2)}) collective-permute-start(bf16[8,144,256]{2,1,0:T(8,128)(2,1)S(1)} %all_to_all.41.refs_3_.refs_4_), channel_id=1, source_target_pairs={{0,1},{1,0},{2,3},{3,2},{4,5},{5,4},{6,7},{7,6},{8,9},{9,8},{10,11... | collective-permute-start | bytes 1769480 | tf_op jit(solution)/shard_map/ppermute | solution.py:460
  82.6 1.9 %image_terms.4.refs_5_ = f32[128,2048]{1,0:T(8,128)S(1)} custom-call(s32[8]{0:T(128)S(1)} %stack.35.refs_0_, bf16[2048,1024]{1,0:T(8,128)(2,1)S(1)} %get-tuple-element.50.refs_4_.refs_1_, bf16[2048,1024]{1,0:T(8,128)(2,1)S(1)} %get-tuple-element.64.refs_5_.refs_2_, bf16[8,144,256]{2,1,0:T(8,128)(2,1)S(1)} %all_to_all.41.refs_3_.refs_4_, ...), custom_call_target="tpu_custom_call" | custom-call | flops 1073741824 | tf_op jit(solution)/shard_map/image_terms/pallas_call | solution.py:91
  84.5 2.3 %turn.7 = (bf16[2048,1024]{1,0:T(8,128)(2,1)S(1)}, f32[8,128]{1,0:T(8,128)}) custom-call(s32[8]{0:T(128)S(1)} %stack.35.refs_0_, bf16[768,4096]{1,0:T(8,128)(2,1)S(1)} %get-tuple-element.59.refs_1_.refs_3_.refs_2_, bf16[256,4096]{1,0:T(8,128)(2,1)S(1)} %get-tuple-element.63.refs_2_.refs_4_.refs_3_), custom_call_target="tpu_custom_call" | custom-call | flops 1000000000 | tf_op jit(solution)/shard_map/turn/pallas_call | solution.py:91
  86.8 2.0 %image_terms.5 = bf16[8,128,256]{2,1,0:T(8,128)(2,1)S(1)} custom-call(s32[8]{0:T(128)S(1)} %stack.35.refs_0_, bf16[2048,1024]{1,0:T(8,128)(2,1)S(1)} %copy-done.1, bf16[2048,1024]{1,0:T(8,128)(2,1)S(1)} %get-tuple-element.72.refs_2_.refs_7_, bf16[8,144,256]{2,1,0:T(8,128)(2,1)S(1)} %collective-permute-done.10.refs_3_.refs_4_, ...), custom_call_target="tpu_custom_call" | custom-call | flops 1073741824 | tf_op jit(solution)/shard_map/image_terms/pallas_call | solution.py:91
  88.8 12.4 %all_to_all.42.refs_8_ = bf16[8,128,256]{2,1,0:T(8,128)(2,1)S(1)} all-to-all(bf16[8,128,256]{2,1,0:T(8,128)(2,1)S(1)} %image_terms.5), channel_id=1, replica_groups=mesh['y'=4,'zh'=2,'x'=4,'zl'=2,'core'=2] {'x','zl'}, dimensions={0} | all-to-all | bytes 1048576 | tf_op jit(solution)/shard_map/all_to_all | solution.py:456
  101.4 11.7 %all_to_all.43.refs_5_ = bf16[8,144,256]{2,1,0:T(8,128)(2,1)S(1)} all-to-all(bf16[8,144,256]{2,1,0:T(8,128)(2,1)S(1)} %owner.2), channel_id=1, replica_groups=mesh['y'=4,'zh'=2,'x'=4,'zl'=2,'core'=2] {'x','zl'}, dimensions={0} | all-to-all | bytes 1179648 | tf_op jit(solution)/shard_map/all_to_all | solution.py:456
  113.1 1.8 side_terms.7
  114.9 2.9 %collective-permute-start.11 = (f32[8,136,256]{2,1,0:T(8,128)S(1)}, f32[8,136,256]{2,1,0:T(8,128)S(1)}, u32[]{:S(2)}, u32[]{:S(2)}) collective-permute-start(f32[8,136,256]{2,1,0:T(8,128)S(1)} %side_terms.7), channel_id=1, source_target_pairs={{0,1},{1,0},{2,3},{3,2},{4,5},{5,4},{6,7},{7,6},{8,9},{9,8},{10,11... | collective-permute-start | bytes 3342344 | tf_op jit(solution)/shard_map/ppermute | solution.py:460
  117.7 1.8 side_terms.6.refs_0_
  119.5 0.6 collective-permute-done.11.refs_1_
  120.1 0.3 pair.3
  120.4 13.8 %all_to_all.44.refs_0_ = bf16[8,144,256]{2,1,0:T(8,128)(2,1)S(1)} all-to-all(bf16[8,144,256]{2,1,0:T(8,128)(2,1)S(1)} %pair.3), channel_id=1, replica_groups=mesh['y'=4,'zh'=2,'x'=4,'zl'=2,'core'=2] {'y','zh'}, dimensions={0} | all-to-all | bytes 1179648 | tf_op jit(solution)/shard_map/all_to_all | solution.py:456
  134.2 0.4 centre.3
  134.6 12.6 %all_to_all.45.refs_3_ = bf16[8,128,256]{2,1,0:T(8,128)(2,1)S(1)} all-to-all(bf16[8,128,256]{2,1,0:T(8,128)(2,1)S(1)} %centre.3), channel_id=1, replica_groups=mesh['y'=4,'zh'=2,'x'=4,'zl'=2,'core'=2] {'y','zh'}, dimensions={0} | all-to-all | bytes 1048576 | tf_op jit(solution)/shard_map/all_to_all | solution.py:456
  147.2 2.6 %collective-permute-start.12 = (bf16[8,128,256]{2,1,0:T(8,128)(2,1)S(1)}, bf16[8,128,256]{2,1,0:T(8,128)(2,1)S(1)}, u32[]{:S(2)}, u32[]{:S(2)}) collective-permute-start(bf16[8,128,256]{2,1,0:T(8,128)(2,1)S(1)} %all_to_all.45.refs_3_), channel_id=1, source_target_pairs={{0,1},{1,0},{2,3},{3,2},{4,5},{5,4},{6,7},{7,6},{8,9},{9,8},{10,11... | collective-permute-start | bytes 1572872 | tf_op jit(solution)/shard_map/ppermute | solution.py:460
  149.8 1.9 %image_terms.6.refs_5_ = f32[128,2048]{1,0:T(8,128)S(1)} custom-call(s32[8]{0:T(128)S(1)} %stack.35.refs_0_, bf16[2048,1024]{1,0:T(8,128)(2,1)S(1)} %copy-done.3, bf16[2048,1024]{1,0:T(8,128)(2,1)S(1)} %copy-done.5, bf16[8,128,256]{2,1,0:T(8,128)(2,1)S(1)} %all_to_all.45.refs_3_, bf16[8,144,256]{2,1,0:T(8,128)(2,1)S(1)} %all_to_all.41.refs_3_.refs_4_), custom_call_target="tpu_custom_call" | custom-call | flops 1073741824 | tf_op jit(solution)/shard_map/image_terms/pallas_call | solution.py:91
  152.0 1.9 %image_terms.7 = bf16[8,128,256]{2,1,0:T(8,128)(2,1)S(1)} custom-call(s32[8]{0:T(128)S(1)} %stack.35.refs_0_, bf16[2048,1024]{1,0:T(8,128)(2,1)S(1)} %copy-done.1, bf16[2048,1024]{1,0:T(8,128)(2,1)S(1)} %copy-done.7, bf16[8,128,256]{2,1,0:T(8,128)(2,1)S(1)} %collective-permute-done.12.refs_3_, ...), custom_call_target="tpu_custom_call" | custom-call | flops 1073741824 | tf_op jit(solution)/shard_map/image_terms/pallas_call | solution.py:91
  153.9 12.0 %all_to_all.46.refs_0_ = bf16[8,128,256]{2,1,0:T(8,128)(2,1)S(1)} all-to-all(bf16[8,128,256]{2,1,0:T(8,128)(2,1)S(1)} %image_terms.7), channel_id=1, replica_groups=mesh['y'=4,'zh'=2,'x'=4,'zl'=2,'core'=2] {'x','zl'}, dimensions={0} | all-to-all | bytes 1048576 | tf_op jit(solution)/shard_map/all_to_all | solution.py:456
  166.2 14.8 %all_to_all.47 = f32[128,1,128]{2,1,0:T(1,128)S(1)} all-to-all(f32[128,1,128]{2,1,0:T(1,128)S(1)} %broadcast_in_dim.14), channel_id=1, replica_groups=mesh['y'=4,'zh'=2,'x'=4,'zl'=2,'core'=2] {'y','zh','x','zl','core'}, dimensions={0} | all-to-all | bytes 131072 | tf_op jit(solution)/shard_map/all_to_all | solution.py:456
  181.1 0.7 broadcast_divide_fusion
  (41 shorter events, 1.2 us)
Async XLA Ops:
  0.0 10.8 %collective-permute-start = (bf16[2048,512]{1,0:T(8,128)(2,1)}, bf16[2048,512]{1,0:T(8,128)(2,1)}, u32[]{:S(2)}, u32[]{:S(2)}) collective-permute-start(bf16[2048,512]{1,0:T(8,128)(2,1)} %in_ref.1), channel_id=1, source_target_pairs={{0,1},{1,0},{2,3},{3,2},{4,5},{5,4},{6,7},{7,6},{8,9},{9,8},{10,11... | collective-permute-start | bytes 6291464 | tf_op jit(solution)/shard_map/ppermute | solution.py:460
  3.4 11.1 %collective-permute-start.3 = (bf16[336,512]{1,0:T(8,128)(2,1)}, bf16[336,512]{1,0:T(8,128)(2,1)S(1)}, u32[]{:S(2)}, u32[]{:S(2)}) collective-permute-start(bf16[336,512]{1,0:T(8,128)(2,1)} %get-tuple-element.42.refs_1_.refs_5_), channel_id=1, source_target_pairs={{0,2},{2,0},{1,3},{3,1},{4,6},{6,4},{5,7},{7,5},{8,10},{10,8},{9,1... | collective-permute-start | bytes 1032200 | tf_op jit(solution)/shard_map/ppermute | solution.py:464
  5.2 10.0 %collective-permute-start.2 = (bf16[336,512]{1,0:T(8,128)(2,1)}, bf16[336,512]{1,0:T(8,128)(2,1)S(1)}, u32[]{:S(2)}, u32[]{:S(2)}) collective-permute-start(bf16[336,512]{1,0:T(8,128)(2,1)} %get-tuple-element.42.refs_1_.refs_5_), channel_id=1, source_target_pairs={{0,12},{4,0},{8,4},{12,8},{1,13},{5,1},{9,5},{13,9},{2,14},{6,2},{... | collective-permute-start | bytes 1032200 | tf_op jit(solution)/shard_map/ppermute | solution.py:472
  7.7 10.5 %collective-permute-start.1 = (bf16[336,512]{1,0:T(8,128)(2,1)}, bf16[336,512]{1,0:T(8,128)(2,1)S(1)}, u32[]{:S(2)}, u32[]{:S(2)}) collective-permute-start(bf16[336,512]{1,0:T(8,128)(2,1)} %get-tuple-element.42.refs_1_.refs_5_), channel_id=1, source_target_pairs={{0,4},{4,8},{8,12},{12,0},{1,5},{5,9},{9,13},{13,1},{2,6},{6,10},{... | collective-permute-start | bytes 1032200 | tf_op jit(solution)/shard_map/ppermute | solution.py:468
  8.4 1.6 copy-start.10
  10.8 2.4 %copy-start.8 = (bf16[336,512]{1,0:T(8,128)(2,1)S(1)}, bf16[336,512]{1,0:T(8,128)(2,1)}, u32[]{:S(2)}) copy-start(bf16[336,512]{1,0:T(8,128)(2,1)} %get-tuple-element.42.refs_1_.refs_5_) | copy-start | bytes 1032196
  18.2 12.2 %collective-permute-start.6 = (bf16[336,512]{1,0:T(8,128)(2,1)S(1)}, bf16[336,512]{1,0:T(8,128)(2,1)S(1)}, u32[]{:S(2)}, u32[]{:S(2)}) collective-permute-start(bf16[336,512]{1,0:T(8,128)(2,1)S(1)} %collective-permute-done.1.refs_1_.refs_6_), channel_id=1, source_target_pairs={{0,2},{2,0},{1,3},{3,1},{4,6},{6,4},{5,7},{7,5},{8,10},{10,8},{9,1... | collective-permute-start | bytes 1032200 | tf_op jit(solution)/shard_map/ppermute | solution.py:464
  18.5 11.8 %collective-permute-start.4 = (bf16[336,512]{1,0:T(8,128)(2,1)S(1)}, bf16[336,512]{1,0:T(8,128)(2,1)S(1)}, u32[]{:S(2)}, u32[]{:S(2)}) collective-permute-start(bf16[336,512]{1,0:T(8,128)(2,1)S(1)} %collective-permute-done.1.refs_1_.refs_6_), channel_id=1, source_target_pairs={{0,4},{4,8},{8,12},{12,0},{1,5},{5,9},{9,13},{13,1},{2,6},{6,10},{... | collective-permute-start | bytes 1032200 | tf_op jit(solution)/shard_map/ppermute | solution.py:468
  18.5 11.8 %collective-permute-start.5 = (bf16[336,512]{1,0:T(8,128)(2,1)S(1)}, bf16[336,512]{1,0:T(8,128)(2,1)S(1)}, u32[]{:S(2)}, u32[]{:S(2)}) collective-permute-start(bf16[336,512]{1,0:T(8,128)(2,1)S(1)} %collective-permute-done.3.refs_3_.refs_8_), channel_id=1, source_target_pairs={{0,12},{4,0},{8,4},{12,8},{1,13},{5,1},{9,5},{13,9},{2,14},{6,2},{... | collective-permute-start | bytes 1032200 | tf_op jit(solution)/shard_map/ppermute | solution.py:472
  26.5 74.6 %copy-start.2 = (bf16[2048,1024]{1,0:T(8,128)(2,1)}, bf16[2048,1024]{1,0:T(8,128)(2,1)S(1)}, u32[]{:S(2)}) copy-start(bf16[2048,1024]{1,0:T(8,128)(2,1)S(1)} %get-tuple-element.50.refs_4_.refs_1_) | copy-start | bytes 12582916
  28.3 2.0 %copy-start = (bf16[2048,1024]{1,0:T(8,128)(2,1)}, bf16[2048,1024]{1,0:T(8,128)(2,1)S(1)}, u32[]{:S(2)}) copy-start(bf16[2048,1024]{1,0:T(8,128)(2,1)S(1)} %get-tuple-element.49.refs_6_.refs_1_) | copy-start | bytes 12582916
  30.4 5.0 %collective-permute-start.7 = (bf16[160,512]{1,0:T(8,128)(2,1)S(1)}, bf16[160,512]{1,0:T(8,128)(2,1)S(1)}, u32[]{:S(2)}, u32[]{:S(2)}) collective-permute-start(bf16[160,512]{1,0:T(8,128)(2,1)S(1)} %slice.9), channel_id=1, source_target_pairs={{0,2},{2,0},{1,3},{3,1},{4,6},{6,4},{5,7},{7,5},{8,10},{10,8},{9,1... | collective-permute-start | bytes 491528 | tf_op jit(solution)/shard_map/ppermute | solution.py:464
  31.6 4.9 %collective-permute-start.8 = (bf16[176,512]{1,0:T(8,128)(2,1)S(1)}, bf16[176,512]{1,0:T(8,128)(2,1)S(1)}, u32[]{:S(2)}, u32[]{:S(2)}) collective-permute-start(bf16[176,512]{1,0:T(8,128)(2,1)S(1)} %slice.10), channel_id=1, source_target_pairs={{0,12},{4,0},{8,4},{12,8},{1,13},{5,1},{9,5},{13,9},{2,14},{6,2},{... | collective-permute-start | bytes 540680 | tf_op jit(solution)/shard_map/ppermute | solution.py:472
  39.6 7.6 %collective-permute-start.9 = (f32[8,136,256]{2,1,0:T(8,128)S(1)}, f32[8,136,256]{2,1,0:T(8,128)S(1)}, u32[]{:S(2)}, u32[]{:S(2)}) collective-permute-start(f32[8,136,256]{2,1,0:T(8,128)S(1)} %side_terms.5), channel_id=1, source_target_pairs={{0,1},{1,0},{2,3},{3,2},{4,5},{5,4},{6,7},{7,6},{8,9},{9,8},{10,11... | collective-permute-start | bytes 3342344 | tf_op jit(solution)/shard_map/ppermute | solution.py:460
  44.9 2.3 %copy-start.1 = (bf16[2048,1024]{1,0:T(8,128)(2,1)S(1)}, bf16[2048,1024]{1,0:T(8,128)(2,1)}, u32[]{:S(2)}) copy-start(bf16[2048,1024]{1,0:T(8,128)(2,1)} %copy-done) | copy-start | bytes 12582916
  47.2 35.4 %copy-start.4 = (bf16[2048,1024]{1,0:T(8,128)(2,1)}, bf16[2048,1024]{1,0:T(8,128)(2,1)S(1)}, u32[]{:S(2)}) copy-start(bf16[2048,1024]{1,0:T(8,128)(2,1)S(1)} %get-tuple-element.64.refs_5_.refs_2_) | copy-start | bytes 12582916
  79.8 7.0 %collective-permute-start.10 = (bf16[8,144,256]{2,1,0:T(8,128)(2,1)S(1)}, bf16[8,144,256]{2,1,0:T(8,128)(2,1)S(1)}, u32[]{:S(2)}, u32[]{:S(2)}) collective-permute-start(bf16[8,144,256]{2,1,0:T(8,128)(2,1)S(1)} %all_to_all.41.refs_3_.refs_4_), channel_id=1, source_target_pairs={{0,1},{1,0},{2,3},{3,2},{4,5},{5,4},{6,7},{7,6},{8,9},{9,8},{10,11... | collective-permute-start | bytes 1769480 | tf_op jit(solution)/shard_map/ppermute | solution.py:460
  86.8 14.4 %copy-start.6 = (bf16[2048,1024]{1,0:T(8,128)(2,1)}, bf16[2048,1024]{1,0:T(8,128)(2,1)S(1)}, u32[]{:S(2)}) copy-start(bf16[2048,1024]{1,0:T(8,128)(2,1)S(1)} %get-tuple-element.72.refs_2_.refs_7_) | copy-start | bytes 12582916
  86.8 14.4 %copy-start.5 = (bf16[2048,1024]{1,0:T(8,128)(2,1)S(1)}, bf16[2048,1024]{1,0:T(8,128)(2,1)}, u32[]{:S(2)}) copy-start(bf16[2048,1024]{1,0:T(8,128)(2,1)} %copy-done.4) | copy-start | bytes 12582916
  86.8 14.4 %copy-start.9 = (f32[8,256]{1,0:T(8,128)S(1)}, f32[8,256]{1,0:T(8,128)}, u32[]{:S(2)}) copy-start(f32[8,256]{1,0:T(8,128)} %get-tuple-element.74.refs_9_.refs_1_) | copy-start | bytes 24580
  114.9 5.2 %collective-permute-start.11 = (f32[8,136,256]{2,1,0:T(8,128)S(1)}, f32[8,136,256]{2,1,0:T(8,128)S(1)}, u32[]{:S(2)}, u32[]{:S(2)}) collective-permute-start(f32[8,136,256]{2,1,0:T(8,128)S(1)} %side_terms.7), channel_id=1, source_target_pairs={{0,1},{1,0},{2,3},{3,2},{4,5},{5,4},{6,7},{7,6},{8,9},{9,8},{10,11... | collective-permute-start | bytes 3342344 | tf_op jit(solution)/shard_map/ppermute | solution.py:460
  134.2 15.7 %copy-start.3 = (bf16[2048,1024]{1,0:T(8,128)(2,1)S(1)}, bf16[2048,1024]{1,0:T(8,128)(2,1)}, u32[]{:S(2)}) copy-start(bf16[2048,1024]{1,0:T(8,128)(2,1)} %copy-done.2) | copy-start | bytes 12582916
  147.2 4.6 %collective-permute-start.12 = (bf16[8,128,256]{2,1,0:T(8,128)(2,1)S(1)}, bf16[8,128,256]{2,1,0:T(8,128)(2,1)S(1)}, u32[]{:S(2)}, u32[]{:S(2)}) collective-permute-start(bf16[8,128,256]{2,1,0:T(8,128)(2,1)S(1)} %all_to_all.45.refs_3_), channel_id=1, source_target_pairs={{0,1},{1,0},{2,3},{3,2},{4,5},{5,4},{6,7},{7,6},{8,9},{9,8},{10,11... | collective-permute-start | bytes 1572872 | tf_op jit(solution)/shard_map/ppermute | solution.py:460
  149.8 2.2 %copy-start.7 = (bf16[2048,1024]{1,0:T(8,128)(2,1)S(1)}, bf16[2048,1024]{1,0:T(8,128)(2,1)}, u32[]{:S(2)}) copy-start(bf16[2048,1024]{1,0:T(8,128)(2,1)} %copy-done.6) | copy-start | bytes 12582916

commit v9 on v8

--- a/solution.py
+++ b/solution.py
@@ -363,7 +363,7 @@
     )
 
 
-def image_kernel(last, slots_ref, early_ref, late_ref, half_ref, means_ref, *refs):
+def image_kernel(base, last, slots_ref, early_ref, two_ref, three_ref, half_ref, means_ref, *refs):
     if last:
         before_ref, out_ref, side_ref, tail_ref = refs
     else:
@@ -374,28 +374,33 @@
         tail_ref[:, lanes] = means_ref[piece, WIDTH:, :]
     shift = dot(side_ref[...], tail_ref[...], 1, 1)
     shift = (shift[:, 2:3] + shift[:, 1:2]) + shift[:, 0:1]
-    for part, ref in enumerate((early_ref, late_ref)):
-        lanes = slice(part * ROWS // 2, (part + 1) * ROWS // 2)
-        term = dot(side_ref[...], ref[...], 1, 0) - shift
+    start = 0
+    for ref in (early_ref, two_ref, three_ref):
+        if start == 0:
+            term = dot(side_ref[...], ref[...], 1, 0)
+        else:
+            term = jnp.transpose(dot(ref[:, base : base + MARKS], side_ref[...], 1, 1))
+        term = term - shift
+        stop = start + term.shape[1]
         if last:
-            term = term + before_ref[:, lanes]
-            for at in range(EIGHT // 2):
-                slot = part * EIGHT // 2 + at
-                out_ref[slots_ref[slot]] = term[:, at * OWN : (at + 1) * OWN].astype(B16)
+            term = term + before_ref[:, start:stop]
+            for at in range(0, stop - start, OWN):
+                out_ref[slots_ref[(start + at) // OWN]] = term[:, at : at + OWN].astype(B16)
         else:
-            out_ref[:, lanes] = term
-
-
-def image_terms(slots, early, late, half, means, before=None):
+            out_ref[:, start:stop] = term
+        start = stop
+
+
+def image_terms(slots, base, early, late, half, means, before=None):
     if before is None:
         more, shape = [], jax.ShapeDtypeStruct((WIDTH, ROWS), F32)
     else:
         more, shape = [before], jax.ShapeDtypeStruct((EIGHT, WIDTH, OWN), B16)
     return call(
-        lambda *refs: image_kernel(before is not None, *refs),
+        lambda *refs: image_kernel(base, before is not None, *refs),
         [shape],
-        [SMEM] + [VMEM] * (4 + len(more)),
-        [slots, early, late, half, means, *more],
+        [SMEM] + [VMEM] * (5 + len(more)),
+        [slots, early, *late, half, means, *more],
         "image_terms",
         scratch=[pltpu.VMEM((WIDTH, MARKS), B16), pltpu.VMEM((16, MARKS), B16)],
         flops=2 * ROWS * MARKS * WIDTH,
@@ -546,25 +551,18 @@
         other = swap_core(side_terms(step == 0, MARKS, slots, tiles, more))
         own = side_terms(step == 0, 0, slots, tiles, more)
         if step == 0:
-            late_own, done = turn(0, slots, [two, three])
-            own, done = lax.optimization_barrier((own, done))
-            keep = [*tiles, early_own, late_own, early_other]
+            keep = [*tiles, early_own, early_other]
             payload, pair_means = pair(True, keep, own, other)
             sides, means = centre(True, total_rows, keep, exchange(payload, MARK_AXES))
         else:
-            keep = []
             (payload,) = pair(False, keep, own, other, pair_means)
             (sides,) = centre(False, total_rows, keep, exchange(payload, MARK_AXES), means)
         sides = exchange(sides, MARK_AXES)
         across_core = swap_core(sides)
         if step == 0:
             tails = (sides, across_core)
-        parts = image_terms(slots, early_own, late_own, sides, tails[0])
-        if step == 0:
-            parts, after = lax.optimization_barrier((parts, slots))
-            late_other, _ = turn(MARKS, after, [two, three])
-            keep = [*keep, late_other]
-        parts = image_terms(slots, early_other, late_other, across_core, tails[1], parts)
+        parts = image_terms(slots, 0, early_own, (two, three), sides, tails[0])
+        parts = image_terms(slots, MARKS, early_other, (two, three), across_core, tails[1], parts)
         parts = exchange(parts, ROW_AXES)
         if step + 1 < ITERS:
             (vectors,) = owner(False, keep, parts, weight)

time: 182 us -> 180 us (0.989)
  Pallas kernels: 39.7 us -> 36.2 us
  local copies, waits for them, and re-layouts: 3.99 us -> 1.97 us
    pallas_call x25 -> x23, Pallas kernels: 39.7 us -> 36.2 us  [call(): pl.pallas_call(kernel, out_shape=shapes, in_specs=specs, out_specs=[VMEM]...]
    unnamed x22 -> x6, local copies, waits for them, and re-layouts: 3.84 us -> 1.82 us
  transfers between devices with their start and end apart: 13 -> 13, of which waited for: 4 -> 5; matrix products, arithmetic and copies ran while one was open for 0% -> 0% of each run, Pallas kernels for 16% -> 13%
where the time goes in v9:
time: 180 us; the launch traced here: 179 us
  blocking collectives  110 us (61%)
  Pallas kernels  36.2 us (20%)
  starting transfers between devices  23.8 us (13%)
  waiting for transfers between devices  6.26 us (3%)
  local copies, waits for them, and re-layouts  1.97 us (1%)
    all_to_all x8, blocking collectives, exchange(): return lax.all_to_all(payload, axes, 0, 0)  110 us
    pallas_call x23, Pallas kernels, call(): pl.pallas_call(kernel, out_shape=shapes, in_specs=specs, out_specs=[VMEM]...  36.2 us
    ppermute x5, starting transfers between devices, swap_core(): return lax.ppermute(values, 'core', [(0, 1), (1, 0)])  13.4 us
    ppermute x3, starting transfers between devices, from_above(): return lax.ppermute(values, 'x', [(at, (at + 3) % 4) for at in range(4)])  7.06 us
  transfers between devices with their start and end apart: 13, of which 5 were waited for; matrix products, arithmetic and copies ran while one was open for 0% of the time, Pallas kernels for 13%

profile of v9, /device:TPU:1, one launch (start us, length us, event | category | flops | bytes accessed | tf_op | source)
XLA Modules:
  0.0 179.4 jit_solution(10834595021219684387)
XLA Ops:
  0.0 1.4 collective-permute-start
  1.4 2.0 %pack.1 = (bf16[336,512]{1,0:T(8,128)(2,1)}, f32[8,256]{1,0:T(8,128)}) custom-call(bf16[256,512]{1,0:T(8,128)(2,1)} %rows_hbm.1, f32[256,128]{1,0:T(8,128)} %start_hbm.1, f32[1,256]{1,0:T(1,128)} %bitcast.13), custom_call_target="tpu_custom_call" | custom-call | tf_op jit(solution)/shard_map/pack/pallas_call | solution.py:91
  3.4 1.8 %collective-permute-start.3 = (bf16[336,512]{1,0:T(8,128)(2,1)}, bf16[336,512]{1,0:T(8,128)(2,1)S(1)}, u32[]{:S(2)}, u32[]{:S(2)}) collective-permute-start(bf16[336,512]{1,0:T(8,128)(2,1)} %get-tuple-element.38.refs_1_.refs_5_), channel_id=1, source_target_pairs={{0,2},{2,0},{1,3},{3,1},{4,6},{6,4},{5,7},{7,5},{8,10},{10,8},{9,1... | collective-permute-start | bytes 1032200 | tf_op jit(solution)/shard_map/ppermute | solution.py:469
  5.2 2.5 %collective-permute-start.2 = (bf16[336,512]{1,0:T(8,128)(2,1)}, bf16[336,512]{1,0:T(8,128)(2,1)S(1)}, u32[]{:S(2)}, u32[]{:S(2)}) collective-permute-start(bf16[336,512]{1,0:T(8,128)(2,1)} %get-tuple-element.38.refs_1_.refs_5_), channel_id=1, source_target_pairs={{0,12},{4,0},{8,4},{12,8},{1,13},{5,1},{9,5},{13,9},{2,14},{6,2},{... | collective-permute-start | bytes 1032200 | tf_op jit(solution)/shard_map/ppermute | solution.py:477
  8.4 1.6 copy-done.2
  10.0 0.7 unit.2.refs_2_.refs_4_.refs_6_.refs_3_
  10.8 0.7 unit.3.refs_3_.refs_5_.refs_7_.refs_4_
  11.8 1.3 build.4
  13.1 0.8 collective-permute-done.3.refs_3_.refs_8_
  13.8 1.3 collective-permute-done.2.refs_2_.refs_7_
  15.2 3.0 %collective-permute-done.1.refs_1_.refs_6_ = bf16[336,512]{1,0:T(8,128)(2,1)S(1)} collective-permute-done((bf16[336,512]{1,0:T(8,128)(2,1)}, bf16[336,512]{1,0:T(8,128)(2,1)S(1)}, u32[]{:S(2)}, u32[]{:S(2)}) %collective-permute-start.1) | collective-permute-done | bytes 344096 | tf_op jit(solution)/shard_map/ppermute | solution.py:473
  18.2 0.4 collective-permute-start.6
  18.6 2.7 %collective-permute-start.5 = (bf16[336,512]{1,0:T(8,128)(2,1)S(1)}, bf16[336,512]{1,0:T(8,128)(2,1)S(1)}, u32[]{:S(2)}, u32[]{:S(2)}) collective-permute-start(bf16[336,512]{1,0:T(8,128)(2,1)S(1)} %collective-permute-done.3.refs_3_.refs_8_), channel_id=1, source_target_pairs={{0,12},{4,0},{8,4},{12,8},{1,13},{5,1},{9,5},{13,9},{2,14},{6,2},{... | collective-permute-start | bytes 1032200 | tf_op jit(solution)/shard_map/ppermute | solution.py:477
  21.2 3.5 %build.5 = (bf16[768,4096]{1,0:T(8,128)(2,1)S(1)}, f32[8,4096]{1,0:T(8,128)S(1)}) custom-call(f32[1]{0:T(128)S(6)} %copy.7.refs_0_.refs_2_, bf16[336,512]{1,0:T(8,128)(2,1)S(1)} %collective-permute-done.1.refs_1_.refs_6_, bf16[336,512]{1,0:T(8,128)(2,1)S(1)} %collective-permute-done.2.refs_2_.refs_7_, ...), custom_call_target="tpu_custom_call" | custom-call | flops 6442450944 | tf_op jit(solution)/shard_map/build/pallas_call | solution.py:91
  24.7 1.8 turn.3
  26.5 1.8 turn.2
  28.4 1.2 collective-permute-start.7
  29.6 1.9 %collective-permute-start.8 = (bf16[176,512]{1,0:T(8,128)(2,1)S(1)}, bf16[176,512]{1,0:T(8,128)(2,1)S(1)}, u32[]{:S(2)}, u32[]{:S(2)}) collective-permute-start(bf16[176,512]{1,0:T(8,128)(2,1)S(1)} %slice.10), channel_id=1, source_target_pairs={{0,12},{4,0},{8,4},{12,8},{1,13},{5,1},{9,5},{13,9},{2,14},{6,2},{... | collective-permute-start | bytes 540680 | tf_op jit(solution)/shard_map/ppermute | solution.py:477
  31.5 3.5 %build.6 = (bf16[768,4096]{1,0:T(8,128)(2,1)S(1)}, f32[8,4096]{1,0:T(8,128)S(1)}) custom-call(f32[8,128]{1,0:T(8,128)S(1)} %get-tuple-element.49.refs_0_, f32[8,128]{1,0:T(8,128)S(1)} %get-tuple-element.50.refs_1_, f32[1]{0:T(128)S(6)} %copy.7.refs_0_.refs_2_, bf16[336,512]{1,0:T(8,128)(2,1)S(1)} %collective-permute-done.4.refs_3_.refs_9_, ...), custom_call_target="tpu_custom_call" | custom-call | flops 6442450944 | tf_op jit(solution)/shard_map/build/pallas_call | solution.py:91
  35.0 1.4 build.7
  36.4 1.8 %side_terms.5 = f32[8,136,256]{2,1,0:T(8,128)S(1)} custom-call(s32[8]{0:T(128)S(1)} %stack.35.refs_0_, bf16[256,4096]{1,0:T(8,128)(2,1)S(1)} %get-tuple-element.39.refs_1_.refs_0_, bf16[768,4096]{1,0:T(8,128)(2,1)S(1)} %get-tuple-element.44.refs_2_.refs_1_, bf16[768,4096]{1,0:T(8,128)(2,1)S(1)} %get-tuple-element.54.refs_3_.refs_2_, ...), custom_call_target="tpu_custom_call" | custom-call | flops 1073741824 | tf_op jit(solution)/shard_map/side_terms/pallas_call | solution.py:91
  38.2 3.5 %collective-permute-start.9 = (f32[8,136,256]{2,1,0:T(8,128)S(1)}, f32[8,136,256]{2,1,0:T(8,128)S(1)}, u32[]{:S(2)}, u32[]{:S(2)}) collective-permute-start(f32[8,136,256]{2,1,0:T(8,128)S(1)} %side_terms.5), channel_id=1, source_target_pairs={{0,1},{1,0},{2,3},{3,2},{4,5},{5,4},{6,7},{7,6},{8,9},{9,8},{10,11... | collective-permute-start | bytes 3342344 | tf_op jit(solution)/shard_map/ppermute | solution.py:465
  41.8 1.8 %side_terms.4.refs_6_ = f32[8,136,256]{2,1,0:T(8,128)S(1)} custom-call(s32[8]{0:T(128)S(1)} %stack.35.refs_0_, bf16[256,4096]{1,0:T(8,128)(2,1)S(1)} %get-tuple-element.39.refs_1_.refs_0_, bf16[768,4096]{1,0:T(8,128)(2,1)S(1)} %get-tuple-element.44.refs_2_.refs_1_, bf16[768,4096]{1,0:T(8,128)(2,1)S(1)} %get-tuple-element.54.refs_3_.refs_2_, ...), custom_call_target="tpu_custom_call" | custom-call | flops 1073741824 | tf_op jit(solution)/shard_map/side_terms/pallas_call | solution.py:91
  43.6 0.6 collective-permute-done.9.refs_7_
  44.1 0.3 pair.2
  44.5 18.5 %all_to_all.40.refs_6_ = bf16[8,144,256]{2,1,0:T(8,128)(2,1)S(1)} all-to-all(bf16[8,144,256]{2,1,0:T(8,128)(2,1)S(1)} %get-tuple-element.64), channel_id=1, replica_groups=mesh['y'=4,'zh'=2,'x'=4,'zl'=2,'core'=2] {'y','zh'}, dimensions={0} | all-to-all | bytes 1179648 | tf_op jit(solution)/shard_map/all_to_all | solution.py:461
  62.9 0.4 centre.2
  63.3 13.1 %all_to_all.41.refs_4_.refs_5_ = bf16[8,144,256]{2,1,0:T(8,128)(2,1)S(1)} all-to-all(bf16[8,144,256]{2,1,0:T(8,128)(2,1)S(1)} %get-tuple-element.65), channel_id=1, replica_groups=mesh['y'=4,'zh'=2,'x'=4,'zl'=2,'core'=2] {'y','zh'}, dimensions={0} | all-to-all | bytes 1179648 | tf_op jit(solution)/shard_map/all_to_all | solution.py:461
  76.4 2.9 %collective-permute-start.10 = (bf16[8,144,256]{2,1,0:T(8,128)(2,1)S(1)}, bf16[8,144,256]{2,1,0:T(8,128)(2,1)S(1)}, u32[]{:S(2)}, u32[]{:S(2)}) collective-permute-start(bf16[8,144,256]{2,1,0:T(8,128)(2,1)S(1)} %all_to_all.41.refs_4_.refs_5_), channel_id=1, source_target_pairs={{0,1},{1,0},{2,3},{3,2},{4,5},{5,4},{6,7},{7,6},{8,9},{9,8},{10,11... | collective-permute-start | bytes 1769480 | tf_op jit(solution)/shard_map/ppermute | solution.py:465
  79.3 2.6 %image_terms.4.refs_6_ = f32[128,2048]{1,0:T(8,128)S(1)} custom-call(s32[8]{0:T(128)S(1)} %stack.35.refs_0_, bf16[2048,1024]{1,0:T(8,128)(2,1)S(1)} %get-tuple-element.59.refs_4_.refs_1_, bf16[768,4096]{1,0:T(8,128)(2,1)S(1)} %get-tuple-element.54.refs_3_.refs_2_, bf16[256,4096]{1,0:T(8,128)(2,1)S(1)} %get-tuple-element.58.refs_4_.refs_3_, ...), custom_call_target="tpu_custom_call" | custom-call | flops 1073741824 | tf_op jit(solution)/shard_map/image_terms/pallas_call | solution.py:91
  81.9 2.6 %image_terms.5 = bf16[8,128,256]{2,1,0:T(8,128)(2,1)S(1)} custom-call(s32[8]{0:T(128)S(1)} %stack.35.refs_0_, bf16[2048,1024]{1,0:T(8,128)(2,1)S(1)} %get-tuple-element.45.refs_5_.refs_1_, bf16[768,4096]{1,0:T(8,128)(2,1)S(1)} %get-tuple-element.54.refs_3_.refs_2_, bf16[256,4096]{1,0:T(8,128)(2,1)S(1)} %get-tuple-element.58.refs_4_.refs_3_, ...), custom_call_target="tpu_custom_call" | custom-call | flops 1073741824 | tf_op jit(solution)/shard_map/image_terms/pallas_call | solution.py:91
  84.5 13.5 %all_to_all.42.refs_6_ = bf16[8,128,256]{2,1,0:T(8,128)(2,1)S(1)} all-to-all(bf16[8,128,256]{2,1,0:T(8,128)(2,1)S(1)} %image_terms.5), channel_id=1, replica_groups=mesh['y'=4,'zh'=2,'x'=4,'zl'=2,'core'=2] {'x','zl'}, dimensions={0} | all-to-all | bytes 1048576 | tf_op jit(solution)/shard_map/all_to_all | solution.py:461
  98.0 0.2 owner.2
  98.2 11.6 %all_to_all.43.refs_5_ = bf16[8,144,256]{2,1,0:T(8,128)(2,1)S(1)} all-to-all(bf16[8,144,256]{2,1,0:T(8,128)(2,1)S(1)} %owner.2), channel_id=1, replica_groups=mesh['y'=4,'zh'=2,'x'=4,'zl'=2,'core'=2] {'x','zl'}, dimensions={0} | all-to-all | bytes 1179648 | tf_op jit(solution)/shard_map/all_to_all | solution.py:461
  109.9 1.8 %side_terms.7 = f32[8,136,256]{2,1,0:T(8,128)S(1)} custom-call(s32[8]{0:T(128)S(1)} %stack.35.refs_0_, bf16[256,4096]{1,0:T(8,128)(2,1)S(1)} %get-tuple-element.39.refs_1_.refs_0_, bf16[768,4096]{1,0:T(8,128)(2,1)S(1)} %get-tuple-element.44.refs_2_.refs_1_, bf16[768,4096]{1,0:T(8,128)(2,1)S(1)} %get-tuple-element.54.refs_3_.refs_2_, ...), custom_call_target="tpu_custom_call" | custom-call | flops 1073741824 | tf_op jit(solution)/shard_map/side_terms/pallas_call | solution.py:91
  111.7 2.9 %collective-permute-start.11 = (f32[8,136,256]{2,1,0:T(8,128)S(1)}, f32[8,136,256]{2,1,0:T(8,128)S(1)}, u32[]{:S(2)}, u32[]{:S(2)}) collective-permute-start(f32[8,136,256]{2,1,0:T(8,128)S(1)} %side_terms.7), channel_id=1, source_target_pairs={{0,1},{1,0},{2,3},{3,2},{4,5},{5,4},{6,7},{7,6},{8,9},{9,8},{10,11... | collective-permute-start | bytes 3342344 | tf_op jit(solution)/shard_map/ppermute | solution.py:465
  114.5 1.8 %side_terms.6.refs_6_ = f32[8,136,256]{2,1,0:T(8,128)S(1)} custom-call(s32[8]{0:T(128)S(1)} %stack.35.refs_0_, bf16[256,4096]{1,0:T(8,128)(2,1)S(1)} %get-tuple-element.39.refs_1_.refs_0_, bf16[768,4096]{1,0:T(8,128)(2,1)S(1)} %get-tuple-element.44.refs_2_.refs_1_, bf16[768,4096]{1,0:T(8,128)(2,1)S(1)} %get-tuple-element.54.refs_3_.refs_2_, ...), custom_call_target="tpu_custom_call" | custom-call | flops 1073741824 | tf_op jit(solution)/shard_map/side_terms/pallas_call | solution.py:91
  116.3 0.6 collective-permute-done.11.refs_7_
  116.9 0.3 pair.3
  117.2 13.8 %all_to_all.44.refs_6_ = bf16[8,144,256]{2,1,0:T(8,128)(2,1)S(1)} all-to-all(bf16[8,144,256]{2,1,0:T(8,128)(2,1)S(1)} %pair.3), channel_id=1, replica_groups=mesh['y'=4,'zh'=2,'x'=4,'zl'=2,'core'=2] {'y','zh'}, dimensions={0} | all-to-all | bytes 1179648 | tf_op jit(solution)/shard_map/all_to_all | solution.py:461
  131.0 0.4 centre.3
  131.4 12.3 %all_to_all.45.refs_4_ = bf16[8,128,256]{2,1,0:T(8,128)(2,1)S(1)} all-to-all(bf16[8,128,256]{2,1,0:T(8,128)(2,1)S(1)} %centre.3), channel_id=1, replica_groups=mesh['y'=4,'zh'=2,'x'=4,'zl'=2,'core'=2] {'y','zh'}, dimensions={0} | all-to-all | bytes 1048576 | tf_op jit(solution)/shard_map/all_to_all | solution.py:461
  143.8 2.6 %collective-permute-start.12 = (bf16[8,128,256]{2,1,0:T(8,128)(2,1)S(1)}, bf16[8,128,256]{2,1,0:T(8,128)(2,1)S(1)}, u32[]{:S(2)}, u32[]{:S(2)}) collective-permute-start(bf16[8,128,256]{2,1,0:T(8,128)(2,1)S(1)} %all_to_all.45.refs_4_), channel_id=1, source_target_pairs={{0,1},{1,0},{2,3},{3,2},{4,5},{5,4},{6,7},{7,6},{8,9},{9,8},{10,11... | collective-permute-start | bytes 1572872 | tf_op jit(solution)/shard_map/ppermute | solution.py:465
  146.4 2.6 %image_terms.6.refs_6_ = f32[128,2048]{1,0:T(8,128)S(1)} custom-call(s32[8]{0:T(128)S(1)} %stack.35.refs_0_, bf16[2048,1024]{1,0:T(8,128)(2,1)S(1)} %get-tuple-element.59.refs_4_.refs_1_, bf16[768,4096]{1,0:T(8,128)(2,1)S(1)} %get-tuple-element.54.refs_3_.refs_2_, bf16[256,4096]{1,0:T(8,128)(2,1)S(1)} %get-tuple-element.58.refs_4_.refs_3_, ...), custom_call_target="tpu_custom_call" | custom-call | flops 1073741824 | tf_op jit(solution)/shard_map/image_terms/pallas_call | solution.py:91
  149.0 2.6 %image_terms.7 = bf16[8,128,256]{2,1,0:T(8,128)(2,1)S(1)} custom-call(s32[8]{0:T(128)S(1)} %stack.35.refs_0_, bf16[2048,1024]{1,0:T(8,128)(2,1)S(1)} %get-tuple-element.45.refs_5_.refs_1_, bf16[768,4096]{1,0:T(8,128)(2,1)S(1)} %get-tuple-element.54.refs_3_.refs_2_, bf16[256,4096]{1,0:T(8,128)(2,1)S(1)} %get-tuple-element.58.refs_4_.refs_3_, ...), custom_call_target="tpu_custom_call" | custom-call | flops 1073741824 | tf_op jit(solution)/shard_map/image_terms/pallas_call | solution.py:91
  151.6 12.0 %all_to_all.46.refs_0_ = bf16[8,128,256]{2,1,0:T(8,128)(2,1)S(1)} all-to-all(bf16[8,128,256]{2,1,0:T(8,128)(2,1)S(1)} %image_terms.7), channel_id=1, replica_groups=mesh['y'=4,'zh'=2,'x'=4,'zl'=2,'core'=2] {'x','zl'}, dimensions={0} | all-to-all | bytes 1048576 | tf_op jit(solution)/shard_map/all_to_all | solution.py:461
  163.9 14.8 %all_to_all.47 = f32[128,1,128]{2,1,0:T(1,128)S(1)} all-to-all(f32[128,1,128]{2,1,0:T(1,128)S(1)} %broadcast_in_dim.14), channel_id=1, replica_groups=mesh['y'=4,'zh'=2,'x'=4,'zl'=2,'core'=2] {'y','zh','x','zl','core'}, dimensions={0} | all-to-all | bytes 131072 | tf_op jit(solution)/shard_map/all_to_all | solution.py:461
  178.7 0.7 broadcast_divide_fusion
  (23 shorter events, 0.6 us)
Async XLA Ops:
  0.0 10.8 %collective-permute-start = (bf16[2048,512]{1,0:T(8,128)(2,1)}, bf16[2048,512]{1,0:T(8,128)(2,1)S(1)}, u32[]{:S(2)}, u32[]{:S(2)}) collective-permute-start(bf16[2048,512]{1,0:T(8,128)(2,1)} %in_ref.1), channel_id=1, source_target_pairs={{0,1},{1,0},{2,3},{3,2},{4,5},{5,4},{6,7},{7,6},{8,9},{9,8},{10,11... | collective-permute-start | bytes 6291464 | tf_op jit(solution)/shard_map/ppermute | solution.py:465
  3.4 10.4 %collective-permute-start.3 = (bf16[336,512]{1,0:T(8,128)(2,1)}, bf16[336,512]{1,0:T(8,128)(2,1)S(1)}, u32[]{:S(2)}, u32[]{:S(2)}) collective-permute-start(bf16[336,512]{1,0:T(8,128)(2,1)} %get-tuple-element.38.refs_1_.refs_5_), channel_id=1, source_target_pairs={{0,2},{2,0},{1,3},{3,1},{4,6},{6,4},{5,7},{7,5},{8,10},{10,8},{9,1... | collective-permute-start | bytes 1032200 | tf_op jit(solution)/shard_map/ppermute | solution.py:469
  5.2 10.0 %collective-permute-start.2 = (bf16[336,512]{1,0:T(8,128)(2,1)}, bf16[336,512]{1,0:T(8,128)(2,1)S(1)}, u32[]{:S(2)}, u32[]{:S(2)}) collective-permute-start(bf16[336,512]{1,0:T(8,128)(2,1)} %get-tuple-element.38.refs_1_.refs_5_), channel_id=1, source_target_pairs={{0,12},{4,0},{8,4},{12,8},{1,13},{5,1},{9,5},{13,9},{2,14},{6,2},{... | collective-permute-start | bytes 1032200 | tf_op jit(solution)/shard_map/ppermute | solution.py:477
  7.7 10.5 %collective-permute-start.1 = (bf16[336,512]{1,0:T(8,128)(2,1)}, bf16[336,512]{1,0:T(8,128)(2,1)S(1)}, u32[]{:S(2)}, u32[]{:S(2)}) collective-permute-start(bf16[336,512]{1,0:T(8,128)(2,1)} %get-tuple-element.38.refs_1_.refs_5_), channel_id=1, source_target_pairs={{0,4},{4,8},{8,12},{12,0},{1,5},{5,9},{9,13},{13,1},{2,6},{6,10},{... | collective-permute-start | bytes 1032200 | tf_op jit(solution)/shard_map/ppermute | solution.py:473
  8.4 1.6 copy-start.2
  10.8 1.0 copy-start
  18.2 10.2 %collective-permute-start.6 = (bf16[336,512]{1,0:T(8,128)(2,1)S(1)}, bf16[336,512]{1,0:T(8,128)(2,1)S(1)}, u32[]{:S(2)}, u32[]{:S(2)}) collective-permute-start(bf16[336,512]{1,0:T(8,128)(2,1)S(1)} %collective-permute-done.1.refs_1_.refs_6_), channel_id=1, source_target_pairs={{0,2},{2,0},{1,3},{3,1},{4,6},{6,4},{5,7},{7,5},{8,10},{10,8},{9,1... | collective-permute-start | bytes 1032200 | tf_op jit(solution)/shard_map/ppermute | solution.py:469
  18.5 9.8 %collective-permute-start.4 = (bf16[336,512]{1,0:T(8,128)(2,1)S(1)}, bf16[336,512]{1,0:T(8,128)(2,1)S(1)}, u32[]{:S(2)}, u32[]{:S(2)}) collective-permute-start(bf16[336,512]{1,0:T(8,128)(2,1)S(1)} %collective-permute-done.1.refs_1_.refs_6_), channel_id=1, source_target_pairs={{0,4},{4,8},{8,12},{12,0},{1,5},{5,9},{9,13},{13,1},{2,6},{6,10},{... | collective-permute-start | bytes 1032200 | tf_op jit(solution)/shard_map/ppermute | solution.py:473
  18.6 9.8 %collective-permute-start.5 = (bf16[336,512]{1,0:T(8,128)(2,1)S(1)}, bf16[336,512]{1,0:T(8,128)(2,1)S(1)}, u32[]{:S(2)}, u32[]{:S(2)}) collective-permute-start(bf16[336,512]{1,0:T(8,128)(2,1)S(1)} %collective-permute-done.3.refs_3_.refs_8_), channel_id=1, source_target_pairs={{0,12},{4,0},{8,4},{12,8},{1,13},{5,1},{9,5},{13,9},{2,14},{6,2},{... | collective-permute-start | bytes 1032200 | tf_op jit(solution)/shard_map/ppermute | solution.py:477
  28.4 6.6 %collective-permute-start.7 = (bf16[160,512]{1,0:T(8,128)(2,1)S(1)}, bf16[160,512]{1,0:T(8,128)(2,1)S(1)}, u32[]{:S(2)}, u32[]{:S(2)}) collective-permute-start(bf16[160,512]{1,0:T(8,128)(2,1)S(1)} %slice.9), channel_id=1, source_target_pairs={{0,2},{2,0},{1,3},{3,1},{4,6},{6,4},{5,7},{7,5},{8,10},{10,8},{9,1... | collective-permute-start | bytes 491528 | tf_op jit(solution)/shard_map/ppermute | solution.py:469
  29.6 5.4 %collective-permute-start.8 = (bf16[176,512]{1,0:T(8,128)(2,1)S(1)}, bf16[176,512]{1,0:T(8,128)(2,1)S(1)}, u32[]{:S(2)}, u32[]{:S(2)}) collective-permute-start(bf16[176,512]{1,0:T(8,128)(2,1)S(1)} %slice.10), channel_id=1, source_target_pairs={{0,12},{4,0},{8,4},{12,8},{1,13},{5,1},{9,5},{13,9},{2,14},{6,2},{... | collective-permute-start | bytes 540680 | tf_op jit(solution)/shard_map/ppermute | solution.py:477
  38.2 5.9 %collective-permute-start.9 = (f32[8,136,256]{2,1,0:T(8,128)S(1)}, f32[8,136,256]{2,1,0:T(8,128)S(1)}, u32[]{:S(2)}, u32[]{:S(2)}) collective-permute-start(f32[8,136,256]{2,1,0:T(8,128)S(1)} %side_terms.5), channel_id=1, source_target_pairs={{0,1},{1,0},{2,3},{3,2},{4,5},{5,4},{6,7},{7,6},{8,9},{9,8},{10,11... | collective-permute-start | bytes 3342344 | tf_op jit(solution)/shard_map/ppermute | solution.py:465
  76.4 5.5 %collective-permute-start.10 = (bf16[8,144,256]{2,1,0:T(8,128)(2,1)S(1)}, bf16[8,144,256]{2,1,0:T(8,128)(2,1)S(1)}, u32[]{:S(2)}, u32[]{:S(2)}) collective-permute-start(bf16[8,144,256]{2,1,0:T(8,128)(2,1)S(1)} %all_to_all.41.refs_4_.refs_5_), channel_id=1, source_target_pairs={{0,1},{1,0},{2,3},{3,2},{4,5},{5,4},{6,7},{7,6},{8,9},{9,8},{10,11... | collective-permute-start | bytes 1769480 | tf_op jit(solution)/shard_map/ppermute | solution.py:465
  81.9 16.1 %copy-start.1 = (f32[8,256]{1,0:T(8,128)S(1)}, f32[8,256]{1,0:T(8,128)}, u32[]{:S(2)}) copy-start(f32[8,256]{1,0:T(8,128)} %get-tuple-element.66.refs_7_.refs_1_) | copy-start | bytes 24580
  111.7 5.3 %collective-permute-start.11 = (f32[8,136,256]{2,1,0:T(8,128)S(1)}, f32[8,136,256]{2,1,0:T(8,128)S(1)}, u32[]{:S(2)}, u32[]{:S(2)}) collective-permute-start(f32[8,136,256]{2,1,0:T(8,128)S(1)} %side_terms.7), channel_id=1, source_target_pairs={{0,1},{1,0},{2,3},{3,2},{4,5},{5,4},{6,7},{7,6},{8,9},{9,8},{10,11... | collective-permute-start | bytes 3342344 | tf_op jit(solution)/shard_map/ppermute | solution.py:465
  143.8 5.2 %collective-permute-start.12 = (bf16[8,128,256]{2,1,0:T(8,128)(2,1)S(1)}, bf16[8,128,256]{2,1,0:T(8,128)(2,1)S(1)}, u32[]{:S(2)}, u32[]{:S(2)}) collective-permute-start(bf16[8,128,256]{2,1,0:T(8,128)(2,1)S(1)} %all_to_all.45.refs_4_), channel_id=1, source_target_pairs={{0,1},{1,0},{2,3},{3,2},{4,5},{5,4},{6,7},{7,6},{8,9},{9,8},{10,11... | collective-permute-start | bytes 1572872 | tf_op jit(solution)/shard_map/ppermute | solution.py:465

commit v10 on v7

--- a/solution.py
+++ b/solution.py
@@ -29,7 +29,7 @@
 
 
 def params(mib):
-    return pltpu.CompilerParams(vmem_limit_bytes=mib * 2**20)
+    return pltpu.CompilerParams(vmem_limit_bytes=int(mib * 2**20))
 
 
 def dot(left, right, left_dim, right_dim):
@@ -386,7 +386,7 @@
     image = terms_ref[0].astype(F32)
     for member in range(1, EIGHT):
         image = image + terms_ref[member].astype(F32)
-    weight = weight_ref[...]
+    weight = jnp.transpose(jnp.broadcast_to(weight_ref[0:1, :], (WIDTH, OWN)))
     image = weight * image
     squares = jnp.sum(image * image, axis=0, keepdims=True)
     if last:
@@ -442,7 +442,7 @@
     return lax.ppermute(values, "x", [(at, (at + 3) % 4) for at in range(4)])
 
 
-def pack_kernel(rows_hbm, start_hbm, weight_hbm, out_ref, wide_ref, rows_ref, start_ref, weight_ref, sems):
+def pack_kernel(rows_hbm, start_hbm, weight_hbm, out_ref, line_ref, rows_ref, start_ref, weight_ref, sems):
     copies = [
         pltpu.make_async_copy(rows_hbm, rows_ref, sems.at[0]),
         pltpu.make_async_copy(start_hbm, start_ref, sems.at[1]),
@@ -450,14 +450,15 @@
     ]
     for copy in copies:
         copy.start()
-    for copy in copies:
-        copy.wait()
+    copies[0].wait()
     values = rows_ref[...].astype(F32)
     scale = lax.rsqrt(jnp.sum(values * values, axis=1, keepdims=True) + 1e-06)
     out_ref[:OWN, :] = (values * scale).astype(B16)
+    copies[1].wait()
+    copies[2].wait()
     weight = weight_ref[...]
     wide = jnp.transpose(jnp.broadcast_to(weight, (WIDTH, OWN)))
-    wide_ref[...] = wide
+    line_ref[...] = jnp.broadcast_to(weight, (8, OWN))
     product = wide * start_ref[...]
     totals = jnp.sum(product, axis=0, keepdims=True)
     vectors = jnp.transpose(product).astype(B16)
@@ -469,7 +470,7 @@
 
 
 def pack(rows, start, weight):
-    shapes = [jax.ShapeDtypeStruct((PACK, rows.shape[1]), B16), jax.ShapeDtypeStruct((OWN, WIDTH), F32)]
+    shapes = [pltpu.VMEM((PACK, rows.shape[1]), B16), jax.ShapeDtypeStruct((8, OWN), F32)]
     scratch = [
         pltpu.VMEM(rows.shape, B16),
         pltpu.VMEM(start.shape, F32),
@@ -477,7 +478,7 @@
         pltpu.SemaphoreType.DMA((3,)),
     ]
     specs = [pl.BlockSpec(memory_space=pl.ANY)] * 3
-    return call(pack_kernel, shapes, specs, [rows, start, weight], "pack", scratch=scratch, mib=56)
+    return call(pack_kernel, shapes, specs, [rows, start, weight], "pack", scratch=scratch, mib=54)
 
 
 def slot_owners():

time: 179 us -> 179 us (level)
  no operation moved by 1% of the time
where the time goes in v10:
time: 179 us; the launch traced here: 178 us
  blocking collectives  109 us (61%)
  Pallas kernels  34 us (19%)
  starting transfers between devices  26 us (15%)
  waiting for transfers between devices  6.27 us (4%)
    all_to_all x8, blocking collectives, exchange(): return lax.all_to_all(payload, axes, 0, 0)  109 us
    pallas_call x21, Pallas kernels, call(): pl.pallas_call(kernel, out_shape=shapes, in_specs=specs, out_specs=[VMEM]...  34 us
    ppermute x5, starting transfers between devices, swap_core(): return lax.ppermute(values, 'core', [(0, 1), (1, 0)])  13.8 us
    ppermute x3, starting transfers between devices, from_above(): return lax.ppermute(values, 'x', [(at, (at + 3) % 4) for at in range(4)])  7.05 us
    ppermute x3, starting transfers between devices, swap_z(): return lax.ppermute(values, 'zl', [(0, 1), (1, 0)])  3.8 us
    ppermute x2, waiting for transfers between devices, from_below(): return lax.ppermute(values, 'x', [(at, (at + 1) % 4) for at in range(4)])  3.62 us
  transfers between devices with their start and end apart: 13, of which 6 were waited for; matrix products, arithmetic and copies ran while one was open for 0% of the time, Pallas kernels for 12%

profile of v10, /device:TPU:1, one launch (start us, length us, event | category | flops | bytes accessed | tf_op | source)
XLA Modules:
  0.0 178.3 jit_solution(1035183054219507048)
XLA Ops:
  0.0 1.4 collective-permute-start
  1.4 1.7 pack.1
  3.1 1.4 collective-permute-start.1
  4.5 1.4 collective-permute-start.2
  5.9 1.7 collective-permute-start.3
  8.3 1.6 copy-done.1
  9.9 0.7 unit.2.refs_2_.refs_4_.refs_3_
  10.7 0.7 unit.3.refs_3_.refs_5_.refs_4_
  11.4 1.3 build.4
  12.8 1.4 collective-permute-done.1.refs_1_.refs_6_
  14.1 1.4 collective-permute-done.3.refs_3_.refs_8_
  15.5 1.2 collective-permute-start.6
  16.7 2.6 %collective-permute-start.5 = (bf16[336,512]{1,0:T(8,128)(2,1)S(1)}, bf16[336,512]{1,0:T(8,128)(2,1)S(1)}, u32[]{:S(2)}, u32[]{:S(2)}) collective-permute-start(bf16[336,512]{1,0:T(8,128)(2,1)S(1)} %collective-permute-done.3.refs_3_.refs_8_), channel_id=1, source_target_pairs={{0,12},{4,0},{8,4},{12,8},{1,13},{5,1},{9,5},{13,9},{2,14},{6,2},{... | collective-permute-start | bytes 1032200 | tf_op jit(solution)/shard_map/ppermute | solution.py:442
  19.3 3.5 %build.5 = (bf16[768,4096]{1,0:T(8,128)(2,1)S(1)}, f32[8,4096]{1,0:T(8,128)S(1)}) custom-call(f32[1]{0:T(128)S(6)} %copy.7.refs_0_, bf16[336,512]{1,0:T(8,128)(2,1)S(1)} %collective-permute-done.1.refs_1_.refs_6_, bf16[336,512]{1,0:T(8,128)(2,1)S(1)} %collective-permute-done.2.refs_2_.refs_7_, bf16[336,512]{1,0:T(8,128)(2,1)S(1)} %collective-permute-done.3.refs_3_.refs_8_, ...), custom_call_target="tpu_custom_call" | custom-call | flops 6442450944 | tf_op jit(solution)/shard_map/build/pallas_call | solution.py:91
  22.9 2.3 %collective-permute-done.4.refs_1_.refs_9_ = bf16[336,512]{1,0:T(8,128)(2,1)S(1)} collective-permute-done((bf16[336,512]{1,0:T(8,128)(2,1)S(1)}, bf16[336,512]{1,0:T(8,128)(2,1)S(1)}, u32[]{:S(2)}, u32[]{:S(2)}) %collective-permute-start.4) | collective-permute-done | bytes 344096 | tf_op jit(solution)/shard_map/ppermute | solution.py:438
  25.2 3.1 %collective-permute-start.8 = (bf16[176,512]{1,0:T(8,128)(2,1)S(1)}, bf16[176,512]{1,0:T(8,128)(2,1)S(1)}, u32[]{:S(2)}, u32[]{:S(2)}) collective-permute-start(bf16[176,512]{1,0:T(8,128)(2,1)S(1)} %slice.10), channel_id=1, source_target_pairs={{0,12},{4,0},{8,4},{12,8},{1,13},{5,1},{9,5},{13,9},{2,14},{6,2},{... | collective-permute-start | bytes 540680 | tf_op jit(solution)/shard_map/ppermute | solution.py:442
  28.2 0.8 collective-permute-start.7
  29.1 3.5 %build.6 = (bf16[768,4096]{1,0:T(8,128)(2,1)S(1)}, f32[8,4096]{1,0:T(8,128)S(1)}) custom-call(f32[1]{0:T(128)S(6)} %copy.7.refs_0_, bf16[336,512]{1,0:T(8,128)(2,1)S(1)} %collective-permute-done.4.refs_1_.refs_9_, bf16[336,512]{1,0:T(8,128)(2,1)S(1)} %collective-permute-done.5.refs_2_.refs_10_, bf16[336,512]{1,0:T(8,128)(2,1)S(1)} %collective-permute-done.6.refs_3_.refs_11_, ...), custom_call_target="tpu_custom_call" | custom-call | flops 6442450944 | tf_op jit(solution)/shard_map/build/pallas_call | solution.py:91
  32.6 0.2 collective-permute-done.7.refs_1_.refs_12_
  32.8 1.3 build.7
  34.1 1.9 %side_terms.5 = f32[8,136,256]{2,1,0:T(8,128)S(1)} custom-call(s32[8]{0:T(128)S(1)} %stack.35.refs_0_, bf16[256,4096]{1,0:T(8,128)(2,1)S(1)} %get-tuple-element.33.refs_1_.refs_0_, bf16[768,4096]{1,0:T(8,128)(2,1)S(1)} %get-tuple-element.38.refs_2_.refs_1_, bf16[768,4096]{1,0:T(8,128)(2,1)S(1)} %get-tuple-element.43.refs_3_.refs_2_, ...), custom_call_target="tpu_custom_call" | custom-call | flops 1073741824 | tf_op jit(solution)/shard_map/side_terms/pallas_call | solution.py:91
  36.0 4.3 %collective-permute-start.9 = (f32[8,136,256]{2,1,0:T(8,128)S(1)}, f32[8,136,256]{2,1,0:T(8,128)S(1)}, u32[]{:S(2)}, u32[]{:S(2)}) collective-permute-start(f32[8,136,256]{2,1,0:T(8,128)S(1)} %side_terms.5), channel_id=1, source_target_pairs={{0,1},{1,0},{2,3},{3,2},{4,5},{5,4},{6,7},{7,6},{8,9},{9,8},{10,11... | collective-permute-start | bytes 3342344 | tf_op jit(solution)/shard_map/ppermute | solution.py:430
  40.3 1.9 %side_terms.4.refs_4_ = f32[8,136,256]{2,1,0:T(8,128)S(1)} custom-call(s32[8]{0:T(128)S(1)} %stack.35.refs_0_, bf16[256,4096]{1,0:T(8,128)(2,1)S(1)} %get-tuple-element.33.refs_1_.refs_0_, bf16[768,4096]{1,0:T(8,128)(2,1)S(1)} %get-tuple-element.38.refs_2_.refs_1_, bf16[768,4096]{1,0:T(8,128)(2,1)S(1)} %get-tuple-element.43.refs_3_.refs_2_, ...), custom_call_target="tpu_custom_call" | custom-call | flops 1073741824 | tf_op jit(solution)/shard_map/side_terms/pallas_call | solution.py:91
  42.2 0.5 collective-permute-done.9.refs_5_
  42.7 0.3 pair.2
  43.0 18.5 %all_to_all.40.refs_4_ = bf16[8,144,256]{2,1,0:T(8,128)(2,1)S(1)} all-to-all(bf16[8,144,256]{2,1,0:T(8,128)(2,1)S(1)} %get-tuple-element.52), channel_id=1, replica_groups=mesh['y'=4,'zh'=2,'x'=4,'zl'=2,'core'=2] {'y','zh'}, dimensions={0} | all-to-all | bytes 1179648 | tf_op jit(solution)/shard_map/all_to_all | solution.py:426
  61.5 0.4 centre.2
  61.9 13.1 %all_to_all.41.refs_5_.refs_6_ = bf16[8,144,256]{2,1,0:T(8,128)(2,1)S(1)} all-to-all(bf16[8,144,256]{2,1,0:T(8,128)(2,1)S(1)} %get-tuple-element.53), channel_id=1, replica_groups=mesh['y'=4,'zh'=2,'x'=4,'zl'=2,'core'=2] {'y','zh'}, dimensions={0} | all-to-all | bytes 1179648 | tf_op jit(solution)/shard_map/all_to_all | solution.py:426
  74.9 2.9 %collective-permute-start.10 = (bf16[8,144,256]{2,1,0:T(8,128)(2,1)S(1)}, bf16[8,144,256]{2,1,0:T(8,128)(2,1)S(1)}, u32[]{:S(2)}, u32[]{:S(2)}) collective-permute-start(bf16[8,144,256]{2,1,0:T(8,128)(2,1)S(1)} %all_to_all.41.refs_5_.refs_6_), channel_id=1, source_target_pairs={{0,1},{1,0},{2,3},{3,2},{4,5},{5,4},{6,7},{7,6},{8,9},{9,8},{10,11... | collective-permute-start | bytes 1769480 | tf_op jit(solution)/shard_map/ppermute | solution.py:430
  77.8 3.0 %image_terms.4.refs_7_ = f32[2048,128]{1,0:T(8,128)S(1)} custom-call(s32[8]{0:T(128)S(1)} %stack.35.refs_0_, bf16[256,4096]{1,0:T(8,128)(2,1)S(1)} %get-tuple-element.33.refs_1_.refs_0_, bf16[768,4096]{1,0:T(8,128)(2,1)S(1)} %get-tuple-element.38.refs_2_.refs_1_, bf16[768,4096]{1,0:T(8,128)(2,1)S(1)} %get-tuple-element.43.refs_3_.refs_2_, ...), custom_call_target="tpu_custom_call" | custom-call | flops 1073741824 | tf_op jit(solution)/shard_map/image_terms/pallas_call | solution.py:91
  80.8 3.0 %image_terms.5 = bf16[8,256,128]{2,1,0:T(8,128)(2,1)S(1)} custom-call(s32[8]{0:T(128)S(1)} %stack.35.refs_0_, bf16[256,4096]{1,0:T(8,128)(2,1)S(1)} %get-tuple-element.33.refs_1_.refs_0_, bf16[768,4096]{1,0:T(8,128)(2,1)S(1)} %get-tuple-element.38.refs_2_.refs_1_, bf16[768,4096]{1,0:T(8,128)(2,1)S(1)} %get-tuple-element.43.refs_3_.refs_2_, ...), custom_call_target="tpu_custom_call" | custom-call | flops 1073741824 | tf_op jit(solution)/shard_map/image_terms/pallas_call | solution.py:91
  83.9 12.1 %all_to_all.42.refs_4_ = bf16[8,256,128]{2,1,0:T(8,128)(2,1)S(1)} all-to-all(bf16[8,256,128]{2,1,0:T(8,128)(2,1)S(1)} %image_terms.5), channel_id=1, replica_groups=mesh['y'=4,'zh'=2,'x'=4,'zl'=2,'core'=2] {'x','zl'}, dimensions={0} | all-to-all | bytes 1048576 | tf_op jit(solution)/shard_map/all_to_all | solution.py:426
  95.9 0.2 owner.2
  96.1 12.1 %all_to_all.43.refs_5_ = bf16[8,144,256]{2,1,0:T(8,128)(2,1)S(1)} all-to-all(bf16[8,144,256]{2,1,0:T(8,128)(2,1)S(1)} %owner.2), channel_id=1, replica_groups=mesh['y'=4,'zh'=2,'x'=4,'zl'=2,'core'=2] {'x','zl'}, dimensions={0} | all-to-all | bytes 1179648 | tf_op jit(solution)/shard_map/all_to_all | solution.py:426
  108.2 1.8 %side_terms.7 = f32[8,136,256]{2,1,0:T(8,128)S(1)} custom-call(s32[8]{0:T(128)S(1)} %stack.35.refs_0_, bf16[256,4096]{1,0:T(8,128)(2,1)S(1)} %get-tuple-element.33.refs_1_.refs_0_, bf16[768,4096]{1,0:T(8,128)(2,1)S(1)} %get-tuple-element.38.refs_2_.refs_1_, bf16[768,4096]{1,0:T(8,128)(2,1)S(1)} %get-tuple-element.43.refs_3_.refs_2_, ...), custom_call_target="tpu_custom_call" | custom-call | flops 1073741824 | tf_op jit(solution)/shard_map/side_terms/pallas_call | solution.py:91
  110.0 2.6 %collective-permute-start.11 = (f32[8,136,256]{2,1,0:T(8,128)S(1)}, f32[8,136,256]{2,1,0:T(8,128)S(1)}, u32[]{:S(2)}, u32[]{:S(2)}) collective-permute-start(f32[8,136,256]{2,1,0:T(8,128)S(1)} %side_terms.7), channel_id=1, source_target_pairs={{0,1},{1,0},{2,3},{3,2},{4,5},{5,4},{6,7},{7,6},{8,9},{9,8},{10,11... | collective-permute-start | bytes 3342344 | tf_op jit(solution)/shard_map/ppermute | solution.py:430
  112.6 1.8 %side_terms.6.refs_4_ = f32[8,136,256]{2,1,0:T(8,128)S(1)} custom-call(s32[8]{0:T(128)S(1)} %stack.35.refs_0_, bf16[256,4096]{1,0:T(8,128)(2,1)S(1)} %get-tuple-element.33.refs_1_.refs_0_, bf16[768,4096]{1,0:T(8,128)(2,1)S(1)} %get-tuple-element.38.refs_2_.refs_1_, bf16[768,4096]{1,0:T(8,128)(2,1)S(1)} %get-tuple-element.43.refs_3_.refs_2_, ...), custom_call_target="tpu_custom_call" | custom-call | flops 1073741824 | tf_op jit(solution)/shard_map/side_terms/pallas_call | solution.py:91
  114.4 0.6 collective-permute-done.11.refs_5_
  115.0 0.3 pair.3
  115.3 13.8 %all_to_all.44.refs_4_ = bf16[8,144,256]{2,1,0:T(8,128)(2,1)S(1)} all-to-all(bf16[8,144,256]{2,1,0:T(8,128)(2,1)S(1)} %pair.3), channel_id=1, replica_groups=mesh['y'=4,'zh'=2,'x'=4,'zl'=2,'core'=2] {'y','zh'}, dimensions={0} | all-to-all | bytes 1179648 | tf_op jit(solution)/shard_map/all_to_all | solution.py:426
  129.1 0.4 centre.3
  129.5 12.3 %all_to_all.45.refs_5_ = bf16[8,128,256]{2,1,0:T(8,128)(2,1)S(1)} all-to-all(bf16[8,128,256]{2,1,0:T(8,128)(2,1)S(1)} %centre.3), channel_id=1, replica_groups=mesh['y'=4,'zh'=2,'x'=4,'zl'=2,'core'=2] {'y','zh'}, dimensions={0} | all-to-all | bytes 1048576 | tf_op jit(solution)/shard_map/all_to_all | solution.py:426
  141.9 2.6 %collective-permute-start.12 = (bf16[8,128,256]{2,1,0:T(8,128)(2,1)S(1)}, bf16[8,128,256]{2,1,0:T(8,128)(2,1)S(1)}, u32[]{:S(2)}, u32[]{:S(2)}) collective-permute-start(bf16[8,128,256]{2,1,0:T(8,128)(2,1)S(1)} %all_to_all.45.refs_5_), channel_id=1, source_target_pairs={{0,1},{1,0},{2,3},{3,2},{4,5},{5,4},{6,7},{7,6},{8,9},{9,8},{10,11... | collective-permute-start | bytes 1572872 | tf_op jit(solution)/shard_map/ppermute | solution.py:430
  144.5 3.0 %image_terms.6.refs_7_ = f32[2048,128]{1,0:T(8,128)S(1)} custom-call(s32[8]{0:T(128)S(1)} %stack.35.refs_0_, bf16[256,4096]{1,0:T(8,128)(2,1)S(1)} %get-tuple-element.33.refs_1_.refs_0_, bf16[768,4096]{1,0:T(8,128)(2,1)S(1)} %get-tuple-element.38.refs_2_.refs_1_, bf16[768,4096]{1,0:T(8,128)(2,1)S(1)} %get-tuple-element.43.refs_3_.refs_2_, ...), custom_call_target="tpu_custom_call" | custom-call | flops 1073741824 | tf_op jit(solution)/shard_map/image_terms/pallas_call | solution.py:91
  147.5 3.0 %image_terms.7 = bf16[8,256,128]{2,1,0:T(8,128)(2,1)S(1)} custom-call(s32[8]{0:T(128)S(1)} %stack.35.refs_0_, bf16[256,4096]{1,0:T(8,128)(2,1)S(1)} %get-tuple-element.33.refs_1_.refs_0_, bf16[768,4096]{1,0:T(8,128)(2,1)S(1)} %get-tuple-element.38.refs_2_.refs_1_, bf16[768,4096]{1,0:T(8,128)(2,1)S(1)} %get-tuple-element.43.refs_3_.refs_2_, ...), custom_call_target="tpu_custom_call" | custom-call | flops 1073741824 | tf_op jit(solution)/shard_map/image_terms/pallas_call | solution.py:91
  150.5 12.0 %all_to_all.46.refs_0_ = bf16[8,256,128]{2,1,0:T(8,128)(2,1)S(1)} all-to-all(bf16[8,256,128]{2,1,0:T(8,128)(2,1)S(1)} %image_terms.7), channel_id=1, replica_groups=mesh['y'=4,'zh'=2,'x'=4,'zl'=2,'core'=2] {'x','zl'}, dimensions={0} | all-to-all | bytes 1048576 | tf_op jit(solution)/shard_map/all_to_all | solution.py:426
  162.7 14.8 %all_to_all.47 = f32[128,1,128]{2,1,0:T(1,128)S(1)} all-to-all(f32[128,1,128]{2,1,0:T(1,128)S(1)} %broadcast_in_dim.14), channel_id=1, replica_groups=mesh['y'=4,'zh'=2,'x'=4,'zl'=2,'core'=2] {'y','zh','x','zl','core'}, dimensions={0} | all-to-all | bytes 131072 | tf_op jit(solution)/shard_map/all_to_all | solution.py:426
  177.6 0.7 broadcast_divide_fusion
  (19 shorter events, 0.3 us)
Async XLA Ops:
  0.0 10.7 %collective-permute-start = (bf16[2048,512]{1,0:T(8,128)(2,1)}, bf16[2048,512]{1,0:T(8,128)(2,1)S(1)}, u32[]{:S(2)}, u32[]{:S(2)}) collective-permute-start(bf16[2048,512]{1,0:T(8,128)(2,1)} %in_ref.1), channel_id=1, source_target_pairs={{0,1},{1,0},{2,3},{3,2},{4,5},{5,4},{6,7},{7,6},{8,9},{9,8},{10,11... | collective-permute-start | bytes 6291464 | tf_op jit(solution)/shard_map/ppermute | solution.py:430
  3.1 11.0 %collective-permute-start.1 = (bf16[336,512]{1,0:T(8,128)(2,1)S(1)}, bf16[336,512]{1,0:T(8,128)(2,1)S(1)}, u32[]{:S(2)}, u32[]{:S(2)}) collective-permute-start(bf16[336,512]{1,0:T(8,128)(2,1)S(1)} %get-tuple-element.32.refs_1_.refs_5_), channel_id=1, source_target_pairs={{0,4},{4,8},{8,12},{12,0},{1,5},{5,9},{9,13},{13,1},{2,6},{6,10},{... | collective-permute-start | bytes 1032200 | tf_op jit(solution)/shard_map/ppermute | solution.py:438
  4.5 9.6 %collective-permute-start.2 = (bf16[336,512]{1,0:T(8,128)(2,1)S(1)}, bf16[336,512]{1,0:T(8,128)(2,1)S(1)}, u32[]{:S(2)}, u32[]{:S(2)}) collective-permute-start(bf16[336,512]{1,0:T(8,128)(2,1)S(1)} %get-tuple-element.32.refs_1_.refs_5_), channel_id=1, source_target_pairs={{0,12},{4,0},{8,4},{12,8},{1,13},{5,1},{9,5},{13,9},{2,14},{6,2},{... | collective-permute-start | bytes 1032200 | tf_op jit(solution)/shard_map/ppermute | solution.py:442
  5.9 9.6 %collective-permute-start.3 = (bf16[336,512]{1,0:T(8,128)(2,1)S(1)}, bf16[336,512]{1,0:T(8,128)(2,1)S(1)}, u32[]{:S(2)}, u32[]{:S(2)}) collective-permute-start(bf16[336,512]{1,0:T(8,128)(2,1)S(1)} %get-tuple-element.32.refs_1_.refs_5_), channel_id=1, source_target_pairs={{0,2},{2,0},{1,3},{3,1},{4,6},{6,4},{5,7},{7,5},{8,10},{10,8},{9,1... | collective-permute-start | bytes 1032200 | tf_op jit(solution)/shard_map/ppermute | solution.py:434
  8.3 1.6 copy-start.1
  15.5 9.6 %collective-permute-start.4 = (bf16[336,512]{1,0:T(8,128)(2,1)S(1)}, bf16[336,512]{1,0:T(8,128)(2,1)S(1)}, u32[]{:S(2)}, u32[]{:S(2)}) collective-permute-start(bf16[336,512]{1,0:T(8,128)(2,1)S(1)} %collective-permute-done.1.refs_1_.refs_6_), channel_id=1, source_target_pairs={{0,4},{4,8},{8,12},{12,0},{1,5},{5,9},{9,13},{13,1},{2,6},{6,10},{... | collective-permute-start | bytes 1032200 | tf_op jit(solution)/shard_map/ppermute | solution.py:438
  15.5 9.6 %collective-permute-start.6 = (bf16[336,512]{1,0:T(8,128)(2,1)S(1)}, bf16[336,512]{1,0:T(8,128)(2,1)S(1)}, u32[]{:S(2)}, u32[]{:S(2)}) collective-permute-start(bf16[336,512]{1,0:T(8,128)(2,1)S(1)} %collective-permute-done.1.refs_1_.refs_6_), channel_id=1, source_target_pairs={{0,2},{2,0},{1,3},{3,1},{4,6},{6,4},{5,7},{7,5},{8,10},{10,8},{9,1... | collective-permute-start | bytes 1032200 | tf_op jit(solution)/shard_map/ppermute | solution.py:434
  16.7 8.4 %collective-permute-start.5 = (bf16[336,512]{1,0:T(8,128)(2,1)S(1)}, bf16[336,512]{1,0:T(8,128)(2,1)S(1)}, u32[]{:S(2)}, u32[]{:S(2)}) collective-permute-start(bf16[336,512]{1,0:T(8,128)(2,1)S(1)} %collective-permute-done.3.refs_3_.refs_8_), channel_id=1, source_target_pairs={{0,12},{4,0},{8,4},{12,8},{1,13},{5,1},{9,5},{13,9},{2,14},{6,2},{... | collective-permute-start | bytes 1032200 | tf_op jit(solution)/shard_map/ppermute | solution.py:442
  25.2 7.7 %collective-permute-start.8 = (bf16[176,512]{1,0:T(8,128)(2,1)S(1)}, bf16[176,512]{1,0:T(8,128)(2,1)S(1)}, u32[]{:S(2)}, u32[]{:S(2)}) collective-permute-start(bf16[176,512]{1,0:T(8,128)(2,1)S(1)} %slice.10), channel_id=1, source_target_pairs={{0,12},{4,0},{8,4},{12,8},{1,13},{5,1},{9,5},{13,9},{2,14},{6,2},{... | collective-permute-start | bytes 540680 | tf_op jit(solution)/shard_map/ppermute | solution.py:442
  28.2 4.6 %collective-permute-start.7 = (bf16[160,512]{1,0:T(8,128)(2,1)S(1)}, bf16[160,512]{1,0:T(8,128)(2,1)S(1)}, u32[]{:S(2)}, u32[]{:S(2)}) collective-permute-start(bf16[160,512]{1,0:T(8,128)(2,1)S(1)} %slice.9), channel_id=1, source_target_pairs={{0,2},{2,0},{1,3},{3,1},{4,6},{6,4},{5,7},{7,5},{8,10},{10,8},{9,1... | collective-permute-start | bytes 491528 | tf_op jit(solution)/shard_map/ppermute | solution.py:434
  36.0 6.6 %collective-permute-start.9 = (f32[8,136,256]{2,1,0:T(8,128)S(1)}, f32[8,136,256]{2,1,0:T(8,128)S(1)}, u32[]{:S(2)}, u32[]{:S(2)}) collective-permute-start(f32[8,136,256]{2,1,0:T(8,128)S(1)} %side_terms.5), channel_id=1, source_target_pairs={{0,1},{1,0},{2,3},{3,2},{4,5},{5,4},{6,7},{7,6},{8,9},{9,8},{10,11... | collective-permute-start | bytes 3342344 | tf_op jit(solution)/shard_map/ppermute | solution.py:430
  74.9 5.9 %collective-permute-start.10 = (bf16[8,144,256]{2,1,0:T(8,128)(2,1)S(1)}, bf16[8,144,256]{2,1,0:T(8,128)(2,1)S(1)}, u32[]{:S(2)}, u32[]{:S(2)}) collective-permute-start(bf16[8,144,256]{2,1,0:T(8,128)(2,1)S(1)} %all_to_all.41.refs_5_.refs_6_), channel_id=1, source_target_pairs={{0,1},{1,0},{2,3},{3,2},{4,5},{5,4},{6,7},{7,6},{8,9},{9,8},{10,11... | collective-permute-start | bytes 1769480 | tf_op jit(solution)/shard_map/ppermute | solution.py:430
  80.8 15.1 %copy-start = (f32[8,256]{1,0:T(8,128)S(1)}, f32[8,256]{1,0:T(8,128)}, u32[]{:S(2)}) copy-start(f32[8,256]{1,0:T(8,128)} %get-tuple-element.54.refs_5_.refs_1_) | copy-start | bytes 24580
  110.0 4.9 %collective-permute-start.11 = (f32[8,136,256]{2,1,0:T(8,128)S(1)}, f32[8,136,256]{2,1,0:T(8,128)S(1)}, u32[]{:S(2)}, u32[]{:S(2)}) collective-permute-start(f32[8,136,256]{2,1,0:T(8,128)S(1)} %side_terms.7), channel_id=1, source_target_pairs={{0,1},{1,0},{2,3},{3,2},{4,5},{5,4},{6,7},{7,6},{8,9},{9,8},{10,11... | collective-permute-start | bytes 3342344 | tf_op jit(solution)/shard_map/ppermute | solution.py:430
  141.9 5.6 %collective-permute-start.12 = (bf16[8,128,256]{2,1,0:T(8,128)(2,1)S(1)}, bf16[8,128,256]{2,1,0:T(8,128)(2,1)S(1)}, u32[]{:S(2)}, u32[]{:S(2)}) collective-permute-start(bf16[8,128,256]{2,1,0:T(8,128)(2,1)S(1)} %all_to_all.45.refs_5_), channel_id=1, source_target_pairs={{0,1},{1,0},{2,3},{3,2},{4,5},{5,4},{6,7},{7,6},{8,9},{9,8},{10,11... | collective-permute-start | bytes 1572872 | tf_op jit(solution)/shard_map/ppermute | solution.py:430

commit v11 on v10

--- a/solution.py
+++ b/solution.py
@@ -26,6 +26,7 @@
 BLOCK = 8 * PIECE
 SPLIT = 160
 TILES = 4
+MOVES = [(0, 0), (3, 0), (1, 0), (0, 1), (2, 0), (1, 1), (3, 1), (2, 1)]
 
 
 def params(mib):
@@ -189,7 +190,7 @@
 
 
 def side_kernel(first, base, *refs):
-    slots_ref, tiles, refs = refs[0], refs[1 : 1 + TILES], refs[1 + TILES :]
+    tiles, refs = refs[:TILES], refs[TILES:]
     half = WIDTH // 2
     if first:
         packed, refs = take(refs, [1] * 7 + [2])
@@ -202,7 +203,7 @@
     else:
         packed_ref, out_ref, wt_ref = refs
         for slot in range(EIGHT):
-            wt_ref[:, slot * OWN : (slot + 1) * OWN] = packed_ref[slots_ref[slot], :WIDTH, :]
+            wt_ref[:, slot * OWN : (slot + 1) * OWN] = packed_ref[slot_owner(slot), :WIDTH, :]
         tails = [packed_ref[source, WIDTH:, :] for source in range(EIGHT)]
     tail = tails[0].astype(F32)
     for more in tails[1:]:
@@ -239,12 +240,12 @@
     lax.fori_loop(0, MARKS // BLOCK, body, 0)
 
 
-def side_terms(first, base, slots, tiles, more):
+def side_terms(first, base, tiles, more):
     return call(
         lambda *refs: side_kernel(first, base, *refs),
         [jax.ShapeDtypeStruct((EIGHT, WIDTH + 8, PIECE), F32)],
-        [SMEM] + [VMEM] * (TILES + len(more)),
-        [slots, *tiles, *more],
+        [VMEM] * (TILES + len(more)),
+        [*tiles, *more],
         "side_terms",
         scratch=[pltpu.VMEM((WIDTH, ROWS), B16)],
         flops=2 * ROWS * MARKS * WIDTH,
@@ -338,7 +339,7 @@
     )
 
 
-def image_kernel(base, slots_ref, *refs):
+def image_kernel(base, *refs):
     tiles, (half_ref, means_ref), refs = refs[:TILES], refs[TILES : TILES + 2], refs[TILES + 2 :]
     if base:
         before_ref, out_ref, side_ref, tail_ref = refs
@@ -357,13 +358,13 @@
         if base:
             term = term + before_ref[slot * OWN : (slot + count) * OWN, :]
             for at in range(count):
-                out_ref[slots_ref[slot + at]] = term[at * OWN : (at + 1) * OWN].astype(B16)
+                out_ref[slot_owner(slot + at)] = term[at * OWN : (at + 1) * OWN].astype(B16)
         else:
             out_ref[slot * OWN : (slot + count) * OWN, :] = term
         slot += count
 
 
-def image_terms(slots, tiles, half, means, before=None):
+def image_terms(tiles, half, means, before=None):
     if before is None:
         base, more, shape = 0, [], jax.ShapeDtypeStruct((ROWS, WIDTH), F32)
     else:
@@ -371,8 +372,8 @@
     return call(
         lambda *refs: image_kernel(base, *refs),
         [shape],
-        [SMEM] + [VMEM] * (TILES + 2 + len(more)),
-        [slots, *tiles, half, means, *more],
+        [VMEM] * (TILES + 2 + len(more)),
+        [*tiles, half, means, *more],
         "image_terms",
         scratch=[pltpu.VMEM((WIDTH, MARKS), B16), pltpu.VMEM((16, MARKS), B16)],
         flops=2 * ROWS * MARKS * WIDTH,
@@ -481,15 +482,13 @@
     return call(pack_kernel, shapes, specs, [rows, start, weight], "pack", scratch=scratch, mib=54)
 
 
-def slot_owners():
-    x, z = lax.axis_index("x"), lax.axis_index("zl")
-    moves = [(0, 0), (3, 0), (1, 0), (0, 1), (2, 0), (1, 1), (3, 1), (2, 1)]
-    return jnp.stack([(x + dx) % 4 * 2 + (z + dz) % 2 for dx, dz in moves]).astype(jnp.int32)
+def slot_owner(slot):
+    dx, dz = MOVES[slot]
+    return (lax.axis_index("x") + dx) % 4 * 2 + (lax.axis_index("zl") + dz) % 2
 
 
 def local(embeddings, landmarks, start_vectors, row_weight, spread):
     total_rows = embeddings.shape[0] * lax.axis_size(AXES)
-    slots = slot_owners()
     packed, weight = pack(embeddings, start_vectors, row_weight[None, :])
     below, above, across = from_below(packed), from_above(packed), swap_z(packed)
     near = unit(landmarks)
@@ -510,8 +509,8 @@
     first = [*packs, sums_zero, sums_one, sums_two, sums_three]
     for step in range(ITERS):
         more = first if step == 0 else [vectors]
-        other = swap_core(side_terms(step == 0, MARKS, slots, tiles, more))
-        own = side_terms(step == 0, 0, slots, tiles, more)
+        other = swap_core(side_terms(step == 0, MARKS, tiles, more))
+        own = side_terms(step == 0, 0, tiles, more)
         if step == 0:
             payload, pair_means = pair(True, tiles, own, other)
             sides, means = centre(True, total_rows, tiles, exchange(payload, MARK_AXES))
@@ -522,8 +521,8 @@
         across_core = swap_core(sides)
         if step == 0:
             tails = (sides, across_core)
-        parts = image_terms(slots, tiles, sides, tails[0])
-        parts = image_terms(slots, tiles, across_core, tails[1], parts)
+        parts = image_terms(tiles, sides, tails[0])
+        parts = image_terms(tiles, across_core, tails[1], parts)
         parts = exchange(parts, ROW_AXES)
         if step + 1 < ITERS:
             (vectors,) = owner(False, tiles, parts, weight)

time: 179 us -> 178 us (level)
  Pallas kernels: 34 us -> 29.5 us
  waiting for transfers between devices: 6.27 us -> 10.6 us
  starting transfers between devices: 26 us -> 24.2 us
    pallas_call x21, Pallas kernels: 34 us -> 29.5 us  [call(): pl.pallas_call(kernel, out_shape=shapes, in_specs=specs, out_specs=[VMEM]...]
    ppermute x3, waiting for transfers between devices: 0.01 us -> 3.38 us  [from_above(): return lax.ppermute(values, 'x', [(at, (at + 3) % 4) for at in range(4)])]
  transfers between devices with their start and end apart: 13 -> 13, of which waited for: 6 -> 7; matrix products, arithmetic and copies ran while one was open for 0% -> 0% of each run, Pallas kernels for 12% -> 11%
where the time goes in v11:
time: 178 us; the launch traced here: 177 us
  blocking collectives  110 us (62%)
  Pallas kernels  29.5 us (17%)
  starting transfers between devices  24.2 us (14%)
  waiting for transfers between devices  10.6 us (6%)
    all_to_all x8, blocking collectives, exchange(): return lax.all_to_all(payload, axes, 0, 0)  110 us
    pallas_call x21, Pallas kernels, call(): pl.pallas_call(kernel, out_shape=shapes, in_specs=specs, out_specs=[VMEM]...  29.5 us
    ppermute x5, starting transfers between devices, swap_core(): return lax.ppermute(values, 'core', [(0, 1), (1, 0)])  13.3 us
    ppermute x3, starting transfers between devices, from_above(): return lax.ppermute(values, 'x', [(at, (at + 3) % 4) for at in range(4)])  7.81 us
    ppermute x2, waiting for transfers between devices, from_below(): return lax.ppermute(values, 'x', [(at, (at + 1) % 4) for at in range(4)])  4.1 us
  transfers between devices with their start and end apart: 13, of which 7 were waited for; matrix products, arithmetic and copies ran while one was open for 0% of the time, Pallas kernels for 11%

profile of v11, /device:TPU:1, one launch (start us, length us, event | category | flops | bytes accessed | tf_op | source)
XLA Modules:
  0.0 177.1 jit_solution(17606954057550187681)
XLA Ops:
  0.0 1.4 collective-permute-start
  1.4 1.7 pack.1
  3.1 1.8 %collective-permute-start.3 = (bf16[336,512]{1,0:T(8,128)(2,1)S(1)}, bf16[336,512]{1,0:T(8,128)(2,1)S(1)}, u32[]{:S(2)}, u32[]{:S(2)}) collective-permute-start(bf16[336,512]{1,0:T(8,128)(2,1)S(1)} %get-tuple-element.32.refs_1_.refs_4_), channel_id=1, source_target_pairs={{0,2},{2,0},{1,3},{3,1},{4,6},{6,4},{5,7},{7,5},{8,10},{10,8},{9,1... | collective-permute-start | bytes 1032200 | tf_op jit(solution)/shard_map/ppermute | solution.py:435
  4.9 2.5 %collective-permute-start.2 = (bf16[336,512]{1,0:T(8,128)(2,1)S(1)}, bf16[336,512]{1,0:T(8,128)(2,1)S(1)}, u32[]{:S(2)}, u32[]{:S(2)}) collective-permute-start(bf16[336,512]{1,0:T(8,128)(2,1)S(1)} %get-tuple-element.32.refs_1_.refs_4_), channel_id=1, source_target_pairs={{0,12},{4,0},{8,4},{12,8},{1,13},{5,1},{9,5},{13,9},{2,14},{6,2},{... | collective-permute-start | bytes 1032200 | tf_op jit(solution)/shard_map/ppermute | solution.py:443
  8.1 1.6 copy-done.1
  9.7 0.7 unit.2.refs_2_.refs_4_.refs_3_
  10.4 0.7 unit.3.refs_3_.refs_5_.refs_4_
  11.2 1.3 build.4
  12.5 0.9 collective-permute-done.3.refs_3_.refs_7_
  13.4 1.2 collective-permute-done.2.refs_2_.refs_6_
  14.6 3.1 %collective-permute-done.1.refs_1_.refs_5_ = bf16[336,512]{1,0:T(8,128)(2,1)S(1)} collective-permute-done((bf16[336,512]{1,0:T(8,128)(2,1)S(1)}, bf16[336,512]{1,0:T(8,128)(2,1)S(1)}, u32[]{:S(2)}, u32[]{:S(2)}) %collective-permute-start.1) | collective-permute-done | bytes 344096 | tf_op jit(solution)/shard_map/ppermute | solution.py:439
  17.7 0.4 collective-permute-start.6
  18.1 2.7 %collective-permute-start.5 = (bf16[336,512]{1,0:T(8,128)(2,1)S(1)}, bf16[336,512]{1,0:T(8,128)(2,1)S(1)}, u32[]{:S(2)}, u32[]{:S(2)}) collective-permute-start(bf16[336,512]{1,0:T(8,128)(2,1)S(1)} %collective-permute-done.3.refs_3_.refs_7_), channel_id=1, source_target_pairs={{0,12},{4,0},{8,4},{12,8},{1,13},{5,1},{9,5},{13,9},{2,14},{6,2},{... | collective-permute-start | bytes 1032200 | tf_op jit(solution)/shard_map/ppermute | solution.py:443
  20.7 3.5 %build.5 = (bf16[768,4096]{1,0:T(8,128)(2,1)S(1)}, f32[8,4096]{1,0:T(8,128)S(1)}) custom-call(f32[1]{0:T(128)S(6)} %copy.7.refs_0_, bf16[336,512]{1,0:T(8,128)(2,1)S(1)} %collective-permute-done.1.refs_1_.refs_5_, bf16[336,512]{1,0:T(8,128)(2,1)S(1)} %collective-permute-done.2.refs_2_.refs_6_, bf16[336,512]{1,0:T(8,128)(2,1)S(1)} %collective-permute-done.3.refs_3_.refs_7_, ...), custom_call_target="tpu_custom_call" | custom-call | flops 6442450944 | tf_op jit(solution)/shard_map/build/pallas_call | solution.py:92
  24.2 2.1 %collective-permute-done.5.refs_2_.refs_9_ = bf16[336,512]{1,0:T(8,128)(2,1)S(1)} collective-permute-done((bf16[336,512]{1,0:T(8,128)(2,1)S(1)}, bf16[336,512]{1,0:T(8,128)(2,1)S(1)}, u32[]{:S(2)}, u32[]{:S(2)}) %collective-permute-start.5) | collective-permute-done | bytes 344096 | tf_op jit(solution)/shard_map/ppermute | solution.py:443
  26.4 1.0 collective-permute-done.4.refs_1_.refs_8_
  27.4 0.9 collective-permute-start.7
  28.3 2.7 %collective-permute-start.8 = (bf16[176,512]{1,0:T(8,128)(2,1)S(1)}, bf16[176,512]{1,0:T(8,128)(2,1)S(1)}, u32[]{:S(2)}, u32[]{:S(2)}) collective-permute-start(bf16[176,512]{1,0:T(8,128)(2,1)S(1)} %slice.10), channel_id=1, source_target_pairs={{0,12},{4,0},{8,4},{12,8},{1,13},{5,1},{9,5},{13,9},{2,14},{6,2},{... | collective-permute-start | bytes 540680 | tf_op jit(solution)/shard_map/ppermute | solution.py:443
  31.0 3.5 %build.6 = (bf16[768,4096]{1,0:T(8,128)(2,1)S(1)}, f32[8,4096]{1,0:T(8,128)S(1)}) custom-call(f32[1]{0:T(128)S(6)} %copy.7.refs_0_, bf16[336,512]{1,0:T(8,128)(2,1)S(1)} %collective-permute-done.4.refs_1_.refs_8_, bf16[336,512]{1,0:T(8,128)(2,1)S(1)} %collective-permute-done.5.refs_2_.refs_9_, bf16[336,512]{1,0:T(8,128)(2,1)S(1)} %collective-permute-done.6.refs_3_.refs_10_, ...), custom_call_target="tpu_custom_call" | custom-call | flops 6442450944 | tf_op jit(solution)/shard_map/build/pallas_call | solution.py:92
  34.5 1.3 build.7
  35.9 1.3 side_terms.5
  37.1 3.5 %collective-permute-start.9 = (f32[8,136,256]{2,1,0:T(8,128)S(1)}, f32[8,136,256]{2,1,0:T(8,128)S(1)}, u32[]{:S(2)}, u32[]{:S(2)}) collective-permute-start(f32[8,136,256]{2,1,0:T(8,128)S(1)} %side_terms.5), channel_id=1, source_target_pairs={{0,1},{1,0},{2,3},{3,2},{4,5},{5,4},{6,7},{7,6},{8,9},{9,8},{10,11... | collective-permute-start | bytes 3342344 | tf_op jit(solution)/shard_map/ppermute | solution.py:431
  40.7 1.3 side_terms.4.refs_4_
  41.9 1.1 collective-permute-done.9.refs_5_
  43.0 0.3 pair.2
  43.3 18.5 %all_to_all.40.refs_4_ = bf16[8,144,256]{2,1,0:T(8,128)(2,1)S(1)} all-to-all(bf16[8,144,256]{2,1,0:T(8,128)(2,1)S(1)} %get-tuple-element.52), channel_id=1, replica_groups=mesh['y'=4,'zh'=2,'x'=4,'zl'=2,'core'=2] {'y','zh'}, dimensions={0} | all-to-all | bytes 1179648 | tf_op jit(solution)/shard_map/all_to_all | solution.py:427
  61.8 0.4 centre.2
  62.2 13.1 %all_to_all.41.refs_4_.refs_5_ = bf16[8,144,256]{2,1,0:T(8,128)(2,1)S(1)} all-to-all(bf16[8,144,256]{2,1,0:T(8,128)(2,1)S(1)} %get-tuple-element.53), channel_id=1, replica_groups=mesh['y'=4,'zh'=2,'x'=4,'zl'=2,'core'=2] {'y','zh'}, dimensions={0} | all-to-all | bytes 1179648 | tf_op jit(solution)/shard_map/all_to_all | solution.py:427
  75.3 2.9 %collective-permute-start.10 = (bf16[8,144,256]{2,1,0:T(8,128)(2,1)S(1)}, bf16[8,144,256]{2,1,0:T(8,128)(2,1)S(1)}, u32[]{:S(2)}, u32[]{:S(2)}) collective-permute-start(bf16[8,144,256]{2,1,0:T(8,128)(2,1)S(1)} %all_to_all.41.refs_4_.refs_5_), channel_id=1, source_target_pairs={{0,1},{1,0},{2,3},{3,2},{4,5},{5,4},{6,7},{7,6},{8,9},{9,8},{10,11... | collective-permute-start | bytes 1769480 | tf_op jit(solution)/shard_map/ppermute | solution.py:431
  78.2 2.5 %image_terms.4.refs_6_ = f32[2048,128]{1,0:T(8,128)S(1)} custom-call(bf16[256,4096]{1,0:T(8,128)(2,1)S(1)} %get-tuple-element.33.refs_0_, bf16[768,4096]{1,0:T(8,128)(2,1)S(1)} %get-tuple-element.38.refs_1_, bf16[768,4096]{1,0:T(8,128)(2,1)S(1)} %get-tuple-element.43.refs_2_, bf16[256,4096]{1,0:T(8,128)(2,1)S(1)} %get-tuple-element.47.refs_3_, ...), custom_call_target="tpu_custom_call" | custom-call | flops 1073741824 | tf_op jit(solution)/shard_map/image_terms/pallas_call | solution.py:92
  80.7 2.5 %image_terms.5 = bf16[8,256,128]{2,1,0:T(8,128)(2,1)S(1)} custom-call(bf16[256,4096]{1,0:T(8,128)(2,1)S(1)} %get-tuple-element.33.refs_0_, bf16[768,4096]{1,0:T(8,128)(2,1)S(1)} %get-tuple-element.38.refs_1_, bf16[768,4096]{1,0:T(8,128)(2,1)S(1)} %get-tuple-element.43.refs_2_, bf16[256,4096]{1,0:T(8,128)(2,1)S(1)} %get-tuple-element.47.refs_3_, ...), custom_call_target="tpu_custom_call" | custom-call | flops 1073741824 | tf_op jit(solution)/shard_map/image_terms/pallas_call | solution.py:92
  83.1 13.5 %all_to_all.42.refs_4_ = bf16[8,256,128]{2,1,0:T(8,128)(2,1)S(1)} all-to-all(bf16[8,256,128]{2,1,0:T(8,128)(2,1)S(1)} %image_terms.5), channel_id=1, replica_groups=mesh['y'=4,'zh'=2,'x'=4,'zl'=2,'core'=2] {'x','zl'}, dimensions={0} | all-to-all | bytes 1048576 | tf_op jit(solution)/shard_map/all_to_all | solution.py:427
  96.6 0.2 owner.2
  96.8 11.6 %all_to_all.43.refs_4_ = bf16[8,144,256]{2,1,0:T(8,128)(2,1)S(1)} all-to-all(bf16[8,144,256]{2,1,0:T(8,128)(2,1)S(1)} %owner.2), channel_id=1, replica_groups=mesh['y'=4,'zh'=2,'x'=4,'zl'=2,'core'=2] {'x','zl'}, dimensions={0} | all-to-all | bytes 1179648 | tf_op jit(solution)/shard_map/all_to_all | solution.py:427
  108.4 1.3 side_terms.7
  109.7 2.9 %collective-permute-start.11 = (f32[8,136,256]{2,1,0:T(8,128)S(1)}, f32[8,136,256]{2,1,0:T(8,128)S(1)}, u32[]{:S(2)}, u32[]{:S(2)}) collective-permute-start(f32[8,136,256]{2,1,0:T(8,128)S(1)} %side_terms.7), channel_id=1, source_target_pairs={{0,1},{1,0},{2,3},{3,2},{4,5},{5,4},{6,7},{7,6},{8,9},{9,8},{10,11... | collective-permute-start | bytes 3342344 | tf_op jit(solution)/shard_map/ppermute | solution.py:431
  112.6 1.3 side_terms.6.refs_4_
  113.9 1.1 collective-permute-done.11.refs_5_
  115.0 0.3 pair.3
  115.3 13.8 %all_to_all.44.refs_4_ = bf16[8,144,256]{2,1,0:T(8,128)(2,1)S(1)} all-to-all(bf16[8,144,256]{2,1,0:T(8,128)(2,1)S(1)} %pair.3), channel_id=1, replica_groups=mesh['y'=4,'zh'=2,'x'=4,'zl'=2,'core'=2] {'y','zh'}, dimensions={0} | all-to-all | bytes 1179648 | tf_op jit(solution)/shard_map/all_to_all | solution.py:427
  129.1 0.4 centre.3
  129.5 12.3 %all_to_all.45.refs_4_ = bf16[8,128,256]{2,1,0:T(8,128)(2,1)S(1)} all-to-all(bf16[8,128,256]{2,1,0:T(8,128)(2,1)S(1)} %centre.3), channel_id=1, replica_groups=mesh['y'=4,'zh'=2,'x'=4,'zl'=2,'core'=2] {'y','zh'}, dimensions={0} | all-to-all | bytes 1048576 | tf_op jit(solution)/shard_map/all_to_all | solution.py:427
  141.9 2.6 %collective-permute-start.12 = (bf16[8,128,256]{2,1,0:T(8,128)(2,1)S(1)}, bf16[8,128,256]{2,1,0:T(8,128)(2,1)S(1)}, u32[]{:S(2)}, u32[]{:S(2)}) collective-permute-start(bf16[8,128,256]{2,1,0:T(8,128)(2,1)S(1)} %all_to_all.45.refs_4_), channel_id=1, source_target_pairs={{0,1},{1,0},{2,3},{3,2},{4,5},{5,4},{6,7},{7,6},{8,9},{9,8},{10,11... | collective-permute-start | bytes 1572872 | tf_op jit(solution)/shard_map/ppermute | solution.py:431
  144.5 2.4 %image_terms.6.refs_6_ = f32[2048,128]{1,0:T(8,128)S(1)} custom-call(bf16[256,4096]{1,0:T(8,128)(2,1)S(1)} %get-tuple-element.33.refs_0_, bf16[768,4096]{1,0:T(8,128)(2,1)S(1)} %get-tuple-element.38.refs_1_, bf16[768,4096]{1,0:T(8,128)(2,1)S(1)} %get-tuple-element.43.refs_2_, bf16[256,4096]{1,0:T(8,128)(2,1)S(1)} %get-tuple-element.47.refs_3_, ...), custom_call_target="tpu_custom_call" | custom-call | flops 1073741824 | tf_op jit(solution)/shard_map/image_terms/pallas_call | solution.py:92
  146.9 2.5 %image_terms.7 = bf16[8,256,128]{2,1,0:T(8,128)(2,1)S(1)} custom-call(bf16[256,4096]{1,0:T(8,128)(2,1)S(1)} %get-tuple-element.33.refs_0_, bf16[768,4096]{1,0:T(8,128)(2,1)S(1)} %get-tuple-element.38.refs_1_, bf16[768,4096]{1,0:T(8,128)(2,1)S(1)} %get-tuple-element.43.refs_2_, bf16[256,4096]{1,0:T(8,128)(2,1)S(1)} %get-tuple-element.47.refs_3_, ...), custom_call_target="tpu_custom_call" | custom-call | flops 1073741824 | tf_op jit(solution)/shard_map/image_terms/pallas_call | solution.py:92
  149.4 12.0 %all_to_all.46.refs_0_ = bf16[8,256,128]{2,1,0:T(8,128)(2,1)S(1)} all-to-all(bf16[8,256,128]{2,1,0:T(8,128)(2,1)S(1)} %image_terms.7), channel_id=1, replica_groups=mesh['y'=4,'zh'=2,'x'=4,'zl'=2,'core'=2] {'x','zl'}, dimensions={0} | all-to-all | bytes 1048576 | tf_op jit(solution)/shard_map/all_to_all | solution.py:427
  161.6 14.8 %all_to_all.47 = f32[128,1,128]{2,1,0:T(1,128)S(1)} all-to-all(f32[128,1,128]{2,1,0:T(1,128)S(1)} %broadcast_in_dim.14), channel_id=1, replica_groups=mesh['y'=4,'zh'=2,'x'=4,'zl'=2,'core'=2] {'y','zh','x','zl','core'}, dimensions={0} | all-to-all | bytes 131072 | tf_op jit(solution)/shard_map/all_to_all | solution.py:427
  176.5 0.7 broadcast_divide_fusion
  (18 shorter events, 0.3 us)
Async XLA Ops:
  0.0 10.4 %collective-permute-start = (bf16[2048,512]{1,0:T(8,128)(2,1)}, bf16[2048,512]{1,0:T(8,128)(2,1)S(1)}, u32[]{:S(2)}, u32[]{:S(2)}) collective-permute-start(bf16[2048,512]{1,0:T(8,128)(2,1)} %in_ref.1), channel_id=1, source_target_pairs={{0,1},{1,0},{2,3},{3,2},{4,5},{5,4},{6,7},{7,6},{8,9},{9,8},{10,11... | collective-permute-start | bytes 6291464 | tf_op jit(solution)/shard_map/ppermute | solution.py:431
  3.1 10.2 %collective-permute-start.3 = (bf16[336,512]{1,0:T(8,128)(2,1)S(1)}, bf16[336,512]{1,0:T(8,128)(2,1)S(1)}, u32[]{:S(2)}, u32[]{:S(2)}) collective-permute-start(bf16[336,512]{1,0:T(8,128)(2,1)S(1)} %get-tuple-element.32.refs_1_.refs_4_), channel_id=1, source_target_pairs={{0,2},{2,0},{1,3},{3,1},{4,6},{6,4},{5,7},{7,5},{8,10},{10,8},{9,1... | collective-permute-start | bytes 1032200 | tf_op jit(solution)/shard_map/ppermute | solution.py:435
  4.9 9.7 %collective-permute-start.2 = (bf16[336,512]{1,0:T(8,128)(2,1)S(1)}, bf16[336,512]{1,0:T(8,128)(2,1)S(1)}, u32[]{:S(2)}, u32[]{:S(2)}) collective-permute-start(bf16[336,512]{1,0:T(8,128)(2,1)S(1)} %get-tuple-element.32.refs_1_.refs_4_), channel_id=1, source_target_pairs={{0,12},{4,0},{8,4},{12,8},{1,13},{5,1},{9,5},{13,9},{2,14},{6,2},{... | collective-permute-start | bytes 1032200 | tf_op jit(solution)/shard_map/ppermute | solution.py:443
  7.4 10.3 %collective-permute-start.1 = (bf16[336,512]{1,0:T(8,128)(2,1)S(1)}, bf16[336,512]{1,0:T(8,128)(2,1)S(1)}, u32[]{:S(2)}, u32[]{:S(2)}) collective-permute-start(bf16[336,512]{1,0:T(8,128)(2,1)S(1)} %get-tuple-element.32.refs_1_.refs_4_), channel_id=1, source_target_pairs={{0,4},{4,8},{8,12},{12,0},{1,5},{5,9},{9,13},{13,1},{2,6},{6,10},{... | collective-permute-start | bytes 1032200 | tf_op jit(solution)/shard_map/ppermute | solution.py:439
  8.1 1.6 copy-start.1
  17.7 8.7 %collective-permute-start.6 = (bf16[336,512]{1,0:T(8,128)(2,1)S(1)}, bf16[336,512]{1,0:T(8,128)(2,1)S(1)}, u32[]{:S(2)}, u32[]{:S(2)}) collective-permute-start(bf16[336,512]{1,0:T(8,128)(2,1)S(1)} %collective-permute-done.1.refs_1_.refs_5_), channel_id=1, source_target_pairs={{0,2},{2,0},{1,3},{3,1},{4,6},{6,4},{5,7},{7,5},{8,10},{10,8},{9,1... | collective-permute-start | bytes 1032200 | tf_op jit(solution)/shard_map/ppermute | solution.py:435
  18.1 9.4 %collective-permute-start.4 = (bf16[336,512]{1,0:T(8,128)(2,1)S(1)}, bf16[336,512]{1,0:T(8,128)(2,1)S(1)}, u32[]{:S(2)}, u32[]{:S(2)}) collective-permute-start(bf16[336,512]{1,0:T(8,128)(2,1)S(1)} %collective-permute-done.1.refs_1_.refs_5_), channel_id=1, source_target_pairs={{0,4},{4,8},{8,12},{12,0},{1,5},{5,9},{9,13},{13,1},{2,6},{6,10},{... | collective-permute-start | bytes 1032200 | tf_op jit(solution)/shard_map/ppermute | solution.py:439
  18.1 8.3 %collective-permute-start.5 = (bf16[336,512]{1,0:T(8,128)(2,1)S(1)}, bf16[336,512]{1,0:T(8,128)(2,1)S(1)}, u32[]{:S(2)}, u32[]{:S(2)}) collective-permute-start(bf16[336,512]{1,0:T(8,128)(2,1)S(1)} %collective-permute-done.3.refs_3_.refs_7_), channel_id=1, source_target_pairs={{0,12},{4,0},{8,4},{12,8},{1,13},{5,1},{9,5},{13,9},{2,14},{6,2},{... | collective-permute-start | bytes 1032200 | tf_op jit(solution)/shard_map/ppermute | solution.py:443
  27.4 7.1 %collective-permute-start.7 = (bf16[160,512]{1,0:T(8,128)(2,1)S(1)}, bf16[160,512]{1,0:T(8,128)(2,1)S(1)}, u32[]{:S(2)}, u32[]{:S(2)}) collective-permute-start(bf16[160,512]{1,0:T(8,128)(2,1)S(1)} %slice.9), channel_id=1, source_target_pairs={{0,2},{2,0},{1,3},{3,1},{4,6},{6,4},{5,7},{7,5},{8,10},{10,8},{9,1... | collective-permute-start | bytes 491528 | tf_op jit(solution)/shard_map/ppermute | solution.py:435
  28.3 6.2 %collective-permute-start.8 = (bf16[176,512]{1,0:T(8,128)(2,1)S(1)}, bf16[176,512]{1,0:T(8,128)(2,1)S(1)}, u32[]{:S(2)}, u32[]{:S(2)}) collective-permute-start(bf16[176,512]{1,0:T(8,128)(2,1)S(1)} %slice.10), channel_id=1, source_target_pairs={{0,12},{4,0},{8,4},{12,8},{1,13},{5,1},{9,5},{13,9},{2,14},{6,2},{... | collective-permute-start | bytes 540680 | tf_op jit(solution)/shard_map/ppermute | solution.py:443
  37.1 5.9 %collective-permute-start.9 = (f32[8,136,256]{2,1,0:T(8,128)S(1)}, f32[8,136,256]{2,1,0:T(8,128)S(1)}, u32[]{:S(2)}, u32[]{:S(2)}) collective-permute-start(f32[8,136,256]{2,1,0:T(8,128)S(1)} %side_terms.5), channel_id=1, source_target_pairs={{0,1},{1,0},{2,3},{3,2},{4,5},{5,4},{6,7},{7,6},{8,9},{9,8},{10,11... | collective-permute-start | bytes 3342344 | tf_op jit(solution)/shard_map/ppermute | solution.py:431
  75.3 5.4 %collective-permute-start.10 = (bf16[8,144,256]{2,1,0:T(8,128)(2,1)S(1)}, bf16[8,144,256]{2,1,0:T(8,128)(2,1)S(1)}, u32[]{:S(2)}, u32[]{:S(2)}) collective-permute-start(bf16[8,144,256]{2,1,0:T(8,128)(2,1)S(1)} %all_to_all.41.refs_4_.refs_5_), channel_id=1, source_target_pairs={{0,1},{1,0},{2,3},{3,2},{4,5},{5,4},{6,7},{7,6},{8,9},{9,8},{10,11... | collective-permute-start | bytes 1769480 | tf_op jit(solution)/shard_map/ppermute | solution.py:431
  80.6 16.0 %copy-start = (f32[8,256]{1,0:T(8,128)S(1)}, f32[8,256]{1,0:T(8,128)}, u32[]{:S(2)}) copy-start(f32[8,256]{1,0:T(8,128)} %get-tuple-element.54.refs_5_.refs_1_) | copy-start | bytes 24580
  109.7 5.3 %collective-permute-start.11 = (f32[8,136,256]{2,1,0:T(8,128)S(1)}, f32[8,136,256]{2,1,0:T(8,128)S(1)}, u32[]{:S(2)}, u32[]{:S(2)}) collective-permute-start(f32[8,136,256]{2,1,0:T(8,128)S(1)} %side_terms.7), channel_id=1, source_target_pairs={{0,1},{1,0},{2,3},{3,2},{4,5},{5,4},{6,7},{7,6},{8,9},{9,8},{10,11... | collective-permute-start | bytes 3342344 | tf_op jit(solution)/shard_map/ppermute | solution.py:431
  141.9 5.1 %collective-permute-start.12 = (bf16[8,128,256]{2,1,0:T(8,128)(2,1)S(1)}, bf16[8,128,256]{2,1,0:T(8,128)(2,1)S(1)}, u32[]{:S(2)}, u32[]{:S(2)}) collective-permute-start(bf16[8,128,256]{2,1,0:T(8,128)(2,1)S(1)} %all_to_all.45.refs_4_), channel_id=1, source_target_pairs={{0,1},{1,0},{2,3},{3,2},{4,5},{5,4},{6,7},{7,6},{8,9},{9,8},{10,11... | collective-permute-start | bytes 1572872 | tf_op jit(solution)/shard_map/ppermute | solution.py:431

commit v12 on v11

--- a/solution.py
+++ b/solution.py
@@ -494,15 +494,16 @@
     near = unit(landmarks)
     far = unit(swap_core(landmarks))
     zero, sums_zero = build((1,), 2048, spread, [[packed]], near, far)
-    below, above, across, sums_zero = lax.optimization_barrier((below, above, across, sums_zero))
+    sums_zero, across, above, below = lax.optimization_barrier((sums_zero, across, above, below))
     opposite, across_above, across_below = from_below(below), from_above(across), swap_z(below)
     one, sums_one = build((3,), 2048, spread, [[below], [above], [across]], near, far)
-    opposite, across_above, across_below, sums_one = lax.optimization_barrier(
-        (opposite, across_above, across_below, sums_one)
+    sums_one, across_above, across_below, opposite = lax.optimization_barrier(
+        (sums_one, across_above, across_below, opposite)
     )
     last = [swap_z(opposite[:SPLIT]), from_above(across_above[SPLIT:])]
     two, sums_two = build((3,), 2048, spread, [[opposite], [across_above], [across_below]], near, far)
-    *last, sums_two = lax.optimization_barrier((*last, sums_two))
+    sums_two, *last = lax.optimization_barrier((sums_two, *last[::-1]))
+    last = last[::-1]
     three, sums_three = build((1,), 2048, spread, [last], near, far)
     packs = [packed, below, above, across, opposite, across_above, across_below, *last]
     tiles = (zero, one, two, three)

time: 178 us -> 176 us (0.989)
  waiting for transfers between devices: 10.6 us -> 7.3 us
    ppermute x2, waiting for transfers between devices: 4.1 us -> 1.85 us  [from_below(): return lax.ppermute(values, 'x', [(at, (at + 1) % 4) for at in range(4)])]
  transfers between devices with their start and end apart: 13 -> 13, of which waited for: 7 -> 6; matrix products, arithmetic and copies ran while one was open for 0% -> 0% of each run, Pallas kernels for 11% -> 11%
where the time goes in v12:
time: 176 us; the launch traced here: 175 us
  blocking collectives  110 us (62%)
  Pallas kernels  29.5 us (17%)
  starting transfers between devices  25.3 us (14%)
  waiting for transfers between devices  7.3 us (4%)
    all_to_all x8, blocking collectives, exchange(): return lax.all_to_all(payload, axes, 0, 0)  110 us
    pallas_call x21, Pallas kernels, call(): pl.pallas_call(kernel, out_shape=shapes, in_specs=specs, out_specs=[VMEM]...  29.5 us
    ppermute x5, starting transfers between devices, swap_core(): return lax.ppermute(values, 'core', [(0, 1), (1, 0)])  13.1 us
    ppermute x3, starting transfers between devices, from_above(): return lax.ppermute(values, 'x', [(at, (at + 3) % 4) for at in range(4)])  6.95 us
    ppermute x3, starting transfers between devices, swap_z(): return lax.ppermute(values, 'zl', [(0, 1), (1, 0)])  3.92 us
  transfers between devices with their start and end apart: 13, of which 6 were waited for; matrix products, arithmetic and copies ran while one was open for 0% of the time, Pallas kernels for 11%

profile of v12, /device:TPU:1, one launch (start us, length us, event | category | flops | bytes accessed | tf_op | source)
XLA Modules:
  0.0 175.2 jit_solution(16371776608847284121)
XLA Ops:
  0.0 1.4 collective-permute-start
  1.4 1.7 pack.1
  3.1 1.4 collective-permute-start.3
  4.5 1.4 collective-permute-start.2
  5.9 1.7 collective-permute-start.1
  8.3 1.6 copy-done.1
  9.9 0.7 unit.2.refs_2_.refs_4_.refs_3_
  10.6 0.7 unit.3.refs_3_.refs_5_.refs_4_
  11.3 1.3 build.4
  12.7 1.4 collective-permute-done.3.refs_1_.refs_5_
  14.1 1.4 collective-permute-done.1.refs_3_.refs_7_
  15.5 1.2 collective-permute-start.5
  16.7 2.6 %collective-permute-start.4 = (bf16[336,512]{1,0:T(8,128)(2,1)S(1)}, bf16[336,512]{1,0:T(8,128)(2,1)S(1)}, u32[]{:S(2)}, u32[]{:S(2)}) collective-permute-start(bf16[336,512]{1,0:T(8,128)(2,1)S(1)} %collective-permute-done.1.refs_3_.refs_7_), channel_id=1, source_target_pairs={{0,12},{4,0},{8,4},{12,8},{1,13},{5,1},{9,5},{13,9},{2,14},{6,2},{... | collective-permute-start | bytes 1032200 | tf_op jit(solution)/shard_map/ppermute | solution.py:443
  19.3 3.5 %build.5 = (bf16[768,4096]{1,0:T(8,128)(2,1)S(1)}, f32[8,4096]{1,0:T(8,128)S(1)}) custom-call(f32[1]{0:T(128)S(6)} %copy.7.refs_0_, bf16[336,512]{1,0:T(8,128)(2,1)S(1)} %collective-permute-done.3.refs_1_.refs_5_, bf16[336,512]{1,0:T(8,128)(2,1)S(1)} %collective-permute-done.2.refs_2_.refs_6_, bf16[336,512]{1,0:T(8,128)(2,1)S(1)} %collective-permute-done.1.refs_3_.refs_7_, ...), custom_call_target="tpu_custom_call" | custom-call | flops 6442450944 | tf_op jit(solution)/shard_map/build/pallas_call | solution.py:92
  22.9 1.9 %collective-permute-done.4.refs_2_.refs_9_ = bf16[336,512]{1,0:T(8,128)(2,1)S(1)} collective-permute-done((bf16[336,512]{1,0:T(8,128)(2,1)S(1)}, bf16[336,512]{1,0:T(8,128)(2,1)S(1)}, u32[]{:S(2)}, u32[]{:S(2)}) %collective-permute-start.4) | collective-permute-done | bytes 344096 | tf_op jit(solution)/shard_map/ppermute | solution.py:443
  24.7 0.4 collective-permute-done.6.refs_1_.refs_8_
  25.1 1.0 collective-permute-start.8
  26.1 3.0 %collective-permute-start.7 = (bf16[176,512]{1,0:T(8,128)(2,1)S(1)}, bf16[176,512]{1,0:T(8,128)(2,1)S(1)}, u32[]{:S(2)}, u32[]{:S(2)}) collective-permute-start(bf16[176,512]{1,0:T(8,128)(2,1)S(1)} %slice.9), channel_id=1, source_target_pairs={{0,12},{4,0},{8,4},{12,8},{1,13},{5,1},{9,5},{13,9},{2,14},{6,2},{... | collective-permute-start | bytes 540680 | tf_op jit(solution)/shard_map/ppermute | solution.py:443
  29.1 3.5 %build.6 = (bf16[768,4096]{1,0:T(8,128)(2,1)S(1)}, f32[8,4096]{1,0:T(8,128)S(1)}) custom-call(f32[1]{0:T(128)S(6)} %copy.7.refs_0_, bf16[336,512]{1,0:T(8,128)(2,1)S(1)} %collective-permute-done.6.refs_1_.refs_8_, bf16[336,512]{1,0:T(8,128)(2,1)S(1)} %collective-permute-done.4.refs_2_.refs_9_, bf16[336,512]{1,0:T(8,128)(2,1)S(1)} %collective-permute-done.5.refs_3_.refs_10_, ...), custom_call_target="tpu_custom_call" | custom-call | flops 6442450944 | tf_op jit(solution)/shard_map/build/pallas_call | solution.py:92
  32.6 1.3 build.7
  34.0 1.3 side_terms.5
  35.2 3.2 %collective-permute-start.9 = (f32[8,136,256]{2,1,0:T(8,128)S(1)}, f32[8,136,256]{2,1,0:T(8,128)S(1)}, u32[]{:S(2)}, u32[]{:S(2)}) collective-permute-start(f32[8,136,256]{2,1,0:T(8,128)S(1)} %side_terms.5), channel_id=1, source_target_pairs={{0,1},{1,0},{2,3},{3,2},{4,5},{5,4},{6,7},{7,6},{8,9},{9,8},{10,11... | collective-permute-start | bytes 3342344 | tf_op jit(solution)/shard_map/ppermute | solution.py:431
  38.5 1.3 side_terms.4.refs_4_
  39.7 1.1 collective-permute-done.9.refs_5_
  40.8 0.3 pair.2
  41.1 18.3 %all_to_all.40.refs_4_ = bf16[8,144,256]{2,1,0:T(8,128)(2,1)S(1)} all-to-all(bf16[8,144,256]{2,1,0:T(8,128)(2,1)S(1)} %get-tuple-element.52), channel_id=1, replica_groups=mesh['y'=4,'zh'=2,'x'=4,'zl'=2,'core'=2] {'y','zh'}, dimensions={0} | all-to-all | bytes 1179648 | tf_op jit(solution)/shard_map/all_to_all | solution.py:427
  59.4 0.4 centre.2
  59.8 13.1 %all_to_all.41.refs_4_.refs_5_ = bf16[8,144,256]{2,1,0:T(8,128)(2,1)S(1)} all-to-all(bf16[8,144,256]{2,1,0:T(8,128)(2,1)S(1)} %get-tuple-element.53), channel_id=1, replica_groups=mesh['y'=4,'zh'=2,'x'=4,'zl'=2,'core'=2] {'y','zh'}, dimensions={0} | all-to-all | bytes 1179648 | tf_op jit(solution)/shard_map/all_to_all | solution.py:427
  72.9 2.9 %collective-permute-start.10 = (bf16[8,144,256]{2,1,0:T(8,128)(2,1)S(1)}, bf16[8,144,256]{2,1,0:T(8,128)(2,1)S(1)}, u32[]{:S(2)}, u32[]{:S(2)}) collective-permute-start(bf16[8,144,256]{2,1,0:T(8,128)(2,1)S(1)} %all_to_all.41.refs_4_.refs_5_), channel_id=1, source_target_pairs={{0,1},{1,0},{2,3},{3,2},{4,5},{5,4},{6,7},{7,6},{8,9},{9,8},{10,11... | collective-permute-start | bytes 1769480 | tf_op jit(solution)/shard_map/ppermute | solution.py:431
  75.8 2.5 %image_terms.4.refs_6_ = f32[2048,128]{1,0:T(8,128)S(1)} custom-call(bf16[256,4096]{1,0:T(8,128)(2,1)S(1)} %get-tuple-element.33.refs_0_, bf16[768,4096]{1,0:T(8,128)(2,1)S(1)} %get-tuple-element.38.refs_1_, bf16[768,4096]{1,0:T(8,128)(2,1)S(1)} %get-tuple-element.43.refs_2_, bf16[256,4096]{1,0:T(8,128)(2,1)S(1)} %get-tuple-element.47.refs_3_, ...), custom_call_target="tpu_custom_call" | custom-call | flops 1073741824 | tf_op jit(solution)/shard_map/image_terms/pallas_call | solution.py:92
  78.3 2.5 %image_terms.5 = bf16[8,256,128]{2,1,0:T(8,128)(2,1)S(1)} custom-call(bf16[256,4096]{1,0:T(8,128)(2,1)S(1)} %get-tuple-element.33.refs_0_, bf16[768,4096]{1,0:T(8,128)(2,1)S(1)} %get-tuple-element.38.refs_1_, bf16[768,4096]{1,0:T(8,128)(2,1)S(1)} %get-tuple-element.43.refs_2_, bf16[256,4096]{1,0:T(8,128)(2,1)S(1)} %get-tuple-element.47.refs_3_, ...), custom_call_target="tpu_custom_call" | custom-call | flops 1073741824 | tf_op jit(solution)/shard_map/image_terms/pallas_call | solution.py:92
  80.8 13.9 %all_to_all.42.refs_4_ = bf16[8,256,128]{2,1,0:T(8,128)(2,1)S(1)} all-to-all(bf16[8,256,128]{2,1,0:T(8,128)(2,1)S(1)} %image_terms.5), channel_id=1, replica_groups=mesh['y'=4,'zh'=2,'x'=4,'zl'=2,'core'=2] {'x','zl'}, dimensions={0} | all-to-all | bytes 1048576 | tf_op jit(solution)/shard_map/all_to_all | solution.py:427
  94.7 0.2 owner.2
  94.9 11.6 %all_to_all.43.refs_4_ = bf16[8,144,256]{2,1,0:T(8,128)(2,1)S(1)} all-to-all(bf16[8,144,256]{2,1,0:T(8,128)(2,1)S(1)} %owner.2), channel_id=1, replica_groups=mesh['y'=4,'zh'=2,'x'=4,'zl'=2,'core'=2] {'x','zl'}, dimensions={0} | all-to-all | bytes 1179648 | tf_op jit(solution)/shard_map/all_to_all | solution.py:427
  106.5 1.3 side_terms.7
  107.8 2.9 %collective-permute-start.11 = (f32[8,136,256]{2,1,0:T(8,128)S(1)}, f32[8,136,256]{2,1,0:T(8,128)S(1)}, u32[]{:S(2)}, u32[]{:S(2)}) collective-permute-start(f32[8,136,256]{2,1,0:T(8,128)S(1)} %side_terms.7), channel_id=1, source_target_pairs={{0,1},{1,0},{2,3},{3,2},{4,5},{5,4},{6,7},{7,6},{8,9},{9,8},{10,11... | collective-permute-start | bytes 3342344 | tf_op jit(solution)/shard_map/ppermute | solution.py:431
  110.7 1.3 side_terms.6.refs_4_
  112.0 1.1 collective-permute-done.11.refs_5_
  113.1 0.3 pair.3
  113.4 14.3 %all_to_all.44.refs_4_ = bf16[8,144,256]{2,1,0:T(8,128)(2,1)S(1)} all-to-all(bf16[8,144,256]{2,1,0:T(8,128)(2,1)S(1)} %pair.3), channel_id=1, replica_groups=mesh['y'=4,'zh'=2,'x'=4,'zl'=2,'core'=2] {'y','zh'}, dimensions={0} | all-to-all | bytes 1179648 | tf_op jit(solution)/shard_map/all_to_all | solution.py:427
  127.7 0.4 centre.3
  128.1 12.3 %all_to_all.45.refs_4_ = bf16[8,128,256]{2,1,0:T(8,128)(2,1)S(1)} all-to-all(bf16[8,128,256]{2,1,0:T(8,128)(2,1)S(1)} %centre.3), channel_id=1, replica_groups=mesh['y'=4,'zh'=2,'x'=4,'zl'=2,'core'=2] {'y','zh'}, dimensions={0} | all-to-all | bytes 1048576 | tf_op jit(solution)/shard_map/all_to_all | solution.py:427
  140.4 2.6 %collective-permute-start.12 = (bf16[8,128,256]{2,1,0:T(8,128)(2,1)S(1)}, bf16[8,128,256]{2,1,0:T(8,128)(2,1)S(1)}, u32[]{:S(2)}, u32[]{:S(2)}) collective-permute-start(bf16[8,128,256]{2,1,0:T(8,128)(2,1)S(1)} %all_to_all.45.refs_4_), channel_id=1, source_target_pairs={{0,1},{1,0},{2,3},{3,2},{4,5},{5,4},{6,7},{7,6},{8,9},{9,8},{10,11... | collective-permute-start | bytes 1572872 | tf_op jit(solution)/shard_map/ppermute | solution.py:431
  143.0 2.5 %image_terms.6.refs_6_ = f32[2048,128]{1,0:T(8,128)S(1)} custom-call(bf16[256,4096]{1,0:T(8,128)(2,1)S(1)} %get-tuple-element.33.refs_0_, bf16[768,4096]{1,0:T(8,128)(2,1)S(1)} %get-tuple-element.38.refs_1_, bf16[768,4096]{1,0:T(8,128)(2,1)S(1)} %get-tuple-element.43.refs_2_, bf16[256,4096]{1,0:T(8,128)(2,1)S(1)} %get-tuple-element.47.refs_3_, ...), custom_call_target="tpu_custom_call" | custom-call | flops 1073741824 | tf_op jit(solution)/shard_map/image_terms/pallas_call | solution.py:92
  145.5 2.5 %image_terms.7 = bf16[8,256,128]{2,1,0:T(8,128)(2,1)S(1)} custom-call(bf16[256,4096]{1,0:T(8,128)(2,1)S(1)} %get-tuple-element.33.refs_0_, bf16[768,4096]{1,0:T(8,128)(2,1)S(1)} %get-tuple-element.38.refs_1_, bf16[768,4096]{1,0:T(8,128)(2,1)S(1)} %get-tuple-element.43.refs_2_, bf16[256,4096]{1,0:T(8,128)(2,1)S(1)} %get-tuple-element.47.refs_3_, ...), custom_call_target="tpu_custom_call" | custom-call | flops 1073741824 | tf_op jit(solution)/shard_map/image_terms/pallas_call | solution.py:92
  147.9 12.0 %all_to_all.46.refs_0_ = bf16[8,256,128]{2,1,0:T(8,128)(2,1)S(1)} all-to-all(bf16[8,256,128]{2,1,0:T(8,128)(2,1)S(1)} %image_terms.7), channel_id=1, replica_groups=mesh['y'=4,'zh'=2,'x'=4,'zl'=2,'core'=2] {'x','zl'}, dimensions={0} | all-to-all | bytes 1048576 | tf_op jit(solution)/shard_map/all_to_all | solution.py:427
  160.2 14.3 %all_to_all.47 = f32[128,1,128]{2,1,0:T(1,128)S(1)} all-to-all(f32[128,1,128]{2,1,0:T(1,128)S(1)} %broadcast_in_dim.14), channel_id=1, replica_groups=mesh['y'=4,'zh'=2,'x'=4,'zl'=2,'core'=2] {'y','zh','x','zl','core'}, dimensions={0} | all-to-all | bytes 131072 | tf_op jit(solution)/shard_map/all_to_all | solution.py:427
  174.5 0.7 broadcast_divide_fusion
  (18 shorter events, 0.3 us)
Async XLA Ops:
  0.0 10.6 %collective-permute-start = (bf16[2048,512]{1,0:T(8,128)(2,1)}, bf16[2048,512]{1,0:T(8,128)(2,1)S(1)}, u32[]{:S(2)}, u32[]{:S(2)}) collective-permute-start(bf16[2048,512]{1,0:T(8,128)(2,1)} %in_ref.1), channel_id=1, source_target_pairs={{0,1},{1,0},{2,3},{3,2},{4,5},{5,4},{6,7},{7,6},{8,9},{9,8},{10,11... | collective-permute-start | bytes 6291464 | tf_op jit(solution)/shard_map/ppermute | solution.py:431
  3.1 11.0 %collective-permute-start.3 = (bf16[336,512]{1,0:T(8,128)(2,1)S(1)}, bf16[336,512]{1,0:T(8,128)(2,1)S(1)}, u32[]{:S(2)}, u32[]{:S(2)}) collective-permute-start(bf16[336,512]{1,0:T(8,128)(2,1)S(1)} %get-tuple-element.32.refs_1_.refs_4_), channel_id=1, source_target_pairs={{0,4},{4,8},{8,12},{12,0},{1,5},{5,9},{9,13},{13,1},{2,6},{6,10},{... | collective-permute-start | bytes 1032200 | tf_op jit(solution)/shard_map/ppermute | solution.py:439
  4.5 9.6 %collective-permute-start.2 = (bf16[336,512]{1,0:T(8,128)(2,1)S(1)}, bf16[336,512]{1,0:T(8,128)(2,1)S(1)}, u32[]{:S(2)}, u32[]{:S(2)}) collective-permute-start(bf16[336,512]{1,0:T(8,128)(2,1)S(1)} %get-tuple-element.32.refs_1_.refs_4_), channel_id=1, source_target_pairs={{0,12},{4,0},{8,4},{12,8},{1,13},{5,1},{9,5},{13,9},{2,14},{6,2},{... | collective-permute-start | bytes 1032200 | tf_op jit(solution)/shard_map/ppermute | solution.py:443
  5.9 9.6 %collective-permute-start.1 = (bf16[336,512]{1,0:T(8,128)(2,1)S(1)}, bf16[336,512]{1,0:T(8,128)(2,1)S(1)}, u32[]{:S(2)}, u32[]{:S(2)}) collective-permute-start(bf16[336,512]{1,0:T(8,128)(2,1)S(1)} %get-tuple-element.32.refs_1_.refs_4_), channel_id=1, source_target_pairs={{0,2},{2,0},{1,3},{3,1},{4,6},{6,4},{5,7},{7,5},{8,10},{10,8},{9,1... | collective-permute-start | bytes 1032200 | tf_op jit(solution)/shard_map/ppermute | solution.py:435
  8.3 1.6 copy-start.1
  15.5 9.6 %collective-permute-start.6 = (bf16[336,512]{1,0:T(8,128)(2,1)S(1)}, bf16[336,512]{1,0:T(8,128)(2,1)S(1)}, u32[]{:S(2)}, u32[]{:S(2)}) collective-permute-start(bf16[336,512]{1,0:T(8,128)(2,1)S(1)} %collective-permute-done.3.refs_1_.refs_5_), channel_id=1, source_target_pairs={{0,4},{4,8},{8,12},{12,0},{1,5},{5,9},{9,13},{13,1},{2,6},{6,10},{... | collective-permute-start | bytes 1032200 | tf_op jit(solution)/shard_map/ppermute | solution.py:439
  15.5 9.6 %collective-permute-start.5 = (bf16[336,512]{1,0:T(8,128)(2,1)S(1)}, bf16[336,512]{1,0:T(8,128)(2,1)S(1)}, u32[]{:S(2)}, u32[]{:S(2)}) collective-permute-start(bf16[336,512]{1,0:T(8,128)(2,1)S(1)} %collective-permute-done.3.refs_1_.refs_5_), channel_id=1, source_target_pairs={{0,2},{2,0},{1,3},{3,1},{4,6},{6,4},{5,7},{7,5},{8,10},{10,8},{9,1... | collective-permute-start | bytes 1032200 | tf_op jit(solution)/shard_map/ppermute | solution.py:435
  16.7 8.0 %collective-permute-start.4 = (bf16[336,512]{1,0:T(8,128)(2,1)S(1)}, bf16[336,512]{1,0:T(8,128)(2,1)S(1)}, u32[]{:S(2)}, u32[]{:S(2)}) collective-permute-start(bf16[336,512]{1,0:T(8,128)(2,1)S(1)} %collective-permute-done.1.refs_3_.refs_7_), channel_id=1, source_target_pairs={{0,12},{4,0},{8,4},{12,8},{1,13},{5,1},{9,5},{13,9},{2,14},{6,2},{... | collective-permute-start | bytes 1032200 | tf_op jit(solution)/shard_map/ppermute | solution.py:443
  25.1 7.5 %collective-permute-start.8 = (bf16[160,512]{1,0:T(8,128)(2,1)S(1)}, bf16[160,512]{1,0:T(8,128)(2,1)S(1)}, u32[]{:S(2)}, u32[]{:S(2)}) collective-permute-start(bf16[160,512]{1,0:T(8,128)(2,1)S(1)} %slice.10), channel_id=1, source_target_pairs={{0,2},{2,0},{1,3},{3,1},{4,6},{6,4},{5,7},{7,5},{8,10},{10,8},{9,1... | collective-permute-start | bytes 491528 | tf_op jit(solution)/shard_map/ppermute | solution.py:435
  26.1 6.5 %collective-permute-start.7 = (bf16[176,512]{1,0:T(8,128)(2,1)S(1)}, bf16[176,512]{1,0:T(8,128)(2,1)S(1)}, u32[]{:S(2)}, u32[]{:S(2)}) collective-permute-start(bf16[176,512]{1,0:T(8,128)(2,1)S(1)} %slice.9), channel_id=1, source_target_pairs={{0,12},{4,0},{8,4},{12,8},{1,13},{5,1},{9,5},{13,9},{2,14},{6,2},{... | collective-permute-start | bytes 540680 | tf_op jit(solution)/shard_map/ppermute | solution.py:443
  35.2 5.6 %collective-permute-start.9 = (f32[8,136,256]{2,1,0:T(8,128)S(1)}, f32[8,136,256]{2,1,0:T(8,128)S(1)}, u32[]{:S(2)}, u32[]{:S(2)}) collective-permute-start(f32[8,136,256]{2,1,0:T(8,128)S(1)} %side_terms.5), channel_id=1, source_target_pairs={{0,1},{1,0},{2,3},{3,2},{4,5},{5,4},{6,7},{7,6},{8,9},{9,8},{10,11... | collective-permute-start | bytes 3342344 | tf_op jit(solution)/shard_map/ppermute | solution.py:431
  72.9 5.4 %collective-permute-start.10 = (bf16[8,144,256]{2,1,0:T(8,128)(2,1)S(1)}, bf16[8,144,256]{2,1,0:T(8,128)(2,1)S(1)}, u32[]{:S(2)}, u32[]{:S(2)}) collective-permute-start(bf16[8,144,256]{2,1,0:T(8,128)(2,1)S(1)} %all_to_all.41.refs_4_.refs_5_), channel_id=1, source_target_pairs={{0,1},{1,0},{2,3},{3,2},{4,5},{5,4},{6,7},{7,6},{8,9},{9,8},{10,11... | collective-permute-start | bytes 1769480 | tf_op jit(solution)/shard_map/ppermute | solution.py:431
  78.3 16.4 %copy-start = (f32[8,256]{1,0:T(8,128)S(1)}, f32[8,256]{1,0:T(8,128)}, u32[]{:S(2)}) copy-start(f32[8,256]{1,0:T(8,128)} %get-tuple-element.54.refs_5_.refs_1_) | copy-start | bytes 24580
  107.8 5.3 %collective-permute-start.11 = (f32[8,136,256]{2,1,0:T(8,128)S(1)}, f32[8,136,256]{2,1,0:T(8,128)S(1)}, u32[]{:S(2)}, u32[]{:S(2)}) collective-permute-start(f32[8,136,256]{2,1,0:T(8,128)S(1)} %side_terms.7), channel_id=1, source_target_pairs={{0,1},{1,0},{2,3},{3,2},{4,5},{5,4},{6,7},{7,6},{8,9},{9,8},{10,11... | collective-permute-start | bytes 3342344 | tf_op jit(solution)/shard_map/ppermute | solution.py:431
  140.4 5.1 %collective-permute-start.12 = (bf16[8,128,256]{2,1,0:T(8,128)(2,1)S(1)}, bf16[8,128,256]{2,1,0:T(8,128)(2,1)S(1)}, u32[]{:S(2)}, u32[]{:S(2)}) collective-permute-start(bf16[8,128,256]{2,1,0:T(8,128)(2,1)S(1)} %all_to_all.45.refs_4_), channel_id=1, source_target_pairs={{0,1},{1,0},{2,3},{3,2},{4,5},{5,4},{6,7},{7,6},{8,9},{9,8},{10,11... | collective-permute-start | bytes 1572872 | tf_op jit(solution)/shard_map/ppermute | solution.py:431

commit v13 on v12

--- a/solution.py
+++ b/solution.py
@@ -500,7 +500,7 @@
     sums_one, across_above, across_below, opposite = lax.optimization_barrier(
         (sums_one, across_above, across_below, opposite)
     )
-    last = [swap_z(opposite[:SPLIT]), from_above(across_above[SPLIT:])]
+    last = [from_above(across_above[:SPLIT]), swap_z(opposite[SPLIT:])]
     two, sums_two = build((3,), 2048, spread, [[opposite], [across_above], [across_below]], near, far)
     sums_two, *last = lax.optimization_barrier((sums_two, *last[::-1]))
     last = last[::-1]

time: 176 us -> 176 us (level)
  transfers between devices with their start and end apart: 13 -> 13, of which waited for: 6 -> 7; matrix products, arithmetic and copies ran while one was open for 0% -> 0% of each run, Pallas kernels for 11% -> 11%
where the time goes in v13:
time: 176 us; the launch traced here: 175 us
  blocking collectives  109 us (62%)
  Pallas kernels  29.5 us (17%)
  starting transfers between devices  26.1 us (15%)
  waiting for transfers between devices  7.54 us (4%)
    all_to_all x8, blocking collectives, exchange(): return lax.all_to_all(payload, axes, 0, 0)  109 us
    pallas_call x21, Pallas kernels, call(): pl.pallas_call(kernel, out_shape=shapes, in_specs=specs, out_specs=[VMEM]...  29.5 us
    ppermute x5, starting transfers between devices, swap_core(): return lax.ppermute(values, 'core', [(0, 1), (1, 0)])  13.9 us
    ppermute x3, starting transfers between devices, from_above(): return lax.ppermute(values, 'x', [(at, (at + 3) % 4) for at in range(4)])  7.06 us
    ppermute x3, starting transfers between devices, swap_z(): return lax.ppermute(values, 'zl', [(0, 1), (1, 0)])  3.8 us
  transfers between devices with their start and end apart: 13, of which 7 were waited for; matrix products, arithmetic and copies ran while one was open for 0% of the time, Pallas kernels for 11%

profile of v13, /device:TPU:1, one launch (start us, length us, event | category | flops | bytes accessed | tf_op | source)
XLA Modules:
  0.0 175.1 jit_solution(2599781781433121305)
XLA Ops:
  0.0 1.4 collective-permute-start
  1.4 1.7 pack.1
  3.1 1.4 collective-permute-start.3
  4.5 1.4 collective-permute-start.2
  5.9 1.7 collective-permute-start.1
  8.3 1.6 copy-done.1
  9.9 0.7 unit.2.refs_2_.refs_4_.refs_3_
  10.6 0.7 unit.3.refs_3_.refs_5_.refs_4_
  11.3 1.3 build.4
  12.7 1.4 collective-permute-done.3.refs_1_.refs_5_
  14.1 1.4 collective-permute-done.1.refs_3_.refs_7_
  15.5 1.2 collective-permute-start.5
  16.7 2.6 %collective-permute-start.4 = (bf16[336,512]{1,0:T(8,128)(2,1)S(1)}, bf16[336,512]{1,0:T(8,128)(2,1)S(1)}, u32[]{:S(2)}, u32[]{:S(2)}) collective-permute-start(bf16[336,512]{1,0:T(8,128)(2,1)S(1)} %collective-permute-done.1.refs_3_.refs_7_), channel_id=1, source_target_pairs={{0,12},{4,0},{8,4},{12,8},{1,13},{5,1},{9,5},{13,9},{2,14},{6,2},{... | collective-permute-start | bytes 1032200 | tf_op jit(solution)/shard_map/ppermute | solution.py:443
  19.3 3.5 %build.5 = (bf16[768,4096]{1,0:T(8,128)(2,1)S(1)}, f32[8,4096]{1,0:T(8,128)S(1)}) custom-call(f32[1]{0:T(128)S(6)} %copy.7.refs_0_, bf16[336,512]{1,0:T(8,128)(2,1)S(1)} %collective-permute-done.3.refs_1_.refs_5_, bf16[336,512]{1,0:T(8,128)(2,1)S(1)} %collective-permute-done.2.refs_2_.refs_6_, bf16[336,512]{1,0:T(8,128)(2,1)S(1)} %collective-permute-done.1.refs_3_.refs_7_, ...), custom_call_target="tpu_custom_call" | custom-call | flops 6442450944 | tf_op jit(solution)/shard_map/build/pallas_call | solution.py:92
  22.9 1.9 %collective-permute-done.4.refs_2_.refs_9_ = bf16[336,512]{1,0:T(8,128)(2,1)S(1)} collective-permute-done((bf16[336,512]{1,0:T(8,128)(2,1)S(1)}, bf16[336,512]{1,0:T(8,128)(2,1)S(1)}, u32[]{:S(2)}, u32[]{:S(2)}) %collective-permute-start.4) | collective-permute-done | bytes 344096 | tf_op jit(solution)/shard_map/ppermute | solution.py:443
  24.7 0.4 collective-permute-done.6.refs_1_.refs_8_
  25.1 3.1 %collective-permute-start.8 = (bf16[160,512]{1,0:T(8,128)(2,1)S(1)}, bf16[160,512]{1,0:T(8,128)(2,1)S(1)}, u32[]{:S(2)}, u32[]{:S(2)}) collective-permute-start(bf16[160,512]{1,0:T(8,128)(2,1)S(1)} %slice.10), channel_id=1, source_target_pairs={{0,12},{4,0},{8,4},{12,8},{1,13},{5,1},{9,5},{13,9},{2,14},{6,2},{... | collective-permute-start | bytes 491528 | tf_op jit(solution)/shard_map/ppermute | solution.py:443
  28.2 0.8 collective-permute-start.7
  29.1 3.5 %build.6 = (bf16[768,4096]{1,0:T(8,128)(2,1)S(1)}, f32[8,4096]{1,0:T(8,128)S(1)}) custom-call(f32[1]{0:T(128)S(6)} %copy.7.refs_0_, bf16[336,512]{1,0:T(8,128)(2,1)S(1)} %collective-permute-done.6.refs_1_.refs_8_, bf16[336,512]{1,0:T(8,128)(2,1)S(1)} %collective-permute-done.4.refs_2_.refs_9_, bf16[336,512]{1,0:T(8,128)(2,1)S(1)} %collective-permute-done.5.refs_3_.refs_10_, ...), custom_call_target="tpu_custom_call" | custom-call | flops 6442450944 | tf_op jit(solution)/shard_map/build/pallas_call | solution.py:92
  32.6 0.2 collective-permute-done.7.refs_2_.refs_12_
  32.8 1.3 build.7
  34.2 1.3 side_terms.5
  35.4 4.4 %collective-permute-start.9 = (f32[8,136,256]{2,1,0:T(8,128)S(1)}, f32[8,136,256]{2,1,0:T(8,128)S(1)}, u32[]{:S(2)}, u32[]{:S(2)}) collective-permute-start(f32[8,136,256]{2,1,0:T(8,128)S(1)} %side_terms.5), channel_id=1, source_target_pairs={{0,1},{1,0},{2,3},{3,2},{4,5},{5,4},{6,7},{7,6},{8,9},{9,8},{10,11... | collective-permute-start | bytes 3342344 | tf_op jit(solution)/shard_map/ppermute | solution.py:431
  39.8 1.3 side_terms.4.refs_4_
  41.1 1.1 collective-permute-done.9.refs_5_
  42.2 0.3 pair.2
  42.5 18.5 %all_to_all.40.refs_4_ = bf16[8,144,256]{2,1,0:T(8,128)(2,1)S(1)} all-to-all(bf16[8,144,256]{2,1,0:T(8,128)(2,1)S(1)} %get-tuple-element.52), channel_id=1, replica_groups=mesh['y'=4,'zh'=2,'x'=4,'zl'=2,'core'=2] {'y','zh'}, dimensions={0} | all-to-all | bytes 1179648 | tf_op jit(solution)/shard_map/all_to_all | solution.py:427
  61.0 0.4 centre.2
  61.4 13.1 %all_to_all.41.refs_4_.refs_5_ = bf16[8,144,256]{2,1,0:T(8,128)(2,1)S(1)} all-to-all(bf16[8,144,256]{2,1,0:T(8,128)(2,1)S(1)} %get-tuple-element.53), channel_id=1, replica_groups=mesh['y'=4,'zh'=2,'x'=4,'zl'=2,'core'=2] {'y','zh'}, dimensions={0} | all-to-all | bytes 1179648 | tf_op jit(solution)/shard_map/all_to_all | solution.py:427
  74.4 2.9 %collective-permute-start.10 = (bf16[8,144,256]{2,1,0:T(8,128)(2,1)S(1)}, bf16[8,144,256]{2,1,0:T(8,128)(2,1)S(1)}, u32[]{:S(2)}, u32[]{:S(2)}) collective-permute-start(bf16[8,144,256]{2,1,0:T(8,128)(2,1)S(1)} %all_to_all.41.refs_4_.refs_5_), channel_id=1, source_target_pairs={{0,1},{1,0},{2,3},{3,2},{4,5},{5,4},{6,7},{7,6},{8,9},{9,8},{10,11... | collective-permute-start | bytes 1769480 | tf_op jit(solution)/shard_map/ppermute | solution.py:431
  77.3 2.5 %image_terms.4.refs_6_ = f32[2048,128]{1,0:T(8,128)S(1)} custom-call(bf16[256,4096]{1,0:T(8,128)(2,1)S(1)} %get-tuple-element.33.refs_0_, bf16[768,4096]{1,0:T(8,128)(2,1)S(1)} %get-tuple-element.38.refs_1_, bf16[768,4096]{1,0:T(8,128)(2,1)S(1)} %get-tuple-element.43.refs_2_, bf16[256,4096]{1,0:T(8,128)(2,1)S(1)} %get-tuple-element.47.refs_3_, ...), custom_call_target="tpu_custom_call" | custom-call | flops 1073741824 | tf_op jit(solution)/shard_map/image_terms/pallas_call | solution.py:92
  79.8 2.5 %image_terms.5 = bf16[8,256,128]{2,1,0:T(8,128)(2,1)S(1)} custom-call(bf16[256,4096]{1,0:T(8,128)(2,1)S(1)} %get-tuple-element.33.refs_0_, bf16[768,4096]{1,0:T(8,128)(2,1)S(1)} %get-tuple-element.38.refs_1_, bf16[768,4096]{1,0:T(8,128)(2,1)S(1)} %get-tuple-element.43.refs_2_, bf16[256,4096]{1,0:T(8,128)(2,1)S(1)} %get-tuple-element.47.refs_3_, ...), custom_call_target="tpu_custom_call" | custom-call | flops 1073741824 | tf_op jit(solution)/shard_map/image_terms/pallas_call | solution.py:92
  82.3 12.1 %all_to_all.42.refs_4_ = bf16[8,256,128]{2,1,0:T(8,128)(2,1)S(1)} all-to-all(bf16[8,256,128]{2,1,0:T(8,128)(2,1)S(1)} %image_terms.5), channel_id=1, replica_groups=mesh['y'=4,'zh'=2,'x'=4,'zl'=2,'core'=2] {'x','zl'}, dimensions={0} | all-to-all | bytes 1048576 | tf_op jit(solution)/shard_map/all_to_all | solution.py:427
  94.6 12.1 %all_to_all.43.refs_4_ = bf16[8,144,256]{2,1,0:T(8,128)(2,1)S(1)} all-to-all(bf16[8,144,256]{2,1,0:T(8,128)(2,1)S(1)} %owner.2), channel_id=1, replica_groups=mesh['y'=4,'zh'=2,'x'=4,'zl'=2,'core'=2] {'x','zl'}, dimensions={0} | all-to-all | bytes 1179648 | tf_op jit(solution)/shard_map/all_to_all | solution.py:427
  106.7 1.3 side_terms.7
  108.0 2.6 %collective-permute-start.11 = (f32[8,136,256]{2,1,0:T(8,128)S(1)}, f32[8,136,256]{2,1,0:T(8,128)S(1)}, u32[]{:S(2)}, u32[]{:S(2)}) collective-permute-start(f32[8,136,256]{2,1,0:T(8,128)S(1)} %side_terms.7), channel_id=1, source_target_pairs={{0,1},{1,0},{2,3},{3,2},{4,5},{5,4},{6,7},{7,6},{8,9},{9,8},{10,11... | collective-permute-start | bytes 3342344 | tf_op jit(solution)/shard_map/ppermute | solution.py:431
  110.6 1.3 side_terms.6.refs_4_
  111.8 1.1 collective-permute-done.11.refs_5_
  112.9 0.3 pair.3
  113.3 13.8 %all_to_all.44.refs_4_ = bf16[8,144,256]{2,1,0:T(8,128)(2,1)S(1)} all-to-all(bf16[8,144,256]{2,1,0:T(8,128)(2,1)S(1)} %pair.3), channel_id=1, replica_groups=mesh['y'=4,'zh'=2,'x'=4,'zl'=2,'core'=2] {'y','zh'}, dimensions={0} | all-to-all | bytes 1179648 | tf_op jit(solution)/shard_map/all_to_all | solution.py:427
  127.0 0.4 centre.3
  127.5 12.4 %all_to_all.45.refs_4_ = bf16[8,128,256]{2,1,0:T(8,128)(2,1)S(1)} all-to-all(bf16[8,128,256]{2,1,0:T(8,128)(2,1)S(1)} %centre.3), channel_id=1, replica_groups=mesh['y'=4,'zh'=2,'x'=4,'zl'=2,'core'=2] {'y','zh'}, dimensions={0} | all-to-all | bytes 1048576 | tf_op jit(solution)/shard_map/all_to_all | solution.py:427
  139.8 2.6 %collective-permute-start.12 = (bf16[8,128,256]{2,1,0:T(8,128)(2,1)S(1)}, bf16[8,128,256]{2,1,0:T(8,128)(2,1)S(1)}, u32[]{:S(2)}, u32[]{:S(2)}) collective-permute-start(bf16[8,128,256]{2,1,0:T(8,128)(2,1)S(1)} %all_to_all.45.refs_4_), channel_id=1, source_target_pairs={{0,1},{1,0},{2,3},{3,2},{4,5},{5,4},{6,7},{7,6},{8,9},{9,8},{10,11... | collective-permute-start | bytes 1572872 | tf_op jit(solution)/shard_map/ppermute | solution.py:431
  142.4 2.4 %image_terms.6.refs_6_ = f32[2048,128]{1,0:T(8,128)S(1)} custom-call(bf16[256,4096]{1,0:T(8,128)(2,1)S(1)} %get-tuple-element.33.refs_0_, bf16[768,4096]{1,0:T(8,128)(2,1)S(1)} %get-tuple-element.38.refs_1_, bf16[768,4096]{1,0:T(8,128)(2,1)S(1)} %get-tuple-element.43.refs_2_, bf16[256,4096]{1,0:T(8,128)(2,1)S(1)} %get-tuple-element.47.refs_3_, ...), custom_call_target="tpu_custom_call" | custom-call | flops 1073741824 | tf_op jit(solution)/shard_map/image_terms/pallas_call | solution.py:92
  144.9 2.5 %image_terms.7 = bf16[8,256,128]{2,1,0:T(8,128)(2,1)S(1)} custom-call(bf16[256,4096]{1,0:T(8,128)(2,1)S(1)} %get-tuple-element.33.refs_0_, bf16[768,4096]{1,0:T(8,128)(2,1)S(1)} %get-tuple-element.38.refs_1_, bf16[768,4096]{1,0:T(8,128)(2,1)S(1)} %get-tuple-element.43.refs_2_, bf16[256,4096]{1,0:T(8,128)(2,1)S(1)} %get-tuple-element.47.refs_3_, ...), custom_call_target="tpu_custom_call" | custom-call | flops 1073741824 | tf_op jit(solution)/shard_map/image_terms/pallas_call | solution.py:92
  147.4 12.0 %all_to_all.46.refs_0_ = bf16[8,256,128]{2,1,0:T(8,128)(2,1)S(1)} all-to-all(bf16[8,256,128]{2,1,0:T(8,128)(2,1)S(1)} %image_terms.7), channel_id=1, replica_groups=mesh['y'=4,'zh'=2,'x'=4,'zl'=2,'core'=2] {'x','zl'}, dimensions={0} | all-to-all | bytes 1048576 | tf_op jit(solution)/shard_map/all_to_all | solution.py:427
  159.6 14.8 %all_to_all.47 = f32[128,1,128]{2,1,0:T(1,128)S(1)} all-to-all(f32[128,1,128]{2,1,0:T(1,128)S(1)} %broadcast_in_dim.14), channel_id=1, replica_groups=mesh['y'=4,'zh'=2,'x'=4,'zl'=2,'core'=2] {'y','zh','x','zl','core'}, dimensions={0} | all-to-all | bytes 131072 | tf_op jit(solution)/shard_map/all_to_all | solution.py:427
  174.4 0.7 broadcast_divide_fusion
  (18 shorter events, 0.4 us)
Async XLA Ops:
  0.0 10.6 %collective-permute-start = (bf16[2048,512]{1,0:T(8,128)(2,1)}, bf16[2048,512]{1,0:T(8,128)(2,1)S(1)}, u32[]{:S(2)}, u32[]{:S(2)}) collective-permute-start(bf16[2048,512]{1,0:T(8,128)(2,1)} %in_ref.1), channel_id=1, source_target_pairs={{0,1},{1,0},{2,3},{3,2},{4,5},{5,4},{6,7},{7,6},{8,9},{9,8},{10,11... | collective-permute-start | bytes 6291464 | tf_op jit(solution)/shard_map/ppermute | solution.py:431
  3.1 11.0 %collective-permute-start.3 = (bf16[336,512]{1,0:T(8,128)(2,1)S(1)}, bf16[336,512]{1,0:T(8,128)(2,1)S(1)}, u32[]{:S(2)}, u32[]{:S(2)}) collective-permute-start(bf16[336,512]{1,0:T(8,128)(2,1)S(1)} %get-tuple-element.32.refs_1_.refs_4_), channel_id=1, source_target_pairs={{0,4},{4,8},{8,12},{12,0},{1,5},{5,9},{9,13},{13,1},{2,6},{6,10},{... | collective-permute-start | bytes 1032200 | tf_op jit(solution)/shard_map/ppermute | solution.py:439
  4.5 9.6 %collective-permute-start.2 = (bf16[336,512]{1,0:T(8,128)(2,1)S(1)}, bf16[336,512]{1,0:T(8,128)(2,1)S(1)}, u32[]{:S(2)}, u32[]{:S(2)}) collective-permute-start(bf16[336,512]{1,0:T(8,128)(2,1)S(1)} %get-tuple-element.32.refs_1_.refs_4_), channel_id=1, source_target_pairs={{0,12},{4,0},{8,4},{12,8},{1,13},{5,1},{9,5},{13,9},{2,14},{6,2},{... | collective-permute-start | bytes 1032200 | tf_op jit(solution)/shard_map/ppermute | solution.py:443
  5.9 9.6 %collective-permute-start.1 = (bf16[336,512]{1,0:T(8,128)(2,1)S(1)}, bf16[336,512]{1,0:T(8,128)(2,1)S(1)}, u32[]{:S(2)}, u32[]{:S(2)}) collective-permute-start(bf16[336,512]{1,0:T(8,128)(2,1)S(1)} %get-tuple-element.32.refs_1_.refs_4_), channel_id=1, source_target_pairs={{0,2},{2,0},{1,3},{3,1},{4,6},{6,4},{5,7},{7,5},{8,10},{10,8},{9,1... | collective-permute-start | bytes 1032200 | tf_op jit(solution)/shard_map/ppermute | solution.py:435
  8.3 1.6 copy-start.1
  15.5 9.6 %collective-permute-start.6 = (bf16[336,512]{1,0:T(8,128)(2,1)S(1)}, bf16[336,512]{1,0:T(8,128)(2,1)S(1)}, u32[]{:S(2)}, u32[]{:S(2)}) collective-permute-start(bf16[336,512]{1,0:T(8,128)(2,1)S(1)} %collective-permute-done.3.refs_1_.refs_5_), channel_id=1, source_target_pairs={{0,4},{4,8},{8,12},{12,0},{1,5},{5,9},{9,13},{13,1},{2,6},{6,10},{... | collective-permute-start | bytes 1032200 | tf_op jit(solution)/shard_map/ppermute | solution.py:439
  15.5 9.6 %collective-permute-start.5 = (bf16[336,512]{1,0:T(8,128)(2,1)S(1)}, bf16[336,512]{1,0:T(8,128)(2,1)S(1)}, u32[]{:S(2)}, u32[]{:S(2)}) collective-permute-start(bf16[336,512]{1,0:T(8,128)(2,1)S(1)} %collective-permute-done.3.refs_1_.refs_5_), channel_id=1, source_target_pairs={{0,2},{2,0},{1,3},{3,1},{4,6},{6,4},{5,7},{7,5},{8,10},{10,8},{9,1... | collective-permute-start | bytes 1032200 | tf_op jit(solution)/shard_map/ppermute | solution.py:435
  16.7 8.0 %collective-permute-start.4 = (bf16[336,512]{1,0:T(8,128)(2,1)S(1)}, bf16[336,512]{1,0:T(8,128)(2,1)S(1)}, u32[]{:S(2)}, u32[]{:S(2)}) collective-permute-start(bf16[336,512]{1,0:T(8,128)(2,1)S(1)} %collective-permute-done.1.refs_3_.refs_7_), channel_id=1, source_target_pairs={{0,12},{4,0},{8,4},{12,8},{1,13},{5,1},{9,5},{13,9},{2,14},{6,2},{... | collective-permute-start | bytes 1032200 | tf_op jit(solution)/shard_map/ppermute | solution.py:443
  25.1 7.5 %collective-permute-start.8 = (bf16[160,512]{1,0:T(8,128)(2,1)S(1)}, bf16[160,512]{1,0:T(8,128)(2,1)S(1)}, u32[]{:S(2)}, u32[]{:S(2)}) collective-permute-start(bf16[160,512]{1,0:T(8,128)(2,1)S(1)} %slice.10), channel_id=1, source_target_pairs={{0,12},{4,0},{8,4},{12,8},{1,13},{5,1},{9,5},{13,9},{2,14},{6,2},{... | collective-permute-start | bytes 491528 | tf_op jit(solution)/shard_map/ppermute | solution.py:443
  28.2 4.6 %collective-permute-start.7 = (bf16[176,512]{1,0:T(8,128)(2,1)S(1)}, bf16[176,512]{1,0:T(8,128)(2,1)S(1)}, u32[]{:S(2)}, u32[]{:S(2)}) collective-permute-start(bf16[176,512]{1,0:T(8,128)(2,1)S(1)} %slice.9), channel_id=1, source_target_pairs={{0,2},{2,0},{1,3},{3,1},{4,6},{6,4},{5,7},{7,5},{8,10},{10,8},{9,1... | collective-permute-start | bytes 540680 | tf_op jit(solution)/shard_map/ppermute | solution.py:435
  35.4 6.8 %collective-permute-start.9 = (f32[8,136,256]{2,1,0:T(8,128)S(1)}, f32[8,136,256]{2,1,0:T(8,128)S(1)}, u32[]{:S(2)}, u32[]{:S(2)}) collective-permute-start(f32[8,136,256]{2,1,0:T(8,128)S(1)} %side_terms.5), channel_id=1, source_target_pairs={{0,1},{1,0},{2,3},{3,2},{4,5},{5,4},{6,7},{7,6},{8,9},{9,8},{10,11... | collective-permute-start | bytes 3342344 | tf_op jit(solution)/shard_map/ppermute | solution.py:431
  74.4 5.4 %collective-permute-start.10 = (bf16[8,144,256]{2,1,0:T(8,128)(2,1)S(1)}, bf16[8,144,256]{2,1,0:T(8,128)(2,1)S(1)}, u32[]{:S(2)}, u32[]{:S(2)}) collective-permute-start(bf16[8,144,256]{2,1,0:T(8,128)(2,1)S(1)} %all_to_all.41.refs_4_.refs_5_), channel_id=1, source_target_pairs={{0,1},{1,0},{2,3},{3,2},{4,5},{5,4},{6,7},{7,6},{8,9},{9,8},{10,11... | collective-permute-start | bytes 1769480 | tf_op jit(solution)/shard_map/ppermute | solution.py:431
  79.8 14.6 %copy-start = (f32[8,256]{1,0:T(8,128)S(1)}, f32[8,256]{1,0:T(8,128)}, u32[]{:S(2)}) copy-start(f32[8,256]{1,0:T(8,128)} %get-tuple-element.54.refs_5_.refs_1_) | copy-start | bytes 24580
  108.0 5.0 %collective-permute-start.11 = (f32[8,136,256]{2,1,0:T(8,128)S(1)}, f32[8,136,256]{2,1,0:T(8,128)S(1)}, u32[]{:S(2)}, u32[]{:S(2)}) collective-permute-start(f32[8,136,256]{2,1,0:T(8,128)S(1)} %side_terms.7), channel_id=1, source_target_pairs={{0,1},{1,0},{2,3},{3,2},{4,5},{5,4},{6,7},{7,6},{8,9},{9,8},{10,11... | collective-permute-start | bytes 3342344 | tf_op jit(solution)/shard_map/ppermute | solution.py:431
  139.8 5.1 %collective-permute-start.12 = (bf16[8,128,256]{2,1,0:T(8,128)(2,1)S(1)}, bf16[8,128,256]{2,1,0:T(8,128)(2,1)S(1)}, u32[]{:S(2)}, u32[]{:S(2)}) collective-permute-start(bf16[8,128,256]{2,1,0:T(8,128)(2,1)S(1)} %all_to_all.45.refs_4_), channel_id=1, source_target_pairs={{0,1},{1,0},{2,3},{3,2},{4,5},{5,4},{6,7},{7,6},{8,9},{9,8},{10,11... | collective-permute-start | bytes 1572872 | tf_op jit(solution)/shard_map/ppermute | solution.py:431

commit v14 on v13

--- a/solution.py
+++ b/solution.py
@@ -24,7 +24,7 @@
 ROWS = EIGHT * OWN
 PACK = OWN + WIDTH // 2 + 16
 BLOCK = 8 * PIECE
-SPLIT = 160
+SPLIT = 192
 TILES = 4
 MOVES = [(0, 0), (3, 0), (1, 0), (0, 1), (2, 0), (1, 1), (3, 1), (2, 1)]
 

time: 176 us -> 176 us (level)
  transfers between devices with their start and end apart: 13 -> 13, of which waited for: 7 -> 6; matrix products, arithmetic and copies ran while one was open for 0% -> 0% of each run, Pallas kernels for 11% -> 11%
where the time goes in v14:
time: 176 us; the launch traced here: 175 us
  blocking collectives  110 us (62%)
  Pallas kernels  29.5 us (17%)
  starting transfers between devices  25.3 us (14%)
  waiting for transfers between devices  7.31 us (4%)
    all_to_all x8, blocking collectives, exchange(): return lax.all_to_all(payload, axes, 0, 0)  110 us
    pallas_call x21, Pallas kernels, call(): pl.pallas_call(kernel, out_shape=shapes, in_specs=specs, out_specs=[VMEM]...  29.5 us
    ppermute x5, starting transfers between devices, swap_core(): return lax.ppermute(values, 'core', [(0, 1), (1, 0)])  13.1 us
    ppermute x3, starting transfers between devices, from_above(): return lax.ppermute(values, 'x', [(at, (at + 3) % 4) for at in range(4)])  6.95 us
    ppermute x3, starting transfers between devices, swap_z(): return lax.ppermute(values, 'zl', [(0, 1), (1, 0)])  3.92 us
  transfers between devices with their start and end apart: 13, of which 6 were waited for; matrix products, arithmetic and copies ran while one was open for 0% of the time, Pallas kernels for 11%

profile of v14, /device:TPU:1, one launch (start us, length us, event | category | flops | bytes accessed | tf_op | source)
XLA Modules:
  0.0 175.3 jit_solution(4196738117887437968)
XLA Ops:
  0.0 1.4 collective-permute-start
  1.4 1.7 pack.1
  3.1 1.4 collective-permute-start.3
  4.5 1.4 collective-permute-start.2
  5.9 1.7 collective-permute-start.1
  8.3 1.6 copy-done.1
  9.9 0.7 unit.2.refs_2_.refs_4_.refs_3_
  10.6 0.7 unit.3.refs_3_.refs_5_.refs_4_
  11.3 1.3 build.4
  12.7 1.4 collective-permute-done.3.refs_1_.refs_5_
  14.1 1.4 collective-permute-done.1.refs_3_.refs_7_
  15.5 1.2 collective-permute-start.5
  16.7 2.6 %collective-permute-start.4 = (bf16[336,512]{1,0:T(8,128)(2,1)S(1)}, bf16[336,512]{1,0:T(8,128)(2,1)S(1)}, u32[]{:S(2)}, u32[]{:S(2)}) collective-permute-start(bf16[336,512]{1,0:T(8,128)(2,1)S(1)} %collective-permute-done.1.refs_3_.refs_7_), channel_id=1, source_target_pairs={{0,12},{4,0},{8,4},{12,8},{1,13},{5,1},{9,5},{13,9},{2,14},{6,2},{... | collective-permute-start | bytes 1032200 | tf_op jit(solution)/shard_map/ppermute | solution.py:443
  19.3 3.5 %build.5 = (bf16[768,4096]{1,0:T(8,128)(2,1)S(1)}, f32[8,4096]{1,0:T(8,128)S(1)}) custom-call(f32[1]{0:T(128)S(6)} %copy.7.refs_0_, bf16[336,512]{1,0:T(8,128)(2,1)S(1)} %collective-permute-done.3.refs_1_.refs_5_, bf16[336,512]{1,0:T(8,128)(2,1)S(1)} %collective-permute-done.2.refs_2_.refs_6_, bf16[336,512]{1,0:T(8,128)(2,1)S(1)} %collective-permute-done.1.refs_3_.refs_7_, ...), custom_call_target="tpu_custom_call" | custom-call | flops 6442450944 | tf_op jit(solution)/shard_map/build/pallas_call | solution.py:92
  22.9 1.9 %collective-permute-done.4.refs_2_.refs_9_ = bf16[336,512]{1,0:T(8,128)(2,1)S(1)} collective-permute-done((bf16[336,512]{1,0:T(8,128)(2,1)S(1)}, bf16[336,512]{1,0:T(8,128)(2,1)S(1)}, u32[]{:S(2)}, u32[]{:S(2)}) %collective-permute-start.4) | collective-permute-done | bytes 344096 | tf_op jit(solution)/shard_map/ppermute | solution.py:443
  24.7 0.4 collective-permute-done.6.refs_1_.refs_8_
  25.1 1.0 collective-permute-start.7
  26.1 3.0 %collective-permute-start.8 = (bf16[192,512]{1,0:T(8,128)(2,1)S(1)}, bf16[192,512]{1,0:T(8,128)(2,1)S(1)}, u32[]{:S(2)}, u32[]{:S(2)}) collective-permute-start(bf16[192,512]{1,0:T(8,128)(2,1)S(1)} %slice.10), channel_id=1, source_target_pairs={{0,12},{4,0},{8,4},{12,8},{1,13},{5,1},{9,5},{13,9},{2,14},{6,2},{... | collective-permute-start | bytes 589832 | tf_op jit(solution)/shard_map/ppermute | solution.py:443
  29.1 3.5 %build.6 = (bf16[768,4096]{1,0:T(8,128)(2,1)S(1)}, f32[8,4096]{1,0:T(8,128)S(1)}) custom-call(f32[1]{0:T(128)S(6)} %copy.7.refs_0_, bf16[336,512]{1,0:T(8,128)(2,1)S(1)} %collective-permute-done.6.refs_1_.refs_8_, bf16[336,512]{1,0:T(8,128)(2,1)S(1)} %collective-permute-done.4.refs_2_.refs_9_, bf16[336,512]{1,0:T(8,128)(2,1)S(1)} %collective-permute-done.5.refs_3_.refs_10_, ...), custom_call_target="tpu_custom_call" | custom-call | flops 6442450944 | tf_op jit(solution)/shard_map/build/pallas_call | solution.py:92
  32.6 1.3 build.7
  34.0 1.3 side_terms.5
  35.2 3.2 %collective-permute-start.9 = (f32[8,136,256]{2,1,0:T(8,128)S(1)}, f32[8,136,256]{2,1,0:T(8,128)S(1)}, u32[]{:S(2)}, u32[]{:S(2)}) collective-permute-start(f32[8,136,256]{2,1,0:T(8,128)S(1)} %side_terms.5), channel_id=1, source_target_pairs={{0,1},{1,0},{2,3},{3,2},{4,5},{5,4},{6,7},{7,6},{8,9},{9,8},{10,11... | collective-permute-start | bytes 3342344 | tf_op jit(solution)/shard_map/ppermute | solution.py:431
  38.5 1.3 side_terms.4.refs_4_
  39.7 1.1 collective-permute-done.9.refs_5_
  40.8 0.3 pair.2
  41.1 18.3 %all_to_all.40.refs_4_ = bf16[8,144,256]{2,1,0:T(8,128)(2,1)S(1)} all-to-all(bf16[8,144,256]{2,1,0:T(8,128)(2,1)S(1)} %get-tuple-element.52), channel_id=1, replica_groups=mesh['y'=4,'zh'=2,'x'=4,'zl'=2,'core'=2] {'y','zh'}, dimensions={0} | all-to-all | bytes 1179648 | tf_op jit(solution)/shard_map/all_to_all | solution.py:427
  59.4 0.4 centre.2
  59.8 13.1 %all_to_all.41.refs_4_.refs_5_ = bf16[8,144,256]{2,1,0:T(8,128)(2,1)S(1)} all-to-all(bf16[8,144,256]{2,1,0:T(8,128)(2,1)S(1)} %get-tuple-element.53), channel_id=1, replica_groups=mesh['y'=4,'zh'=2,'x'=4,'zl'=2,'core'=2] {'y','zh'}, dimensions={0} | all-to-all | bytes 1179648 | tf_op jit(solution)/shard_map/all_to_all | solution.py:427
  72.9 2.9 %collective-permute-start.10 = (bf16[8,144,256]{2,1,0:T(8,128)(2,1)S(1)}, bf16[8,144,256]{2,1,0:T(8,128)(2,1)S(1)}, u32[]{:S(2)}, u32[]{:S(2)}) collective-permute-start(bf16[8,144,256]{2,1,0:T(8,128)(2,1)S(1)} %all_to_all.41.refs_4_.refs_5_), channel_id=1, source_target_pairs={{0,1},{1,0},{2,3},{3,2},{4,5},{5,4},{6,7},{7,6},{8,9},{9,8},{10,11... | collective-permute-start | bytes 1769480 | tf_op jit(solution)/shard_map/ppermute | solution.py:431
  75.8 2.5 %image_terms.4.refs_6_ = f32[2048,128]{1,0:T(8,128)S(1)} custom-call(bf16[256,4096]{1,0:T(8,128)(2,1)S(1)} %get-tuple-element.33.refs_0_, bf16[768,4096]{1,0:T(8,128)(2,1)S(1)} %get-tuple-element.38.refs_1_, bf16[768,4096]{1,0:T(8,128)(2,1)S(1)} %get-tuple-element.43.refs_2_, bf16[256,4096]{1,0:T(8,128)(2,1)S(1)} %get-tuple-element.47.refs_3_, ...), custom_call_target="tpu_custom_call" | custom-call | flops 1073741824 | tf_op jit(solution)/shard_map/image_terms/pallas_call | solution.py:92
  78.3 2.5 %image_terms.5 = bf16[8,256,128]{2,1,0:T(8,128)(2,1)S(1)} custom-call(bf16[256,4096]{1,0:T(8,128)(2,1)S(1)} %get-tuple-element.33.refs_0_, bf16[768,4096]{1,0:T(8,128)(2,1)S(1)} %get-tuple-element.38.refs_1_, bf16[768,4096]{1,0:T(8,128)(2,1)S(1)} %get-tuple-element.43.refs_2_, bf16[256,4096]{1,0:T(8,128)(2,1)S(1)} %get-tuple-element.47.refs_3_, ...), custom_call_target="tpu_custom_call" | custom-call | flops 1073741824 | tf_op jit(solution)/shard_map/image_terms/pallas_call | solution.py:92
  80.8 14.1 %all_to_all.42.refs_4_ = bf16[8,256,128]{2,1,0:T(8,128)(2,1)S(1)} all-to-all(bf16[8,256,128]{2,1,0:T(8,128)(2,1)S(1)} %image_terms.5), channel_id=1, replica_groups=mesh['y'=4,'zh'=2,'x'=4,'zl'=2,'core'=2] {'x','zl'}, dimensions={0} | all-to-all | bytes 1048576 | tf_op jit(solution)/shard_map/all_to_all | solution.py:427
  94.9 0.2 owner.2
  95.1 11.6 %all_to_all.43.refs_4_ = bf16[8,144,256]{2,1,0:T(8,128)(2,1)S(1)} all-to-all(bf16[8,144,256]{2,1,0:T(8,128)(2,1)S(1)} %owner.2), channel_id=1, replica_groups=mesh['y'=4,'zh'=2,'x'=4,'zl'=2,'core'=2] {'x','zl'}, dimensions={0} | all-to-all | bytes 1179648 | tf_op jit(solution)/shard_map/all_to_all | solution.py:427
  106.7 1.3 side_terms.7
  108.0 2.9 %collective-permute-start.11 = (f32[8,136,256]{2,1,0:T(8,128)S(1)}, f32[8,136,256]{2,1,0:T(8,128)S(1)}, u32[]{:S(2)}, u32[]{:S(2)}) collective-permute-start(f32[8,136,256]{2,1,0:T(8,128)S(1)} %side_terms.7), channel_id=1, source_target_pairs={{0,1},{1,0},{2,3},{3,2},{4,5},{5,4},{6,7},{7,6},{8,9},{9,8},{10,11... | collective-permute-start | bytes 3342344 | tf_op jit(solution)/shard_map/ppermute | solution.py:431
  110.9 1.3 side_terms.6.refs_4_
  112.2 1.1 collective-permute-done.11.refs_5_
  113.2 0.3 pair.3
  113.6 14.3 %all_to_all.44.refs_4_ = bf16[8,144,256]{2,1,0:T(8,128)(2,1)S(1)} all-to-all(bf16[8,144,256]{2,1,0:T(8,128)(2,1)S(1)} %pair.3), channel_id=1, replica_groups=mesh['y'=4,'zh'=2,'x'=4,'zl'=2,'core'=2] {'y','zh'}, dimensions={0} | all-to-all | bytes 1179648 | tf_op jit(solution)/shard_map/all_to_all | solution.py:427
  127.9 0.4 centre.3
  128.3 12.3 %all_to_all.45.refs_4_ = bf16[8,128,256]{2,1,0:T(8,128)(2,1)S(1)} all-to-all(bf16[8,128,256]{2,1,0:T(8,128)(2,1)S(1)} %centre.3), channel_id=1, replica_groups=mesh['y'=4,'zh'=2,'x'=4,'zl'=2,'core'=2] {'y','zh'}, dimensions={0} | all-to-all | bytes 1048576 | tf_op jit(solution)/shard_map/all_to_all | solution.py:427
  140.6 2.6 %collective-permute-start.12 = (bf16[8,128,256]{2,1,0:T(8,128)(2,1)S(1)}, bf16[8,128,256]{2,1,0:T(8,128)(2,1)S(1)}, u32[]{:S(2)}, u32[]{:S(2)}) collective-permute-start(bf16[8,128,256]{2,1,0:T(8,128)(2,1)S(1)} %all_to_all.45.refs_4_), channel_id=1, source_target_pairs={{0,1},{1,0},{2,3},{3,2},{4,5},{5,4},{6,7},{7,6},{8,9},{9,8},{10,11... | collective-permute-start | bytes 1572872 | tf_op jit(solution)/shard_map/ppermute | solution.py:431
  143.2 2.5 %image_terms.6.refs_6_ = f32[2048,128]{1,0:T(8,128)S(1)} custom-call(bf16[256,4096]{1,0:T(8,128)(2,1)S(1)} %get-tuple-element.33.refs_0_, bf16[768,4096]{1,0:T(8,128)(2,1)S(1)} %get-tuple-element.38.refs_1_, bf16[768,4096]{1,0:T(8,128)(2,1)S(1)} %get-tuple-element.43.refs_2_, bf16[256,4096]{1,0:T(8,128)(2,1)S(1)} %get-tuple-element.47.refs_3_, ...), custom_call_target="tpu_custom_call" | custom-call | flops 1073741824 | tf_op jit(solution)/shard_map/image_terms/pallas_call | solution.py:92
  145.6 2.5 %image_terms.7 = bf16[8,256,128]{2,1,0:T(8,128)(2,1)S(1)} custom-call(bf16[256,4096]{1,0:T(8,128)(2,1)S(1)} %get-tuple-element.33.refs_0_, bf16[768,4096]{1,0:T(8,128)(2,1)S(1)} %get-tuple-element.38.refs_1_, bf16[768,4096]{1,0:T(8,128)(2,1)S(1)} %get-tuple-element.43.refs_2_, bf16[256,4096]{1,0:T(8,128)(2,1)S(1)} %get-tuple-element.47.refs_3_, ...), custom_call_target="tpu_custom_call" | custom-call | flops 1073741824 | tf_op jit(solution)/shard_map/image_terms/pallas_call | solution.py:92
  148.1 12.0 %all_to_all.46.refs_0_ = bf16[8,256,128]{2,1,0:T(8,128)(2,1)S(1)} all-to-all(bf16[8,256,128]{2,1,0:T(8,128)(2,1)S(1)} %image_terms.7), channel_id=1, replica_groups=mesh['y'=4,'zh'=2,'x'=4,'zl'=2,'core'=2] {'x','zl'}, dimensions={0} | all-to-all | bytes 1048576 | tf_op jit(solution)/shard_map/all_to_all | solution.py:427
  160.3 14.3 %all_to_all.47 = f32[128,1,128]{2,1,0:T(1,128)S(1)} all-to-all(f32[128,1,128]{2,1,0:T(1,128)S(1)} %broadcast_in_dim.14), channel_id=1, replica_groups=mesh['y'=4,'zh'=2,'x'=4,'zl'=2,'core'=2] {'y','zh','x','zl','core'}, dimensions={0} | all-to-all | bytes 131072 | tf_op jit(solution)/shard_map/all_to_all | solution.py:427
  174.7 0.7 broadcast_divide_fusion
  (18 shorter events, 0.3 us)
Async XLA Ops:
  0.0 10.6 %collective-permute-start = (bf16[2048,512]{1,0:T(8,128)(2,1)}, bf16[2048,512]{1,0:T(8,128)(2,1)S(1)}, u32[]{:S(2)}, u32[]{:S(2)}) collective-permute-start(bf16[2048,512]{1,0:T(8,128)(2,1)} %in_ref.1), channel_id=1, source_target_pairs={{0,1},{1,0},{2,3},{3,2},{4,5},{5,4},{6,7},{7,6},{8,9},{9,8},{10,11... | collective-permute-start | bytes 6291464 | tf_op jit(solution)/shard_map/ppermute | solution.py:431
  3.1 11.0 %collective-permute-start.3 = (bf16[336,512]{1,0:T(8,128)(2,1)S(1)}, bf16[336,512]{1,0:T(8,128)(2,1)S(1)}, u32[]{:S(2)}, u32[]{:S(2)}) collective-permute-start(bf16[336,512]{1,0:T(8,128)(2,1)S(1)} %get-tuple-element.32.refs_1_.refs_4_), channel_id=1, source_target_pairs={{0,4},{4,8},{8,12},{12,0},{1,5},{5,9},{9,13},{13,1},{2,6},{6,10},{... | collective-permute-start | bytes 1032200 | tf_op jit(solution)/shard_map/ppermute | solution.py:439
  4.5 9.6 %collective-permute-start.2 = (bf16[336,512]{1,0:T(8,128)(2,1)S(1)}, bf16[336,512]{1,0:T(8,128)(2,1)S(1)}, u32[]{:S(2)}, u32[]{:S(2)}) collective-permute-start(bf16[336,512]{1,0:T(8,128)(2,1)S(1)} %get-tuple-element.32.refs_1_.refs_4_), channel_id=1, source_target_pairs={{0,12},{4,0},{8,4},{12,8},{1,13},{5,1},{9,5},{13,9},{2,14},{6,2},{... | collective-permute-start | bytes 1032200 | tf_op jit(solution)/shard_map/ppermute | solution.py:443
  5.9 9.6 %collective-permute-start.1 = (bf16[336,512]{1,0:T(8,128)(2,1)S(1)}, bf16[336,512]{1,0:T(8,128)(2,1)S(1)}, u32[]{:S(2)}, u32[]{:S(2)}) collective-permute-start(bf16[336,512]{1,0:T(8,128)(2,1)S(1)} %get-tuple-element.32.refs_1_.refs_4_), channel_id=1, source_target_pairs={{0,2},{2,0},{1,3},{3,1},{4,6},{6,4},{5,7},{7,5},{8,10},{10,8},{9,1... | collective-permute-start | bytes 1032200 | tf_op jit(solution)/shard_map/ppermute | solution.py:435
  8.3 1.6 copy-start.1
  15.5 9.6 %collective-permute-start.6 = (bf16[336,512]{1,0:T(8,128)(2,1)S(1)}, bf16[336,512]{1,0:T(8,128)(2,1)S(1)}, u32[]{:S(2)}, u32[]{:S(2)}) collective-permute-start(bf16[336,512]{1,0:T(8,128)(2,1)S(1)} %collective-permute-done.3.refs_1_.refs_5_), channel_id=1, source_target_pairs={{0,4},{4,8},{8,12},{12,0},{1,5},{5,9},{9,13},{13,1},{2,6},{6,10},{... | collective-permute-start | bytes 1032200 | tf_op jit(solution)/shard_map/ppermute | solution.py:439
  15.5 9.6 %collective-permute-start.5 = (bf16[336,512]{1,0:T(8,128)(2,1)S(1)}, bf16[336,512]{1,0:T(8,128)(2,1)S(1)}, u32[]{:S(2)}, u32[]{:S(2)}) collective-permute-start(bf16[336,512]{1,0:T(8,128)(2,1)S(1)} %collective-permute-done.3.refs_1_.refs_5_), channel_id=1, source_target_pairs={{0,2},{2,0},{1,3},{3,1},{4,6},{6,4},{5,7},{7,5},{8,10},{10,8},{9,1... | collective-permute-start | bytes 1032200 | tf_op jit(solution)/shard_map/ppermute | solution.py:435
  16.7 8.0 %collective-permute-start.4 = (bf16[336,512]{1,0:T(8,128)(2,1)S(1)}, bf16[336,512]{1,0:T(8,128)(2,1)S(1)}, u32[]{:S(2)}, u32[]{:S(2)}) collective-permute-start(bf16[336,512]{1,0:T(8,128)(2,1)S(1)} %collective-permute-done.1.refs_3_.refs_7_), channel_id=1, source_target_pairs={{0,12},{4,0},{8,4},{12,8},{1,13},{5,1},{9,5},{13,9},{2,14},{6,2},{... | collective-permute-start | bytes 1032200 | tf_op jit(solution)/shard_map/ppermute | solution.py:443
  25.1 7.5 %collective-permute-start.7 = (bf16[144,512]{1,0:T(8,128)(2,1)S(1)}, bf16[144,512]{1,0:T(8,128)(2,1)S(1)}, u32[]{:S(2)}, u32[]{:S(2)}) collective-permute-start(bf16[144,512]{1,0:T(8,128)(2,1)S(1)} %slice.9), channel_id=1, source_target_pairs={{0,2},{2,0},{1,3},{3,1},{4,6},{6,4},{5,7},{7,5},{8,10},{10,8},{9,1... | collective-permute-start | bytes 442376 | tf_op jit(solution)/shard_map/ppermute | solution.py:435
  26.1 6.5 %collective-permute-start.8 = (bf16[192,512]{1,0:T(8,128)(2,1)S(1)}, bf16[192,512]{1,0:T(8,128)(2,1)S(1)}, u32[]{:S(2)}, u32[]{:S(2)}) collective-permute-start(bf16[192,512]{1,0:T(8,128)(2,1)S(1)} %slice.10), channel_id=1, source_target_pairs={{0,12},{4,0},{8,4},{12,8},{1,13},{5,1},{9,5},{13,9},{2,14},{6,2},{... | collective-permute-start | bytes 589832 | tf_op jit(solution)/shard_map/ppermute | solution.py:443
  35.2 5.6 %collective-permute-start.9 = (f32[8,136,256]{2,1,0:T(8,128)S(1)}, f32[8,136,256]{2,1,0:T(8,128)S(1)}, u32[]{:S(2)}, u32[]{:S(2)}) collective-permute-start(f32[8,136,256]{2,1,0:T(8,128)S(1)} %side_terms.5), channel_id=1, source_target_pairs={{0,1},{1,0},{2,3},{3,2},{4,5},{5,4},{6,7},{7,6},{8,9},{9,8},{10,11... | collective-permute-start | bytes 3342344 | tf_op jit(solution)/shard_map/ppermute | solution.py:431
  72.9 5.4 %collective-permute-start.10 = (bf16[8,144,256]{2,1,0:T(8,128)(2,1)S(1)}, bf16[8,144,256]{2,1,0:T(8,128)(2,1)S(1)}, u32[]{:S(2)}, u32[]{:S(2)}) collective-permute-start(bf16[8,144,256]{2,1,0:T(8,128)(2,1)S(1)} %all_to_all.41.refs_4_.refs_5_), channel_id=1, source_target_pairs={{0,1},{1,0},{2,3},{3,2},{4,5},{5,4},{6,7},{7,6},{8,9},{9,8},{10,11... | collective-permute-start | bytes 1769480 | tf_op jit(solution)/shard_map/ppermute | solution.py:431
  78.3 16.6 %copy-start = (f32[8,256]{1,0:T(8,128)S(1)}, f32[8,256]{1,0:T(8,128)}, u32[]{:S(2)}) copy-start(f32[8,256]{1,0:T(8,128)} %get-tuple-element.54.refs_5_.refs_1_) | copy-start | bytes 24580
  108.0 5.3 %collective-permute-start.11 = (f32[8,136,256]{2,1,0:T(8,128)S(1)}, f32[8,136,256]{2,1,0:T(8,128)S(1)}, u32[]{:S(2)}, u32[]{:S(2)}) collective-permute-start(f32[8,136,256]{2,1,0:T(8,128)S(1)} %side_terms.7), channel_id=1, source_target_pairs={{0,1},{1,0},{2,3},{3,2},{4,5},{5,4},{6,7},{7,6},{8,9},{9,8},{10,11... | collective-permute-start | bytes 3342344 | tf_op jit(solution)/shard_map/ppermute | solution.py:431
  140.6 5.1 %collective-permute-start.12 = (bf16[8,128,256]{2,1,0:T(8,128)(2,1)S(1)}, bf16[8,128,256]{2,1,0:T(8,128)(2,1)S(1)}, u32[]{:S(2)}, u32[]{:S(2)}) collective-permute-start(bf16[8,128,256]{2,1,0:T(8,128)(2,1)S(1)} %all_to_all.45.refs_4_), channel_id=1, source_target_pairs={{0,1},{1,0},{2,3},{3,2},{4,5},{5,4},{6,7},{7,6},{8,9},{9,8},{10,11... | collective-permute-start | bytes 1572872 | tf_op jit(solution)/shard_map/ppermute | solution.py:431

commit v15 on v14

--- a/solution.py
+++ b/solution.py
@@ -24,7 +24,7 @@
 ROWS = EIGHT * OWN
 PACK = OWN + WIDTH // 2 + 16
 BLOCK = 8 * PIECE
-SPLIT = 192
+SPLIT = 128
 TILES = 4
 MOVES = [(0, 0), (3, 0), (1, 0), (0, 1), (2, 0), (1, 1), (3, 1), (2, 1)]
 

time: 176 us -> 176 us (level)
  transfers between devices with their start and end apart: 13 -> 13, of which waited for: 6 -> 7; matrix products, arithmetic and copies ran while one was open for 0% -> 0% of each run, Pallas kernels for 11% -> 11%
where the time goes in v15:
time: 176 us; the launch traced here: 175 us
  blocking collectives  109 us (62%)
  Pallas kernels  29.5 us (17%)
  starting transfers between devices  26.1 us (15%)
  waiting for transfers between devices  7.9 us (4%)
    all_to_all x8, blocking collectives, exchange(): return lax.all_to_all(payload, axes, 0, 0)  109 us
    pallas_call x21, Pallas kernels, call(): pl.pallas_call(kernel, out_shape=shapes, in_specs=specs, out_specs=[VMEM]...  29.5 us
    ppermute x5, starting transfers between devices, swap_core(): return lax.ppermute(values, 'core', [(0, 1), (1, 0)])  13.9 us
    ppermute x3, starting transfers between devices, from_above(): return lax.ppermute(values, 'x', [(at, (at + 3) % 4) for at in range(4)])  7.06 us
    ppermute x3, starting transfers between devices, swap_z(): return lax.ppermute(values, 'zl', [(0, 1), (1, 0)])  3.8 us
  transfers between devices with their start and end apart: 13, of which 7 were waited for; matrix products, arithmetic and copies ran while one was open for 0% of the time, Pallas kernels for 11%

profile of v15, /device:TPU:1, one launch (start us, length us, event | category | flops | bytes accessed | tf_op | source)
XLA Modules:
  0.0 175.4 jit_solution(16151979461909587330)
XLA Ops:
  0.0 1.4 collective-permute-start
  1.4 1.7 pack.1
  3.1 1.4 collective-permute-start.3
  4.5 1.4 collective-permute-start.2
  5.9 1.7 collective-permute-start.1
  8.3 1.6 copy-done.1
  9.9 0.7 unit.2.refs_2_.refs_4_.refs_3_
  10.6 0.7 unit.3.refs_3_.refs_5_.refs_4_
  11.3 1.3 build.4
  12.7 1.4 collective-permute-done.3.refs_1_.refs_5_
  14.1 1.4 collective-permute-done.1.refs_3_.refs_7_
  15.5 1.2 collective-permute-start.5
  16.7 2.6 %collective-permute-start.4 = (bf16[336,512]{1,0:T(8,128)(2,1)S(1)}, bf16[336,512]{1,0:T(8,128)(2,1)S(1)}, u32[]{:S(2)}, u32[]{:S(2)}) collective-permute-start(bf16[336,512]{1,0:T(8,128)(2,1)S(1)} %collective-permute-done.1.refs_3_.refs_7_), channel_id=1, source_target_pairs={{0,12},{4,0},{8,4},{12,8},{1,13},{5,1},{9,5},{13,9},{2,14},{6,2},{... | collective-permute-start | bytes 1032200 | tf_op jit(solution)/shard_map/ppermute | solution.py:443
  19.3 3.5 %build.5 = (bf16[768,4096]{1,0:T(8,128)(2,1)S(1)}, f32[8,4096]{1,0:T(8,128)S(1)}) custom-call(f32[1]{0:T(128)S(6)} %copy.7.refs_0_, bf16[336,512]{1,0:T(8,128)(2,1)S(1)} %collective-permute-done.3.refs_1_.refs_5_, bf16[336,512]{1,0:T(8,128)(2,1)S(1)} %collective-permute-done.2.refs_2_.refs_6_, bf16[336,512]{1,0:T(8,128)(2,1)S(1)} %collective-permute-done.1.refs_3_.refs_7_, ...), custom_call_target="tpu_custom_call" | custom-call | flops 6442450944 | tf_op jit(solution)/shard_map/build/pallas_call | solution.py:92
  22.9 1.9 %collective-permute-done.4.refs_2_.refs_9_ = bf16[336,512]{1,0:T(8,128)(2,1)S(1)} collective-permute-done((bf16[336,512]{1,0:T(8,128)(2,1)S(1)}, bf16[336,512]{1,0:T(8,128)(2,1)S(1)}, u32[]{:S(2)}, u32[]{:S(2)}) %collective-permute-start.4) | collective-permute-done | bytes 344096 | tf_op jit(solution)/shard_map/ppermute | solution.py:443
  24.7 0.4 collective-permute-done.6.refs_1_.refs_8_
  25.1 3.1 %collective-permute-start.8 = (bf16[128,512]{1,0:T(8,128)(2,1)S(1)}, bf16[128,512]{1,0:T(8,128)(2,1)S(1)}, u32[]{:S(2)}, u32[]{:S(2)}) collective-permute-start(bf16[128,512]{1,0:T(8,128)(2,1)S(1)} %slice.10), channel_id=1, source_target_pairs={{0,12},{4,0},{8,4},{12,8},{1,13},{5,1},{9,5},{13,9},{2,14},{6,2},{... | collective-permute-start | bytes 393224 | tf_op jit(solution)/shard_map/ppermute | solution.py:443
  28.2 0.8 collective-permute-start.7
  29.1 3.5 %build.6 = (bf16[768,4096]{1,0:T(8,128)(2,1)S(1)}, f32[8,4096]{1,0:T(8,128)S(1)}) custom-call(f32[1]{0:T(128)S(6)} %copy.7.refs_0_, bf16[336,512]{1,0:T(8,128)(2,1)S(1)} %collective-permute-done.6.refs_1_.refs_8_, bf16[336,512]{1,0:T(8,128)(2,1)S(1)} %collective-permute-done.4.refs_2_.refs_9_, bf16[336,512]{1,0:T(8,128)(2,1)S(1)} %collective-permute-done.5.refs_3_.refs_10_, ...), custom_call_target="tpu_custom_call" | custom-call | flops 6442450944 | tf_op jit(solution)/shard_map/build/pallas_call | solution.py:92
  32.6 0.6 collective-permute-done.7.refs_2_.refs_12_
  33.2 1.3 build.7
  34.5 1.3 side_terms.5
  35.8 4.4 %collective-permute-start.9 = (f32[8,136,256]{2,1,0:T(8,128)S(1)}, f32[8,136,256]{2,1,0:T(8,128)S(1)}, u32[]{:S(2)}, u32[]{:S(2)}) collective-permute-start(f32[8,136,256]{2,1,0:T(8,128)S(1)} %side_terms.5), channel_id=1, source_target_pairs={{0,1},{1,0},{2,3},{3,2},{4,5},{5,4},{6,7},{7,6},{8,9},{9,8},{10,11... | collective-permute-start | bytes 3342344 | tf_op jit(solution)/shard_map/ppermute | solution.py:431
  40.2 1.3 side_terms.4.refs_4_
  41.4 1.1 collective-permute-done.9.refs_5_
  42.6 0.3 pair.2
  42.9 18.5 %all_to_all.40.refs_4_ = bf16[8,144,256]{2,1,0:T(8,128)(2,1)S(1)} all-to-all(bf16[8,144,256]{2,1,0:T(8,128)(2,1)S(1)} %get-tuple-element.52), channel_id=1, replica_groups=mesh['y'=4,'zh'=2,'x'=4,'zl'=2,'core'=2] {'y','zh'}, dimensions={0} | all-to-all | bytes 1179648 | tf_op jit(solution)/shard_map/all_to_all | solution.py:427
  61.3 0.4 centre.2
  61.7 13.1 %all_to_all.41.refs_4_.refs_5_ = bf16[8,144,256]{2,1,0:T(8,128)(2,1)S(1)} all-to-all(bf16[8,144,256]{2,1,0:T(8,128)(2,1)S(1)} %get-tuple-element.53), channel_id=1, replica_groups=mesh['y'=4,'zh'=2,'x'=4,'zl'=2,'core'=2] {'y','zh'}, dimensions={0} | all-to-all | bytes 1179648 | tf_op jit(solution)/shard_map/all_to_all | solution.py:427
  74.8 2.9 %collective-permute-start.10 = (bf16[8,144,256]{2,1,0:T(8,128)(2,1)S(1)}, bf16[8,144,256]{2,1,0:T(8,128)(2,1)S(1)}, u32[]{:S(2)}, u32[]{:S(2)}) collective-permute-start(bf16[8,144,256]{2,1,0:T(8,128)(2,1)S(1)} %all_to_all.41.refs_4_.refs_5_), channel_id=1, source_target_pairs={{0,1},{1,0},{2,3},{3,2},{4,5},{5,4},{6,7},{7,6},{8,9},{9,8},{10,11... | collective-permute-start | bytes 1769480 | tf_op jit(solution)/shard_map/ppermute | solution.py:431
  77.7 2.5 %image_terms.4.refs_6_ = f32[2048,128]{1,0:T(8,128)S(1)} custom-call(bf16[256,4096]{1,0:T(8,128)(2,1)S(1)} %get-tuple-element.33.refs_0_, bf16[768,4096]{1,0:T(8,128)(2,1)S(1)} %get-tuple-element.38.refs_1_, bf16[768,4096]{1,0:T(8,128)(2,1)S(1)} %get-tuple-element.43.refs_2_, bf16[256,4096]{1,0:T(8,128)(2,1)S(1)} %get-tuple-element.47.refs_3_, ...), custom_call_target="tpu_custom_call" | custom-call | flops 1073741824 | tf_op jit(solution)/shard_map/image_terms/pallas_call | solution.py:92
  80.2 2.5 %image_terms.5 = bf16[8,256,128]{2,1,0:T(8,128)(2,1)S(1)} custom-call(bf16[256,4096]{1,0:T(8,128)(2,1)S(1)} %get-tuple-element.33.refs_0_, bf16[768,4096]{1,0:T(8,128)(2,1)S(1)} %get-tuple-element.38.refs_1_, bf16[768,4096]{1,0:T(8,128)(2,1)S(1)} %get-tuple-element.43.refs_2_, bf16[256,4096]{1,0:T(8,128)(2,1)S(1)} %get-tuple-element.47.refs_3_, ...), custom_call_target="tpu_custom_call" | custom-call | flops 1073741824 | tf_op jit(solution)/shard_map/image_terms/pallas_call | solution.py:92
  82.7 12.1 %all_to_all.42.refs_4_ = bf16[8,256,128]{2,1,0:T(8,128)(2,1)S(1)} all-to-all(bf16[8,256,128]{2,1,0:T(8,128)(2,1)S(1)} %image_terms.5), channel_id=1, replica_groups=mesh['y'=4,'zh'=2,'x'=4,'zl'=2,'core'=2] {'x','zl'}, dimensions={0} | all-to-all | bytes 1048576 | tf_op jit(solution)/shard_map/all_to_all | solution.py:427
  94.9 12.1 %all_to_all.43.refs_4_ = bf16[8,144,256]{2,1,0:T(8,128)(2,1)S(1)} all-to-all(bf16[8,144,256]{2,1,0:T(8,128)(2,1)S(1)} %owner.2), channel_id=1, replica_groups=mesh['y'=4,'zh'=2,'x'=4,'zl'=2,'core'=2] {'x','zl'}, dimensions={0} | all-to-all | bytes 1179648 | tf_op jit(solution)/shard_map/all_to_all | solution.py:427
  107.0 1.3 side_terms.7
  108.3 2.6 %collective-permute-start.11 = (f32[8,136,256]{2,1,0:T(8,128)S(1)}, f32[8,136,256]{2,1,0:T(8,128)S(1)}, u32[]{:S(2)}, u32[]{:S(2)}) collective-permute-start(f32[8,136,256]{2,1,0:T(8,128)S(1)} %side_terms.7), channel_id=1, source_target_pairs={{0,1},{1,0},{2,3},{3,2},{4,5},{5,4},{6,7},{7,6},{8,9},{9,8},{10,11... | collective-permute-start | bytes 3342344 | tf_op jit(solution)/shard_map/ppermute | solution.py:431
  110.9 1.3 side_terms.6.refs_4_
  112.2 1.1 collective-permute-done.11.refs_5_
  113.3 0.3 pair.3
  113.6 13.8 %all_to_all.44.refs_4_ = bf16[8,144,256]{2,1,0:T(8,128)(2,1)S(1)} all-to-all(bf16[8,144,256]{2,1,0:T(8,128)(2,1)S(1)} %pair.3), channel_id=1, replica_groups=mesh['y'=4,'zh'=2,'x'=4,'zl'=2,'core'=2] {'y','zh'}, dimensions={0} | all-to-all | bytes 1179648 | tf_op jit(solution)/shard_map/all_to_all | solution.py:427
  127.4 0.4 centre.3
  127.8 12.4 %all_to_all.45.refs_4_ = bf16[8,128,256]{2,1,0:T(8,128)(2,1)S(1)} all-to-all(bf16[8,128,256]{2,1,0:T(8,128)(2,1)S(1)} %centre.3), channel_id=1, replica_groups=mesh['y'=4,'zh'=2,'x'=4,'zl'=2,'core'=2] {'y','zh'}, dimensions={0} | all-to-all | bytes 1048576 | tf_op jit(solution)/shard_map/all_to_all | solution.py:427
  140.2 2.6 %collective-permute-start.12 = (bf16[8,128,256]{2,1,0:T(8,128)(2,1)S(1)}, bf16[8,128,256]{2,1,0:T(8,128)(2,1)S(1)}, u32[]{:S(2)}, u32[]{:S(2)}) collective-permute-start(bf16[8,128,256]{2,1,0:T(8,128)(2,1)S(1)} %all_to_all.45.refs_4_), channel_id=1, source_target_pairs={{0,1},{1,0},{2,3},{3,2},{4,5},{5,4},{6,7},{7,6},{8,9},{9,8},{10,11... | collective-permute-start | bytes 1572872 | tf_op jit(solution)/shard_map/ppermute | solution.py:431
  142.8 2.4 %image_terms.6.refs_6_ = f32[2048,128]{1,0:T(8,128)S(1)} custom-call(bf16[256,4096]{1,0:T(8,128)(2,1)S(1)} %get-tuple-element.33.refs_0_, bf16[768,4096]{1,0:T(8,128)(2,1)S(1)} %get-tuple-element.38.refs_1_, bf16[768,4096]{1,0:T(8,128)(2,1)S(1)} %get-tuple-element.43.refs_2_, bf16[256,4096]{1,0:T(8,128)(2,1)S(1)} %get-tuple-element.47.refs_3_, ...), custom_call_target="tpu_custom_call" | custom-call | flops 1073741824 | tf_op jit(solution)/shard_map/image_terms/pallas_call | solution.py:92
  145.3 2.5 %image_terms.7 = bf16[8,256,128]{2,1,0:T(8,128)(2,1)S(1)} custom-call(bf16[256,4096]{1,0:T(8,128)(2,1)S(1)} %get-tuple-element.33.refs_0_, bf16[768,4096]{1,0:T(8,128)(2,1)S(1)} %get-tuple-element.38.refs_1_, bf16[768,4096]{1,0:T(8,128)(2,1)S(1)} %get-tuple-element.43.refs_2_, bf16[256,4096]{1,0:T(8,128)(2,1)S(1)} %get-tuple-element.47.refs_3_, ...), custom_call_target="tpu_custom_call" | custom-call | flops 1073741824 | tf_op jit(solution)/shard_map/image_terms/pallas_call | solution.py:92
  147.7 12.0 %all_to_all.46.refs_0_ = bf16[8,256,128]{2,1,0:T(8,128)(2,1)S(1)} all-to-all(bf16[8,256,128]{2,1,0:T(8,128)(2,1)S(1)} %image_terms.7), channel_id=1, replica_groups=mesh['y'=4,'zh'=2,'x'=4,'zl'=2,'core'=2] {'x','zl'}, dimensions={0} | all-to-all | bytes 1048576 | tf_op jit(solution)/shard_map/all_to_all | solution.py:427
  159.9 14.8 %all_to_all.47 = f32[128,1,128]{2,1,0:T(1,128)S(1)} all-to-all(f32[128,1,128]{2,1,0:T(1,128)S(1)} %broadcast_in_dim.14), channel_id=1, replica_groups=mesh['y'=4,'zh'=2,'x'=4,'zl'=2,'core'=2] {'y','zh','x','zl','core'}, dimensions={0} | all-to-all | bytes 131072 | tf_op jit(solution)/shard_map/all_to_all | solution.py:427
  174.8 0.7 broadcast_divide_fusion
  (18 shorter events, 0.4 us)
Async XLA Ops:
  0.0 10.6 %collective-permute-start = (bf16[2048,512]{1,0:T(8,128)(2,1)}, bf16[2048,512]{1,0:T(8,128)(2,1)S(1)}, u32[]{:S(2)}, u32[]{:S(2)}) collective-permute-start(bf16[2048,512]{1,0:T(8,128)(2,1)} %in_ref.1), channel_id=1, source_target_pairs={{0,1},{1,0},{2,3},{3,2},{4,5},{5,4},{6,7},{7,6},{8,9},{9,8},{10,11... | collective-permute-start | bytes 6291464 | tf_op jit(solution)/shard_map/ppermute | solution.py:431
  3.1 11.0 %collective-permute-start.3 = (bf16[336,512]{1,0:T(8,128)(2,1)S(1)}, bf16[336,512]{1,0:T(8,128)(2,1)S(1)}, u32[]{:S(2)}, u32[]{:S(2)}) collective-permute-start(bf16[336,512]{1,0:T(8,128)(2,1)S(1)} %get-tuple-element.32.refs_1_.refs_4_), channel_id=1, source_target_pairs={{0,4},{4,8},{8,12},{12,0},{1,5},{5,9},{9,13},{13,1},{2,6},{6,10},{... | collective-permute-start | bytes 1032200 | tf_op jit(solution)/shard_map/ppermute | solution.py:439
  4.5 9.6 %collective-permute-start.2 = (bf16[336,512]{1,0:T(8,128)(2,1)S(1)}, bf16[336,512]{1,0:T(8,128)(2,1)S(1)}, u32[]{:S(2)}, u32[]{:S(2)}) collective-permute-start(bf16[336,512]{1,0:T(8,128)(2,1)S(1)} %get-tuple-element.32.refs_1_.refs_4_), channel_id=1, source_target_pairs={{0,12},{4,0},{8,4},{12,8},{1,13},{5,1},{9,5},{13,9},{2,14},{6,2},{... | collective-permute-start | bytes 1032200 | tf_op jit(solution)/shard_map/ppermute | solution.py:443
  5.9 9.6 %collective-permute-start.1 = (bf16[336,512]{1,0:T(8,128)(2,1)S(1)}, bf16[336,512]{1,0:T(8,128)(2,1)S(1)}, u32[]{:S(2)}, u32[]{:S(2)}) collective-permute-start(bf16[336,512]{1,0:T(8,128)(2,1)S(1)} %get-tuple-element.32.refs_1_.refs_4_), channel_id=1, source_target_pairs={{0,2},{2,0},{1,3},{3,1},{4,6},{6,4},{5,7},{7,5},{8,10},{10,8},{9,1... | collective-permute-start | bytes 1032200 | tf_op jit(solution)/shard_map/ppermute | solution.py:435
  8.3 1.6 copy-start.1
  15.5 9.6 %collective-permute-start.6 = (bf16[336,512]{1,0:T(8,128)(2,1)S(1)}, bf16[336,512]{1,0:T(8,128)(2,1)S(1)}, u32[]{:S(2)}, u32[]{:S(2)}) collective-permute-start(bf16[336,512]{1,0:T(8,128)(2,1)S(1)} %collective-permute-done.3.refs_1_.refs_5_), channel_id=1, source_target_pairs={{0,4},{4,8},{8,12},{12,0},{1,5},{5,9},{9,13},{13,1},{2,6},{6,10},{... | collective-permute-start | bytes 1032200 | tf_op jit(solution)/shard_map/ppermute | solution.py:439
  15.5 9.6 %collective-permute-start.5 = (bf16[336,512]{1,0:T(8,128)(2,1)S(1)}, bf16[336,512]{1,0:T(8,128)(2,1)S(1)}, u32[]{:S(2)}, u32[]{:S(2)}) collective-permute-start(bf16[336,512]{1,0:T(8,128)(2,1)S(1)} %collective-permute-done.3.refs_1_.refs_5_), channel_id=1, source_target_pairs={{0,2},{2,0},{1,3},{3,1},{4,6},{6,4},{5,7},{7,5},{8,10},{10,8},{9,1... | collective-permute-start | bytes 1032200 | tf_op jit(solution)/shard_map/ppermute | solution.py:435
  16.7 8.0 %collective-permute-start.4 = (bf16[336,512]{1,0:T(8,128)(2,1)S(1)}, bf16[336,512]{1,0:T(8,128)(2,1)S(1)}, u32[]{:S(2)}, u32[]{:S(2)}) collective-permute-start(bf16[336,512]{1,0:T(8,128)(2,1)S(1)} %collective-permute-done.1.refs_3_.refs_7_), channel_id=1, source_target_pairs={{0,12},{4,0},{8,4},{12,8},{1,13},{5,1},{9,5},{13,9},{2,14},{6,2},{... | collective-permute-start | bytes 1032200 | tf_op jit(solution)/shard_map/ppermute | solution.py:443
  25.1 7.5 %collective-permute-start.8 = (bf16[128,512]{1,0:T(8,128)(2,1)S(1)}, bf16[128,512]{1,0:T(8,128)(2,1)S(1)}, u32[]{:S(2)}, u32[]{:S(2)}) collective-permute-start(bf16[128,512]{1,0:T(8,128)(2,1)S(1)} %slice.10), channel_id=1, source_target_pairs={{0,12},{4,0},{8,4},{12,8},{1,13},{5,1},{9,5},{13,9},{2,14},{6,2},{... | collective-permute-start | bytes 393224 | tf_op jit(solution)/shard_map/ppermute | solution.py:443
  28.2 5.0 %collective-permute-start.7 = (bf16[208,512]{1,0:T(8,128)(2,1)S(1)}, bf16[208,512]{1,0:T(8,128)(2,1)S(1)}, u32[]{:S(2)}, u32[]{:S(2)}) collective-permute-start(bf16[208,512]{1,0:T(8,128)(2,1)S(1)} %slice.9), channel_id=1, source_target_pairs={{0,2},{2,0},{1,3},{3,1},{4,6},{6,4},{5,7},{7,5},{8,10},{10,8},{9,1... | collective-permute-start | bytes 638984 | tf_op jit(solution)/shard_map/ppermute | solution.py:435
  35.8 6.8 %collective-permute-start.9 = (f32[8,136,256]{2,1,0:T(8,128)S(1)}, f32[8,136,256]{2,1,0:T(8,128)S(1)}, u32[]{:S(2)}, u32[]{:S(2)}) collective-permute-start(f32[8,136,256]{2,1,0:T(8,128)S(1)} %side_terms.5), channel_id=1, source_target_pairs={{0,1},{1,0},{2,3},{3,2},{4,5},{5,4},{6,7},{7,6},{8,9},{9,8},{10,11... | collective-permute-start | bytes 3342344 | tf_op jit(solution)/shard_map/ppermute | solution.py:431
  74.8 5.4 %collective-permute-start.10 = (bf16[8,144,256]{2,1,0:T(8,128)(2,1)S(1)}, bf16[8,144,256]{2,1,0:T(8,128)(2,1)S(1)}, u32[]{:S(2)}, u32[]{:S(2)}) collective-permute-start(bf16[8,144,256]{2,1,0:T(8,128)(2,1)S(1)} %all_to_all.41.refs_4_.refs_5_), channel_id=1, source_target_pairs={{0,1},{1,0},{2,3},{3,2},{4,5},{5,4},{6,7},{7,6},{8,9},{9,8},{10,11... | collective-permute-start | bytes 1769480 | tf_op jit(solution)/shard_map/ppermute | solution.py:431
  80.2 14.6 %copy-start = (f32[8,256]{1,0:T(8,128)S(1)}, f32[8,256]{1,0:T(8,128)}, u32[]{:S(2)}) copy-start(f32[8,256]{1,0:T(8,128)} %get-tuple-element.54.refs_5_.refs_1_) | copy-start | bytes 24580
  108.3 5.0 %collective-permute-start.11 = (f32[8,136,256]{2,1,0:T(8,128)S(1)}, f32[8,136,256]{2,1,0:T(8,128)S(1)}, u32[]{:S(2)}, u32[]{:S(2)}) collective-permute-start(f32[8,136,256]{2,1,0:T(8,128)S(1)} %side_terms.7), channel_id=1, source_target_pairs={{0,1},{1,0},{2,3},{3,2},{4,5},{5,4},{6,7},{7,6},{8,9},{9,8},{10,11... | collective-permute-start | bytes 3342344 | tf_op jit(solution)/shard_map/ppermute | solution.py:431
  140.2 5.1 %collective-permute-start.12 = (bf16[8,128,256]{2,1,0:T(8,128)(2,1)S(1)}, bf16[8,128,256]{2,1,0:T(8,128)(2,1)S(1)}, u32[]{:S(2)}, u32[]{:S(2)}) collective-permute-start(bf16[8,128,256]{2,1,0:T(8,128)(2,1)S(1)} %all_to_all.45.refs_4_), channel_id=1, source_target_pairs={{0,1},{1,0},{2,3},{3,2},{4,5},{5,4},{6,7},{7,6},{8,9},{9,8},{10,11... | collective-permute-start | bytes 1572872 | tf_op jit(solution)/shard_map/ppermute | solution.py:431

commit v16 on v13

--- a/solution.py
+++ b/solution.py
@@ -530,7 +530,7 @@
             vectors = exchange(vectors, ROW_AXES)
     image, squares = owner(True, tiles, parts, weight)
     count = lax.axis_size(AXES)
-    every = exchange(jnp.broadcast_to(squares[:1][None], (count, 1, WIDTH)), AXES)
+    every = exchange(jnp.broadcast_to(squares[:1][None], (count, 1, WIDTH)), AXES[::-1])
     scale = jnp.sqrt(jnp.sum(every[:, 0], axis=0) / total_rows + 1e-06)
     return image / scale[None, :]
 

time: 176 us -> 176 us (level)
  no operation moved by 1% of the time
where the time goes in v16:
time: 176 us; the launch traced here: 175 us
  blocking collectives  109 us (62%)
  Pallas kernels  29.5 us (17%)
  starting transfers between devices  26.1 us (15%)
  waiting for transfers between devices  7.54 us (4%)
    all_to_all x8, blocking collectives, exchange(): return lax.all_to_all(payload, axes, 0, 0)  109 us
    pallas_call x21, Pallas kernels, call(): pl.pallas_call(kernel, out_shape=shapes, in_specs=specs, out_specs=[VMEM]...  29.5 us
    ppermute x5, starting transfers between devices, swap_core(): return lax.ppermute(values, 'core', [(0, 1), (1, 0)])  13.9 us
    ppermute x3, starting transfers between devices, from_above(): return lax.ppermute(values, 'x', [(at, (at + 3) % 4) for at in range(4)])  7.06 us
    ppermute x3, starting transfers between devices, swap_z(): return lax.ppermute(values, 'zl', [(0, 1), (1, 0)])  3.8 us
  transfers between devices with their start and end apart: 13, of which 7 were waited for; matrix products, arithmetic and copies ran while one was open for 0% of the time, Pallas kernels for 11%

profile of v16, /device:TPU:1, one launch (start us, length us, event | category | flops | bytes accessed | tf_op | source)
XLA Modules:
  0.0 175.2 jit_solution(1232513187691239504)
XLA Ops:
  0.0 1.4 collective-permute-start
  1.4 1.7 pack.1
  3.1 1.4 collective-permute-start.3
  4.5 1.4 collective-permute-start.2
  5.9 1.7 collective-permute-start.1
  8.3 1.6 copy-done.1
  9.9 0.7 unit.2.refs_2_.refs_4_.refs_3_
  10.6 0.7 unit.3.refs_3_.refs_5_.refs_4_
  11.3 1.3 build.4
  12.7 1.4 collective-permute-done.3.refs_1_.refs_5_
  14.1 1.4 collective-permute-done.1.refs_3_.refs_7_
  15.5 1.2 collective-permute-start.5
  16.7 2.6 %collective-permute-start.4 = (bf16[336,512]{1,0:T(8,128)(2,1)S(1)}, bf16[336,512]{1,0:T(8,128)(2,1)S(1)}, u32[]{:S(2)}, u32[]{:S(2)}) collective-permute-start(bf16[336,512]{1,0:T(8,128)(2,1)S(1)} %collective-permute-done.1.refs_3_.refs_7_), channel_id=1, source_target_pairs={{0,12},{4,0},{8,4},{12,8},{1,13},{5,1},{9,5},{13,9},{2,14},{6,2},{... | collective-permute-start | bytes 1032200 | tf_op jit(solution)/shard_map/ppermute | solution.py:443
  19.3 3.5 %build.5 = (bf16[768,4096]{1,0:T(8,128)(2,1)S(1)}, f32[8,4096]{1,0:T(8,128)S(1)}) custom-call(f32[1]{0:T(128)S(6)} %copy.7.refs_0_, bf16[336,512]{1,0:T(8,128)(2,1)S(1)} %collective-permute-done.3.refs_1_.refs_5_, bf16[336,512]{1,0:T(8,128)(2,1)S(1)} %collective-permute-done.2.refs_2_.refs_6_, bf16[336,512]{1,0:T(8,128)(2,1)S(1)} %collective-permute-done.1.refs_3_.refs_7_, ...), custom_call_target="tpu_custom_call" | custom-call | flops 6442450944 | tf_op jit(solution)/shard_map/build/pallas_call | solution.py:92
  22.9 1.9 %collective-permute-done.4.refs_2_.refs_9_ = bf16[336,512]{1,0:T(8,128)(2,1)S(1)} collective-permute-done((bf16[336,512]{1,0:T(8,128)(2,1)S(1)}, bf16[336,512]{1,0:T(8,128)(2,1)S(1)}, u32[]{:S(2)}, u32[]{:S(2)}) %collective-permute-start.4) | collective-permute-done | bytes 344096 | tf_op jit(solution)/shard_map/ppermute | solution.py:443
  24.7 0.4 collective-permute-done.6.refs_1_.refs_8_
  25.1 3.1 %collective-permute-start.8 = (bf16[160,512]{1,0:T(8,128)(2,1)S(1)}, bf16[160,512]{1,0:T(8,128)(2,1)S(1)}, u32[]{:S(2)}, u32[]{:S(2)}) collective-permute-start(bf16[160,512]{1,0:T(8,128)(2,1)S(1)} %slice.10), channel_id=1, source_target_pairs={{0,12},{4,0},{8,4},{12,8},{1,13},{5,1},{9,5},{13,9},{2,14},{6,2},{... | collective-permute-start | bytes 491528 | tf_op jit(solution)/shard_map/ppermute | solution.py:443
  28.2 0.8 collective-permute-start.7
  29.1 3.5 %build.6 = (bf16[768,4096]{1,0:T(8,128)(2,1)S(1)}, f32[8,4096]{1,0:T(8,128)S(1)}) custom-call(f32[1]{0:T(128)S(6)} %copy.7.refs_0_, bf16[336,512]{1,0:T(8,128)(2,1)S(1)} %collective-permute-done.6.refs_1_.refs_8_, bf16[336,512]{1,0:T(8,128)(2,1)S(1)} %collective-permute-done.4.refs_2_.refs_9_, bf16[336,512]{1,0:T(8,128)(2,1)S(1)} %collective-permute-done.5.refs_3_.refs_10_, ...), custom_call_target="tpu_custom_call" | custom-call | flops 6442450944 | tf_op jit(solution)/shard_map/build/pallas_call | solution.py:92
  32.6 0.2 collective-permute-done.7.refs_2_.refs_12_
  32.8 1.3 build.7
  34.2 1.3 side_terms.5
  35.4 4.4 %collective-permute-start.9 = (f32[8,136,256]{2,1,0:T(8,128)S(1)}, f32[8,136,256]{2,1,0:T(8,128)S(1)}, u32[]{:S(2)}, u32[]{:S(2)}) collective-permute-start(f32[8,136,256]{2,1,0:T(8,128)S(1)} %side_terms.5), channel_id=1, source_target_pairs={{0,1},{1,0},{2,3},{3,2},{4,5},{5,4},{6,7},{7,6},{8,9},{9,8},{10,11... | collective-permute-start | bytes 3342344 | tf_op jit(solution)/shard_map/ppermute | solution.py:431
  39.8 1.3 side_terms.4.refs_4_
  41.1 1.1 collective-permute-done.9.refs_5_
  42.2 0.3 pair.2
  42.5 18.5 %all_to_all.40.refs_4_ = bf16[8,144,256]{2,1,0:T(8,128)(2,1)S(1)} all-to-all(bf16[8,144,256]{2,1,0:T(8,128)(2,1)S(1)} %get-tuple-element.52), channel_id=1, replica_groups=mesh['y'=4,'zh'=2,'x'=4,'zl'=2,'core'=2] {'y','zh'}, dimensions={0} | all-to-all | bytes 1179648 | tf_op jit(solution)/shard_map/all_to_all | solution.py:427
  61.0 0.4 centre.2
  61.4 13.1 %all_to_all.41.refs_4_.refs_5_ = bf16[8,144,256]{2,1,0:T(8,128)(2,1)S(1)} all-to-all(bf16[8,144,256]{2,1,0:T(8,128)(2,1)S(1)} %get-tuple-element.53), channel_id=1, replica_groups=mesh['y'=4,'zh'=2,'x'=4,'zl'=2,'core'=2] {'y','zh'}, dimensions={0} | all-to-all | bytes 1179648 | tf_op jit(solution)/shard_map/all_to_all | solution.py:427
  74.4 2.9 %collective-permute-start.10 = (bf16[8,144,256]{2,1,0:T(8,128)(2,1)S(1)}, bf16[8,144,256]{2,1,0:T(8,128)(2,1)S(1)}, u32[]{:S(2)}, u32[]{:S(2)}) collective-permute-start(bf16[8,144,256]{2,1,0:T(8,128)(2,1)S(1)} %all_to_all.41.refs_4_.refs_5_), channel_id=1, source_target_pairs={{0,1},{1,0},{2,3},{3,2},{4,5},{5,4},{6,7},{7,6},{8,9},{9,8},{10,11... | collective-permute-start | bytes 1769480 | tf_op jit(solution)/shard_map/ppermute | solution.py:431
  77.3 2.5 %image_terms.4.refs_6_ = f32[2048,128]{1,0:T(8,128)S(1)} custom-call(bf16[256,4096]{1,0:T(8,128)(2,1)S(1)} %get-tuple-element.33.refs_0_, bf16[768,4096]{1,0:T(8,128)(2,1)S(1)} %get-tuple-element.38.refs_1_, bf16[768,4096]{1,0:T(8,128)(2,1)S(1)} %get-tuple-element.43.refs_2_, bf16[256,4096]{1,0:T(8,128)(2,1)S(1)} %get-tuple-element.47.refs_3_, ...), custom_call_target="tpu_custom_call" | custom-call | flops 1073741824 | tf_op jit(solution)/shard_map/image_terms/pallas_call | solution.py:92
  79.8 2.5 %image_terms.5 = bf16[8,256,128]{2,1,0:T(8,128)(2,1)S(1)} custom-call(bf16[256,4096]{1,0:T(8,128)(2,1)S(1)} %get-tuple-element.33.refs_0_, bf16[768,4096]{1,0:T(8,128)(2,1)S(1)} %get-tuple-element.38.refs_1_, bf16[768,4096]{1,0:T(8,128)(2,1)S(1)} %get-tuple-element.43.refs_2_, bf16[256,4096]{1,0:T(8,128)(2,1)S(1)} %get-tuple-element.47.refs_3_, ...), custom_call_target="tpu_custom_call" | custom-call | flops 1073741824 | tf_op jit(solution)/shard_map/image_terms/pallas_call | solution.py:92
  82.3 12.1 %all_to_all.42.refs_4_ = bf16[8,256,128]{2,1,0:T(8,128)(2,1)S(1)} all-to-all(bf16[8,256,128]{2,1,0:T(8,128)(2,1)S(1)} %image_terms.5), channel_id=1, replica_groups=mesh['y'=4,'zh'=2,'x'=4,'zl'=2,'core'=2] {'x','zl'}, dimensions={0} | all-to-all | bytes 1048576 | tf_op jit(solution)/shard_map/all_to_all | solution.py:427
  94.6 12.1 %all_to_all.43.refs_4_ = bf16[8,144,256]{2,1,0:T(8,128)(2,1)S(1)} all-to-all(bf16[8,144,256]{2,1,0:T(8,128)(2,1)S(1)} %owner.2), channel_id=1, replica_groups=mesh['y'=4,'zh'=2,'x'=4,'zl'=2,'core'=2] {'x','zl'}, dimensions={0} | all-to-all | bytes 1179648 | tf_op jit(solution)/shard_map/all_to_all | solution.py:427
  106.7 1.3 side_terms.7
  108.0 2.6 %collective-permute-start.11 = (f32[8,136,256]{2,1,0:T(8,128)S(1)}, f32[8,136,256]{2,1,0:T(8,128)S(1)}, u32[]{:S(2)}, u32[]{:S(2)}) collective-permute-start(f32[8,136,256]{2,1,0:T(8,128)S(1)} %side_terms.7), channel_id=1, source_target_pairs={{0,1},{1,0},{2,3},{3,2},{4,5},{5,4},{6,7},{7,6},{8,9},{9,8},{10,11... | collective-permute-start | bytes 3342344 | tf_op jit(solution)/shard_map/ppermute | solution.py:431
  110.6 1.3 side_terms.6.refs_4_
  111.8 1.1 collective-permute-done.11.refs_5_
  112.9 0.3 pair.3
  113.3 13.8 %all_to_all.44.refs_4_ = bf16[8,144,256]{2,1,0:T(8,128)(2,1)S(1)} all-to-all(bf16[8,144,256]{2,1,0:T(8,128)(2,1)S(1)} %pair.3), channel_id=1, replica_groups=mesh['y'=4,'zh'=2,'x'=4,'zl'=2,'core'=2] {'y','zh'}, dimensions={0} | all-to-all | bytes 1179648 | tf_op jit(solution)/shard_map/all_to_all | solution.py:427
  127.0 0.4 centre.3
  127.5 12.4 %all_to_all.45.refs_4_ = bf16[8,128,256]{2,1,0:T(8,128)(2,1)S(1)} all-to-all(bf16[8,128,256]{2,1,0:T(8,128)(2,1)S(1)} %centre.3), channel_id=1, replica_groups=mesh['y'=4,'zh'=2,'x'=4,'zl'=2,'core'=2] {'y','zh'}, dimensions={0} | all-to-all | bytes 1048576 | tf_op jit(solution)/shard_map/all_to_all | solution.py:427
  139.8 2.6 %collective-permute-start.12 = (bf16[8,128,256]{2,1,0:T(8,128)(2,1)S(1)}, bf16[8,128,256]{2,1,0:T(8,128)(2,1)S(1)}, u32[]{:S(2)}, u32[]{:S(2)}) collective-permute-start(bf16[8,128,256]{2,1,0:T(8,128)(2,1)S(1)} %all_to_all.45.refs_4_), channel_id=1, source_target_pairs={{0,1},{1,0},{2,3},{3,2},{4,5},{5,4},{6,7},{7,6},{8,9},{9,8},{10,11... | collective-permute-start | bytes 1572872 | tf_op jit(solution)/shard_map/ppermute | solution.py:431
  142.4 2.4 %image_terms.6.refs_6_ = f32[2048,128]{1,0:T(8,128)S(1)} custom-call(bf16[256,4096]{1,0:T(8,128)(2,1)S(1)} %get-tuple-element.33.refs_0_, bf16[768,4096]{1,0:T(8,128)(2,1)S(1)} %get-tuple-element.38.refs_1_, bf16[768,4096]{1,0:T(8,128)(2,1)S(1)} %get-tuple-element.43.refs_2_, bf16[256,4096]{1,0:T(8,128)(2,1)S(1)} %get-tuple-element.47.refs_3_, ...), custom_call_target="tpu_custom_call" | custom-call | flops 1073741824 | tf_op jit(solution)/shard_map/image_terms/pallas_call | solution.py:92
  144.9 2.5 %image_terms.7 = bf16[8,256,128]{2,1,0:T(8,128)(2,1)S(1)} custom-call(bf16[256,4096]{1,0:T(8,128)(2,1)S(1)} %get-tuple-element.33.refs_0_, bf16[768,4096]{1,0:T(8,128)(2,1)S(1)} %get-tuple-element.38.refs_1_, bf16[768,4096]{1,0:T(8,128)(2,1)S(1)} %get-tuple-element.43.refs_2_, bf16[256,4096]{1,0:T(8,128)(2,1)S(1)} %get-tuple-element.47.refs_3_, ...), custom_call_target="tpu_custom_call" | custom-call | flops 1073741824 | tf_op jit(solution)/shard_map/image_terms/pallas_call | solution.py:92
  147.4 12.0 %all_to_all.46.refs_0_ = bf16[8,256,128]{2,1,0:T(8,128)(2,1)S(1)} all-to-all(bf16[8,256,128]{2,1,0:T(8,128)(2,1)S(1)} %image_terms.7), channel_id=1, replica_groups=mesh['y'=4,'zh'=2,'x'=4,'zl'=2,'core'=2] {'x','zl'}, dimensions={0} | all-to-all | bytes 1048576 | tf_op jit(solution)/shard_map/all_to_all | solution.py:427
  159.6 14.9 %all_to_all.47 = f32[128,1,128]{2,1,0:T(1,128)S(1)} all-to-all(f32[128,1,128]{2,1,0:T(1,128)S(1)} %broadcast_in_dim.14), channel_id=1, replica_groups=mesh['y'=4,'zh'=2,'x'=4,'zl'=2,'core'=2] {'core','zl','x','zh','y'}, dimensions={0} | all-to-all | bytes 131072 | tf_op jit(solution)/shard_map/all_to_all | solution.py:427
  174.5 0.7 broadcast_divide_fusion
  (18 shorter events, 0.4 us)
Async XLA Ops:
  0.0 10.6 %collective-permute-start = (bf16[2048,512]{1,0:T(8,128)(2,1)}, bf16[2048,512]{1,0:T(8,128)(2,1)S(1)}, u32[]{:S(2)}, u32[]{:S(2)}) collective-permute-start(bf16[2048,512]{1,0:T(8,128)(2,1)} %in_ref.1), channel_id=1, source_target_pairs={{0,1},{1,0},{2,3},{3,2},{4,5},{5,4},{6,7},{7,6},{8,9},{9,8},{10,11... | collective-permute-start | bytes 6291464 | tf_op jit(solution)/shard_map/ppermute | solution.py:431
  3.1 11.0 %collective-permute-start.3 = (bf16[336,512]{1,0:T(8,128)(2,1)S(1)}, bf16[336,512]{1,0:T(8,128)(2,1)S(1)}, u32[]{:S(2)}, u32[]{:S(2)}) collective-permute-start(bf16[336,512]{1,0:T(8,128)(2,1)S(1)} %get-tuple-element.32.refs_1_.refs_4_), channel_id=1, source_target_pairs={{0,4},{4,8},{8,12},{12,0},{1,5},{5,9},{9,13},{13,1},{2,6},{6,10},{... | collective-permute-start | bytes 1032200 | tf_op jit(solution)/shard_map/ppermute | solution.py:439
  4.5 9.6 %collective-permute-start.2 = (bf16[336,512]{1,0:T(8,128)(2,1)S(1)}, bf16[336,512]{1,0:T(8,128)(2,1)S(1)}, u32[]{:S(2)}, u32[]{:S(2)}) collective-permute-start(bf16[336,512]{1,0:T(8,128)(2,1)S(1)} %get-tuple-element.32.refs_1_.refs_4_), channel_id=1, source_target_pairs={{0,12},{4,0},{8,4},{12,8},{1,13},{5,1},{9,5},{13,9},{2,14},{6,2},{... | collective-permute-start | bytes 1032200 | tf_op jit(solution)/shard_map/ppermute | solution.py:443
  5.9 9.6 %collective-permute-start.1 = (bf16[336,512]{1,0:T(8,128)(2,1)S(1)}, bf16[336,512]{1,0:T(8,128)(2,1)S(1)}, u32[]{:S(2)}, u32[]{:S(2)}) collective-permute-start(bf16[336,512]{1,0:T(8,128)(2,1)S(1)} %get-tuple-element.32.refs_1_.refs_4_), channel_id=1, source_target_pairs={{0,2},{2,0},{1,3},{3,1},{4,6},{6,4},{5,7},{7,5},{8,10},{10,8},{9,1... | collective-permute-start | bytes 1032200 | tf_op jit(solution)/shard_map/ppermute | solution.py:435
  8.3 1.6 copy-start.1
  15.5 9.6 %collective-permute-start.6 = (bf16[336,512]{1,0:T(8,128)(2,1)S(1)}, bf16[336,512]{1,0:T(8,128)(2,1)S(1)}, u32[]{:S(2)}, u32[]{:S(2)}) collective-permute-start(bf16[336,512]{1,0:T(8,128)(2,1)S(1)} %collective-permute-done.3.refs_1_.refs_5_), channel_id=1, source_target_pairs={{0,4},{4,8},{8,12},{12,0},{1,5},{5,9},{9,13},{13,1},{2,6},{6,10},{... | collective-permute-start | bytes 1032200 | tf_op jit(solution)/shard_map/ppermute | solution.py:439
  15.5 9.6 %collective-permute-start.5 = (bf16[336,512]{1,0:T(8,128)(2,1)S(1)}, bf16[336,512]{1,0:T(8,128)(2,1)S(1)}, u32[]{:S(2)}, u32[]{:S(2)}) collective-permute-start(bf16[336,512]{1,0:T(8,128)(2,1)S(1)} %collective-permute-done.3.refs_1_.refs_5_), channel_id=1, source_target_pairs={{0,2},{2,0},{1,3},{3,1},{4,6},{6,4},{5,7},{7,5},{8,10},{10,8},{9,1... | collective-permute-start | bytes 1032200 | tf_op jit(solution)/shard_map/ppermute | solution.py:435
  16.7 8.0 %collective-permute-start.4 = (bf16[336,512]{1,0:T(8,128)(2,1)S(1)}, bf16[336,512]{1,0:T(8,128)(2,1)S(1)}, u32[]{:S(2)}, u32[]{:S(2)}) collective-permute-start(bf16[336,512]{1,0:T(8,128)(2,1)S(1)} %collective-permute-done.1.refs_3_.refs_7_), channel_id=1, source_target_pairs={{0,12},{4,0},{8,4},{12,8},{1,13},{5,1},{9,5},{13,9},{2,14},{6,2},{... | collective-permute-start | bytes 1032200 | tf_op jit(solution)/shard_map/ppermute | solution.py:443
  25.1 7.5 %collective-permute-start.8 = (bf16[160,512]{1,0:T(8,128)(2,1)S(1)}, bf16[160,512]{1,0:T(8,128)(2,1)S(1)}, u32[]{:S(2)}, u32[]{:S(2)}) collective-permute-start(bf16[160,512]{1,0:T(8,128)(2,1)S(1)} %slice.10), channel_id=1, source_target_pairs={{0,12},{4,0},{8,4},{12,8},{1,13},{5,1},{9,5},{13,9},{2,14},{6,2},{... | collective-permute-start | bytes 491528 | tf_op jit(solution)/shard_map/ppermute | solution.py:443
  28.2 4.6 %collective-permute-start.7 = (bf16[176,512]{1,0:T(8,128)(2,1)S(1)}, bf16[176,512]{1,0:T(8,128)(2,1)S(1)}, u32[]{:S(2)}, u32[]{:S(2)}) collective-permute-start(bf16[176,512]{1,0:T(8,128)(2,1)S(1)} %slice.9), channel_id=1, source_target_pairs={{0,2},{2,0},{1,3},{3,1},{4,6},{6,4},{5,7},{7,5},{8,10},{10,8},{9,1... | collective-permute-start | bytes 540680 | tf_op jit(solution)/shard_map/ppermute | solution.py:435
  35.4 6.8 %collective-permute-start.9 = (f32[8,136,256]{2,1,0:T(8,128)S(1)}, f32[8,136,256]{2,1,0:T(8,128)S(1)}, u32[]{:S(2)}, u32[]{:S(2)}) collective-permute-start(f32[8,136,256]{2,1,0:T(8,128)S(1)} %side_terms.5), channel_id=1, source_target_pairs={{0,1},{1,0},{2,3},{3,2},{4,5},{5,4},{6,7},{7,6},{8,9},{9,8},{10,11... | collective-permute-start | bytes 3342344 | tf_op jit(solution)/shard_map/ppermute | solution.py:431
  74.4 5.4 %collective-permute-start.10 = (bf16[8,144,256]{2,1,0:T(8,128)(2,1)S(1)}, bf16[8,144,256]{2,1,0:T(8,128)(2,1)S(1)}, u32[]{:S(2)}, u32[]{:S(2)}) collective-permute-start(bf16[8,144,256]{2,1,0:T(8,128)(2,1)S(1)} %all_to_all.41.refs_4_.refs_5_), channel_id=1, source_target_pairs={{0,1},{1,0},{2,3},{3,2},{4,5},{5,4},{6,7},{7,6},{8,9},{9,8},{10,11... | collective-permute-start | bytes 1769480 | tf_op jit(solution)/shard_map/ppermute | solution.py:431
  79.8 14.6 %copy-start = (f32[8,256]{1,0:T(8,128)S(1)}, f32[8,256]{1,0:T(8,128)}, u32[]{:S(2)}) copy-start(f32[8,256]{1,0:T(8,128)} %get-tuple-element.54.refs_5_.refs_1_) | copy-start | bytes 24580
  108.0 5.0 %collective-permute-start.11 = (f32[8,136,256]{2,1,0:T(8,128)S(1)}, f32[8,136,256]{2,1,0:T(8,128)S(1)}, u32[]{:S(2)}, u32[]{:S(2)}) collective-permute-start(f32[8,136,256]{2,1,0:T(8,128)S(1)} %side_terms.7), channel_id=1, source_target_pairs={{0,1},{1,0},{2,3},{3,2},{4,5},{5,4},{6,7},{7,6},{8,9},{9,8},{10,11... | collective-permute-start | bytes 3342344 | tf_op jit(solution)/shard_map/ppermute | solution.py:431
  139.8 5.1 %collective-permute-start.12 = (bf16[8,128,256]{2,1,0:T(8,128)(2,1)S(1)}, bf16[8,128,256]{2,1,0:T(8,128)(2,1)S(1)}, u32[]{:S(2)}, u32[]{:S(2)}) collective-permute-start(bf16[8,128,256]{2,1,0:T(8,128)(2,1)S(1)} %all_to_all.45.refs_4_), channel_id=1, source_target_pairs={{0,1},{1,0},{2,3},{3,2},{4,5},{5,4},{6,7},{7,6},{8,9},{9,8},{10,11... | collective-permute-start | bytes 1572872 | tf_op jit(solution)/shard_map/ppermute | solution.py:431
